TPU v7x, 32 devices: a whole 2x2x4 slice. The times are simulated.
32 devices in a mesh: tm: 8 (over z, x), seq: 4 (over y, core).
Axes of the slice: x: 2, y: 2, z: 4, core: 2. Of those that a mesh axis runs over, the one named last changes fastest.
Arguments:
- large_view: bfloat16 [8, 2048, 768], P('seq', 'tm'), may hold values from -6 to 6
- small_view: bfloat16 [8, 1024, 768], P('seq', 'tm'), may hold values from -6 to 6
- clip_ids: int32 [8, 2048], P('seq', 'tm'), may hold values from 0 to 3, as said below
- first_gain: bfloat16 [768], replicated, may hold values from 0.099609375 to 1.8984375
- query_weight: bfloat16 [768, 768], replicated, may hold values from -0.21875 to 0.21875
- key_weight: bfloat16 [768, 768], replicated, may hold values from -0.21875 to 0.21875
- value_weight: bfloat16 [768, 768], replicated, may hold values from -0.21875 to 0.21875
- output_weight: bfloat16 [768, 768], replicated, may hold values from -0.875 to 0.875
- second_gain: bfloat16 [768], replicated, may hold values from 0.099609375 to 1.8984375
- up_weight: bfloat16 [768, 3072], replicated, may hold values from -0.21875 to 0.21875
- down_weight: bfloat16 [3072, 768], replicated, may hold values from -0.109375 to 0.109375
- query_gain: bfloat16 [768], replicated, may hold values from 0.099609375 to 1.8984375
- context_gain: bfloat16 [768], replicated, may hold values from 0.099609375 to 1.8984375
- cross_query: bfloat16 [768, 768], replicated, may hold values from -0.21875 to 0.21875
- cross_key: bfloat16 [768, 768], replicated, may hold values from -0.21875 to 0.21875
- cross_value: bfloat16 [768, 768], replicated, may hold values from -0.21875 to 0.21875
- cross_output: bfloat16 [768, 768], replicated, may hold values from -0.875 to 0.875
- cotangent: bfloat16 [8, 2048, 768], P('seq', 'tm'), may hold values from -6 to 6
Outputs:
- united_view: bfloat16 [8, 2048, 768], P('seq', 'tm')
- large_grad: float32 [8, 2048, 768], P('seq', 'tm')
- small_grad: float32 [8, 1024, 768], P('seq', 'tm')
- first_gain_grad: float32 [768], P('tm')
- query_weight_grad: float32 [768, 768], P('tm')
- key_weight_grad: float32 [768, 768], P('tm')
- value_weight_grad: float32 [768, 768], P('tm')
- output_weight_grad: float32 [768, 768], P('tm')
- second_gain_grad: float32 [768], P('tm')
- up_weight_grad: float32 [768, 3072], P('tm')
- down_weight_grad: float32 [3072, 768], P('tm')
- query_gain_grad: float32 [768], P('tm')
- context_gain_grad: float32 [768], P('tm')
- cross_query_grad: float32 [768, 768], P('tm')
- cross_key_grad: float32 [768, 768], P('tm')
- cross_value_grad: float32 [768, 768], P('tm')
- cross_output_grad: float32 [768, 768], P('tm')
Inputs may be any that keep to these rules, and one draw needn't show every extreme that they name: `clip_ids`: clip numbers start at 0 and never fall along a sequence; every clip starts at an even position and has an even number of tokens; of the 2 sequences on one index of seq, one is a single clip, and each of the others holds exactly four clips.
All inputs are finite; a program needn't handle non-finite values.
Results may differ from a plain program's by a relative error of at most 0.034.
Values may be sent and summed in bfloat16 or wider, within the bound.
A program may use at most 512 MiB of HBM per device.

v0:
```python
import jax
import jax.numpy as jnp
from jax import lax
from jax.sharding import PartitionSpec as P

HEADS = 12


EPS = 1e-05
NEGATIVE = -1e30


def layer_norm(value, gain):
    mean = jnp.mean(value, axis=-1, keepdims=True)
    centred = value - mean
    spread = jnp.mean(centred * centred, axis=-1, keepdims=True)
    return centred * lax.rsqrt(spread + EPS) * gain


def matmul(left, right):
    return jnp.einsum("std,de->ste", left, right, preferred_element_type=jnp.float32)


def matmul_back(grad, weight):
    return jnp.einsum("ste,de->std", grad, weight, preferred_element_type=jnp.float32)


def weight_grad(left, grad):
    return jnp.einsum("std,ste->de", left, grad, preferred_element_type=jnp.float32)


def split_heads(value, heads):
    return value.reshape(value.shape[0], value.shape[1], heads, value.shape[2] // heads)


def key_block():
    return 512


def gelu_tanh(value):
    return jax.nn.gelu(value, approximate=True)


def forward_fold(carry, keys, values, query, query_clip, key_clip):
    seqs, count, width = keys.shape
    heads = query.shape[2]
    scale = query.shape[3] ** (-0.5)
    block = key_block()

    def forward_one_block(state, number):
        running, totals, summed = state
        first = number * block
        keys_part = split_heads(lax.dynamic_slice_in_dim(keys, first, block, 1), heads)
        values_part = split_heads(lax.dynamic_slice_in_dim(values, first, block, 1), heads)
        clip_part = lax.dynamic_slice_in_dim(key_clip, first, block, 1)
        allowed = query_clip[:, None, :, None] == clip_part[:, None, None, :]
        score = (
            jnp.einsum("sqhe,skhe->shqk", query, keys_part, preferred_element_type=jnp.float32)
            * scale
        )
        score = jnp.where(allowed, score, NEGATIVE)
        highest = jnp.maximum(running, jnp.max(score, axis=-1))
        weight = jnp.where(allowed, jnp.exp(score - highest[..., None]), 0.0)
        shrink = jnp.exp(running - highest)
        totals = totals * shrink + jnp.sum(weight, axis=-1)
        update = jnp.einsum(
            "shqk,skhe->sqhe",
            weight.astype(jnp.bfloat16),
            values_part,
            preferred_element_type=jnp.float32,
        )
        summed = summed * jnp.transpose(shrink, (0, 2, 1))[..., None] + update
        return ((highest, totals, summed), None)

    state, _ = lax.scan(forward_one_block, carry, jnp.arange(count // block, dtype=jnp.int32))
    return state


def block_terms(query, keys_part, values_part, allowed, logsum, grad_out, delta, scale):
    score = (
        jnp.einsum("sqhe,skhe->shqk", query, keys_part, preferred_element_type=jnp.float32) * scale
    )
    prob = jnp.where(allowed, jnp.exp(score - logsum[..., None]), 0.0)
    prob_grad = jnp.einsum(
        "sqhe,skhe->shqk", grad_out, values_part, preferred_element_type=jnp.float32
    )
    score_grad = (prob * (prob_grad - delta[..., None])).astype(jnp.bfloat16)
    return (prob, score_grad)


def backward_fold(carry, keys, values, query, query_clip, key_clip, logsum, grad_out, delta):
    seqs, count, width = keys.shape
    heads = query.shape[2]
    scale = query.shape[3] ** (-0.5)
    block = key_block()

    def backward_one_block(state, number):
        first = number * block
        keys_part = split_heads(lax.dynamic_slice_in_dim(keys, first, block, 1), heads)
        values_part = split_heads(lax.dynamic_slice_in_dim(values, first, block, 1), heads)
        clip_part = lax.dynamic_slice_in_dim(key_clip, first, block, 1)
        allowed = query_clip[:, None, :, None] == clip_part[:, None, None, :]
        prob, score_grad = block_terms(
            query, keys_part, values_part, allowed, logsum, grad_out, delta, scale
        )
        step_grad = (
            jnp.einsum("shqk,skhe->sqhe", score_grad, keys_part, preferred_element_type=jnp.float32)
            * scale
        )
        return (state + step_grad, None)

    state, _ = lax.scan(backward_one_block, carry, jnp.arange(count // block, dtype=jnp.int32))
    return state


def key_fold(carry, query, grad_out, logsum_all, delta_all, clip_all, keys, values, key_clip):
    seqs, count, heads, size = query.shape
    scale = size ** (-0.5)
    block = key_block()
    keys_split = split_heads(keys, heads)
    values_split = split_heads(values, heads)

    def key_one_block(state, number):
        key_grad, value_grad = state
        first = number * block
        query_part = lax.dynamic_slice_in_dim(query, first, block, 1)
        grad_part = lax.dynamic_slice_in_dim(grad_out, first, block, 1)
        logsum = lax.dynamic_slice_in_dim(logsum_all, first, block, 2)
        delta = lax.dynamic_slice_in_dim(delta_all, first, block, 2)
        clips = lax.dynamic_slice_in_dim(clip_all, first, block, 1)
        allowed = clips[:, None, :, None] == key_clip[:, None, None, :]
        prob, score_grad = block_terms(
            query_part, keys_split, values_split, allowed, logsum, grad_part, delta, scale
        )
        value_grad = value_grad + jnp.einsum(
            "shqk,sqhe->skhe",
            prob.astype(jnp.bfloat16),
            grad_part,
            preferred_element_type=jnp.float32,
        )
        key_grad = (
            key_grad
            + jnp.einsum(
                "shqk,sqhe->skhe", score_grad, query_part, preferred_element_type=jnp.float32
            )
            * scale
        )
        return ((key_grad, value_grad), None)

    state, _ = lax.scan(key_one_block, carry, jnp.arange(count // block, dtype=jnp.int32))
    return state


def finish(state):
    running, totals, summed = state
    output = summed / jnp.transpose(totals, (0, 2, 1))[..., None]
    return (output, running + jnp.log(totals))


def encode_front(view, first_gain, query_weight, key_weight, value_weight):
    normed, first_back = jax.vjp(layer_norm, view, first_gain.astype(jnp.float32))
    normed_low = normed.astype(jnp.bfloat16)
    query = matmul(normed_low, query_weight).astype(jnp.bfloat16)
    keys = matmul(normed_low, key_weight).astype(jnp.bfloat16)
    values = matmul(normed_low, value_weight).astype(jnp.bfloat16)
    return (normed_low, first_back, query, keys, values)


def encode_rest(view, mixed_low, output_weight, second_gain, up_weight, down_weight):
    hidden = view + matmul(mixed_low, output_weight)
    second, second_back = jax.vjp(layer_norm, hidden, second_gain.astype(jnp.float32))
    second_low = second.astype(jnp.bfloat16)
    inner = matmul(second_low, up_weight)
    active_full, gelu_back = jax.vjp(gelu_tanh, inner)
    active = active_full.astype(jnp.bfloat16)
    merged = hidden + matmul(active, down_weight)
    return (merged, (second_low, second_back, active, gelu_back))


def encode_back(merged_grad, saved, mixed_low, output_weight, up_weight, down_weight):
    second_low, second_back, active, gelu_back = saved
    branch_grad = merged_grad.astype(jnp.bfloat16)
    down_part = weight_grad(active, branch_grad)
    inner_grad = gelu_back(matmul_back(branch_grad, down_weight))[0].astype(jnp.bfloat16)
    up_part = weight_grad(second_low, inner_grad)
    hidden_extra, second_part = second_back(matmul_back(inner_grad, up_weight))
    hidden_grad = merged_grad + hidden_extra
    attend_grad = hidden_grad.astype(jnp.bfloat16)
    output_part = weight_grad(mixed_low, attend_grad)
    mixed_grad = matmul_back(attend_grad, output_weight).astype(jnp.bfloat16)
    return (hidden_grad, mixed_grad, (second_part, up_part, down_part, output_part))


def front_back(
    hidden_grad,
    normed_low,
    first_back,
    query_grad,
    key_grad,
    value_grad,
    query_weight,
    key_weight,
    value_weight,
):
    query_part = weight_grad(normed_low, query_grad)
    key_part = weight_grad(normed_low, key_grad)
    value_part = weight_grad(normed_low, value_grad)
    normed_grad = (
        matmul_back(query_grad, query_weight)
        + matmul_back(key_grad, key_weight)
        + matmul_back(value_grad, value_weight)
    )
    extra, gain_part = first_back(normed_grad)
    return (hidden_grad + extra, (gain_part, query_part, key_part, value_part))


def output_delta(grad_heads, output):
    return jnp.transpose(jnp.sum(grad_heads.astype(jnp.float32) * output, axis=-1), (0, 2, 1))


def per_device(
    large_view,
    small_view,
    clip_ids,
    first_gain,
    query_weight,
    key_weight,
    value_weight,
    output_weight,
    second_gain,
    up_weight,
    down_weight,
    query_gain,
    context_gain,
    cross_query,
    cross_key,
    cross_value,
    cross_output,
    cotangent,
):
    seqs, count, width = large_view.shape
    heads = HEADS
    size = width // heads
    half = count // 2
    all_clips = lax.all_gather(clip_ids, "tm", axis=1, tiled=True)
    short_clips = all_clips[:, ::2]
    local_short = clip_ids[:, ::2]
    large = large_view.astype(jnp.float32)
    small = small_view.astype(jnp.float32)
    large_normed, large_first_back, large_q, large_k, large_v = encode_front(
        large, first_gain, query_weight, key_weight, value_weight
    )
    small_normed, small_first_back, small_q, small_k, small_v = encode_front(
        small, first_gain, query_weight, key_weight, value_weight
    )
    large_heads = split_heads(large_q, heads)
    small_heads = split_heads(small_q, heads)

    def empty_state(rows):
        return (
            jnp.full((seqs, heads, rows), NEGATIVE, jnp.float32),
            jnp.zeros((seqs, heads, rows), jnp.float32),
            jnp.zeros((seqs, rows, heads, size), jnp.float32),
        )

    carry = (empty_state(count), empty_state(half))
    pieces = (
        lax.all_gather(large_k, "tm", axis=1, tiled=True),
        lax.all_gather(large_v, "tm", axis=1, tiled=True),
        lax.all_gather(small_k, "tm", axis=1, tiled=True),
        lax.all_gather(small_v, "tm", axis=1, tiled=True),
    )
    large_state = forward_fold(carry[0], pieces[0], pieces[1], large_heads, clip_ids, all_clips)
    small_state = forward_fold(
        carry[1], pieces[2], pieces[3], small_heads, local_short, short_clips
    )
    large_mixed, large_logsum = finish(large_state)
    small_mixed, small_logsum = finish(small_state)
    large_mixed_low = large_mixed.reshape(seqs, count, width).astype(jnp.bfloat16)
    small_mixed_low = small_mixed.reshape(seqs, half, width).astype(jnp.bfloat16)
    large_merged, large_saved = encode_rest(
        large, large_mixed_low, output_weight, second_gain, up_weight, down_weight
    )
    small_merged, small_saved = encode_rest(
        small, small_mixed_low, output_weight, second_gain, up_weight, down_weight
    )
    asked, asked_back = jax.vjp(layer_norm, large_merged, query_gain.astype(jnp.float32))
    context, context_back = jax.vjp(layer_norm, small_merged, context_gain.astype(jnp.float32))
    asked_low = asked.astype(jnp.bfloat16)
    context_low = context.astype(jnp.bfloat16)
    cross_q = matmul(asked_low, cross_query).astype(jnp.bfloat16)
    cross_k = matmul(context_low, cross_key).astype(jnp.bfloat16)
    cross_v = matmul(context_low, cross_value).astype(jnp.bfloat16)
    cross_heads = split_heads(cross_q, heads)
    pieces = (
        lax.all_gather(cross_k, "tm", axis=1, tiled=True),
        lax.all_gather(cross_v, "tm", axis=1, tiled=True),
    )
    cross_state = forward_fold(
        empty_state(count), pieces[0], pieces[1], cross_heads, clip_ids, short_clips
    )
    united, cross_logsum = finish(cross_state)
    united_low = united.reshape(seqs, count, width).astype(jnp.bfloat16)
    united_view = (large_merged + matmul(united_low, cross_output)).astype(jnp.bfloat16)
    cross_output_grad = weight_grad(united_low, cotangent)
    united_grad = split_heads(matmul_back(cotangent, cross_output).astype(jnp.bfloat16), heads)
    cross_delta = output_delta(united_grad, united)
    query_zero = jnp.zeros((seqs, count, heads, size), jnp.float32)
    short_zero = jnp.zeros((seqs, half, heads, size), jnp.float32)
    pieces = (
        lax.all_gather(cross_k, "tm", axis=1, tiled=True),
        lax.all_gather(cross_v, "tm", axis=1, tiled=True),
    )
    cross_result = backward_fold(
        query_zero,
        pieces[0],
        pieces[1],
        cross_heads,
        clip_ids,
        short_clips,
        cross_logsum,
        united_grad,
        cross_delta,
    )
    cross_stats = (
        lax.all_gather(cross_logsum, "tm", axis=2, tiled=True),
        lax.all_gather(cross_delta, "tm", axis=2, tiled=True),
    )
    pieces = (
        lax.all_gather(cross_heads, "tm", axis=1, tiled=True),
        lax.all_gather(united_grad, "tm", axis=1, tiled=True),
    )
    cross_key_part, cross_value_part = key_fold(
        (short_zero, short_zero),
        pieces[0],
        pieces[1],
        cross_stats[0],
        cross_stats[1],
        all_clips,
        cross_k,
        cross_v,
        local_short,
    )
    cross_k_grad = cross_key_part.reshape(seqs, half, width).astype(jnp.bfloat16)
    cross_v_grad = cross_value_part.reshape(seqs, half, width).astype(jnp.bfloat16)
    cross_q_grad = cross_result.reshape(seqs, count, width).astype(jnp.bfloat16)
    cross_query_grad = weight_grad(asked_low, cross_q_grad)
    cross_key_grad = weight_grad(context_low, cross_k_grad)
    cross_value_grad = weight_grad(context_low, cross_v_grad)
    merged_extra, query_gain_grad = asked_back(matmul_back(cross_q_grad, cross_query))
    context_grad = matmul_back(cross_k_grad, cross_key) + matmul_back(cross_v_grad, cross_value)
    small_merged_grad, context_gain_grad = context_back(context_grad)
    large_merged_grad = cotangent.astype(jnp.float32) + merged_extra
    large_hidden_grad, large_mixed_flat, large_parts = encode_back(
        large_merged_grad, large_saved, large_mixed_low, output_weight, up_weight, down_weight
    )
    small_hidden_grad, small_mixed_flat, small_parts = encode_back(
        small_merged_grad, small_saved, small_mixed_low, output_weight, up_weight, down_weight
    )
    large_mixed_grad = split_heads(large_mixed_flat, heads)
    small_mixed_grad = split_heads(small_mixed_flat, heads)
    large_delta = output_delta(large_mixed_grad, large_mixed)
    small_delta = output_delta(small_mixed_grad, small_mixed)
    self_init = (query_zero, short_zero)
    pieces = (
        lax.all_gather(large_k, "tm", axis=1, tiled=True),
        lax.all_gather(large_v, "tm", axis=1, tiled=True),
        lax.all_gather(small_k, "tm", axis=1, tiled=True),
        lax.all_gather(small_v, "tm", axis=1, tiled=True),
    )
    self_result = (
        backward_fold(
            self_init[0],
            pieces[0],
            pieces[1],
            large_heads,
            clip_ids,
            all_clips,
            large_logsum,
            large_mixed_grad,
            large_delta,
        ),
        backward_fold(
            self_init[1],
            pieces[2],
            pieces[3],
            small_heads,
            local_short,
            short_clips,
            small_logsum,
            small_mixed_grad,
            small_delta,
        ),
    )
    large_q_part, small_q_part = self_result
    self_stats = (
        lax.all_gather(large_logsum, "tm", axis=2, tiled=True),
        lax.all_gather(large_delta, "tm", axis=2, tiled=True),
        lax.all_gather(small_logsum, "tm", axis=2, tiled=True),
        lax.all_gather(small_delta, "tm", axis=2, tiled=True),
    )
    carry = ((query_zero, query_zero), (short_zero, short_zero))
    pieces = (
        lax.all_gather(large_heads, "tm", axis=1, tiled=True),
        lax.all_gather(large_mixed_grad, "tm", axis=1, tiled=True),
        lax.all_gather(small_heads, "tm", axis=1, tiled=True),
        lax.all_gather(small_mixed_grad, "tm", axis=1, tiled=True),
    )
    large_pair = key_fold(
        carry[0],
        pieces[0],
        pieces[1],
        self_stats[0],
        self_stats[1],
        all_clips,
        large_k,
        large_v,
        clip_ids,
    )
    small_pair = key_fold(
        carry[1],
        pieces[2],
        pieces[3],
        self_stats[2],
        self_stats[3],
        short_clips,
        small_k,
        small_v,
        local_short,
    )
    large_k_grad = large_pair[0].reshape(seqs, count, width).astype(jnp.bfloat16)
    large_v_grad = large_pair[1].reshape(seqs, count, width).astype(jnp.bfloat16)
    small_k_grad = small_pair[0].reshape(seqs, half, width).astype(jnp.bfloat16)
    small_v_grad = small_pair[1].reshape(seqs, half, width).astype(jnp.bfloat16)
    large_q_grad = large_q_part.reshape(seqs, count, width).astype(jnp.bfloat16)
    small_q_grad = small_q_part.reshape(seqs, half, width).astype(jnp.bfloat16)
    large_grad, large_front = front_back(
        large_hidden_grad,
        large_normed,
        large_first_back,
        large_q_grad,
        large_k_grad,
        large_v_grad,
        query_weight,
        key_weight,
        value_weight,
    )
    small_grad, small_front = front_back(
        small_hidden_grad,
        small_normed,
        small_first_back,
        small_q_grad,
        small_k_grad,
        small_v_grad,
        query_weight,
        key_weight,
        value_weight,
    )
    local_grads = (
        large_front[0] + small_front[0],
        large_front[1] + small_front[1],
        large_front[2] + small_front[2],
        large_front[3] + small_front[3],
        large_parts[3] + small_parts[3],
        large_parts[0] + small_parts[0],
        large_parts[1] + small_parts[1],
        large_parts[2] + small_parts[2],
        query_gain_grad,
        context_gain_grad,
        cross_query_grad,
        cross_key_grad,
        cross_value_grad,
        cross_output_grad,
    )
    shared = (
        lax.psum_scatter(local_grads[0], "tm", scatter_dimension=0, tiled=True),
        lax.psum_scatter(local_grads[1], "tm", scatter_dimension=0, tiled=True),
        lax.psum_scatter(local_grads[2], "tm", scatter_dimension=0, tiled=True),
        lax.psum_scatter(local_grads[3], "tm", scatter_dimension=0, tiled=True),
        lax.psum_scatter(local_grads[4], "tm", scatter_dimension=0, tiled=True),
        lax.psum_scatter(local_grads[5], "tm", scatter_dimension=0, tiled=True),
        lax.psum_scatter(local_grads[6], "tm", scatter_dimension=0, tiled=True),
        lax.psum_scatter(local_grads[7], "tm", scatter_dimension=0, tiled=True),
        lax.psum_scatter(local_grads[8], "tm", scatter_dimension=0, tiled=True),
        lax.psum_scatter(local_grads[9], "tm", scatter_dimension=0, tiled=True),
        lax.psum_scatter(local_grads[10], "tm", scatter_dimension=0, tiled=True),
        lax.psum_scatter(local_grads[11], "tm", scatter_dimension=0, tiled=True),
        lax.psum_scatter(local_grads[12], "tm", scatter_dimension=0, tiled=True),
        lax.psum_scatter(local_grads[13], "tm", scatter_dimension=0, tiled=True),
    )
    summed = (
        lax.psum(shared[0].astype(jnp.bfloat16), "seq").astype(jnp.float32),
        lax.psum(shared[1].astype(jnp.bfloat16), "seq").astype(jnp.float32),
        lax.psum(shared[2].astype(jnp.bfloat16), "seq").astype(jnp.float32),
        lax.psum(shared[3].astype(jnp.bfloat16), "seq").astype(jnp.float32),
        lax.psum(shared[4].astype(jnp.bfloat16), "seq").astype(jnp.float32),
        lax.psum(shared[5].astype(jnp.bfloat16), "seq").astype(jnp.float32),
        lax.psum(shared[6].astype(jnp.bfloat16), "seq").astype(jnp.float32),
        lax.psum(shared[7].astype(jnp.bfloat16), "seq").astype(jnp.float32),
        lax.psum(shared[8].astype(jnp.bfloat16), "seq").astype(jnp.float32),
        lax.psum(shared[9].astype(jnp.bfloat16), "seq").astype(jnp.float32),
        lax.psum(shared[10].astype(jnp.bfloat16), "seq").astype(jnp.float32),
        lax.psum(shared[11].astype(jnp.bfloat16), "seq").astype(jnp.float32),
        lax.psum(shared[12].astype(jnp.bfloat16), "seq").astype(jnp.float32),
        lax.psum(shared[13].astype(jnp.bfloat16), "seq").astype(jnp.float32),
    )
    return (
        united_view,
        large_grad,
        small_grad,
        summed[0],
        summed[1],
        summed[2],
        summed[3],
        summed[4],
        summed[5],
        summed[6],
        summed[7],
        summed[8],
        summed[9],
        summed[10],
        summed[11],
        summed[12],
        summed[13],
    )


def solution(mesh):
    in_specs = (
        P("seq", "tm", None),
        P("seq", "tm", None),
        P("seq", "tm"),
        P(),
        P(),
        P(),
        P(),
        P(),
        P(),
        P(),
        P(),
        P(),
        P(),
        P(),
        P(),
        P(),
        P(),
        P("seq", "tm", None),
    )
    out_specs = (
        P("seq", "tm", None),
        P("seq", "tm", None),
        P("seq", "tm", None),
        P("tm"),
        P("tm", None),
        P("tm", None),
        P("tm", None),
        P("tm", None),
        P("tm"),
        P("tm", None),
        P("tm", None),
        P("tm"),
        P("tm"),
        P("tm", None),
        P("tm", None),
        P("tm", None),
        P("tm", None),
    )
    return jax.shard_map(
        per_device, mesh=mesh, in_specs=in_specs, out_specs=out_specs, check_vma=False
    )
```

profile of v0, /device:TPU:1, one launch (start us, length us, event | category | flops | bytes accessed | tf_op | source)
XLA Modules:
  0.0 1983.0 jit_solution(3213202700557901204)
XLA Ops:
  79.9 56.7 %all-gather.19.cloned.1.call-done = bf16[2,1024,768]{2,1,0:T(8,128)(2,1)} async-done(((bf16[2,128,768]{2,1,0:T(8,128)(2,1)}), bf16[2,1024,768]{2,1,0:T(8,128)(2,1)}) %all-gather.19.cloned.1.call-update) | async-done | bytes 3145744 | tf_op jit(solution)/shard_map/all_gather | solution.py:271
  141.3 30.3 %while.118 = (s32[]{:T(128)}, f32[2,12,128]{2,1,0:T(8,128)S(1)}, f32[2,12,128]{2,1,0:T(8,128)S(1)}, f32[2,128,12,64]{1,3,2,0:T(8,128)}, s32[2,128]{1,0:T(2,128)S...) while((s32[]{:T(128)}, f32[2,12,128]{2,1,0:T(8,128)S(1)}, ...), condition=%wide.region_13.14_spmd.clone, body=%wide.region_10.13_spmd.clone.sunk | while | flops 423839744 | bytes 57750792 | solution.py:75
  193.2 44.1 %all-gather.13.cloned.1.call-done = bf16[2,2048,768]{2,1,0:T(8,128)(2,1)} async-done(((bf16[2,256,768]{2,1,0:T(8,128)(2,1)}), bf16[2,2048,768]{2,1,0:T(8,128)(2,1)}) %all-gather.13.cloned.1.call-update) | async-done | bytes 6291472 | tf_op jit(solution)/shard_map/all_gather | solution.py:268
  246.0 91.2 %all-gather.15.cloned.1.call-done = bf16[2,2048,768]{2,1,0:T(8,128)(2,1)} async-done(((bf16[2,256,768]{2,1,0:T(8,128)(2,1)}), bf16[2,2048,768]{2,1,0:T(8,128)(2,1)}) %all-gather.15.cloned.1.call-update) | async-done | bytes 6291472 | tf_op jit(solution)/shard_map/all_gather | solution.py:269
  345.9 101.7 %while.117 = (s32[]{:T(128)}, f32[2,12,256]{2,1,0:T(8,128)S(1)}, f32[2,12,256]{2,1,0:T(8,128)S(1)}, f32[2,256,12,64]{1,3,2,0:T(8,128)}, s32[2,256]{1,0:T(2,128)S...) while((s32[]{:T(128)}, f32[2,12,256]{2,1,0:T(8,128)S(1)}, ...), condition=%wide.region_5.6_spmd.clone, body=%wide.region_2.5_spmd.clone.sunk | while | flops 847679488 | bytes 102906088 | solution.py:75
  474.8 49.2 %while.119 = (s32[]{:T(128)}, f32[2,12,256]{2,1,0:T(8,128)S(1)}, f32[2,12,256]{2,1,0:T(8,128)S(1)}, f32[2,256,12,64]{1,3,2,0:T(8,128)}, s32[2,256]{1,0:T(2,128)S...) while((s32[]{:T(128)}, f32[2,12,256]{2,1,0:T(8,128)S(1)}, ...), condition=%wide.region_23.24_spmd.clone, body=%wide.region_20.23_spmd.clone.sunk | while | flops 847679488 | bytes 102906088 | solution.py:75
  528.1 42.5 %while.120 = (s32[]{:T(128)}, f32[2,256,12,64]{1,3,2,0:T(8,128)}, s32[2]{0:T(128)S(1)}, bf16[2,1024,768]{1,2,0:T(8,128)(2,1)}, s32[2,256]{1,0:T(2,128)S(1)}, /*i...) while((s32[]{:T(128)}, f32[2,256,12,64]{1,3,2,0:T(8,128)}, ...), condition=%wide.region_26.27_spmd.clone, body=%wide.region_25.26_spmd.clone.sunk | while | flops 1228275712 | bytes 41482576 | solution.py:112
  598.0 29.2 %all_gather.75 = f32[2,12,2048]{2,1,0:T(8,128)} all-gather(f32[2,12,256]{2,1,0:T(8,128)} %get-tuple-element.2643), channel_id=1, replica_groups=mesh['tm'=8,'seq'=4] {'tm'}, dimensions={2}, use_global_device_ids=true | all-gather | bytes 221184 | tf_op jit(solution)/shard_map/all_gather | solution.py:326
  627.3 27.9 %all_gather.77 = f32[2,12,2048]{2,1,0:T(8,128)} all-gather(f32[2,12,256]{2,1,0:T(8,128)} %get-tuple-element.2641), channel_id=1, replica_groups=mesh['tm'=8,'seq'=4] {'tm'}, dimensions={2}, use_global_device_ids=true | all-gather | bytes 221184 | tf_op jit(solution)/shard_map/all_gather | solution.py:327
  667.9 88.0 %while.123 = (s32[]{:T(128)}, f32[2,128,12,64]{1,3,2,0:T(8,128)}, f32[2,128,12,64]{1,3,2,0:T(8,128)}, s32[4]{0:T(128)S(1)}, bf16[2,2048,12,64]{1,3,2,0:T(8,128)(...) while((s32[]{:T(128)}, f32[2,128,12,64]{1,3,2,0:T(8,128)}, ...), condition=%wide.region_39.40_spmd.clone, body=%wide.region_38.39_spmd.clone.sunk | while | flops 822149120 | bytes 29850344 | solution.py:150
  789.8 26.4 %all_gather.79 = f32[2,12,1024]{2,1,0:T(8,128)} all-gather(f32[2,12,128]{2,1,0:T(8,128)S(1)} %log_add_fusion.2), channel_id=1, replica_groups=mesh['tm'=8,'seq'=4] {'tm'}, dimensions={2}, use_global_device_ids=true | all-gather | bytes 110592 | tf_op jit(solution)/shard_map/all_gather | solution.py:399
  822.5 81.7 %while.121 = (s32[]{:T(128)}, f32[2,256,12,64]{1,3,2,0:T(8,128)}, s32[4]{0:T(128)S(1)}, bf16[2,2048,768]{1,2,0:T(8,128)(2,1)}, s32[2,256]{1,0:T(2,128)S(1)}, /*i...) while((s32[]{:T(128)}, f32[2,256,12,64]{1,3,2,0:T(8,128)}, ...), condition=%wide.region_33.34_spmd.clone, body=%wide.region_32.33_spmd.clone.sunk | while | flops 1228275712 | bytes 41482456 | solution.py:112
  931.5 27.2 %all_gather.71 = f32[2,12,2048]{2,1,0:T(8,128)} all-gather(f32[2,12,256]{2,1,0:T(8,128)S(1)} %get-tuple-element.2644), channel_id=1, replica_groups=mesh['tm'=8,'seq'=4] {'tm'}, dimensions={2}, use_global_device_ids=true | all-gather | bytes 221184 | tf_op jit(solution)/shard_map/all_gather | solution.py:397
  965.8 119.3 %while.122 = (s32[]{:T(128)}, f32[2,256,12,64]{1,3,2,0:T(8,128)S(1)}, f32[2,256,12,64]{1,3,2,0:T(8,128)}, s32[4]{0:T(128)S(1)}, bf16[2,2048,12,64]{1,3,2,0:T(8,1...) while((s32[]{:T(128)}, ...), condition=%wide.region_35.36_spmd.clone, body=%wide.region_34.35_spmd.clone.sunk | while | flops 1644298240 | bytes 53051112 | solution.py:150
  1088.4 28.2 %while.124 = (s32[]{:T(128)}, f32[2,128,12,64]{1,3,2,0:T(8,128)}, s32[2]{0:T(128)S(1)}, bf16[2,1024,768]{1,2,0:T(8,128)(2,1)}, s32[2,128]{1,0:T(2,128)S(1)}, /*i...) while((s32[]{:T(128)}, f32[2,128,12,64]{1,3,2,0:T(8,128)}, ...), condition=%wide.region_46.47_spmd.clone, body=%wide.region_45.46_spmd.clone.sunk | while | flops 614137856 | bytes 24679640 | solution.py:112
  1150.2 41.7 %while.125 = (s32[]{:T(128)}, f32[2,128,12,64]{1,3,2,0:T(8,128)S(1)}, f32[2,128,12,64]{1,3,2,0:T(8,128)}, s32[2]{0:T(128)S(1)}, bf16[2,1024,12,64]{1,3,2,0:T(8,1...) while((s32[]{:T(128)}, ...), condition=%wide.region_48.49_spmd.clone, body=%wide.region_47.48_spmd.clone.sunk | while | flops 822149120 | bytes 31423236 | solution.py:150
  1247.1 39.5 %reduce-scatter.27.cloned.1.call-done = f32[96,768]{1,0:T(8,128)} async-done(((f32[768,768]{1,0:T(8,128)}), f32[96,768]{1,0:T(8,128)}) %reduce-scatter.27.cloned.1.call-update) | async-done | bytes 294928 | tf_op jit(solution)/shard_map/reduce_scatter | solution.py:488
  1288.3 69.7 %reduce-scatter.17.cloned.1.call-done = f32[96,768]{1,0:T(8,128)} async-done(((f32[768,768]{1,0:T(8,128)}), f32[96,768]{1,0:T(8,128)}) %reduce-scatter.17.cloned.1.call-update) | async-done | bytes 294928 | tf_op jit(solution)/shard_map/reduce_scatter | solution.py:480
  1359.7 69.8 %reduce-scatter.11.cloned.1.call-done = f32[96,768]{1,0:T(8,128)} async-done(((f32[768,768]{1,0:T(8,128)}), f32[96,768]{1,0:T(8,128)}) %reduce-scatter.11.cloned.1.call-update) | async-done | bytes 294928 | tf_op jit(solution)/shard_map/reduce_scatter | solution.py:477
  1432.5 68.4 %reduce-scatter.15.cloned.1.call-done = f32[96,768]{1,0:T(8,128)} async-done(((f32[768,768]{1,0:T(8,128)}), f32[96,768]{1,0:T(8,128)}) %reduce-scatter.15.cloned.1.call-update) | async-done | bytes 294928 | tf_op jit(solution)/shard_map/reduce_scatter | solution.py:479
  1502.5 69.8 %reduce-scatter.13.cloned.1.call-done = f32[96,768]{1,0:T(8,128)} async-done(((f32[768,768]{1,0:T(8,128)}), f32[96,768]{1,0:T(8,128)}) %reduce-scatter.13.cloned.1.call-update) | async-done | bytes 294928 | tf_op jit(solution)/shard_map/reduce_scatter | solution.py:478
  1573.9 165.6 %reduce-scatter.21.cloned.1.call-done = f32[384,768]{1,0:T(8,128)} async-done(((f32[3072,768]{1,0:T(8,128)}), f32[384,768]{1,0:T(8,128)}) %reduce-scatter.21.cloned.1.call-update) | async-done | bytes 1179664 | tf_op jit(solution)/shard_map/reduce_scatter | solution.py:483
  1741.7 164.0 %reduce-scatter.19.cloned.1.call-done = f32[96,3072]{1,0:T(8,128)} async-done(((f32[768,3072]{1,0:T(8,128)}), f32[96,3072]{1,0:T(8,128)}) %reduce-scatter.19.cloned.1.call-update) | async-done | bytes 1179664 | tf_op jit(solution)/shard_map/reduce_scatter | solution.py:482
  1911.7 28.1 %all-reduce.4 = (bf16[768]{0:T(1024)(128)(2,1)S(1)}, bf16[768]{0:T(1024)(128)(2,1)S(1)}, bf16[768]{0:T(1024)(128)(2,1)S(1)}, bf16[768]{0:T(1024)(128)(2,1)S(1)}) all-reduce(f32[768]{0:T(1024)S(1)} %add.359, f32[768]{0:T(1024)S(1)} %copy-done.189, f32[768]{0:T(1024)S(1)} %copy-done.202, ...), channel_id=2, replica_groups=mesh['tm'=8,'seq'=4] {'tm'}, use_global_device_ids=true, to_apply=%region_53.54.clone | all-reduce | flops 3072 | bytes 18432
  (918 shorter events, 968.4 us)
Async XLA Ops:
  7.2 68.0 %all-gather.17.cloned.1.call-start = ((), (), s32[]{:S(2)}) async-start(), calls=%async_computation.12 | async-start | bytes 3538944 | tf_op jit(solution)/shard_map/all_gather | solution.py:270
  13.2 123.3 %all-gather.19.cloned.1.call-start = ((), (), s32[]{:S(2)}) async-start(), calls=%async_computation.13 | async-start | bytes 3538944 | tf_op jit(solution)/shard_map/all_gather | solution.py:271
  15.9 221.4 %all-gather.13.cloned.1.call-start = ((), (), s32[]{:S(2)}) async-start(), calls=%async_computation.10 | async-start | bytes 7077888 | tf_op jit(solution)/shard_map/all_gather | solution.py:268
  19.6 317.6 %all-gather.15.cloned.1.call-start = ((), (), s32[]{:S(2)}) async-start(), calls=%async_computation.11 | async-start | bytes 7077888 | tf_op jit(solution)/shard_map/all_gather | solution.py:269
  22.7 442.6 %all-gather.21.cloned.1.call-start = ((), (), s32[]{:S(2)}) async-start(), calls=%async_computation.14 | async-start | bytes 3538944 | tf_op jit(solution)/shard_map/all_gather | solution.py:296
  22.8 428.0 %copy-start.80 = (f32[768]{0:T(1024)}, f32[768]{0:T(1024)S(1)}, u32[]{:S(2)}) copy-start(f32[768]{0:T(1024)S(1)} %convert_element_type.313) | copy-start | bytes 9220
  181.5 288.5 %all-gather.23.cloned.1.call-start = ((), (), s32[]{:S(2)}) async-start(), calls=%async_computation.15 | async-start | bytes 3538944 | tf_op jit(solution)/shard_map/all_gather | solution.py:297
  182.8 472.4 %all-gather.31.cloned.1.call-start = ((), (), s32[]{:S(2)}) async-start(), calls=%async_computation.19 | async-start | bytes 7077888 | tf_op jit(solution)/shard_map/all_gather | solution.py:331
  188.7 479.2 %all-gather.29.cloned.1.call-start = ((), (), s32[]{:S(2)}) async-start(), calls=%async_computation.18 | async-start | bytes 7077888 | tf_op jit(solution)/shard_map/all_gather | solution.py:330
  464.4 500.4 %all-gather.25.cloned.1.call-start = ((), (), s32[]{:S(2)}) async-start(), calls=%async_computation.16 | async-start | bytes 7077888 | tf_op jit(solution)/shard_map/all_gather | solution.py:404
  465.2 499.7 %all-gather.27.cloned.1.call-start = ((), (), s32[]{:S(2)}) async-start(), calls=%async_computation.17 | async-start | bytes 7077888 | tf_op jit(solution)/shard_map/all_gather | solution.py:405
  595.0 555.1 %all-gather.33.cloned.1.call-start = ((), (), s32[]{:S(2)}) async-start(), calls=%async_computation.20 | async-start | bytes 3538944 | tf_op jit(solution)/shard_map/all_gather | solution.py:406
  595.8 554.4 %all-gather.35.cloned.1.call-start = ((), (), s32[]{:S(2)}) async-start(), calls=%async_computation.21 | async-start | bytes 3538944 | tf_op jit(solution)/shard_map/all_gather | solution.py:407
  772.5 460.7 %reduce-scatter.23.cloned.1.call-start = ((), (), s32[]{:S(2)}) async-start(), calls=%async_computation.28 | async-start | bytes 2654208 | tf_op jit(solution)/shard_map/reduce_scatter | solution.py:486
  775.3 459.5 %reduce-scatter.29.cloned.1.call-start = ((), (), s32[]{:S(2)}) async-start(), calls=%async_computation.31 | async-start | bytes 2654208 | tf_op jit(solution)/shard_map/reduce_scatter | solution.py:489
  778.8 466.6 %reduce-scatter.25.cloned.1.call-start = ((), (), s32[]{:S(2)}) async-start(), calls=%async_computation.29 | async-start | bytes 2654208 | tf_op jit(solution)/shard_map/reduce_scatter | solution.py:487
  781.8 504.9 %reduce-scatter.27.cloned.1.call-start = ((), (), s32[]{:S(2)}) async-start(), calls=%async_computation.30 | async-start | bytes 2654208 | tf_op jit(solution)/shard_map/reduce_scatter | solution.py:488
  821.4 536.7 %reduce-scatter.17.cloned.1.call-start = ((), (), s32[]{:S(2)}) async-start(), calls=%async_computation.25 | async-start | bytes 2654208 | tf_op jit(solution)/shard_map/reduce_scatter | solution.py:480
  964.4 465.0 %reduce-scatter.11.cloned.1.call-start = ((), (), s32[]{:S(2)}) async-start(), calls=%async_computation.22 | async-start | bytes 2654208 | tf_op jit(solution)/shard_map/reduce_scatter | solution.py:477
  1121.8 379.1 %reduce-scatter.15.cloned.1.call-start = ((), (), s32[]{:S(2)}) async-start(), calls=%async_computation.24 | async-start | bytes 2654208 | tf_op jit(solution)/shard_map/reduce_scatter | solution.py:479
  1197.4 374.8 %reduce-scatter.13.cloned.1.call-start = ((), (), s32[]{:S(2)}) async-start(), calls=%async_computation.23 | async-start | bytes 2654208 | tf_op jit(solution)/shard_map/reduce_scatter | solution.py:478
  1202.6 536.9 %reduce-scatter.21.cloned.1.call-start = ((), (), s32[]{:S(2)}) async-start(), calls=%async_computation.27 | async-start | bytes 10616832 | tf_op jit(solution)/shard_map/reduce_scatter | solution.py:483
  1215.5 690.1 %reduce-scatter.19.cloned.1.call-start = ((), (), s32[]{:S(2)}) async-start(), calls=%async_computation.26 | async-start | bytes 10616832 | tf_op jit(solution)/shard_map/reduce_scatter | solution.py:482
  1227.0 739.7 %all-reduce.9.cloned.1.call-start = ((), (), s32[]{:S(2)}) async-start(), calls=%async_computation.32 | async-start | bytes 4718592 | tf_op jit(solution)/shard_map/psum | solution.py:493
  (230 other events, 2500.1 us)
Sparse Core Ops, SparseCore 0:
  13.3 61.8 all-gather.16
  77.4 59.1 all-gather.18
  139.3 97.9 all-gather.12
  240.0 97.2 all-gather.14
  339.3 58.2 all-gather.20
  399.7 59.0 all-gather.22
  461.4 98.9 all-gather.30
  563.0 104.8 all-gather.28
  669.9 98.8 all-gather.24
  770.6 99.0 all-gather.26
  871.8 64.5 all-gather.32
  938.3 64.8 all-gather.34
  1006.7 65.0 reduce-scatter.22
  1075.2 68.2 reduce-scatter.28
  1146.8 68.3 reduce-scatter.24
  1218.6 68.0 reduce-scatter.26
  1290.0 67.9 reduce-scatter.16
  1361.4 67.9 reduce-scatter.10
  1432.9 67.9 reduce-scatter.14
  1504.2 68.0 reduce-scatter.12
  1575.9 163.5 reduce-scatter.20
  1743.1 162.5 reduce-scatter.18
  1910.5 56.1 all-reduce.8
where the time goes:
time: 1990 us; the launch traced here: 1980 us
  waiting for transfers between devices  889 us (45%)
  matrix products  580 us (29%)
  blocking collectives  225 us (11%)
  local copies, waits for them, and re-layouts  155 us (8%)
  other arithmetic  95.7 us (5%)
    reduce_scatter x1, waiting for transfers between devices, per_device(): lax.psum_scatter(local_grads[7], 'tm', scatter_dimension=0, tiled=True)  166 us
    reduce_scatter x1, waiting for transfers between devices, per_device(): lax.psum_scatter(local_grads[6], 'tm', scatter_dimension=0, tiled=True)  164 us
    dot_general x16, matrix products, block_terms(): jnp.einsum('sqhe,skhe->shqk', query, keys_part, preferred_element_type=jn...  101 us
    dot_general x10, matrix products, key_one_block(): jnp.einsum('shqk,sqhe->skhe', score_grad, query_part, preferred_element_t...  94.4 us
    all_gather x1, waiting for transfers between devices, per_device(): lax.all_gather(large_v, 'tm', axis=1, tiled=True)  91.2 us
    dot_general x8, matrix products, forward_one_block(): jnp.einsum('shqk,skhe->sqhe', weight.astype(jnp.bfloat16), values_part, p...  71.2 us
    reduce_scatter x1, waiting for transfers between devices, per_device(): lax.psum_scatter(local_grads[2], 'tm', scatter_dimension=0, tiled=True)  69.8 us
    reduce_scatter x1, waiting for transfers between devices, per_device(): lax.psum_scatter(local_grads[1], 'tm', scatter_dimension=0, tiled=True)  69.8 us
  transfers between devices with their start and end apart: 23, of which 13 were waited for; matrix products, arithmetic and copies ran while one was open for 40% of the time, Pallas kernels for 0%

commit v1 on v0

v1 whole, which is shorter than its diff:
```python
import functools

import jax
import jax.numpy as jnp
from jax import lax
from jax.experimental import pallas as pl
from jax.experimental.pallas import tpu as pltpu
from jax.sharding import PartitionSpec as P

HEADS = 12
EPS = 1e-05
NEGATIVE = -1e30
LOG2E = 1.4426950408889634
LN2 = 0.6931471805599453
LANES = 128
HALF = 64

bf16 = jnp.bfloat16
f32 = jnp.float32
NT = (((1,), (1,)), ((), ()))
NN = (((1,), (0,)), ((), ()))
TN = (((0,), (0,)), ((), ()))


def dot(a, b, dims=NN):
    return lax.dot_general(a, b, dims, preferred_element_type=f32)


def part_block(rows):
    block = min(rows, 512)
    while rows % block or block % 16:
        block -= 1
    return block


def attend_kernel(parts, block, *refs):
    q_ref, mq_ref, mk_ref = refs[0], refs[1], refs[2]
    k_refs = refs[3 : 3 + parts]
    v_refs = refs[3 + parts : 3 + 2 * parts]
    o_ref, l_ref, ka0, ka1, va0, va1 = refs[3 + 2 * parts :]
    count = q_ref.shape[0]
    first = 0
    for part in range(parts):
        rows = k_refs[part].shape[0]
        lane = lax.broadcasted_iota(jnp.int32, (rows, LANES), 1)
        here = pl.ds(first, rows)
        keys, values, mask = k_refs[part][...], v_refs[part][...], mk_ref[here, :]
        one = jnp.ones_like(values)
        ka0[here, :] = jnp.where(lane < HALF, keys, mask)
        ka1[here, :] = jnp.where(lane < HALF, mask, keys)
        va0[here, :] = jnp.where(lane < HALF, values, one)
        va1[here, :] = jnp.where(lane < HALF, one, values)
        first += rows
    lane = lax.broadcasted_iota(jnp.int32, (block, LANES), 1)
    low = lane < HALF
    for number in range(count // block):
        here = pl.ds(number * block, block)
        query, mask = q_ref[here, :], mq_ref[here, :]
        tops, sums = [], []
        for head, keys, values in ((0, ka0, va0), (1, ka1, va1)):
            mine = jnp.where(low, query, mask) if head == 0 else jnp.where(low, mask, query)
            score = dot(mine, keys[...], NT)
            top = jnp.max(score, axis=1, keepdims=True)
            weight = jnp.exp2(score - top).astype(bf16)
            sums.append(dot(weight, values[...]))
            tops.append(jnp.broadcast_to(top, (block, LANES)))
        total = jnp.where(low, sums[1], sums[0])
        top = jnp.where(low, tops[1], tops[0])
        out = jnp.where(low, sums[0], sums[1])
        o_ref[here, :] = (out / pltpu.roll(total, HALF, 1)).astype(bf16)
        l_ref[here, :] = top + jnp.log2(total)


def attend(query, keys, values, mask_q, mask_k):
    count, width = query.shape
    parts = len(keys)
    total = sum(k.shape[0] for k in keys)
    block = min(count, 256)
    if count % block:
        block = count
    pair = lambda rows: pl.BlockSpec((rows, LANES), lambda i: (0, i))
    whole = lambda rows: pl.BlockSpec((rows, LANES), lambda i: (0, 0))
    return pl.pallas_call(
        functools.partial(attend_kernel, parts, block),
        grid=(width // LANES,),
        in_specs=[pair(count), whole(count), whole(total)]
        + [pair(k.shape[0]) for k in keys]
        + [pair(v.shape[0]) for v in values],
        out_specs=[pair(count), pair(count)],
        out_shape=[
            jax.ShapeDtypeStruct((count, width), bf16),
            jax.ShapeDtypeStruct((count, width), f32),
        ],
        scratch_shapes=[pltpu.VMEM((total, LANES), bf16)] * 4,
        compiler_params=pltpu.CompilerParams(vmem_limit_bytes=40 << 20),
        cost_estimate=pl.CostEstimate(
            flops=16 * count * total * width,
            bytes_accessed=width * (count * 8 + total * 4),
            transcendentals=count * total * width // HALF,
        ),
        name="attend",
    )(query, mask_q, mask_k, *keys, *values)


def three(value):
    first = value.astype(bf16)
    rest = value - first.astype(f32)
    second = rest.astype(bf16)
    return first, second, (rest - second.astype(f32)).astype(bf16)


def attend_back_kernel(parts, *refs):
    q_ref, do_ref, o_ref, l_ref, mq_ref, mk_ref = refs[:6]
    k_refs = refs[6 : 6 + parts]
    v_refs = refs[6 + parts : 6 + 2 * parts]
    dq_ref = refs[6 + 2 * parts]
    dk_refs = refs[7 + 2 * parts : 7 + 3 * parts]
    dv_refs = refs[7 + 3 * parts : 7 + 4 * parts]
    count = q_ref.shape[0]
    lane = lax.broadcasted_iota(jnp.int32, (count, LANES), 1)
    low = lane < HALF
    spot = lane % HALF
    query, grad, mask = q_ref[...], do_ref[...], mq_ref[...]
    zero = jnp.zeros_like(query)
    product = grad.astype(f32) * o_ref[...].astype(f32)
    delta0 = jnp.sum(jnp.where(low, product, 0.0), axis=1, keepdims=True)
    delta1 = jnp.sum(jnp.where(low, 0.0, product), axis=1, keepdims=True)
    delta = jnp.where(low, delta1, delta0)

    def beside(base, value):
        a, b, c = three(-value)
        return jnp.where(spot == 4, a, jnp.where(spot == 5, b, jnp.where(spot == 6, c, base)))

    query_side = beside(mask, l_ref[...])
    grad_side = beside(zero, delta)
    query_a = (jnp.where(low, query, query_side), jnp.where(low, query_side, query))
    grad_a = (jnp.where(low, grad, grad_side), jnp.where(low, grad_side, grad))
    query_m = (jnp.where(low, query, zero), jnp.where(low, zero, query))
    grad_m = (jnp.where(low, grad, zero), jnp.where(low, zero, grad))
    dq = jnp.zeros((count, LANES), f32)
    first = 0
    for part in range(parts):
        rows = k_refs[part].shape[0]
        block = part_block(rows)
        lane_k = lax.broadcasted_iota(jnp.int32, (block, LANES), 1)
        low_k = lane_k < HALF
        spot_k = lane_k % HALF
        one = jnp.where((spot_k >= 4) & (spot_k < 7), 1.0, 0.0).astype(bf16)
        for number in range(rows // block):
            here = pl.ds(number * block, block)
            keys, values = k_refs[part][here, :], v_refs[part][here, :]
            side = mk_ref[pl.ds(first + number * block, block), :] + one
            nought = jnp.zeros_like(keys)
            dk = jnp.zeros((block, LANES), f32)
            dv = jnp.zeros((block, LANES), f32)
            for head in (0, 1):
                pick = lambda a, b: jnp.where(low_k, a, b) if head == 0 else jnp.where(low_k, b, a)
                prob = jnp.exp2(dot(query_a[head], pick(keys, side), NT))
                change = dot(grad_a[head], pick(values, one), NT)
                score_grad = (prob * change).astype(bf16)
                dv += dot(prob.astype(bf16), grad_m[head], TN)
                dk += dot(score_grad, query_m[head], TN)
                dq += dot(score_grad, pick(keys, nought))
            dk_refs[part][here, :] = (dk * LN2).astype(bf16)
            dv_refs[part][here, :] = dv.astype(bf16)
        first += rows
    dq_ref[...] = (dq * HALF**-0.5).astype(bf16)


def attend_back(query, keys, values, grad, out, logsum, mask_q, mask_k):
    count, width = query.shape
    parts = len(keys)
    total = sum(k.shape[0] for k in keys)
    pair = lambda rows: pl.BlockSpec((rows, LANES), lambda i: (0, i))
    whole = lambda rows: pl.BlockSpec((rows, LANES), lambda i: (0, 0))
    result = pl.pallas_call(
        functools.partial(attend_back_kernel, parts),
        grid=(width // LANES,),
        in_specs=[pair(count)] * 4
        + [whole(count), whole(total)]
        + [pair(k.shape[0]) for k in keys]
        + [pair(v.shape[0]) for v in values],
        out_specs=[pair(count)]
        + [pair(k.shape[0]) for k in keys]
        + [pair(v.shape[0]) for v in values],
        out_shape=[jax.ShapeDtypeStruct((count, width), bf16)]
        + [jax.ShapeDtypeStruct(k.shape, bf16) for k in keys]
        + [jax.ShapeDtypeStruct(v.shape, bf16) for v in values],
        compiler_params=pltpu.CompilerParams(vmem_limit_bytes=40 << 20),
        cost_estimate=pl.CostEstimate(
            flops=40 * count * total * width // 2,
            bytes_accessed=width * (count * 12 + total * 8),
            transcendentals=count * total * width // HALF,
        ),
        name="attend_back",
    )(query, grad, out, logsum, mask_q, mask_k, *keys, *values)
    return result[0], result[1 : 1 + parts], result[1 + parts :]


def norm_stats(value):
    mean = jnp.mean(value, axis=-1, keepdims=True)
    centred = value - mean
    spread = jnp.mean(centred * centred, axis=-1, keepdims=True)
    return mean, lax.rsqrt(spread + EPS)


def norm(value, gain):
    mean, scale = norm_stats(value)
    return ((value - mean) * scale * gain).astype(bf16)


def norm_back(grad, value, gain):
    mean, scale = norm_stats(value)
    unit = (value - mean) * scale
    gain_grad = jnp.sum(grad * unit, axis=0)
    grad = grad * gain
    extra = scale * (
        grad
        - jnp.mean(grad, axis=-1, keepdims=True)
        - unit * jnp.mean(grad * unit, axis=-1, keepdims=True)
    )
    return extra, gain_grad


def gelu_tanh(value):
    return jax.nn.gelu(value, approximate=True)


def per_device(tm, seq_size, *args):
    (
        large_view,
        small_view,
        clip_ids,
        first_gain,
        query_weight,
        key_weight,
        value_weight,
        output_weight,
        second_gain,
        up_weight,
        down_weight,
        query_gain,
        context_gain,
        cross_query,
        cross_key,
        cross_value,
        cross_output,
        cotangent,
    ) = args
    seqs, count, width = large_view.shape
    half = count // 2
    side = tm // 4
    gains = [g.astype(f32) for g in (first_gain, second_gain, query_gain, context_gain)]
    first_gain, second_gain, query_gain, context_gain = gains

    tm_at = lax.axis_index("tm")
    seq_at = lax.axis_index("seq")
    z, x = tm_at // side, tm_at % side
    y, core = seq_at // 2, seq_at % 2

    def permute(value, place):
        pairs = []
        for pz in range(4):
            for px in range(side):
                for py in range(2):
                    for pc in range(2):
                        to = place(pz, px, py, pc)
                        source = (pz * side + px) * seq_size + py * 2 + pc
                        target = (to[0] * side + to[1]) * seq_size + to[2] * 2 + to[3]
                        pairs.append((source, target))
        return lax.ppermute(value, ("tm", "seq"), pairs)

    def inverse(place):
        table = {}
        for pz in range(4):
            for px in range(side):
                for py in range(2):
                    for pc in range(2):
                        table[place(pz, px, py, pc)] = (pz, px, py, pc)
        return lambda *at: table[at]

    go = (
        lambda z, x, y, c: (2 * c + z % 2, x, y, z // 2),
        lambda z, x, y, c: (2 * c + 1 - z % 2, x, y, z // 2),
    )
    back = tuple(inverse(place) for place in go)
    other_core = lambda value: permute(value, lambda z, x, y, c: (z, x, y, 1 - c))
    other_y = lambda value: permute(value, lambda z, x, y, c: (z, x, 1 - y, c))
    by_x = lambda value, d: permute(value, lambda z, x, y, c: (z, (x + d) % side, y, c))
    by_z = lambda value, d: permute(value, lambda z, x, y, c: (z ^ d, x, y, c))

    odd = z % 2 == 1

    def relocate(value):
        near = jnp.where(odd, value[1], value[0])
        far = jnp.where(odd, value[0], value[1])
        return jnp.concatenate([permute(near, go[0]), permute(far, go[1])], axis=0)

    def restore(value):
        rows = value.shape[0] // 2
        near, far = permute(value[:rows], back[0]), permute(value[rows:], back[1])
        return jnp.where(odd, jnp.stack([far, near]), jnp.stack([near, far]))

    all_clips = lax.all_gather(clip_ids, ("tm", "seq"), axis=0, tiled=False)
    owner = 2 * y + z // 2
    mine = lax.dynamic_index_in_dim(
        all_clips.reshape(tm, seq_size, seqs, count), owner, 1, keepdims=False
    )
    mine = lax.dynamic_index_in_dim(mine, z % 2, 1, keepdims=False)
    order = []
    for dx in range(side):
        for dc in ((0, 1) if dx == 0 else (0,)):
            order.append((dx, dc))
    order += [(dx, 1) for dx in range(1, side)]
    slots = []
    for dx, dc in order:
        held = (core + dc) % 2
        for slot in (0, 1):
            from_z = 2 * held + (z + slot) % 2
            slots.append(from_z * side + (x - dx) % side)
    clips = jnp.concatenate(
        [lax.dynamic_index_in_dim(mine, at, 0, keepdims=False) for at in slots]
    )
    short_clips = clips[::2]
    spot = lax.broadcasted_iota(jnp.int32, (1, LANES), 1) % HALF

    def mask_of_keys(numbers):
        return jnp.where((spot < 4) & (numbers[:, None] != spot), NEGATIVE, 0.0).astype(bf16)

    def mask_of_queries(numbers):
        return jnp.where((spot < 4) & (numbers[:, None] == spot), 1.0, 0.0).astype(bf16)

    large_mask_k, small_mask_k = mask_of_keys(clips), mask_of_keys(short_clips)
    large_mask_q = mask_of_queries(clips[: 2 * count])
    small_mask_q = mask_of_queries(short_clips[: 2 * half])

    def gather(value):
        beside = other_core(value)
        across = [by_x(value, d) for d in range(1, side)]
        across = across[0] if len(across) == 1 else jnp.concatenate(across, axis=0)
        return (value, beside, across, other_core(across))

    def scatter(pieces):
        own, beside, across, diagonal = pieces
        across = across.astype(f32) + other_core(diagonal).astype(f32)
        across = across.astype(bf16)
        total = own.astype(f32) + other_core(beside).astype(f32)
        rows = own.shape[0]
        for d in range(1, side):
            part = across[(d - 1) * rows : d * rows]
            total = total + by_x(part, -d).astype(f32)
        return total.astype(bf16)

    small = relocate(small_view)
    large = relocate(large_view)
    grad_out = relocate(cotangent)
    small, large = small.astype(f32), large.astype(f32)
    q_scale = LOG2E * HALF**-0.5

    def front(view):
        normed = norm(view, first_gain)
        keys = dot(normed, key_weight).astype(bf16)
        values = dot(normed, value_weight).astype(bf16)
        query = (dot(normed, query_weight) * q_scale).astype(bf16)
        return normed, query, gather(keys), gather(values)

    def rest(view, mixed):
        hidden = view + dot(mixed, output_weight)
        second = norm(hidden, second_gain)
        inner = dot(second, up_weight)
        active = gelu_tanh(inner).astype(bf16)
        merged = hidden + dot(active, down_weight)
        return merged, (hidden, second, inner, active)

    small_normed, small_q, small_k, small_v = front(small)
    large_normed, large_q, large_k, large_v = front(large)
    small_mixed, small_logsum = attend(small_q, small_k, small_v, small_mask_q, small_mask_k)
    small_merged, small_saved = rest(small, small_mixed)
    context = norm(small_merged, context_gain)
    cross_k = gather(dot(context, cross_key).astype(bf16))
    cross_v = gather(dot(context, cross_value).astype(bf16))
    large_mixed, large_logsum = attend(large_q, large_k, large_v, large_mask_q, large_mask_k)
    large_merged, large_saved = rest(large, large_mixed)
    asked = norm(large_merged, query_gain)
    cross_q = (dot(asked, cross_query) * q_scale).astype(bf16)
    united, cross_logsum = attend(cross_q, cross_k, cross_v, large_mask_q, small_mask_k)
    united_view = restore((large_merged + dot(united, cross_output)).astype(bf16))

    def bucket(pieces):
        parts = []
        for piece in pieces:
            rows, columns = piece.shape
            piece = piece.reshape(tm, rows // tm, columns)
            for at in range(0, columns, width):
                parts.append(piece[:, :, at : at + width])
        return jnp.concatenate(parts, axis=1) if len(parts) > 1 else parts[0]

    def unbucket(total, shapes):
        out, at = [], 0
        for rows, columns in shapes:
            rows //= tm
            parts = []
            for _ in range(columns // width):
                parts.append(total[at : at + rows])
                at += rows
            out.append(jnp.concatenate(parts, axis=1) if len(parts) > 1 else parts[0])
        return out

    def pick(value, axis, size, at):
        return lax.dynamic_slice_in_dim(value, at * size, size, axis)

    def add(a, b):
        return (a.astype(f32) + b.astype(f32)).astype(bf16)

    def reduce(local):
        rows = local.shape[1] // 2
        columns = local.shape[2] // 2
        value = add(
            pick(local, 1, rows, core), other_core(pick(local, 1, rows, 1 - core))
        )
        value = add(pick(value, 2, columns, y), other_y(pick(value, 2, columns, 1 - y)))
        value = value.reshape(4, side, rows, columns)
        total = lax.dynamic_index_in_dim(value, x, 1, keepdims=False).astype(f32)
        for d in range(1, side):
            sent = lax.dynamic_index_in_dim(value, (x + d) % side, 1, keepdims=False)
            total = total + by_x(sent, d).astype(f32)
        value = total.astype(bf16)
        total = lax.dynamic_index_in_dim(value, z, 0, keepdims=False).astype(f32)
        for d in range(1, 4):
            sent = lax.dynamic_index_in_dim(value, z ^ d, 0, keepdims=False)
            total = total + by_z(sent, d).astype(f32)
        value = total.astype(bf16)
        other = other_y(value)
        value = jnp.where(
            y == 0,
            jnp.concatenate([value, other], axis=1),
            jnp.concatenate([other, value], axis=1),
        )
        other = other_core(value)
        return jnp.where(
            core == 0,
            jnp.concatenate([value, other], axis=0),
            jnp.concatenate([other, value], axis=0),
        ).astype(f32)

    def encode_back(merged_grad, saved, mixed):
        hidden, second, inner, active = saved
        branch = merged_grad.astype(bf16)
        down_part = dot(active, branch, TN)
        _, pull = jax.vjp(gelu_tanh, inner)
        inner_grad = pull(dot(branch, down_weight, NT))[0].astype(bf16)
        up_part = dot(second, inner_grad, TN)
        extra, gain_part = norm_back(dot(inner_grad, up_weight, NT), hidden, second_gain)
        hidden_grad = merged_grad + extra
        attend_grad = hidden_grad.astype(bf16)
        output_part = dot(mixed, attend_grad, TN)
        mixed_grad = dot(attend_grad, output_weight, NT).astype(bf16)
        return hidden_grad, mixed_grad, (gain_part, up_part, down_part, output_part)

    def front_back(view, hidden_grad, normed, dq, dk, dv):
        parts = (dot(normed, dq, TN), dot(normed, dk, TN), dot(normed, dv, TN))
        grad = (
            dot(dq, query_weight, NT) + dot(dk, key_weight, NT) + dot(dv, value_weight, NT)
        )
        extra, gain_part = norm_back(grad, view, first_gain)
        return (hidden_grad + extra).astype(bf16), (gain_part,) + parts

    cross_output_grad = dot(united, grad_out, TN)
    united_grad = dot(grad_out, cross_output, NT).astype(bf16)
    dcq, dck, dcv = attend_back(
        cross_q, cross_k, cross_v, united_grad, united, cross_logsum, large_mask_q, small_mask_k
    )
    dck, dcv = scatter(dck), scatter(dcv)
    cross_query_grad = dot(asked, dcq, TN)
    extra, query_gain_grad = norm_back(dot(dcq, cross_query, NT), large_merged, query_gain)
    large_hidden, large_mixed_grad, large_parts = encode_back(
        grad_out.astype(f32) + extra, large_saved, large_mixed
    )
    large_dq, large_dk, large_dv = attend_back(
        large_q, large_k, large_v, large_mixed_grad, large_mixed, large_logsum,
        large_mask_q, large_mask_k,
    )
    large_dk, large_dv = scatter(large_dk), scatter(large_dv)
    cross_key_grad = dot(context, dck, TN)
    cross_value_grad = dot(context, dcv, TN)
    small_merged_grad, context_gain_grad = norm_back(
        dot(dck, cross_key, NT) + dot(dcv, cross_value, NT), small_merged, context_gain
    )
    small_hidden, small_mixed_grad, small_parts = encode_back(
        small_merged_grad, small_saved, small_mixed
    )
    small_dq, small_dk, small_dv = attend_back(
        small_q, small_k, small_v, small_mixed_grad, small_mixed, small_logsum,
        small_mask_q, small_mask_k,
    )
    small_dk, small_dv = scatter(small_dk), scatter(small_dv)
    large_grad, large_front = front_back(
        large, large_hidden, large_normed, large_dq, large_dk, large_dv
    )
    small_grad, small_front = front_back(
        small, small_hidden, small_normed, small_dq, small_dk, small_dv
    )
    large_grad = restore(large_grad).astype(f32)
    small_grad = restore(small_grad).astype(f32)

    square = (width, width)
    cross_shapes = [square] * 4
    cross_total = reduce(
        bucket(
            [
                g.astype(bf16)
                for g in (cross_output_grad, cross_query_grad, cross_key_grad, cross_value_grad)
            ]
        )
    )
    cross_grads = unbucket(cross_total, cross_shapes)
    dense_shapes = [up_weight.shape, down_weight.shape, square]
    dense_total = reduce(
        bucket([(large_parts[i] + small_parts[i]).astype(bf16) for i in (1, 2, 3)])
    )
    dense_grads = unbucket(dense_total, dense_shapes)
    gain_rows = jnp.stack(
        [
            large_front[0] + small_front[0],
            large_parts[0] + small_parts[0],
            query_gain_grad,
            context_gain_grad,
        ]
    )
    gain_rows = jnp.transpose(gain_rows.reshape(4, tm, width // tm), (1, 0, 2)).astype(bf16)
    gain_rows = jnp.pad(gain_rows, ((0, 0), (0, 28), (0, width - width // tm)))
    last = bucket([(large_front[i] + small_front[i]).astype(bf16) for i in (1, 2, 3)])
    last_total = reduce(jnp.concatenate([last, gain_rows], axis=1))
    last_grads = unbucket(last_total, [square] * 3)
    gain_at = 3 * width // tm
    gain_grads = [last_total[gain_at + i, : width // tm] for i in range(4)]
    return (
        united_view,
        large_grad,
        small_grad,
        gain_grads[0],
        last_grads[0],
        last_grads[1],
        last_grads[2],
        dense_grads[2],
        gain_grads[1],
        dense_grads[0],
        dense_grads[1],
        gain_grads[2],
        gain_grads[3],
        cross_grads[1],
        cross_grads[2],
        cross_grads[3],
        cross_grads[0],
    )


def solution(mesh):
    token = P("seq", "tm", None)
    in_specs = (token, token, P("seq", "tm")) + (P(),) * 14 + (token,)
    vector, matrix = P("tm"), P("tm", None)
    out_specs = (
        (token, token, token, vector)
        + (matrix,) * 4
        + (vector, matrix, matrix, vector, vector)
        + (matrix,) * 4
    )
    return jax.shard_map(
        functools.partial(per_device, mesh.shape["tm"], mesh.shape["seq"]),
        mesh=mesh,
        in_specs=in_specs,
        out_specs=out_specs,
        check_vma=False,
    )
```

time: 1990 us -> 711 us (0.36)
  waiting for transfers between devices: 889 us -> 231 us
  matrix products: 580 us -> 103 us
  blocking collectives: 225 us -> 47.6 us
  Pallas kernels: 0 us -> 123 us
  local copies, waits for them, and re-layouts: 155 us -> 50.2 us
  starting transfers between devices: 2.26 us -> 101 us
  other arithmetic: 95.7 us -> 42.1 us
    reduce_scatter x10 -> x0, waiting for transfers between devices: 647 us -> none  [the longest x1 166 us: per_device(): lax.psum_scatter(local_grads[7], 'tm', scatter_dimension=0, tiled=True)]
    dot_general x110 -> x48, matrix products: 580 us -> 103 us  [dot(): return lax.dot_general(a, b, dims, preferred_element_type=f32)]
    ppermute x0 -> x72, waiting for transfers between devices: none -> 231 us  [permute(): return lax.ppermute(value, ('tm', 'seq'), pairs)]
    all_gather x12 -> x0, waiting for transfers between devices: 230 us -> none  [the longest x1 91.2 us: per_device(): lax.all_gather(large_v, 'tm', axis=1, tiled=True)]
    all_gather x7 -> x1, blocking collectives: 184 us -> 47.6 us  [per_device(): all_clips = lax.all_gather(clip_ids, ('tm', 'seq'), axis=0, tiled=False)]
    pallas_call x0 -> x6, Pallas kernels: none -> 123 us  [the longest x3 79.4 us: attend_back(): pl.pallas_call(functools.partial(attend_back_kernel, parts), grid=(width...]
    ppermute x0 -> x72, starting transfers between devices: none -> 101 us  [permute(): return lax.ppermute(value, ('tm', 'seq'), pairs)]
    dynamic_slice x78 -> x7, local copies, waits for them, and re-layouts: 76.4 us -> 7.97 us  [the longest x6 7.95 us: pick(): return lax.dynamic_slice_in_dim(value, at * size, size, axis)]
  transfers between devices with their start and end apart: 23 -> 72, of which waited for: 13 -> 19; matrix products, arithmetic and copies ran while one was open for 40% -> 20% of each run, Pallas kernels for 0% -> 12%
where the time goes in v1:
time: 711 us; the launch traced here: 703 us
  waiting for transfers between devices  231 us (32%)
  Pallas kernels  123 us (17%)
  matrix products  103 us (14%)
  starting transfers between devices  101 us (14%)
  local copies, waits for them, and re-layouts  50.2 us (7%)
  blocking collectives  47.6 us (7%)
  other arithmetic  42.1 us (6%)
    ppermute x72, waiting for transfers between devices, permute(): return lax.ppermute(value, ('tm', 'seq'), pairs)  231 us
    dot_general x48, matrix products, dot(): return lax.dot_general(a, b, dims, preferred_element_type=f32)  103 us
    ppermute x72, starting transfers between devices, permute(): return lax.ppermute(value, ('tm', 'seq'), pairs)  101 us
    pallas_call x3, Pallas kernels, attend_back(): pl.pallas_call(functools.partial(attend_back_kernel, parts), grid=(width...  79.4 us
    all_gather x1, blocking collectives, per_device(): all_clips = lax.all_gather(clip_ids, ('tm', 'seq'), axis=0, tiled=False)  47.6 us
    pallas_call x3, Pallas kernels, attend(): pl.pallas_call(functools.partial(attend_kernel, parts, block), grid=(widt...  43.7 us
    unnamed x366, local copies, waits for them, and re-layouts  31.6 us
  transfers between devices with their start and end apart: 72, of which 19 were waited for; matrix products, arithmetic and copies ran while one was open for 20% of the time, Pallas kernels for 12%

profile of v1, /device:TPU:1, one launch (start us, length us, event | category | flops | bytes accessed | tf_op | source)
XLA Modules:
  0.0 702.9 jit_solution(8396109625341583436)
XLA Ops:
  2.6 5.6 collective-permute-start.8
  19.8 47.6 %all-gather.1 = s32[32,2,256]{2,1,0:T(2,128)S(1)} all-gather(s32[1,2,256]{2,1,0:T(2,128)S(1)} %bitcast.185), channel_id=2, replica_groups=mesh['tm'=8,'seq'=4] {'tm','seq'}, dimensions={0}, use_global_device_ids=true | all-gather | bytes 67584 | tf_op jit(solution)/shard_map/all_gather | solution.py:304
  96.6 8.5 %attend.4 = (bf16[256,768]{1,0:T(8,128)(2,1)S(1)}, f32[256,768]{1,0:T(8,128)S(1)}) custom-call(bf16[256,768]{1,0:T(8,128)(2,1)S(1)} %fusion.33.refs_0_, bf16[256,128]{1,0:T(8,128)(2,1)S(1)} %select_convert_fusion.3.refs_1_.refs_4_, bf16[1024,128]{1,0:T(8,128)(2,1)S(1)} %select_convert_fusion.1.refs_2_.refs_5_, ...), custom_call_target="tpu_custom_call" | custom-call | flops 3221225472 | bytes 4718592 | tf_op jit(solution)/shard_map/attend/pallas_call | solution.py:83
  114.9 14.5 %collective-permute-done.6.refs_9_.refs_12_ = bf16[512,768]{1,0:T(8,128)(2,1)S(1)} collective-permute-done((bf16[512,768]{1,0:T(8,128)(2,1)S(1)}, bf16[512,768]{1,0:T(8,128)(2,1)S(1)}, u32[]{:S(2)}, u32[]{:S(2)}) %collective-permute-start.6) | collective-permute-done | bytes 786464 | tf_op jit(solution)/shard_map/ppermute | solution.py:271
  135.9 6.7 collective-permute-done.17.refs_5_.refs_8_
  143.8 7.2 %collective-permute-done.20.refs_9_.refs_12_ = bf16[256,768]{1,0:T(8,128)(2,1)S(1)} collective-permute-done((bf16[256,768]{1,0:T(8,128)(2,1)S(1)}, bf16[256,768]{1,0:T(8,128)(2,1)S(1)}, u32[]{:S(2)}, u32[]{:S(2)}) %collective-permute-start.20) | collective-permute-done | bytes 393248 | tf_op jit(solution)/shard_map/ppermute | solution.py:271
  151.9 21.2 %attend.3 = (bf16[512,768]{1,0:T(8,128)(2,1)S(1)}, f32[512,768]{1,0:T(8,128)S(1)}) custom-call(bf16[512,768]{1,0:T(8,128)(2,1)S(1)} %multiply_convert_fusion.5.refs_0_, bf16[512,128]{1,0:T(8,128)(2,1)S(1)} %select_convert_fusion.2.refs_1_.refs_4_, bf16[2048,128]{1,0:T(8,128)(2,1)S(1)} %select_convert_fusion.refs_2_.refs_5_, ...), custom_call_target="tpu_custom_call" | custom-call | flops 12884901888 | bytes 9437184 | tf_op jit(solution)/shard_map/attend/pallas_call | solution.py:83
  183.4 14.0 %attend.5 = (bf16[512,768]{1,0:T(8,128)(2,1)S(1)}, f32[512,768]{1,0:T(8,128)S(1)}) custom-call(bf16[512,768]{1,0:T(8,128)(2,1)S(1)} %multiply_convert_fusion.2.refs_0_, bf16[512,128]{1,0:T(8,128)(2,1)S(1)} %select_convert_fusion.2.refs_1_.refs_4_, bf16[1024,128]{1,0:T(8,128)(2,1)S(1)} %select_convert_fusion.1.refs_2_.refs_5_, ...), custom_call_target="tpu_custom_call" | custom-call | flops 6442450944 | bytes 6291456 | tf_op jit(solution)/shard_map/attend/pallas_call | solution.py:83
  199.1 22.4 %attend_back.3 = (bf16[512,768]{1,0:T(8,128)(2,1)S(1)}, bf16[256,768]{1,0:T(8,128)(2,1)S(1)}, bf16[256,768]{1,0:T(8,128)(2,1)S(1)}, bf16[256,768]{1,0:T(8,128)(2...) custom-call(bf16[512,768]{1,0:T(8,128)(2,1)S(1)} %multiply_convert_f, ...), custom_call_target="tpu_custom_call" | custom-call | flops 8053063680 | bytes 11010048 | tf_op jit(solution)/shard_map/attend_back/pallas_call | solution.py:176
  223.2 9.5 %fusion.7 = bf16[512,3072]{1,0:T(8,128)(2,1)S(1)} fusion(f32[512,3072]{1,0:T(8,128)} %copy-done.160, bf16[3072,768]{1,0:T(8,128)(2,1)} %param.28, f32[512,768]{1,0:T(8,128)S(1)} %multiply_add_fusion.1), kind=kOutput, calls=%fused_computation.13 | convolution fusion | flops 2447769600 | bytes 15728640 | tf_op jit(solution)/shard_map/dot_general | solution.py:26
  250.7 39.9 %attend_back.4 = (bf16[512,768]{1,0:T(8,128)(2,1)S(1)}, bf16[512,768]{1,0:T(8,128)(2,1)S(1)}, bf16[512,768]{1,0:T(8,128)(2,1)S(1)}, bf16[512,768]{1,0:T(8,128)(2...) custom-call(bf16[512,768]{1,0:T(8,128)(2,1)S(1)} %multiply_convert_f, ...), custom_call_target="tpu_custom_call" | custom-call | flops 16106127360 | bytes 17301504 | tf_op jit(solution)/shard_map/attend_back/pallas_call | solution.py:176
  308.0 6.5 collective-permute-done.36
  328.7 5.8 fusion.73
  348.0 17.2 %attend_back.5 = (bf16[256,768]{1,0:T(8,128)(2,1)S(1)}, bf16[256,768]{1,0:T(8,128)(2,1)S(1)}, bf16[256,768]{1,0:T(8,128)(2,1)}, bf16[256,768]{1,0:T(8,128)(2,1)S...) custom-call(bf16[256,768]{1,0:T(8,128)(2,1)S(1)} %copy-done.49, ...), custom_call_target="tpu_custom_call" | custom-call | flops 4026531840 | bytes 8650752 | tf_op jit(solution)/shard_map/attend_back/pallas_call | solution.py:176
  374.2 8.7 %add_convert_fusion.1 = bf16[3072,768]{1,0:T(8,128)(2,1)} fusion(f32[3072,768]{1,0:T(8,128)S(1)} %bitcast.154, f32[512,768]{1,0:T(8,128)S(1)} %copy-done.76, f32[512,3072]{1,0:T(8,128)} %copy-done.160), kind=kOutput, calls=%fused_computation.1 | convolution fusion | flops 2435186688 | bytes 22020096 | tf_op jit(solution)/shard_map/dot_general | solution.py:26
  432.3 10.8 %collective-permute-done.28 = bf16[512,768]{1,0:T(8,128)(2,1)S(1)} collective-permute-done((bf16[512,768]{1,0:T(8,128)(2,1)S(1)}, bf16[512,768]{1,0:T(8,128)(2,1)S(1)}, u32[]{:S(2)}, u32[]{:S(2)}) %collective-permute-start.28) | collective-permute-done | bytes 786464 | tf_op jit(solution)/shard_map/ppermute | solution.py:271
  444.1 15.9 %collective-permute-done.31 = bf16[512,768]{1,0:T(8,128)(2,1)S(1)} collective-permute-done((bf16[512,768]{1,0:T(8,128)(2,1)S(1)}, bf16[512,768]{1,0:T(8,128)(2,1)S(1)}, u32[]{:S(2)}, u32[]{:S(2)}) %collective-permute-start.31) | collective-permute-done | bytes 786464 | tf_op jit(solution)/shard_map/ppermute | solution.py:271
  477.6 5.6 add_convert_fusion
  500.2 67.8 %collective-permute-done.65 = bf16[8,192,384]{2,1,0:T(8,128)(2,1)S(1)} collective-permute-done((bf16[8,192,384]{2,1,0:T(8,128)(2,1)S(1)}, bf16[8,192,384]{2,1,0:T(8,128)(2,1)S(1)}, u32[]{:S(2)}, u32[]{:S(2)}) %collective-permute-start.65) | collective-permute-done | bytes 1179680 | tf_op jit(solution)/shard_map/ppermute | solution.py:271
  573.1 15.9 %collective-permute-done.49 = bf16[8,160,384]{2,1,0:T(8,128)(2,1)S(1)} collective-permute-done((bf16[8,160,384]{2,1,0:T(8,128)(2,1)S(1)}, bf16[8,160,384]{2,1,0:T(8,128)(2,1)S(1)}, u32[]{:S(2)}, u32[]{:S(2)}) %collective-permute-start.49) | collective-permute-done | bytes 983072 | tf_op jit(solution)/shard_map/ppermute | solution.py:271
  594.9 34.5 %collective-permute-done.50 = bf16[4,160,384]{2,1,0:T(8,128)(2,1)S(1)} collective-permute-done((bf16[4,160,384]{2,1,0:T(8,128)(2,1)S(1)}, bf16[4,160,384]{2,1,0:T(8,128)(2,1)S(1)}, u32[]{:S(2)}, u32[]{:S(2)}) %collective-permute-start.50) | collective-permute-done | bytes 491552 | tf_op jit(solution)/shard_map/ppermute | solution.py:271
  636.3 14.6 %collective-permute-start.33 = (bf16[256,768]{1,0:T(8,128)(2,1)S(1)}, bf16[256,768]{1,0:T(8,128)(2,1)S(1)}, u32[]{:S(2)}, u32[]{:S(2)}) collective-permute-start(bf16[256,768]{1,0:T(8,128)(2,1)S(1)} %get-tuple-element.121), channel_id=1, source_target_pairs={{0,0},{1,16},{2,2},{3,18},{4,4},{5,20},{6,6},{7,22},{8,8},{9,24},{... | collective-permute-start | bytes 1179656 | tf_op jit(solution)/shard_map/ppermute | solution.py:271
  653.8 13.2 %collective-permute-done.59 = bf16[432,384]{1,0:T(8,128)(2,1)S(1)} collective-permute-done((bf16[432,384]{1,0:T(8,128)(2,1)S(1)}, bf16[432,384]{1,0:T(8,128)(2,1)S(1)}, u32[]{:S(2)}, u32[]{:S(2)}) %collective-permute-start.59) | collective-permute-done | bytes 331808 | tf_op jit(solution)/shard_map/ppermute | solution.py:271
  672.0 13.6 %collective-permute-done.60 = bf16[432,384]{1,0:T(8,128)(2,1)S(1)} collective-permute-done((bf16[432,384]{1,0:T(8,128)(2,1)S(1)}, bf16[432,384]{1,0:T(8,128)(2,1)S(1)}, u32[]{:S(2)}, u32[]{:S(2)}) %collective-permute-start.60) | collective-permute-done | bytes 331808 | tf_op jit(solution)/shard_map/ppermute | solution.py:271
  (663 shorter events, 271.5 us)
Async XLA Ops:
  2.6 66.2 %collective-permute-start.8 = (bf16[128,768]{1,0:T(8,128)(2,1)}, bf16[128,768]{1,0:T(8,128)(2,1)S(1)}, u32[]{:S(2)}, u32[]{:S(2)}) collective-permute-start(bf16[128,768]{1,0:T(8,128)(2,1)} %get-tuple-element.136), channel_id=1, source_target_pairs={{0,0},{1,16},{2,2},{3,18},{4,4},{5,20},{6,6},{7,22},{8,8},{9,24},{... | collective-permute-start | bytes 589832 | tf_op jit(solution)/shard_map/ppermute | solution.py:271
  8.2 66.0 %collective-permute-start.9 = (bf16[128,768]{1,0:T(8,128)(2,1)S(1)}, bf16[128,768]{1,0:T(8,128)(2,1)S(1)}, u32[]{:S(2)}, u32[]{:S(2)}) collective-permute-start(bf16[128,768]{1,0:T(8,128)(2,1)S(1)} %get-tuple-element.137), channel_id=1, source_target_pairs={{0,8},{1,24},{2,10},{3,26},{4,12},{5,28},{6,14},{7,30},{8,0},{9,16... | collective-permute-start | bytes 589832 | tf_op jit(solution)/shard_map/ppermute | solution.py:271
  11.3 66.4 %collective-permute-start = (bf16[256,768]{1,0:T(8,128)(2,1)}, bf16[256,768]{1,0:T(8,128)(2,1)S(1)}, u32[]{:S(2)}, u32[]{:S(2)}) collective-permute-start(bf16[256,768]{1,0:T(8,128)(2,1)} %get-tuple-element.126), channel_id=1, source_target_pairs={{0,0},{1,16},{2,2},{3,18},{4,4},{5,20},{6,6},{7,22},{8,8},{9,24},{... | collective-permute-start | bytes 1179656 | tf_op jit(solution)/shard_map/ppermute | solution.py:271
  15.1 62.7 %collective-permute-start.1 = (bf16[256,768]{1,0:T(8,128)(2,1)}, bf16[256,768]{1,0:T(8,128)(2,1)S(1)}, u32[]{:S(2)}, u32[]{:S(2)}) collective-permute-start(bf16[256,768]{1,0:T(8,128)(2,1)} %get-tuple-element.127), channel_id=1, source_target_pairs={{0,8},{1,24},{2,10},{3,26},{4,12},{5,28},{6,14},{7,30},{8,0},{9,16... | collective-permute-start | bytes 1179656 | tf_op jit(solution)/shard_map/ppermute | solution.py:271
  17.0 114.8 %collective-permute-start.25 = (bf16[256,768]{1,0:T(8,128)(2,1)}, bf16[256,768]{1,0:T(8,128)(2,1)}, u32[]{:S(2)}, u32[]{:S(2)}) collective-permute-start(bf16[256,768]{1,0:T(8,128)(2,1)} %get-tuple-element.122), channel_id=1, source_target_pairs={{0,8},{1,24},{2,10},{3,26},{4,12},{5,28},{6,14},{7,30},{8,0},{9,16... | collective-permute-start | bytes 1179656 | tf_op jit(solution)/shard_map/ppermute | solution.py:271
  135.3 48.1 %collective-permute-start.16 = (bf16[256,768]{1,0:T(8,128)(2,1)S(1)}, bf16[256,768]{1,0:T(8,128)(2,1)S(1)}, u32[]{:S(2)}, u32[]{:S(2)}) collective-permute-start(bf16[256,768]{1,0:T(8,128)(2,1)S(1)} %convolution_convert_fusion.10.refs_3_.refs_6_), channel_id=1, source_target_pairs={{0,1},{1,0},{2,3},{3,2},{4,5},{5,4},{6,7},{7,6},{8,9},{9,8},{10,11... | collective-permute-start | bytes 1179656 | tf_op jit(solution)/shard_map/ppermute | solution.py:271
  241.5 56.9 %collective-permute-start.35 = (bf16[256,768]{1,0:T(8,128)(2,1)}, bf16[256,768]{1,0:T(8,128)(2,1)}, u32[]{:S(2)}, u32[]{:S(2)}) collective-permute-start(bf16[256,768]{1,0:T(8,128)(2,1)} %get-tuple-element.68), channel_id=1, source_target_pairs={{0,1},{1,0},{2,3},{3,2},{4,5},{5,4},{6,7},{7,6},{8,9},{9,8},{10,11... | collective-permute-start | bytes 1179656 | tf_op jit(solution)/shard_map/ppermute | solution.py:271
  242.0 61.8 %collective-permute-start.37 = (bf16[256,768]{1,0:T(8,128)(2,1)}, bf16[256,768]{1,0:T(8,128)(2,1)}, u32[]{:S(2)}, u32[]{:S(2)}) collective-permute-start(bf16[256,768]{1,0:T(8,128)(2,1)} %get-tuple-element.70), channel_id=1, source_target_pairs={{0,1},{1,0},{2,3},{3,2},{4,5},{5,4},{6,7},{7,6},{8,9},{9,8},{10,11... | collective-permute-start | bytes 1179656 | tf_op jit(solution)/shard_map/ppermute | solution.py:271
  242.0 52.7 %collective-permute-start.38 = (bf16[256,768]{1,0:T(8,128)(2,1)S(1)}, bf16[256,768]{1,0:T(8,128)(2,1)S(1)}, u32[]{:S(2)}, u32[]{:S(2)}) collective-permute-start(bf16[256,768]{1,0:T(8,128)(2,1)S(1)} %get-tuple-element.72), channel_id=1, source_target_pairs={{0,1},{1,0},{2,3},{3,2},{4,5},{5,4},{6,7},{7,6},{8,9},{9,8},{10,11... | collective-permute-start | bytes 1179656 | tf_op jit(solution)/shard_map/ppermute | solution.py:271
  243.4 57.7 %collective-permute-start.22 = (bf16[256,768]{1,0:T(8,128)(2,1)}, bf16[256,768]{1,0:T(8,128)(2,1)}, u32[]{:S(2)}, u32[]{:S(2)}) collective-permute-start(bf16[256,768]{1,0:T(8,128)(2,1)} %get-tuple-element.124), channel_id=1, source_target_pairs={{0,8},{1,24},{2,10},{3,26},{4,12},{5,28},{6,14},{7,30},{8,0},{9,16... | collective-permute-start | bytes 1179656 | tf_op jit(solution)/shard_map/ppermute | solution.py:271
  244.9 56.5 %collective-permute-start.23 = (bf16[256,768]{1,0:T(8,128)(2,1)}, bf16[256,768]{1,0:T(8,128)(2,1)}, u32[]{:S(2)}, u32[]{:S(2)}) collective-permute-start(bf16[256,768]{1,0:T(8,128)(2,1)} %get-tuple-element.125), channel_id=1, source_target_pairs={{0,0},{1,16},{2,2},{3,18},{4,4},{5,20},{6,6},{7,22},{8,8},{9,24},{... | collective-permute-start | bytes 1179656 | tf_op jit(solution)/shard_map/ppermute | solution.py:271
  301.2 92.9 %collective-permute-start.27 = (bf16[512,768]{1,0:T(8,128)(2,1)}, bf16[512,768]{1,0:T(8,128)(2,1)}, u32[]{:S(2)}, u32[]{:S(2)}) collective-permute-start(bf16[512,768]{1,0:T(8,128)(2,1)} %get-tuple-element.60), channel_id=1, source_target_pairs={{0,1},{1,0},{2,3},{3,2},{4,5},{5,4},{6,7},{7,6},{8,9},{9,8},{10,11... | collective-permute-start | bytes 2359304 | tf_op jit(solution)/shard_map/ppermute | solution.py:271
  303.8 98.9 %collective-permute-start.30 = (bf16[512,768]{1,0:T(8,128)(2,1)}, bf16[512,768]{1,0:T(8,128)(2,1)}, u32[]{:S(2)}, u32[]{:S(2)}) collective-permute-start(bf16[512,768]{1,0:T(8,128)(2,1)} %get-tuple-element.64), channel_id=1, source_target_pairs={{0,1},{1,0},{2,3},{3,2},{4,5},{5,4},{6,7},{7,6},{8,9},{9,8},{10,11... | collective-permute-start | bytes 2359304 | tf_op jit(solution)/shard_map/ppermute | solution.py:271
  365.2 54.9 %collective-permute-start.40 = (bf16[256,768]{1,0:T(8,128)(2,1)}, bf16[256,768]{1,0:T(8,128)(2,1)}, u32[]{:S(2)}, u32[]{:S(2)}) collective-permute-start(bf16[256,768]{1,0:T(8,128)(2,1)} %get-tuple-element.76), channel_id=1, source_target_pairs={{0,1},{1,0},{2,3},{3,2},{4,5},{5,4},{6,7},{7,6},{8,9},{9,8},{10,11... | collective-permute-start | bytes 1179656 | tf_op jit(solution)/shard_map/ppermute | solution.py:271
  366.5 46.7 %collective-permute-start.43 = (bf16[256,768]{1,0:T(8,128)(2,1)}, bf16[256,768]{1,0:T(8,128)(2,1)}, u32[]{:S(2)}, u32[]{:S(2)}) collective-permute-start(bf16[256,768]{1,0:T(8,128)(2,1)} %get-tuple-element.80), channel_id=1, source_target_pairs={{0,1},{1,0},{2,3},{3,2},{4,5},{5,4},{6,7},{7,6},{8,9},{9,8},{10,11... | collective-permute-start | bytes 1179656 | tf_op jit(solution)/shard_map/ppermute | solution.py:271
  402.7 74.9 %collective-permute-start.56 = (bf16[8,432,768]{2,1,0:T(8,128)(2,1)}, bf16[8,432,768]{2,1,0:T(8,128)(2,1)}, u32[]{:S(2)}, u32[]{:S(2)}) collective-permute-start(bf16[8,432,768]{2,1,0:T(8,128)(2,1)} %constant_dynamic-slice_fusion.3), channel_id=1, source_target_pairs={{0,1},{1,0},{2,3},{3,2},{4,5},{5,4},{6,7},{7,6},{8,9},{9,8},{10,11... | collective-permute-start | bytes 15925256 | tf_op jit(solution)/shard_map/ppermute | solution.py:271
  430.5 60.4 %collective-permute-start.64 = (bf16[8,192,768]{2,1,0:T(8,128)(2,1)}, bf16[8,192,768]{2,1,0:T(8,128)(2,1)}, u32[]{:S(2)}, u32[]{:S(2)}) collective-permute-start(bf16[8,192,768]{2,1,0:T(8,128)(2,1)} %constant_dynamic-slice_fusion.1), channel_id=1, source_target_pairs={{0,1},{1,0},{2,3},{3,2},{4,5},{5,4},{6,7},{7,6},{8,9},{9,8},{10,11... | collective-permute-start | bytes 7077896 | tf_op jit(solution)/shard_map/ppermute | solution.py:271
  483.5 88.7 %collective-permute-start.57 = (bf16[8,432,384]{2,1,0:T(8,128)(2,1)S(1)}, bf16[8,432,384]{2,1,0:T(8,128)(2,1)S(1)}, u32[]{:S(2)}, u32[]{:S(2)}) collective-permute-start(bf16[8,432,384]{2,1,0:T(8,128)(2,1)S(1)} %constant_dynamic-slice_fusion.2), channel_id=1, source_target_pairs={{0,2},{1,3},{2,0},{3,1},{4,6},{5,7},{6,4},{7,5},{8,10},{9,11},{10,... | collective-permute-start | bytes 7962632 | tf_op jit(solution)/shard_map/ppermute | solution.py:271
  484.9 105.0 %collective-permute-start.46 = (bf16[128,768]{1,0:T(8,128)(2,1)S(1)}, bf16[128,768]{1,0:T(8,128)(2,1)S(1)}, u32[]{:S(2)}, u32[]{:S(2)}) collective-permute-start(bf16[128,768]{1,0:T(8,128)(2,1)S(1)} %get-tuple-element.134), channel_id=1, source_target_pairs={{0,8},{1,24},{2,10},{3,26},{4,12},{5,28},{6,14},{7,30},{8,0},{9,16... | collective-permute-start | bytes 589832 | tf_op jit(solution)/shard_map/ppermute | solution.py:271
  487.5 103.4 %collective-permute-start.47 = (bf16[128,768]{1,0:T(8,128)(2,1)S(1)}, bf16[128,768]{1,0:T(8,128)(2,1)S(1)}, u32[]{:S(2)}, u32[]{:S(2)}) collective-permute-start(bf16[128,768]{1,0:T(8,128)(2,1)S(1)} %get-tuple-element.135), channel_id=1, source_target_pairs={{0,0},{1,16},{2,2},{3,18},{4,4},{5,20},{6,6},{7,22},{8,8},{9,24},{... | collective-permute-start | bytes 589832 | tf_op jit(solution)/shard_map/ppermute | solution.py:271
  493.5 74.5 %collective-permute-start.65 = (bf16[8,192,384]{2,1,0:T(8,128)(2,1)S(1)}, bf16[8,192,384]{2,1,0:T(8,128)(2,1)S(1)}, u32[]{:S(2)}, u32[]{:S(2)}) collective-permute-start(bf16[8,192,384]{2,1,0:T(8,128)(2,1)S(1)} %constant_dynamic-slice_fusion), channel_id=1, source_target_pairs={{0,2},{1,3},{2,0},{3,1},{4,6},{5,7},{6,4},{7,5},{8,10},{9,11},{10,... | collective-permute-start | bytes 3538952 | tf_op jit(solution)/shard_map/ppermute | solution.py:271
  499.1 90.0 %collective-permute-start.49 = (bf16[8,160,384]{2,1,0:T(8,128)(2,1)S(1)}, bf16[8,160,384]{2,1,0:T(8,128)(2,1)S(1)}, u32[]{:S(2)}, u32[]{:S(2)}) collective-permute-start(bf16[8,160,384]{2,1,0:T(8,128)(2,1)S(1)} %constant_dynamic-slice_fusion.4), channel_id=1, source_target_pairs={{0,2},{1,3},{2,0},{3,1},{4,6},{5,7},{6,4},{7,5},{8,10},{9,11},{10,... | collective-permute-start | bytes 2949128 | tf_op jit(solution)/shard_map/ppermute | solution.py:271
  568.0 117.9 %collective-permute-start.32 = (bf16[256,768]{1,0:T(8,128)(2,1)S(1)}, bf16[256,768]{1,0:T(8,128)(2,1)S(1)}, u32[]{:S(2)}, u32[]{:S(2)}) collective-permute-start(bf16[256,768]{1,0:T(8,128)(2,1)S(1)} %get-tuple-element.120), channel_id=1, source_target_pairs={{0,8},{1,24},{2,10},{3,26},{4,12},{5,28},{6,14},{7,30},{8,0},{9,16... | collective-permute-start | bytes 1179656 | tf_op jit(solution)/shard_map/ppermute | solution.py:271
  636.3 49.6 %collective-permute-start.33 = (bf16[256,768]{1,0:T(8,128)(2,1)S(1)}, bf16[256,768]{1,0:T(8,128)(2,1)S(1)}, u32[]{:S(2)}, u32[]{:S(2)}) collective-permute-start(bf16[256,768]{1,0:T(8,128)(2,1)S(1)} %get-tuple-element.121), channel_id=1, source_target_pairs={{0,0},{1,16},{2,2},{3,18},{4,4},{5,20},{6,6},{7,22},{8,8},{9,24},{... | collective-permute-start | bytes 1179656 | tf_op jit(solution)/shard_map/ppermute | solution.py:271
  (224 other events, 2995.2 us)

commit v2 on v1

v2 whole, which is shorter than its diff:
```python
import functools

import jax
import jax.numpy as jnp
from jax import lax
from jax.experimental import pallas as pl
from jax.experimental.pallas import tpu as pltpu
from jax.sharding import PartitionSpec as P

HEADS = 12
EPS = 1e-05
NEGATIVE = -1e30
LOG2E = 1.4426950408889634
LN2 = 0.6931471805599453
LANES = 128
HALF = 64

bf16 = jnp.bfloat16
f32 = jnp.float32
NT = (((1,), (1,)), ((), ()))
NN = (((1,), (0,)), ((), ()))
TN = (((0,), (0,)), ((), ()))


def dot(a, b, dims=NN):
    return lax.dot_general(a, b, dims, preferred_element_type=f32)


def largest_block(rows, most):
    block = min(rows, most)
    while rows % block or block % 16:
        block -= 1
    return block


def columns(rows, at):
    return pl.BlockSpec((rows, LANES), lambda i: (0, i + at))


def pair_columns(rows, at):
    return pl.BlockSpec((2, rows, LANES), lambda i: (0, 0, i + at))


def whole(shape):
    return pl.BlockSpec(shape, lambda i: (0,) * len(shape))


def attend_kernel(parts, block, *refs):
    q_ref, mq_ref, mk_ref = refs[:3]
    kv_refs = refs[3 : 3 + parts]
    o_ref, l_ref, ka0, ka1, va0, va1 = refs[-6:]
    count = q_ref.shape[0]
    first = 0
    for kv_ref in kv_refs:
        rows = kv_ref.shape[1]
        low = lax.broadcasted_iota(jnp.int32, (rows, LANES), 1) < HALF
        here = pl.ds(first, rows)
        keys, values, mask = kv_ref[0], kv_ref[1], mk_ref[here, :]
        one = jnp.ones_like(values)
        ka0[here, :] = jnp.where(low, keys, mask)
        ka1[here, :] = jnp.where(low, mask, keys)
        va0[here, :] = jnp.where(low, values, one)
        va1[here, :] = jnp.where(low, one, values)
        first += rows
    low = lax.broadcasted_iota(jnp.int32, (block, LANES), 1) < HALF
    for number in range(count // block):
        here = pl.ds(number * block, block)
        query, mask = q_ref[here, :], mq_ref[here, :]
        tops, sums = [], []
        for head, keys, values in ((0, ka0, va0), (1, ka1, va1)):
            mine = jnp.where(low, query, mask) if head == 0 else jnp.where(low, mask, query)
            score = dot(mine, keys[...], NT)
            top = jnp.max(score, axis=1, keepdims=True)
            weight = jnp.exp2(score - top).astype(bf16)
            sums.append(dot(weight, values[...]))
            tops.append(jnp.broadcast_to(top, (block, LANES)))
        total = jnp.where(low, sums[1], sums[0])
        top = jnp.where(low, tops[1], tops[0])
        out = jnp.where(low, sums[0], sums[1])
        o_ref[here, :] = (out / pltpu.roll(total, HALF, 1)).astype(bf16)
        l_ref[here, :] = top + jnp.log2(total)


def attend(query, kv, mask_q, mask_k, at, width, earlier=()):
    count = query.shape[0]
    total = sum(part.shape[1] for part in kv)
    out = lambda kind: jax.ShapeDtypeStruct((count, query.shape[1]), kind)
    given = 3 + len(kv)
    return pl.pallas_call(
        functools.partial(attend_kernel, len(kv), largest_block(count, 256)),
        grid=(width // LANES,),
        in_specs=[columns(count, at // LANES), whole((count, LANES)), whole((total, LANES))]
        + [pair_columns(part.shape[1], 0) for part in kv]
        + [pl.BlockSpec(memory_space=pl.ANY)] * len(earlier),
        out_specs=[columns(count, at // LANES)] * 2,
        out_shape=[out(bf16), out(f32)],
        scratch_shapes=[pltpu.VMEM((total, LANES), bf16)] * 4,
        input_output_aliases={given + i: i for i in range(len(earlier))},
        compiler_params=pltpu.CompilerParams(vmem_limit_bytes=40 << 20),
        cost_estimate=pl.CostEstimate(
            flops=16 * count * total * width,
            bytes_accessed=width * (count * 8 + total * 4),
            transcendentals=count * total * width // HALF,
        ),
        name="attend",
    )(query, mask_q, mask_k, *kv, *earlier)


def three(value):
    first = value.astype(bf16)
    rest = value - first.astype(f32)
    second = rest.astype(bf16)
    return first, second, (rest - second.astype(f32)).astype(bf16)


def attend_back_kernel(parts, block, *refs):
    q_ref, do_ref, o_ref, l_ref, mq_ref, mk_ref = refs[:6]
    kv_refs = refs[6 : 6 + parts]
    dq_ref, keep_ref, send_ref, keys_at, values_at = refs[6 + parts :]
    count = q_ref.shape[0]
    first = 0
    for kv_ref in kv_refs:
        here = pl.ds(first, kv_ref.shape[1])
        keys_at[here, :] = kv_ref[0]
        values_at[here, :] = kv_ref[1]
        first += kv_ref.shape[1]
    lane = lax.broadcasted_iota(jnp.int32, (count, LANES), 1)
    low = lane < HALF
    spot = lane % HALF
    query, grad, mask = q_ref[...], do_ref[...], mq_ref[...]
    zero = jnp.zeros_like(query)
    product = grad.astype(f32) * o_ref[...].astype(f32)
    delta0 = jnp.sum(jnp.where(low, product, 0.0), axis=1, keepdims=True)
    delta1 = jnp.sum(jnp.where(low, 0.0, product), axis=1, keepdims=True)
    delta = jnp.where(low, delta1, delta0)

    def beside(base, value):
        a, b, c = three(-value)
        return jnp.where(spot == 4, a, jnp.where(spot == 5, b, jnp.where(spot == 6, c, base)))

    query_side = beside(mask, l_ref[...])
    grad_side = beside(zero, delta)
    query_a = (jnp.where(low, query, query_side), jnp.where(low, query_side, query))
    grad_a = (jnp.where(low, grad, grad_side), jnp.where(low, grad_side, grad))
    query_m = (jnp.where(low, query, zero), jnp.where(low, zero, query))
    grad_m = (jnp.where(low, grad, zero), jnp.where(low, zero, grad))
    lane_k = lax.broadcasted_iota(jnp.int32, (block, LANES), 1)
    low_k = lane_k < HALF
    spot_k = lane_k % HALF
    one = jnp.where((spot_k >= 4) & (spot_k < 7), 1.0, 0.0).astype(bf16)
    dq = jnp.zeros((count, LANES), f32)
    for number in range(first // block):
        here = pl.ds(number * block, block)
        keys, values = keys_at[here, :], values_at[here, :]
        side = mk_ref[here, :] + one
        nought = jnp.zeros_like(keys)
        dk = jnp.zeros((block, LANES), f32)
        dv = jnp.zeros((block, LANES), f32)
        for head in (0, 1):
            pick = lambda a, b: jnp.where(low_k, a, b) if head == 0 else jnp.where(low_k, b, a)
            prob = jnp.exp2(dot(query_a[head], pick(keys, side), NT))
            change = dot(grad_a[head], pick(values, one), NT)
            score_grad = (prob * change).astype(bf16)
            dv += dot(prob.astype(bf16), grad_m[head], TN)
            dk += dot(score_grad, query_m[head], TN)
            dq += dot(score_grad, pick(keys, nought))
        out_ref = keep_ref if number * block < first // 2 else send_ref
        there = pl.ds(number * block % (first // 2), block)
        out_ref[0, there, :] = (dk * LN2).astype(bf16)
        out_ref[1, there, :] = dv.astype(bf16)
    dq_ref[...] = (dq * HALF**-0.5).astype(bf16)


def attend_back(query, kv, grad, out, logsum, mask_q, mask_k, at, at_out, at_kv, width):
    count = query.shape[0]
    total = sum(part.shape[1] for part in kv)
    return pl.pallas_call(
        functools.partial(attend_back_kernel, len(kv), largest_block(total // 2, 512)),
        grid=(width // LANES,),
        in_specs=[columns(count, at // LANES)] * 2
        + [columns(count, at_out // LANES)] * 2
        + [whole((count, LANES)), whole((total, LANES))]
        + [pair_columns(part.shape[1], at_kv // LANES) for part in kv],
        out_specs=[columns(count, 0)] + [pair_columns(total // 2, 0)] * 2,
        out_shape=[jax.ShapeDtypeStruct((count, width), bf16)]
        + [jax.ShapeDtypeStruct((2, total // 2, width), bf16)] * 2,
        scratch_shapes=[pltpu.VMEM((total, LANES), bf16)] * 2,
        compiler_params=pltpu.CompilerParams(vmem_limit_bytes=40 << 20),
        cost_estimate=pl.CostEstimate(
            flops=20 * count * total * width,
            bytes_accessed=width * (count * 12 + total * 8),
            transcendentals=count * total * width // HALF,
        ),
        name="attend_back",
    )(query, grad, out, logsum, mask_q, mask_k, *kv)


def norm_stats(value):
    mean = jnp.mean(value, axis=-1, keepdims=True)
    centred = value - mean
    spread = jnp.mean(centred * centred, axis=-1, keepdims=True)
    return centred, lax.rsqrt(spread + EPS)


def norm(value, gain):
    centred, scale = norm_stats(value)
    return (centred * scale * gain).astype(bf16)


def norm_back(grad, value, gain):
    centred, scale = norm_stats(value)
    unit = centred * scale
    gain_grad = jnp.sum(grad * unit, axis=0, keepdims=True)
    grad = grad * gain
    extra = scale * (
        grad
        - jnp.mean(grad, axis=-1, keepdims=True)
        - unit * jnp.mean(grad * unit, axis=-1, keepdims=True)
    )
    return extra, gain_grad


Q_SCALE = LOG2E * HALF**-0.5


def front_kernel(x_ref, gain_ref, wq_ref, wk_ref, wv_ref, n_ref, q_ref, *kv_refs):
    normed = norm(x_ref[...].astype(f32), gain_ref[...])
    n_ref[...] = normed
    width = kv_refs[0].shape[2]
    keys = dot(normed, wk_ref[...]).astype(bf16)
    values = dot(normed, wv_ref[...]).astype(bf16)
    for group, kv_ref in enumerate(kv_refs):
        kv_ref[0] = keys[:, group * width : (group + 1) * width]
        kv_ref[1] = values[:, group * width : (group + 1) * width]
    q_ref[...] = (dot(normed, wq_ref[...]) * Q_SCALE).astype(bf16)


def front(view, gain, wq, wk, wv, groups):
    rows, width = view.shape
    part = width // groups
    result = pl.pallas_call(
        front_kernel,
        out_shape=[jax.ShapeDtypeStruct((rows, width), bf16)] * 2
        + [jax.ShapeDtypeStruct((2, rows, part), bf16)] * groups,
        compiler_params=pltpu.CompilerParams(vmem_limit_bytes=40 << 20),
        cost_estimate=pl.CostEstimate(
            flops=6 * rows * width * width,
            bytes_accessed=6 * width * width + 10 * rows * width,
            transcendentals=0,
        ),
        name="front",
    )(view, gain, wq, wk, wv)
    return result[0], result[1], result[2:]


GELU_A = 0.7978845608028654
GELU_B = 0.044715


def gelu_both(value):
    square = value * value
    bent = jnp.tanh(GELU_A * value * (1.0 + GELU_B * square))
    half = 0.5 * (1.0 + bent)
    slope = half + 0.5 * value * (1.0 - bent * bent) * (
        GELU_A * (1.0 + 3.0 * GELU_B * square)
    )
    return value * half, slope


def rest_kernel(steps, mixes, is_query, *refs):
    x_ref = refs[0]
    mixed_refs = refs[1 : 1 + mixes]
    wo_ref, gain_ref, up_ref, down_ref, next_gain_ref = refs[1 + mixes : 6 + mixes]
    next_refs = refs[6 + mixes : -9]
    merged_ref, hidden_ref, second_ref, active_ref, slope_ref = refs[-9:-4]
    asked_ref, out_ref, total, scratch = refs[-4:]
    step = pl.program_id(0)

    @pl.when(step == 0)
    def _():
        at = 0
        hidden = x_ref[...].astype(f32)
        for mixed_ref in mixed_refs:
            wide = mixed_ref.shape[1]
            scratch[:, pl.ds(at, wide)] = mixed_ref[...]
            at += wide
        hidden = hidden + dot(scratch[...], wo_ref[...])
        hidden_ref[...] = hidden
        second_ref[...] = norm(hidden, gain_ref[...])
        total[...] = hidden

    inner = dot(second_ref[...], up_ref[...])
    active, slope = gelu_both(inner)
    active = active.astype(bf16)
    active_ref[...] = active
    slope_ref[...] = slope.astype(bf16)
    total[...] += dot(active, down_ref[...])

    @pl.when(step == steps - 1)
    def _():
        merged = total[...]
        merged_ref[...] = merged
        asked = norm(merged, next_gain_ref[...])
        asked_ref[...] = asked
        if is_query:
            out_ref[...] = (dot(asked, next_refs[0][...]) * Q_SCALE).astype(bf16)
        else:
            out_ref[0] = dot(asked, next_refs[0][...]).astype(bf16)
            out_ref[1] = dot(asked, next_refs[1][...]).astype(bf16)


def rest(view, mixed, wo, gain, up, down, next_gain, next_weights):
    rows, width = view.shape
    steps = up.shape[1] // width
    is_query = len(next_weights) == 1
    flat = whole((rows, width))
    slab = pl.BlockSpec((rows, width), lambda i: (0, i))
    square = whole((width, width))
    shape = lambda kind: jax.ShapeDtypeStruct((rows, width), kind)
    wide = jax.ShapeDtypeStruct((rows, up.shape[1]), bf16)
    last = (rows, width) if is_query else (2, rows, width)
    return pl.pallas_call(
        functools.partial(rest_kernel, steps, len(mixed), is_query),
        grid=(steps,),
        in_specs=[flat]
        + [whole(m.shape) for m in mixed]
        + [square, whole((1, width))]
        + [slab_of(width, width), pl.BlockSpec((width, width), lambda i: (i, 0))]
        + [whole((1, width))]
        + [square] * len(next_weights),
        out_specs=[flat, flat, flat, slab, slab, flat, whole(last)],
        out_shape=[shape(f32), shape(f32), shape(bf16), wide, wide, shape(bf16)]
        + [jax.ShapeDtypeStruct(last, bf16)],
        scratch_shapes=[pltpu.VMEM((rows, width), f32), pltpu.VMEM((rows, width), bf16)],
        compiler_params=pltpu.CompilerParams(vmem_limit_bytes=48 << 20),
        cost_estimate=pl.CostEstimate(
            flops=2 * rows * width * (4 * up.shape[1] // 2 + 2 * width),
            bytes_accessed=width * width * 22 + rows * width * 32,
            transcendentals=rows * up.shape[1],
        ),
        name="rest",
    )(view, *mixed, wo, gain, up, down, next_gain, *next_weights)


def slab_of(rows, width):
    return pl.BlockSpec((rows, width), lambda i: (0, i))


def back_kernel(steps, mixes, sizes, laid, *refs):
    gl_ref, gs_ref, al_ref, as_ref, sl_ref, ss_ref = refs[:6]
    cl_ref, cs_ref, hl_ref, hs_ref = refs[6:10]
    mixed_refs = refs[10 : 10 + mixes]
    mixed_s_ref, wo_ref, gain_ref, up_ref, down_ref = refs[10 + mixes : 15 + mixes]
    outs = refs[15 + mixes :]
    (hgl_ref, hgs_ref, ml_ref, ms_ref, dup_ref, ddown_ref, dwo_ref, dgain_ref) = outs[:8]
    branch, second, total, active, inner_grad, mixed = outs[8:]
    large, small = sizes
    top, bottom = pl.ds(0, large), pl.ds(large, small)
    step = pl.program_id(0)

    @pl.when(step == 0)
    def _():
        branch[top, :] = gl_ref[...].astype(bf16)
        branch[bottom, :] = gs_ref[...].astype(bf16)
        second[top, :] = cl_ref[...]
        second[bottom, :] = cs_ref[...]
        total[...] = jnp.zeros_like(total)

    grad = dot(branch[...], down_ref[...], NT)
    inner_grad[top, :] = (grad[:large] * sl_ref[...].astype(f32)).astype(bf16)
    inner_grad[bottom, :] = (grad[large:] * ss_ref[...].astype(f32)).astype(bf16)
    active[top, :] = al_ref[...]
    active[bottom, :] = as_ref[...]
    down = dot(active[...], branch[...], TN).astype(bf16)
    upper = dot(second[...], inner_grad[...], TN).astype(bf16)
    if laid:
        rows = dup_ref.shape[1]
        for at in range(8):
            zl, x, zh = at // 4, at // 2 % 2, at % 2
            first = ((zh * 2 + zl) * 2 + x) * rows
            dup_ref[at] = upper[first : first + rows]
        for x, core, y in ((a, b, c) for a in (0, 1) for b in (0, 1) for c in (0, 1)):
            first = (x * 4 + core * 2 + y) * rows
            there = core * 16 + (step % 2) * 8 + y * 4 + x * 2 + step // 2
            ddown_ref[there] = down[first : first + rows]
    else:
        dup_ref[...] = upper
        ddown_ref[...] = down
    total[...] += dot(inner_grad[...], up_ref[...], NT)

    @pl.when(step == steps - 1)
    def _():
        extra, gain_l = norm_back(total[top, :], hl_ref[...], gain_ref[...])
        hidden_grad = gl_ref[...] + extra
        hgl_ref[...] = hidden_grad
        branch[top, :] = hidden_grad.astype(bf16)
        extra, gain_s = norm_back(total[bottom, :], hs_ref[...], gain_ref[...])
        hidden_grad = gs_ref[...] + extra
        hgs_ref[...] = hidden_grad
        branch[bottom, :] = hidden_grad.astype(bf16)
        dgain_ref[...] = gain_l + gain_s
        mixed_grad = dot(branch[...], wo_ref[...], NT).astype(bf16)
        ml_ref[...] = mixed_grad[:large]
        ms_ref[...] = mixed_grad[large:]
        at = 0
        for mixed_ref in mixed_refs:
            wide = mixed_ref.shape[1]
            mixed[top, pl.ds(at, wide)] = mixed_ref[...]
            at += wide
        mixed[bottom, :] = mixed_s_ref[...]
        value = dot(mixed[...], branch[...], TN).astype(bf16)
        if laid:
            rows, wide = dwo_ref.shape[1:]
            for at, (core, y, tm) in enumerate(spots(BY_Y)):
                first = (tm * 2 + core) * rows
                dwo_ref[at] = value[first : first + rows, y * wide : (y + 1) * wide]
        else:
            dwo_ref[...] = value


def back(grad_l, grad_s, saved_l, saved_s, mixed_l, mixed_s, wo, gain, up, down, laid=False):
    (hidden_l, second_l, active_l, slope_l) = saved_l
    (hidden_s, second_s, active_s, slope_s) = saved_s
    large, width = grad_l.shape
    small = grad_s.shape[0]
    rows = large + small
    hidden = up.shape[1]
    part = width
    steps = hidden // part
    fl, fs = whole((large, width)), whole((small, width))
    square = whole((width, width))
    up_slab = slab_of(width, part)
    down_slab = pl.BlockSpec((part, width), lambda i: (i, 0))
    shape = jax.ShapeDtypeStruct
    out_up, out_down, out_square = up_slab, down_slab, square
    up_shape, down_shape, square_shape = up.shape, down.shape, (width, width)
    if laid:
        block = (width // 8, width)
        up_shape = down_shape = (32,) + block
        square_shape = (32, width // 16, width // 2)
        out_up = pl.BlockSpec((8,) + block, lambda i: (i, 0, 0))
        out_down, out_square = whole(down_shape), whole(square_shape)
    return pl.pallas_call(
        functools.partial(back_kernel, steps, len(mixed_l), (large, small), laid),
        grid=(steps,),
        in_specs=[fl, fs]
        + [slab_of(large, part), slab_of(small, part)] * 2
        + [fl, fs, fl, fs]
        + [whole(m.shape) for m in mixed_l]
        + [fs, square, whole((1, width)), up_slab, down_slab],
        out_specs=[fl, fs, fl, fs, out_up, out_down, out_square, whole((1, width))],
        out_shape=[
            shape((large, width), f32),
            shape((small, width), f32),
            shape((large, width), bf16),
            shape((small, width), bf16),
            shape(up_shape, bf16),
            shape(down_shape, bf16),
            shape(square_shape, bf16),
            shape((1, width), f32),
        ],
        scratch_shapes=[
            pltpu.VMEM((rows, width), bf16),
            pltpu.VMEM((rows, width), bf16),
            pltpu.VMEM((rows, width), f32),
            pltpu.VMEM((rows, part), bf16),
            pltpu.VMEM((rows, part), bf16),
            pltpu.VMEM((rows, width), bf16),
        ],
        compiler_params=pltpu.CompilerParams(vmem_limit_bytes=56 << 20),
        cost_estimate=pl.CostEstimate(
            flops=2 * rows * width * (4 * hidden + 2 * width),
            bytes_accessed=width * width * 36 + rows * width * 40,
            transcendentals=0,
        ),
        name="back",
    )(
        grad_l, grad_s, active_l, active_s, slope_l, slope_s, second_l, second_s, hidden_l, hidden_s,
        *mixed_l, mixed_s, wo, gain, up, down,
    )


MESH = pl.DeviceIdType.MESH
BY_Y = ("core", "y", "zl", "x", "zh")
BY_ZL = ("core", "zl", "y", "x", "zh")
BY_X = ("core", "x", "zl", "y", "zh")
BY_YX = ("core", "y", "x", "zl", "zh")


def spots(order):
    out = []
    for at in range(32):
        bit = {name: (at >> (4 - i)) & 1 for i, name in enumerate(order)}
        out.append((bit["core"], bit["y"], (bit["zh"] * 2 + bit["zl"]) * 2 + bit["x"]))
    return out


class Here:
    def __init__(self):
        tm, seq = lax.axis_index("tm"), lax.axis_index("seq")
        self.tm, self.seq = tm, seq
        self.bit = {
            "zh": tm // 4,
            "zl": (tm // 2) % 2,
            "x": tm % 2,
            "y": seq // 2,
            "core": seq % 2,
        }

    def partner(self, *names):
        tm, seq = self.tm, self.seq
        for name in names:
            one = 1 - 2 * self.bit[name]
            if name in ("y", "core"):
                seq = seq + one * (2 if name == "y" else 1)
            else:
                tm = tm + one * {"zh": 4, "zl": 2, "x": 1}[name]
        return (tm, seq)

    def greet(self, partners):
        barrier = pltpu.get_barrier_semaphore()
        for names in partners:
            pl.semaphore_signal(
                barrier, inc=1, device_id=self.partner(*names), device_id_type=MESH
            )
        pl.semaphore_wait(barrier, len(partners))


ALL_PARTNERS = (("core",), ("y",), ("zl",), ("x",), ("zh",), ("y", "core"))


class Flow:
    def __init__(self, here, order, refs):
        self.here, self.order = here, order
        self.local, self.keep = refs[0], refs[1]
        self.got = refs[2:7]
        self.out = refs[7]
        self.send_sem, self.recv_sem = refs[8], refs[9]

    def copy(self, step):
        name = self.order[step]
        half = 16 >> step
        source = self.local if step == 0 else self.got[step - 1]
        at = (1 - self.here.bit[name]) * half
        return pltpu.make_async_remote_copy(
            src_ref=source.at[pl.ds(at, half)],
            dst_ref=self.got[step],
            send_sem=self.send_sem.at[step],
            recv_sem=self.recv_sem.at[step],
            device_id=self.here.partner(name),
            device_id_type=MESH,
        )

    def keep_copy(self):
        at = self.here.bit[self.order[0]] * 16
        return pltpu.make_async_copy(
            self.local.at[pl.ds(at, 16)], self.keep, self.send_sem.at[8]
        )

    def start(self, step):
        self.copy(step).start()
        if step == 0 and self.keep is not None:
            self.keep_copy().start()

    def finish(self, step):
        half = 16 >> step
        self.copy(step).wait()
        got = self.got[step]
        at = self.here.bit[self.order[step]] * half
        if step == 0 and self.keep is not None:
            self.keep_copy().wait()
            source, at = self.keep, 0
        else:
            source = self.local if step == 0 else self.got[step - 1]

        def body(i, carry):
            got[i] = got[i] + source[at + i]
            return carry

        if half == 1:
            got[0] = got[0] + source[at]
        else:
            lax.fori_loop(0, half, body, 0)

    def spread_copies(self):
        here = self.here
        slot = here.bit["core"] * 2 + here.bit["y"]
        return [
            pltpu.make_async_remote_copy(
                src_ref=self.got[4].at[0],
                dst_ref=self.out.at[slot],
                send_sem=self.send_sem.at[5 + i],
                recv_sem=self.recv_sem.at[5 + i],
                device_id=here.partner(*names),
                device_id_type=MESH,
            )
            for i, names in enumerate((("core",), ("y",), ("y", "core")))
        ]

    def spread(self):
        for copy in self.spread_copies():
            copy.start()
        slot = self.here.bit["core"] * 2 + self.here.bit["y"]
        self.out[slot] = self.got[4][0]

    def gathered(self):
        for copy in self.spread_copies():
            copy.wait()

    def act(self, stage):
        if stage == 0:
            self.start(0)
        elif stage < 5:
            self.finish(stage - 1)
            self.start(stage)
        elif stage == 5:
            self.finish(4)
            self.spread()
        else:
            self.gathered()


def flow_scratch(rows, wide, keep):
    blocks = [pltpu.VMEM((16, rows, wide), bf16)] if keep else []
    for half in (16, 8, 4, 2, 1):
        blocks.append(pltpu.VMEM((half, rows, wide), bf16))
    blocks.append(pltpu.VMEM((4, rows, wide), bf16))
    return blocks + [pltpu.SemaphoreType.DMA((9,)), pltpu.SemaphoreType.DMA((8,))]


def pair_back(query, grad, out, logsum, mask, keys_at, values_at, mk_ref, block, store):
    count = query.shape[0]
    total = keys_at.shape[0]
    lane = lax.broadcasted_iota(jnp.int32, (count, LANES), 1)
    low = lane < HALF
    spot = lane % HALF
    zero = jnp.zeros_like(query)
    product = grad.astype(f32) * out.astype(f32)
    delta0 = jnp.sum(jnp.where(low, product, 0.0), axis=1, keepdims=True)
    delta1 = jnp.sum(jnp.where(low, 0.0, product), axis=1, keepdims=True)
    delta = jnp.where(low, delta1, delta0)

    def beside(base, value):
        a, b, c = three(-value)
        return jnp.where(spot == 4, a, jnp.where(spot == 5, b, jnp.where(spot == 6, c, base)))

    query_side = beside(mask, logsum)
    grad_side = beside(zero, delta)
    query_a = (jnp.where(low, query, query_side), jnp.where(low, query_side, query))
    grad_a = (jnp.where(low, grad, grad_side), jnp.where(low, grad_side, grad))
    query_m = (jnp.where(low, query, zero), jnp.where(low, zero, query))
    grad_m = (jnp.where(low, grad, zero), jnp.where(low, zero, grad))
    lane_k = lax.broadcasted_iota(jnp.int32, (block, LANES), 1)
    low_k = lane_k < HALF
    spot_k = lane_k % HALF
    one = jnp.where((spot_k >= 4) & (spot_k < 7), 1.0, 0.0).astype(bf16)
    dq = jnp.zeros((count, LANES), f32)
    for number in range(total // block):
        here = pl.ds(number * block, block)
        keys, values = keys_at[here, :], values_at[here, :]
        side = mk_ref[here, :] + one
        nought = jnp.zeros_like(keys)
        dk = jnp.zeros((block, LANES), f32)
        dv = jnp.zeros((block, LANES), f32)
        for head in (0, 1):
            pick = lambda a, b: jnp.where(low_k, a, b) if head == 0 else jnp.where(low_k, b, a)
            prob = jnp.exp2(dot(query_a[head], pick(keys, side), NT))
            change = dot(grad_a[head], pick(values, one), NT)
            score_grad = (prob * change).astype(bf16)
            dv += dot(prob.astype(bf16), grad_m[head], TN)
            dk += dot(score_grad, query_m[head], TN)
            dq += dot(score_grad, pick(keys, nought))
        store(number, (dk * LN2).astype(bf16), dv.astype(bf16))
    return (dq * HALF**-0.5).astype(bf16)


class Exchange:
    def __init__(self, here, rows, refs):
        self.here, self.rows = here, rows
        self.sums, self.send, self.got_core, self.across, self.got_x = refs[:5]
        self.sems = refs[5]

    def copy_core(self, pair):
        return pltpu.make_async_remote_copy(
            src_ref=self.send.at[pair % 2],
            dst_ref=self.got_core.at[pair],
            send_sem=self.sems.at[0, pair],
            recv_sem=self.sems.at[1, pair],
            device_id=self.here.partner("core"),
            device_id_type=MESH,
        )

    def copy_x(self, pair):
        return pltpu.make_async_remote_copy(
            src_ref=self.across.at[pair % 2],
            dst_ref=self.got_x.at[pair],
            send_sem=self.sems.at[2, pair],
            recv_sem=self.sems.at[3, pair],
            device_id=self.here.partner("x"),
            device_id_type=MESH,
        )

    def free(self, pair):
        self.copy_core(pair).wait_send()

    def put(self, pair, total, block):
        half = total // 2

        def store(number, dk, dv):
            there = pl.ds(number * block % half, block)
            if number * block < half:
                self.sums[pair % 3, 0, there, :] = dk
                self.sums[pair % 3, 1, there, :] = dv
            else:
                self.send[pair % 2, 0, there, :] = dk
                self.send[pair % 2, 1, there, :] = dv

        return store

    def pass_on(self, pair, wait_before):
        rows = self.rows
        self.copy_core(pair).wait_recv()
        if wait_before:
            self.copy_x(pair - 2).wait_send()
        far = pl.ds(rows, rows)
        for i in (0, 1):
            self.across[pair % 2, i] = (
                self.sums[pair % 3, i, far, :] + self.got_core[pair, i, far, :]
            )
        self.copy_x(pair).start()

    def take(self, pair, out_ref):
        near = pl.ds(0, self.rows)
        self.copy_x(pair).wait_recv()
        for i in (0, 1):
            out_ref[pair, i] = (
                self.sums[pair % 3, i, near, :].astype(f32)
                + self.got_core[pair, i, near, :].astype(f32)
                + self.got_x[pair, i].astype(f32)
            ).astype(bf16)


def exchange_scratch(pairs, rows):
    return [
        pltpu.VMEM((3, 2, 2 * rows, LANES), bf16),
        pltpu.VMEM((2, 2, 2 * rows, LANES), bf16),
        pltpu.VMEM((pairs, 2, 2 * rows, LANES), bf16),
        pltpu.VMEM((2, 2, rows, LANES), bf16),
        pltpu.VMEM((pairs, 2, rows, LANES), bf16),
        pltpu.SemaphoreType.DMA((4, pairs)),
    ]


def selves_kernel(pairs, plan, blocks, *refs):
    orders, shapes, stages = plan
    large_refs, refs = refs[:6], refs[6:]
    groups = 3
    kv_large = [refs[4 * g : 4 * g + 4] for g in range(groups)]
    refs = refs[4 * groups :]
    small_refs, kv_small, refs = refs[:6], refs[6:10], refs[10:]
    flows = len(orders)
    locals_, refs = refs[:flows], refs[flows:]
    dq_l, dkv_l, dq_s, dkv_s = refs[:4]
    sums, refs = refs[4 : 4 + flows], refs[4 + flows :]
    keys_l, values_l, keys_s, values_s = refs[:4]
    ex_l, ex_s, refs = refs[4:10], refs[10:16], refs[16:]
    here = Here()
    rows_l, rows_s = keys_l.shape[0] // 4, keys_s.shape[0] // 4
    large, small = Exchange(here, rows_l, ex_l), Exchange(here, rows_s, ex_s)
    running = []
    for flow in range(flows):
        running.append(Flow(here, orders[flow], [locals_[flow]] + list(refs[:9])))
        refs = refs[9:]
    step = pl.program_id(0)

    @pl.when(step == 0)
    def _():
        here.greet(ALL_PARTNERS)
        for flow in running:
            flow.act(0)

    def move(exchange, pair, out_ref):
        exchange.copy_core(pair).start()

        @pl.when((pair >= 1) & (pair < 3))
        def _():
            exchange.pass_on(pair - 1, False)

        @pl.when(pair >= 3)
        def _():
            exchange.pass_on(pair - 1, True)

        @pl.when(pair >= 2)
        def _():
            exchange.take(pair - 2, out_ref)

    def attention(exchange, pair, refs, kv_of, keys_at, values_at, block, dq_ref):
        q_ref, do_ref, o_ref, l_ref, mq_ref, mk_ref = refs
        for when, kv_refs in kv_of:

            def fill(kv_refs=kv_refs):
                at = 0
                for kv_ref in kv_refs:
                    there = pl.ds(at, kv_ref.shape[1])
                    keys_at[there, :] = kv_ref[0]
                    values_at[there, :] = kv_ref[1]
                    at += kv_ref.shape[1]

            if when is None:
                fill()
            else:
                pl.when(when)(fill)

        @pl.when(pair >= 2)
        def _():
            exchange.free(pair - 2)

        dq_ref[...] = pair_back(
            q_ref[...], do_ref[...], o_ref[...], l_ref[...], mq_ref[...],
            keys_at, values_at, mk_ref, block, exchange.put(pair, keys_at.shape[0], block),
        )

    @pl.when(step < pairs)
    def _():
        kv_of = [(step // 2 == g, kv_large[g]) for g in range(groups)]
        attention(large, step, large_refs, kv_of, keys_l, values_l, blocks[0], dq_l)
        move(large, step, dkv_l)

    @pl.when(step >= pairs)
    def _():
        pair = step - pairs
        attention(small, pair, small_refs, [(None, kv_small)], keys_s, values_s, blocks[1], dq_s)
        move(small, pair, dkv_s)

    @pl.when(step == pairs)
    def _():
        large.pass_on(pairs - 1, True)
        large.take(pairs - 2, dkv_l)

    @pl.when(step == pairs + 1)
    def _():
        large.take(pairs - 1, dkv_l)
        for pair in (pairs - 2, pairs - 1):
            large.free(pair)
            large.copy_x(pair).wait_send()

    @pl.when(step == 2 * pairs - 1)
    def _():
        small.pass_on(pairs - 1, True)

    for at in range(2 * pairs):
        todo = []
        for stage in range(1, 7):
            for flow in range(flows):
                if stages[flow][stage - 1] == at:
                    todo.append((running[flow], stage))
        if todo:

            @pl.when(step == at)
            def _(todo=todo):
                for flow, stage in todo:
                    flow.act(stage)

    @pl.when(step == 2 * pairs - 1)
    def _():
        small.take(pairs - 2, dkv_s)
        small.take(pairs - 1, dkv_s)
        for pair in (pairs - 2, pairs - 1):
            small.free(pair)
            small.copy_x(pair).wait_send()
        for flow, sum_ref in zip(running, sums):
            sum_ref[...] = flow.out[...]


def selves_back(large, large_kv, small, small_kv, flows, orders, stages):
    count, width = large[0].shape
    few = small[0].shape[0]
    pairs = width // LANES
    total, less = large[5].shape[0], small[5].shape[0]
    shapes = [flow.shape[1:] for flow in flows]
    blocks = (largest_block(total // 2, 512), largest_block(less // 2, 512))
    first = lambda i: jnp.minimum(i, pairs - 1)
    last = lambda i: jnp.maximum(i - pairs, 0)
    in_specs = [pl.BlockSpec((count, LANES), lambda i: (0, first(i)))] * 4
    in_specs += [whole((count, LANES)), whole((total, LANES))]
    for group in range(3):
        spec = pl.BlockSpec(
            (2, count, LANES), lambda i, g=group: (0, 0, jnp.clip(i - 2 * g, 0, 1))
        )
        in_specs += [spec] * 4
    in_specs += [pl.BlockSpec((few, LANES), lambda i: (0, last(i)))] * 4
    in_specs += [whole((few, LANES)), whole((less, LANES))]
    in_specs += [pl.BlockSpec((2, few, LANES), lambda i: (0, 0, last(i)))] * 4
    in_specs += [pl.BlockSpec(memory_space=pl.ANY)] * len(flows)
    shape = jax.ShapeDtypeStruct
    out_shape = [
        shape((count, width), bf16),
        shape((pairs, 2, count, LANES), bf16),
        shape((few, width), bf16),
        shape((pairs, 2, few, LANES), bf16),
    ] + [shape((4,) + block, bf16) for block in shapes]
    out_specs = [
        pl.BlockSpec((count, LANES), lambda i: (0, first(i))),
        whole((pairs, 2, count, LANES)),
        pl.BlockSpec((few, LANES), lambda i: (0, last(i))),
        whole((pairs, 2, few, LANES)),
    ] + [whole((4,) + block) for block in shapes]
    scratch = [pltpu.VMEM((total, LANES), bf16)] * 2 + [pltpu.VMEM((less, LANES), bf16)] * 2
    scratch += exchange_scratch(pairs, count) + exchange_scratch(pairs, few)
    for block in shapes:
        scratch += flow_scratch(*block, True)
    result = pl.pallas_call(
        functools.partial(selves_kernel, pairs, (orders, shapes, stages), blocks),
        grid=(2 * pairs,),
        in_specs=in_specs,
        out_specs=out_specs,
        out_shape=out_shape,
        scratch_shapes=scratch,
        compiler_params=pltpu.CompilerParams(
            vmem_limit_bytes=60 << 20, collective_id=1, has_side_effects=True
        ),
        cost_estimate=pl.CostEstimate(
            flops=20 * width * (count * total + few * less),
            bytes_accessed=64 * count * width,
            transcendentals=count * total * width // HALF,
        ),
        name="selves_back",
    )(*large, *[p for kv in large_kv for p in kv], *small, *small_kv, *flows)
    return result[:4], result[4:]


def view_kernel(pairs, sizes, *refs):
    (dql, dkvl, dqs, dkvs, xl, xs, hl, hs, gain, wq, wk, wv) = refs[:12]
    gl_ref, gs_ref, gain_ref, grads = refs[12:]
    large, small = sizes
    top, bottom = pl.ds(0, large), pl.ds(large, small)
    total = None
    for which, weight in enumerate((wq, wk, wv)):
        if which == 0:
            grads[top, :] = dql[...]
            grads[bottom, :] = dqs[...]
        else:
            for pair in range(pairs):
                lanes = pl.ds(pair * LANES, LANES)
                grads[top, lanes] = dkvl[pair, which - 1]
                grads[bottom, lanes] = dkvs[pair, which - 1]
        part = dot(grads[...], weight[...], NT)
        total = part if total is None else total + part
    extra, gain_l = norm_back(total[:large], xl[...].astype(f32), gain[...])
    gl_ref[...] = (hl[...] + extra).astype(bf16)
    extra, gain_s = norm_back(total[large:], xs[...].astype(f32), gain[...])
    gs_ref[...] = (hs[...] + extra).astype(bf16)
    gain_ref[...] = gain_l + gain_s


def view_grads(selves, large, small, hidden_l, hidden_s, gain, weights):
    count, width = large.shape
    few = small.shape[0]
    shape = jax.ShapeDtypeStruct
    return pl.pallas_call(
        functools.partial(view_kernel, width // LANES, (count, few)),
        out_shape=[
            shape((count, width), bf16),
            shape((few, width), bf16),
            shape((1, width), f32),
        ],
        scratch_shapes=[pltpu.VMEM((count + few, width), bf16)],
        compiler_params=pltpu.CompilerParams(vmem_limit_bytes=48 << 20),
        cost_estimate=pl.CostEstimate(
            flops=6 * (count + few) * width * width,
            bytes_accessed=6 * width * width + 20 * (count + few) * width,
            transcendentals=0,
        ),
        name="view_grads",
    )(*selves, large, small, hidden_l, hidden_s, gain, *weights)


LAST_ORDERS = (BY_YX, BY_X, BY_ZL)
GAIN_ORDER = ("core", "y", "x", "zl", "zh")


def last_kernel(pairs, sizes, *refs):
    dql, dkvl, dqs, dkvs, nl, ns, gains = refs[:7]
    sum_refs, gain_ref = refs[7:10], refs[10]
    normed, grads, refs = refs[11], refs[12], refs[13:]
    here = Here()
    flows = []
    for order in LAST_ORDERS:
        local, refs = refs[0], refs[1:]
        flows.append(Flow(here, order, [local, None] + list(refs[:8])))
        refs = refs[8:]
    state, got, gain_sems = refs
    large, small = sizes
    top, bottom = pl.ds(0, large), pl.ds(large, small)
    here.greet(ALL_PARTNERS)

    def gain_copy(step):
        return pltpu.make_async_remote_copy(
            src_ref=state.at[step],
            dst_ref=got.at[step],
            send_sem=gain_sems.at[0, step],
            recv_sem=gain_sems.at[1, step],
            device_id=here.partner(GAIN_ORDER[step]),
            device_id_type=MESH,
        )

    state[0] = gains[...]
    gain_copy(0).start()
    normed[top, :] = nl[...]
    normed[bottom, :] = ns[...]
    for which, flow in enumerate(flows):
        if which == 0:
            grads[top, :] = dql[...]
            grads[bottom, :] = dqs[...]
        else:
            for pair in range(pairs):
                lanes = pl.ds(pair * LANES, LANES)
                grads[top, lanes] = dkvl[pair, which - 1]
                grads[bottom, lanes] = dkvs[pair, which - 1]
        value = dot(normed[...], grads[...], TN).astype(bf16)
        rows, wide = flow.local.shape[1:]
        for at, (core, y, tm) in enumerate(spots(flow.order)):
            first = tm * 2 * rows + core * rows
            flow.local[at] = value[first : first + rows, y * wide : (y + 1) * wide]
        flow.act(0)
    for stage in range(1, 7):
        for flow in flows:
            flow.act(stage)
        if stage <= 5:
            gain_copy(stage - 1).wait()
            total = state[stage - 1] + got[stage - 1]
            if stage < 5:
                state[stage] = total
                gain_copy(stage).start()
            else:
                gain_ref[...] = total
    for flow, sum_ref in zip(flows, sum_refs):
        sum_ref[...] = flow.out[...]


def last_sums(selves, normed_l, normed_s, gains):
    count, width = normed_l.shape
    few = normed_s.shape[0]
    rows, wide = width // 16, width // 2
    shape = jax.ShapeDtypeStruct
    scratch = [pltpu.VMEM((count + few, width), bf16), pltpu.VMEM((count + few, width), bf16)]
    for _ in LAST_ORDERS:
        scratch += [pltpu.VMEM((32, rows, wide), bf16)] + flow_scratch(rows, wide, False)
    scratch += [
        pltpu.VMEM((5,) + gains.shape, f32),
        pltpu.VMEM((5,) + gains.shape, f32),
        pltpu.SemaphoreType.DMA((2, 5)),
    ]
    result = pl.pallas_call(
        functools.partial(last_kernel, width // LANES, (count, few)),
        out_shape=[shape((4, rows, wide), bf16)] * 3 + [shape(gains.shape, f32)],
        scratch_shapes=scratch,
        compiler_params=pltpu.CompilerParams(
            vmem_limit_bytes=48 << 20, collective_id=2, has_side_effects=True
        ),
        cost_estimate=pl.CostEstimate(
            flops=40 * (count + few) * width * width,
            bytes_accessed=40 * (count + few) * width,
            transcendentals=0,
        ),
        name="last_sums",
    )(*selves, normed_l, normed_s, gains)
    return result[:3], result[3]


def after(value, *needed):
    return lax.optimization_barrier((value, needed))[0]


SELVES_ORDERS = (BY_Y, BY_ZL, BY_Y, BY_ZL)
SELVES_STAGES = (
    (0, 4, 6, 8, 9, 11),
    (0, 4, 6, 8, 9, 11),
    (0, 4, 6, 8, 10, 11),
    (0, 6, 8, 9, 10, 11),
)


def paired_end(views, weights, large, large_kv, small, small_kv, grads, normed, gains, united_view, restore):
    large_view, small_view, large_hidden, small_hidden, first_gain = views
    up_grad, down_grad, output_grad, cross_parts = grads
    width = large_view.shape[1]
    rows = width // 8
    names = ("core", "y", "zh", "zl", "x")
    turn = [names.index(name) for name in SELVES_ORDERS[3]] + [5, 6]
    cross = jnp.stack(cross_parts).reshape(2, 2, 2, 2, 2, rows, width)
    cross = jnp.transpose(cross, turn).reshape(32, rows, width)
    selves, sums = selves_back(
        large, large_kv, small, small_kv, (up_grad, down_grad, output_grad, cross),
        SELVES_ORDERS, SELVES_STAGES,
    )
    large_grad, small_grad, gain = view_grads(
        selves, large_view, small_view, large_hidden, small_hidden, first_gain, weights
    )
    large_grad, small_grad = restore(large_grad), restore(small_grad)
    gains = jnp.concatenate((gain,) + gains + (jnp.zeros((4, width), f32),), axis=0)
    last, gains = last_sums(selves, *normed, gains)

    def square(total):
        total = total.astype(f32).reshape(2, 2, width // 16, width // 2)
        return jnp.transpose(total, (0, 2, 1, 3)).reshape(rows, width)

    up, down, output, cross = (total.astype(f32) for total in sums)
    at = lax.axis_index("tm") * rows
    gains = [lax.dynamic_slice(gains, (i, at), (1, rows))[0] for i in range(4)]
    return (
        united_view,
        large_grad.astype(f32),
        small_grad.astype(f32),
        gains[0],
        square(last[0]),
        square(last[1]),
        square(last[2]),
        square(output),
        gains[1],
        jnp.transpose(up, (1, 0, 2)).reshape(rows, 4 * width),
        down.reshape(4 * rows, width),
        gains[2],
        gains[3],
        cross[1],
        cross[2],
        cross[3],
        cross[0],
    )


def per_device(tm, seq_size, *args):
    (
        large_view,
        small_view,
        clip_ids,
        first_gain,
        query_weight,
        key_weight,
        value_weight,
        output_weight,
        second_gain,
        up_weight,
        down_weight,
        query_gain,
        context_gain,
        cross_query,
        cross_key,
        cross_value,
        cross_output,
        cotangent,
    ) = args
    seqs, count, width = large_view.shape
    side = tm // 4
    gains = [
        g.astype(f32).reshape(1, width)
        for g in (first_gain, second_gain, query_gain, context_gain)
    ]
    first_gain, second_gain, query_gain, context_gain = gains

    tm_at = lax.axis_index("tm")
    seq_at = lax.axis_index("seq")
    z, x = tm_at // side, tm_at % side
    y, core = seq_at // 2, seq_at % 2
    places = [
        (pz, px, py, pc)
        for pz in range(4)
        for px in range(side)
        for py in range(2)
        for pc in range(2)
    ]

    def number(place):
        return (place[0] * side + place[1]) * seq_size + place[2] * 2 + place[3]

    def permute(value, place):
        pairs = [(number(at), number(place(*at))) for at in places]
        return lax.ppermute(value, ("tm", "seq"), pairs)

    def inverse(place):
        table = {place(*at): at for at in places}
        return lambda *at: table[at]

    go = (
        lambda z, x, y, c: (2 * c + z % 2, x, y, z // 2),
        lambda z, x, y, c: (2 * c + 1 - z % 2, x, y, z // 2),
    )
    back_home = tuple(inverse(place) for place in go)
    other_core = lambda value: permute(value, lambda z, x, y, c: (z, x, y, 1 - c))
    other_y = lambda value: permute(value, lambda z, x, y, c: (z, x, 1 - y, c))
    by_x = lambda value, d: permute(value, lambda z, x, y, c: (z, (x + d) % side, y, c))
    odd = z % 2 == 1

    def relocate(value):
        near = jnp.where(odd, value[1], value[0])
        far = jnp.where(odd, value[0], value[1])
        return jnp.concatenate([permute(near, go[0]), permute(far, go[1])], axis=0)

    def restore(value):
        rows = value.shape[0] // 2
        near, far = permute(value[:rows], back_home[0]), permute(value[rows:], back_home[1])
        return jnp.where(odd, jnp.stack([far, near]), jnp.stack([near, far]))

    def join(parts, axis):
        return parts[0] if len(parts) == 1 else jnp.concatenate(parts, axis=axis)

    def gather(value, axis=1):
        across = join([by_x(value, d) for d in range(1, side)], axis)
        return (value, across, other_core(value), other_core(across))

    def add(a, b):
        return (a.astype(f32) + b.astype(f32)).astype(bf16)

    def scatter_core(keep, send):
        return add(keep, other_core(send))

    def scatter_x(sums):
        rows = sums.shape[1] // side
        total = sums[:, :rows].astype(f32)
        for d in range(1, side):
            total = total + by_x(sums[:, d * rows : (d + 1) * rows], -d).astype(f32)
        return total.astype(bf16)

    groups = 3
    part = width // groups
    short_clips = gather(relocate(clip_ids[:, ::2].astype(f32)), 0)
    small = relocate(small_view)
    large = relocate(large_view)
    grad_out = relocate(after(cotangent, large))
    spot = lax.broadcasted_iota(jnp.int32, (1, LANES), 1) % HALF

    def mask_of_keys(numbers):
        away = numbers.astype(jnp.int32)[:, None] != spot
        return jnp.where((spot < 4) & away, NEGATIVE, 0.0).astype(bf16)

    def mask_of_queries(numbers):
        same = numbers.astype(jnp.int32)[:, None] == spot
        return jnp.where((spot < 4) & same, 1.0, 0.0).astype(bf16)

    short = jnp.concatenate(short_clips)
    small_mask_k = mask_of_keys(short)
    large_mask_k = mask_of_keys(jnp.repeat(short, 2))
    small_mask_q = mask_of_queries(short_clips[0])
    large_mask_q = mask_of_queries(jnp.repeat(short_clips[0], 2))

    small_normed, small_q, small_kv = front(
        small, first_gain, query_weight, key_weight, value_weight, 1
    )
    small_kv = gather(small_kv[0])
    large_normed, large_q, large_kv = front(
        large, first_gain, query_weight, key_weight, value_weight, groups
    )
    large_kv = [gather(kv) for kv in large_kv]
    small_mixed, small_logsum = attend(small_q, small_kv, small_mask_q, small_mask_k, 0, width)
    small_merged, *small_saved, context, cross_kv = rest(
        small, [small_mixed], output_weight, second_gain, up_weight, down_weight,
        context_gain, (cross_key, cross_value),
    )
    cross_kv = gather(cross_kv)
    united_grad = dot(grad_out, cross_output, NT).astype(bf16)
    large_out = ()
    for group, kv in enumerate(large_kv):
        large_out = attend(large_q, kv, large_mask_q, large_mask_k, group * part, part, large_out)
    large_mixed, large_logsum = large_out
    large_merged, *large_saved, asked, cross_q = rest(
        large, [large_mixed], output_weight, second_gain, up_weight, down_weight,
        query_gain, (cross_query,),
    )
    united, cross_logsum = attend(cross_q, cross_kv, large_mask_q, small_mask_k, 0, width)
    united_view = restore((large_merged + dot(united, cross_output)).astype(bf16))

    bits = side.bit_length() - 1
    moves = {"zh": lambda z, x, y, c: (z ^ 2, x, y, c), "zl": lambda z, x, y, c: (z ^ 1, x, y, c)}
    mine = {"zh": z // 2, "zl": z % 2}
    axes = {"zh": 0, "zl": 1}
    for bit in range(bits):
        flip = 1 << (bits - 1 - bit)
        moves[f"x{bit}"] = lambda z, x, y, c, flip=flip: (z, x ^ flip, y, c)
        mine[f"x{bit}"] = (x // flip) % 2
        axes[f"x{bit}"] = 2 + bit
    moves["core"] = lambda z, x, y, c: (z, x, y, 1 - c)
    moves["y"] = lambda z, x, y, c: (z, x, 1 - y, c)
    mine["core"], mine["y"] = core, y
    axes["core"], axes["y"] = 2 + bits, 3 + bits
    by_y = ["core", "y", "zl"] + [f"x{bit}" for bit in range(bits)] + ["zh"]
    by_zl = ["core", "zl", "y"] + [f"x{bit}" for bit in range(bits)] + ["zh"]
    by_yx = ["core", "y"] + [f"x{bit}" for bit in range(bits)] + ["zl", "zh"]

    class Sum:
        def __init__(self, local, order):
            rows, wide = local.shape
            self.value = local.reshape((2,) * (2 + bits) + (rows // tm, wide))
            self.todo = list(order)
            self.rows, self.wide = rows // tm, wide

        def step(self, *needed):
            name = self.todo.pop(0)
            axis = axes[name]
            size = self.value.shape[axis] // 2
            at = mine[name]
            keep = lax.dynamic_slice_in_dim(self.value, at * size, size, axis)
            send = lax.dynamic_slice_in_dim(self.value, (1 - at) * size, size, axis)
            self.value = add(keep, permute(send, moves[name]))
            return self.value

        def finish(self):
            while self.todo:
                self.step()
            value = self.value.reshape(self.rows // 2, self.wide // 2)
            other = other_y(value)
            value = jnp.where(
                y == 0,
                jnp.concatenate([value, other], axis=1),
                jnp.concatenate([other, value], axis=1),
            )
            other = other_core(value)
            return jnp.where(
                core == 0,
                jnp.concatenate([value, other], axis=0),
                jnp.concatenate([other, value], axis=0),
            ).astype(f32)

    cross_groups = 2
    cross_part = width // cross_groups
    dcq, dckv = [], []
    for group in range(cross_groups):
        query = after(cross_q, *dcq[-1:])
        at = group * cross_part
        dq, keep, send = attend_back(
            query, cross_kv, united_grad, united, cross_logsum,
            large_mask_q, small_mask_k, at, at, at, cross_part,
        )
        dcq.append(dq)
        dckv.append(scatter_x(scatter_core(keep, send)))
    dcq = jnp.concatenate(dcq, axis=1)
    dck = jnp.concatenate([kv[0] for kv in dckv], axis=1)
    dcv = jnp.concatenate([kv[1] for kv in dckv], axis=1)
    extra, query_gain_grad = norm_back(dot(dcq, cross_query, NT), large_merged, query_gain)
    large_merged_grad = grad_out.astype(f32) + extra
    small_merged_grad, context_gain_grad = norm_back(
        dot(dck, cross_key, NT) + dot(dcv, cross_value, NT), small_merged, context_gain
    )
    cross_parts = [
        dot(united, grad_out, TN).astype(bf16),
        dot(asked, dcq, TN).astype(bf16),
        dot(context, dck, TN).astype(bf16),
        dot(context, dcv, TN).astype(bf16),
    ]
    (
        large_hidden_grad,
        small_hidden_grad,
        large_mixed_grad,
        small_mixed_grad,
        up_grad,
        down_grad,
        output_grad,
        second_gain_grad,
    ) = back(
        large_merged_grad, small_merged_grad, large_saved, small_saved, [large_mixed], small_mixed,
        output_weight, second_gain, up_weight, down_weight, side == 2,
    )
    if side == 2:
        return paired_end(
            (large, small, large_hidden_grad, small_hidden_grad, first_gain),
            (query_weight, key_weight, value_weight),
            (large_q, large_mixed_grad, large_mixed, large_logsum, large_mask_q, large_mask_k),
            large_kv,
            (small_q, small_mixed_grad, small_mixed, small_logsum, small_mask_q, small_mask_k),
            small_kv,
            (up_grad, down_grad, output_grad, cross_parts),
            (large_normed, small_normed),
            (second_gain_grad, query_gain_grad, context_gain_grad),
            united_view,
            restore,
        )
    cross_sum = Sum(jnp.concatenate(cross_parts, axis=1), by_y)
    up_sum = Sum(up_grad, by_y)
    down_sum = Sum(down_grad, by_zl)
    cross_sum.step()
    small_dq, keep, send = attend_back(
        after(small_q, cross_sum.value), small_kv, small_mixed_grad, small_mixed, small_logsum,
        small_mask_q, small_mask_k, 0, 0, 0, width,
    )
    small_sums = scatter_core(keep, send)
    up_sum.step()
    down_sum.step()
    cross_sum.step()
    needed = [small_dq, up_sum.value, down_sum.value]
    normed = jnp.concatenate([large_normed, small_normed], axis=0)
    last_sums, dqs, dkvs = [], [], []
    pending = None
    for group in range(groups):
        at = group * part
        dq, keep, send = attend_back(
            after(large_q, *needed), large_kv[group], large_mixed_grad, large_mixed, large_logsum,
            large_mask_q, large_mask_k, at, at, 0, part,
        )
        sums = scatter_core(keep, send)
        dqs.append(dq)
        needed = [dq]
        if group == 0:
            small_dkv = scatter_x(small_sums)
            needed += [cross_sum.value, small_sums]
        if group == 1:
            needed += [small_dkv, up_sum.step(), down_sum.step(), cross_sum.step()]
        if pending is not None:
            needed.append(pending.step())
        dkv = scatter_x(sums)
        dkvs.append(dkv)
        local = jnp.concatenate(
            [
                jnp.concatenate([dq, dkv[0], dkv[1]], axis=1),
                jnp.concatenate(
                    [
                        small_dq[:, at : at + part],
                        small_dkv[0, :, at : at + part],
                        small_dkv[1, :, at : at + part],
                    ],
                    axis=1,
                ),
            ],
            axis=0,
        )
        local = dot(normed, local, TN).astype(bf16)
        pending = Sum(local, by_yx)
        last_sums.append(pending)

    def front_back(view, hidden_grad, dq, dk, dv):
        grad = (
            dot(dq, query_weight, NT) + dot(dk, key_weight, NT) + dot(dv, value_weight, NT)
        )
        extra, gain_part = norm_back(grad, view.astype(f32), first_gain)
        return (hidden_grad + extra).astype(bf16), gain_part

    small_grad, small_gain = front_back(
        small, small_hidden_grad, small_dq, small_dkv[0], small_dkv[1]
    )
    large_grad, large_gain = front_back(
        large,
        large_hidden_grad,
        jnp.concatenate(dqs, axis=1),
        jnp.concatenate([kv[0] for kv in dkvs], axis=1),
        jnp.concatenate([kv[1] for kv in dkvs], axis=1),
    )
    small_grad = restore(small_grad).astype(f32)
    large_grad = restore(large_grad).astype(f32)
    output_sum = Sum(output_grad, by_yx)
    gain_rows = jnp.concatenate(
        [large_gain + small_gain, second_gain_grad, query_gain_grad, context_gain_grad], axis=0
    )
    wide = width // tm
    gain_rows = jnp.transpose(gain_rows.reshape(4, tm, wide), (1, 0, 2)).astype(bf16)
    gain_rows = jnp.pad(gain_rows, ((0, 0), (0, 28), (0, 2 * LANES - wide)))
    gain_sum = Sum(gain_rows.reshape(tm * 32, 2 * LANES), by_yx)

    cross_total = cross_sum.finish()
    up_total = up_sum.finish()
    down_total = down_sum.finish()
    output_total = output_sum.finish()
    last_totals = [total.finish() for total in last_sums]
    gain_total = gain_sum.finish()
    cross_grads = [cross_total[:, i * width : (i + 1) * width] for i in range(4)]
    last_grads = [
        jnp.concatenate([total[:, i * part : (i + 1) * part] for total in last_totals], axis=1)
        for i in range(3)
    ]
    gain_grads = [gain_total[i, :wide] for i in range(4)]
    return (
        united_view,
        large_grad,
        small_grad,
        gain_grads[0],
        last_grads[0],
        last_grads[1],
        last_grads[2],
        output_total,
        gain_grads[1],
        up_total,
        down_total,
        gain_grads[2],
        gain_grads[3],
        cross_grads[1],
        cross_grads[2],
        cross_grads[3],
        cross_grads[0],
    )


def solution(mesh):
    token = P("seq", "tm", None)
    in_specs = (token, token, P("seq", "tm")) + (P(),) * 14 + (token,)
    vector, matrix = P("tm"), P("tm", None)
    out_specs = (
        (token, token, token, vector)
        + (matrix,) * 4
        + (vector, matrix, matrix, vector, vector)
        + (matrix,) * 4
    )
    return jax.shard_map(
        functools.partial(per_device, mesh.shape["tm"], mesh.shape["seq"]),
        mesh=mesh,
        in_specs=in_specs,
        out_specs=out_specs,
        check_vma=False,
    )
```

time: 711 us -> 485 us (0.68)
  Pallas kernels: 123 us -> 301 us
  waiting for transfers between devices: 231 us -> 70 us
  matrix products: 103 us -> 7.45 us
  starting transfers between devices: 101 us -> 46 us
  blocking collectives: 47.6 us -> 0 us
  other arithmetic: 42.1 us -> 20.9 us
  local copies, waits for them, and re-layouts: 50.2 us -> 29.9 us
    pallas_call x6 -> x15, Pallas kernels: 123 us -> 301 us  [the longest x1 137 us: selves_back(): pl.pallas_call(functools.partial(selves_kernel, pairs, (orders, shapes, s...]
    ppermute x72 -> x36, waiting for transfers between devices: 231 us -> 70 us  [permute(): return lax.ppermute(value, ('tm', 'seq'), pairs)]
    dot_general x48 -> x9, matrix products: 103 us -> 7.45 us  [dot(): return lax.dot_general(a, b, dims, preferred_element_type=f32)]
    ppermute x72 -> x36, starting transfers between devices: 101 us -> 46 us  [permute(): return lax.ppermute(value, ('tm', 'seq'), pairs)]
    all_gather x1 -> x0, blocking collectives: 47.6 us -> none  [per_device(): all_clips = lax.all_gather(clip_ids, ('tm', 'seq'), axis=0, tiled=False)]
    unnamed x366 -> x162, local copies, waits for them, and re-layouts: 31.6 us -> 19.9 us
    convert_element_type x6 -> x2, other arithmetic: 11.3 us -> 0.41 us  [add(): return (a.astype(f32) + b.astype(f32)).astype(bf16)]
    convert_element_type x29 -> x14, other arithmetic: 15 us -> 5.81 us  [the longest x2 1.53 us: mask_of_queries(): return jnp.where((spot < 4) & same, 1.0, 0.0).astype(bf16)]
  transfers between devices with their start and end apart: 72 -> 36, of which waited for: 19 -> 13; matrix products, arithmetic and copies ran while one was open for 20% -> 6% of each run, Pallas kernels for 12% -> 11%
where the time goes in v2:
time: 485 us; the launch traced here: 477 us
  Pallas kernels  301 us (62%)
  waiting for transfers between devices  70 us (14%)
  starting transfers between devices  46 us (9%)
  local copies, waits for them, and re-layouts  29.9 us (6%)
  other arithmetic  20.9 us (4%)
  matrix products  7.45 us (2%)
    pallas_call x1, Pallas kernels, selves_back(): pl.pallas_call(functools.partial(selves_kernel, pairs, (orders, shapes, s...  137 us
    ppermute x36, waiting for transfers between devices, permute(): return lax.ppermute(value, ('tm', 'seq'), pairs)  70 us
    ppermute x36, starting transfers between devices, permute(): return lax.ppermute(value, ('tm', 'seq'), pairs)  46 us
    pallas_call x5, Pallas kernels, attend(): pl.pallas_call(functools.partial(attend_kernel, len(kv), largest_block(co...  43.9 us
    pallas_call x1, Pallas kernels, last_sums(): pl.pallas_call(functools.partial(last_kernel, width // LANES, (count, few...  31.2 us
    pallas_call x1, Pallas kernels, back(): pl.pallas_call(functools.partial(back_kernel, steps, len(mixed_l), (large...  28.7 us
    pallas_call x2, Pallas kernels, rest(): pl.pallas_call(functools.partial(rest_kernel, steps, len(mixed), is_query...  26.4 us
    pallas_call x2, Pallas kernels, attend_back(): pl.pallas_call(functools.partial(attend_back_kernel, len(kv), largest_blo...  22.9 us
  transfers between devices with their start and end apart: 36, of which 13 were waited for; matrix products, arithmetic and copies ran while one was open for 6% of the time, Pallas kernels for 11%

profile of v2, /device:TPU:1, one launch (start us, length us, event | category | flops | bytes accessed | tf_op | source)
XLA Modules:
  0.0 477.5 jit_solution(18122845301993043715)
XLA Ops:
  1.7 4.8 %collective-permute-start.3 = (f32[128]{0:T(128)S(1)}, f32[128]{0:T(128)S(1)}, u32[]{:S(2)}, u32[]{:S(2)}) collective-permute-start(f32[128]{0:T(128)S(1)} %get-tuple-element.173), channel_id=1, source_target_pairs={{0,8},{1,24},{2,10},{3,26},{4,12},{5,28},{6,14},{7,30},{8,0},{9,16... | collective-permute-start | bytes 1544 | tf_op jit(solution)/shard_map/ppermute | solution.py:1178
  28.9 10.8 %collective-permute-done = bf16[256,768]{1,0:T(8,128)(2,1)} collective-permute-done((bf16[256,768]{1,0:T(8,128)(2,1)}, bf16[256,768]{1,0:T(8,128)(2,1)}, u32[]{:S(2)}, u32[]{:S(2)}) %collective-permute-start) | collective-permute-done | bytes 393248 | tf_op jit(solution)/shard_map/ppermute | solution.py:1178
  56.5 4.0 collective-permute-done.26
  62.4 6.6 %collective-permute-done.7.refs_4_.refs_15_ = bf16[2,512,256]{2,1,0:T(8,128)(2,1)S(1)} collective-permute-done((bf16[2,512,256]{2,1,0:T(8,128)(2,1)S(1)}, bf16[2,512,256]{2,1,0:T(8,128)(2,1)S(1)}, u32[]{:S(2)}, u32[]{:S(2)}) %collective-permute-start.7) | collective-permute-done | bytes 524320 | tf_op jit(solution)/shard_map/ppermute | solution.py:1178
  69.0 11.2 %collective-permute-done.10.refs_4_.refs_11_ = bf16[2,512,256]{2,1,0:T(8,128)(2,1)S(1)} collective-permute-done((bf16[2,512,256]{2,1,0:T(8,128)(2,1)S(1)}, bf16[2,512,256]{2,1,0:T(8,128)(2,1)S(1)}, u32[]{:S(2)}, u32[]{:S(2)}) %collective-permute-start.10) | collective-permute-done | bytes 524320 | tf_op jit(solution)/shard_map/ppermute | solution.py:1178
  82.6 7.1 %attend.5 = (bf16[512,768]{1,0:T(8,128)(2,1)S(1)}, f32[512,768]{1,0:T(8,128)S(1)}) custom-call(bf16[512,768]{1,0:T(8,128)(2,1)S(1)} %get-tuple-element.80.refs_0_, bf16[512,128]{1,0:T(8,128)(2,1)S(1)} %copy-done.20, bf16[2048,128]{1,0:T(8,128)(2,1)S(1)} %select_convert_fusion.refs_2_.refs_5_, bf16[2,512,256]{2,1,0:T(8,128)(2,1)S(1)} %get-tuple-element.83.refs_3_.refs_6_, ...), custom_call_target="tpu_custom_call" | custom-call | flops 4294967296 | bytes 3145728 | tf_op jit(solution)/shard_map/attend/pallas_call | solution.py:89
  90.4 6.9 %attend.6 = (bf16[512,768]{1,0:T(8,128)(2,1)S(1)}, f32[512,768]{1,0:T(8,128)S(1)}) custom-call(bf16[512,768]{1,0:T(8,128)(2,1)S(1)} %get-tuple-element.80.refs_0_, bf16[512,128]{1,0:T(8,128)(2,1)S(1)} %copy-done.20, bf16[2048,128]{1,0:T(8,128)(2,1)S(1)} %select_convert_fusion.refs_2_.refs_5_, ...), custom_call_target="tpu_custom_call", output_to_operand_aliasing={{0}: (7, {}), {1}: (8, {})} | custom-call | flops 4294967296 | bytes 3145728 | tf_op jit(solution)/shard_map/attend/pallas_call | solution.py:89
  97.4 7.0 %attend.7 = (bf16[512,768]{1,0:T(8,128)(2,1)S(1)}, f32[512,768]{1,0:T(8,128)S(1)}) custom-call(bf16[512,768]{1,0:T(8,128)(2,1)S(1)} %get-tuple-element.80.refs_0_, bf16[512,128]{1,0:T(8,128)(2,1)S(1)} %copy-done.20, bf16[2048,128]{1,0:T(8,128)(2,1)S(1)} %select_convert_fusion.refs_2_.refs_5_, ...), custom_call_target="tpu_custom_call", output_to_operand_aliasing={{0}: (7, {}), {1}: (8, {})} | custom-call | flops 4294967296 | bytes 3145728 | tf_op jit(solution)/shard_map/attend/pallas_call | solution.py:89
  105.7 8.2 %attend.8 = (bf16[256,768]{1,0:T(8,128)(2,1)S(1)}, f32[256,768]{1,0:T(8,128)S(1)}) custom-call(bf16[256,768]{1,0:T(8,128)(2,1)S(1)} %get-tuple-element.91.refs_0_.refs_18_, bf16[256,128]{1,0:T(8,128)(2,1)S(1)} %copy-done.21, bf16[1024,128]{1,0:T(8,128)(2,1)S(1)} %select_convert_fusion.1.refs_2_.refs_5_.refs_23_, ...), custom_call_target="tpu_custom_call" | custom-call | flops 3221225472 | bytes 4718592 | tf_op jit(solution)/shard_map/attend/pallas_call | solution.py:89
  114.0 11.3 %rest.3 = (f32[256,768]{1,0:T(8,128)S(1)}, f32[256,768]{1,0:T(8,128)S(1)}, bf16[256,768]{1,0:T(8,128)(2,1)S(1)}, bf16[256,3072]{1,0:T(8,128)(2,1)}, bf16[256,307...) custom-call(bf16[256,768]{1,0:T(8,128)(2,1)S(1)} %constant_dynamic-update-slice_fusion.4.x_ref.refs_0_.refs, ...), custom_call_target="tpu_custom_call" | custom-call | flops 3019898880 | bytes 19267584 | tf_op jit(solution)/shard_map/rest/pallas_call | solution.py:322
  127.0 15.1 %rest.2 = (f32[512,768]{1,0:T(8,128)}, f32[512,768]{1,0:T(8,128)}, bf16[512,768]{1,0:T(8,128)(2,1)S(1)}, bf16[512,3072]{1,0:T(8,128)(2,1)}, bf16[512,3072]{1,0:T...) custom-call(bf16[512,768]{1,0:T(8,128)(2,1)S(1)} %constant_dynamic-update-slice_fusion.x_ref.refs_0_.refs_4_, ...), custom_call_target="tpu_custom_call" | custom-call | flops 6039797760 | bytes 25559040 | tf_op jit(solution)/shard_map/rest/pallas_call | solution.py:322
  153.3 14.7 %attend.9 = (bf16[512,768]{1,0:T(8,128)(2,1)S(1)}, f32[512,768]{1,0:T(8,128)S(1)}) custom-call(bf16[512,768]{1,0:T(8,128)(2,1)S(1)} %copy-done.52, bf16[512,128]{1,0:T(8,128)(2,1)S(1)} %copy-done.20, bf16[1024,128]{1,0:T(8,128)(2,1)S(1)} %copy-done.19, bf16[2,256,768]{2,1,0:T(8,128)(2,1)} %get-tuple-element.94.refs_3_.refs_6_, ...), custom_call_target="tpu_custom_call" | custom-call | flops 6442450944 | bytes 6291456 | tf_op jit(solution)/shard_map/attend/pallas_call | solution.py:89
  169.1 11.2 %attend_back.2 = (bf16[512,384]{1,0:T(8,128)(2,1)S(1)}, bf16[2,512,384]{2,1,0:T(8,128)(2,1)S(1)}, bf16[2,512,384]{2,1,0:T(8,128)(2,1)S(1)}) custom-call(bf16[512,768]{1,0:T(8,128)(2,1)S(1)} %copy-done.52, bf16[512,768]{1,0:T(8,128)(2,1)S(1)} %copy-done.46, bf16[512,768]{1,0:T(8,128)(2,1)S(1)} %get-tuple-element.95.refs_2_, ...), custom_call_target="tpu_custom_call" | custom-call | flops 4026531840 | bytes 5505024 | tf_op jit(solution)/shard_map/attend_back/pallas_call | solution.py:177
  186.1 11.7 %attend_back.3 = (bf16[512,384]{1,0:T(8,128)(2,1)S(1)}, bf16[2,512,384]{2,1,0:T(8,128)(2,1)S(1)}, bf16[2,512,384]{2,1,0:T(8,128)(2,1)S(1)}) custom-call(bf16[512,768]{1,0:T(8,128)(2,1)S(1)} %copy-done.52, bf16[512,768]{1,0:T(8,128)(2,1)S(1)} %copy-done.46, bf16[512,768]{1,0:T(8,128)(2,1)S(1)} %get-tuple-element.95.refs_2_, ...), custom_call_target="tpu_custom_call" | custom-call | flops 4026531840 | bytes 5505024 | tf_op jit(solution)/shard_map/attend_back/pallas_call | solution.py:177
  206.4 7.9 %collective-permute-done.31 = bf16[2,256,384]{2,1,0:T(8,128)(2,1)S(1)} collective-permute-done((bf16[2,256,384]{2,1,0:T(8,128)(2,1)S(1)}, bf16[2,256,384]{2,1,0:T(8,128)(2,1)S(1)}, u32[]{:S(2)}, u32[]{:S(2)}) %collective-permute-start.31) | collective-permute-done | bytes 393248 | tf_op jit(solution)/shard_map/ppermute | solution.py:1178
  214.4 8.3 %collective-permute-done.29 = bf16[2,256,384]{2,1,0:T(8,128)(2,1)S(1)} collective-permute-done((bf16[2,256,384]{2,1,0:T(8,128)(2,1)S(1)}, bf16[2,256,384]{2,1,0:T(8,128)(2,1)S(1)}, u32[]{:S(2)}, u32[]{:S(2)}) %collective-permute-start.29) | collective-permute-done | bytes 393248 | tf_op jit(solution)/shard_map/ppermute | solution.py:1178
  229.8 28.7 %back.1 = (f32[512,768]{1,0:T(8,128)}, f32[256,768]{1,0:T(8,128)}, bf16[512,768]{1,0:T(8,128)(2,1)}, bf16[256,768]{1,0:T(8,128)(2,1)}, bf16[32,96,768]{2,1,0:T(8...) custom-call(f32[512,768]{1,0:T(8,128)} %multiply_add_fusion.refs_0_, ...), custom_call_target="tpu_custom_call" | custom-call | flops 16307453952 | bytes 44826624 | tf_op jit(solution)/shard_map/back/pallas_call | solution.py:443
  258.5 136.9 %selves_back.1 = (bf16[512,768]{1,0:T(8,128)(2,1)}, bf16[6,2,512,128]{3,2,1,0:T(8,128)(2,1)}, bf16[256,768]{1,0:T(8,128)(2,1)}, bf16[6,2,256,128]{3,2,1,0:T(8,12...) custom-call(bf16[512,768]{1,0:T(8,128)(2,1)} %copy-done.49, ...), custom_call_target="tpu_custom_call" | custom-call | flops 20132659200 | bytes 25165824 | tf_op jit(solution)/shard_map/selves_back/pallas_call | solution.py:912
  398.7 7.2 %view_grads.1 = (bf16[512,768]{1,0:T(8,128)(2,1)S(1)}, bf16[256,768]{1,0:T(8,128)(2,1)S(1)}, f32[1,768]{1,0:T(1,128)S(1)}) custom-call(bf16[512,768]{1,0:T(8,128)(2,1)S(1)} %copy-done.9, bf16[6,2,512,128]{3,2,1,0:T(8,128)(2,1)} %get-tuple-element.124.refs_1_, bf16[256,768]{1,0:T(8,128)(2,1)S(1)} %copy-done.16, bf16[6,2,256,128]{3,2,1,0:T(8,128)(2,1)S(1)} %copy-done.11, ...), custom_call_target="tpu_custom_call" | custom-call | flops 2717908992 | bytes 15335424 | tf_op jit(solution)/shard_map/view_grads/pallas_call | solution.py:960
  410.9 31.2 %last_sums.1 = (bf16[4,48,384]{2,1,0:T(8,128)(2,1)S(1)}, bf16[4,48,384]{2,1,0:T(8,128)(2,1)S(1)}, bf16[4,48,384]{2,1,0:T(8,128)(2,1)S(1)}, f32[8,768]{1,0:T(8,128)S(1)}) custom-call(bf16[512,768]{1,0:T(8,128)(2,1)S(1)} %copy-done.10, bf16[6,2,512,128]{3,2,1,0:T(8,128)(2,1)S(1)} %copy-done.7, bf16[256,768]{1,0:T(8,128)(2,1)S(1)} %copy-done.17, ...), custom_call_target="tpu_custom_call" | custom-call | flops 18119393280 | bytes 23592960 | tf_op jit(solution)/shard_map/last_sums/pallas_call | solution.py:1054
  445.8 3.2 collective-permute-start.34
  451.4 4.1 collective-permute-start.33
  460.7 3.9 collective-permute-done.32
  464.6 11.3 %collective-permute-done.33 = bf16[256,768]{1,0:T(8,128)(2,1)S(1)} collective-permute-done((bf16[256,768]{1,0:T(8,128)(2,1)S(1)}, bf16[256,768]{1,0:T(8,128)(2,1)S(1)}, u32[]{:S(2)}, u32[]{:S(2)}) %collective-permute-start.33) | collective-permute-done | bytes 393248 | tf_op jit(solution)/shard_map/ppermute | solution.py:1178
  (311 shorter events, 102.0 us)
Async XLA Ops:
  1.7 20.9 %collective-permute-start.3 = (f32[128]{0:T(128)S(1)}, f32[128]{0:T(128)S(1)}, u32[]{:S(2)}, u32[]{:S(2)}) collective-permute-start(f32[128]{0:T(128)S(1)} %get-tuple-element.173), channel_id=1, source_target_pairs={{0,8},{1,24},{2,10},{3,26},{4,12},{5,28},{6,14},{7,30},{8,0},{9,16... | collective-permute-start | bytes 1544 | tf_op jit(solution)/shard_map/ppermute | solution.py:1178
  6.5 14.1 %collective-permute-start.2 = (f32[128]{0:T(128)S(1)}, f32[128]{0:T(128)S(1)}, u32[]{:S(2)}, u32[]{:S(2)}) collective-permute-start(f32[128]{0:T(128)S(1)} %get-tuple-element.174), channel_id=1, source_target_pairs={{0,0},{1,16},{2,2},{3,18},{4,4},{5,20},{6,6},{7,22},{8,8},{9,24},{... | collective-permute-start | bytes 1544 | tf_op jit(solution)/shard_map/ppermute | solution.py:1178
  10.2 41.6 %collective-permute-start.17 = (bf16[128,768]{1,0:T(8,128)(2,1)}, bf16[128,768]{1,0:T(8,128)(2,1)}, u32[]{:S(2)}, u32[]{:S(2)}) collective-permute-start(bf16[128,768]{1,0:T(8,128)(2,1)} %get-tuple-element.167), channel_id=1, source_target_pairs={{0,8},{1,24},{2,10},{3,26},{4,12},{5,28},{6,14},{7,30},{8,0},{9,16... | collective-permute-start | bytes 589832 | tf_op jit(solution)/shard_map/ppermute | solution.py:1178
  11.8 40.3 %collective-permute-start.16 = (bf16[128,768]{1,0:T(8,128)(2,1)S(1)}, bf16[128,768]{1,0:T(8,128)(2,1)}, u32[]{:S(2)}, u32[]{:S(2)}) collective-permute-start(bf16[128,768]{1,0:T(8,128)(2,1)S(1)} %get-tuple-element.168), channel_id=1, source_target_pairs={{0,0},{1,16},{2,2},{3,18},{4,4},{5,20},{6,6},{7,22},{8,8},{9,24},{... | collective-permute-start | bytes 589832 | tf_op jit(solution)/shard_map/ppermute | solution.py:1178
  16.8 23.9 %collective-permute-start.1 = (bf16[256,768]{1,0:T(8,128)(2,1)}, bf16[256,768]{1,0:T(8,128)(2,1)S(1)}, u32[]{:S(2)}, u32[]{:S(2)}) collective-permute-start(bf16[256,768]{1,0:T(8,128)(2,1)} %get-tuple-element.159), channel_id=1, source_target_pairs={{0,8},{1,24},{2,10},{3,26},{4,12},{5,28},{6,14},{7,30},{8,0},{9,16... | collective-permute-start | bytes 1179656 | tf_op jit(solution)/shard_map/ppermute | solution.py:1178
  20.7 19.0 %collective-permute-start = (bf16[256,768]{1,0:T(8,128)(2,1)}, bf16[256,768]{1,0:T(8,128)(2,1)}, u32[]{:S(2)}, u32[]{:S(2)}) collective-permute-start(bf16[256,768]{1,0:T(8,128)(2,1)} %get-tuple-element.160), channel_id=1, source_target_pairs={{0,0},{1,16},{2,2},{3,18},{4,4},{5,20},{6,6},{7,22},{8,8},{9,24},{... | collective-permute-start | bytes 1179656 | tf_op jit(solution)/shard_map/ppermute | solution.py:1178
  42.2 18.3 %collective-permute-start.26 = (bf16[256,768]{1,0:T(8,128)(2,1)S(1)}, bf16[256,768]{1,0:T(8,128)(2,1)S(1)}, u32[]{:S(2)}, u32[]{:S(2)}) collective-permute-start(bf16[256,768]{1,0:T(8,128)(2,1)S(1)} %get-tuple-element.156), channel_id=1, source_target_pairs={{0,0},{1,16},{2,2},{3,18},{4,4},{5,20},{6,6},{7,22},{8,8},{9,24},{... | collective-permute-start | bytes 1179656 | tf_op jit(solution)/shard_map/ppermute | solution.py:1178
  47.4 14.1 %collective-permute-start.13 = (bf16[2,512,256]{2,1,0:T(8,128)(2,1)S(1)}, bf16[2,512,256]{2,1,0:T(8,128)(2,1)S(1)}, u32[]{:S(2)}, u32[]{:S(2)}) collective-permute-start(bf16[2,512,256]{2,1,0:T(8,128)(2,1)S(1)} %get-tuple-element.83.refs_3_.refs_6_), channel_id=1, source_target_pairs={{0,4},{1,5},{2,6},{3,7},{4,0},{5,1},{6,2},{7,3},{8,12},{9,13},{10,... | collective-permute-start | bytes 1572872 | tf_op jit(solution)/shard_map/ppermute | solution.py:1178
  51.8 17.2 %collective-permute-start.7 = (bf16[2,512,256]{2,1,0:T(8,128)(2,1)S(1)}, bf16[2,512,256]{2,1,0:T(8,128)(2,1)S(1)}, u32[]{:S(2)}, u32[]{:S(2)}) collective-permute-start(bf16[2,512,256]{2,1,0:T(8,128)(2,1)S(1)} %get-tuple-element.81.refs_3_.refs_14_), channel_id=1, source_target_pairs={{0,4},{1,5},{2,6},{3,7},{4,0},{5,1},{6,2},{7,3},{8,12},{9,13},{10,... | collective-permute-start | bytes 1572872 | tf_op jit(solution)/shard_map/ppermute | solution.py:1178
  52.1 28.1 %collective-permute-start.10 = (bf16[2,512,256]{2,1,0:T(8,128)(2,1)S(1)}, bf16[2,512,256]{2,1,0:T(8,128)(2,1)S(1)}, u32[]{:S(2)}, u32[]{:S(2)}) collective-permute-start(bf16[2,512,256]{2,1,0:T(8,128)(2,1)S(1)} %get-tuple-element.82.refs_3_.refs_10_), channel_id=1, source_target_pairs={{0,4},{1,5},{2,6},{3,7},{4,0},{5,1},{6,2},{7,3},{8,12},{9,13},{10,... | collective-permute-start | bytes 1572872 | tf_op jit(solution)/shard_map/ppermute | solution.py:1178
  60.5 21.4 %collective-permute-start.14 = (bf16[2,512,256]{2,1,0:T(8,128)(2,1)S(1)}, bf16[2,512,256]{2,1,0:T(8,128)(2,1)S(1)}, u32[]{:S(2)}, u32[]{:S(2)}) collective-permute-start(bf16[2,512,256]{2,1,0:T(8,128)(2,1)S(1)} %get-tuple-element.83.refs_3_.refs_6_), channel_id=1, source_target_pairs={{0,1},{1,0},{2,3},{3,2},{4,5},{5,4},{6,7},{7,6},{8,9},{9,8},{10,11... | collective-permute-start | bytes 1572872 | tf_op jit(solution)/shard_map/ppermute | solution.py:1178
  61.5 21.0 %collective-permute-start.15 = (bf16[2,512,256]{2,1,0:T(8,128)(2,1)S(1)}, bf16[2,512,256]{2,1,0:T(8,128)(2,1)S(1)}, u32[]{:S(2)}, u32[]{:S(2)}) collective-permute-start(bf16[2,512,256]{2,1,0:T(8,128)(2,1)S(1)} %collective-permute-done.13.refs_4_.refs_7_), channel_id=1, source_target_pairs={{0,1},{1,0},{2,3},{3,2},{4,5},{5,4},{6,7},{7,6},{8,9},{9,8},{10,11... | collective-permute-start | bytes 1572872 | tf_op jit(solution)/shard_map/ppermute | solution.py:1178
  61.5 28.7 %collective-permute-start.18 = (bf16[2,256,768]{2,1,0:T(8,128)(2,1)S(1)}, bf16[2,256,768]{2,1,0:T(8,128)(2,1)S(1)}, u32[]{:S(2)}, u32[]{:S(2)}) collective-permute-start(bf16[2,256,768]{2,1,0:T(8,128)(2,1)S(1)} %get-tuple-element.92.refs_3_.refs_24_), channel_id=1, source_target_pairs={{0,4},{1,5},{2,6},{3,7},{4,0},{5,1},{6,2},{7,3},{8,12},{9,13},{10,... | collective-permute-start | bytes 2359304 | tf_op jit(solution)/shard_map/ppermute | solution.py:1178
  69.0 20.8 %collective-permute-start.11 = (bf16[2,512,256]{2,1,0:T(8,128)(2,1)S(1)}, bf16[2,512,256]{2,1,0:T(8,128)(2,1)S(1)}, u32[]{:S(2)}, u32[]{:S(2)}) collective-permute-start(bf16[2,512,256]{2,1,0:T(8,128)(2,1)S(1)} %get-tuple-element.82.refs_3_.refs_10_), channel_id=1, source_target_pairs={{0,1},{1,0},{2,3},{3,2},{4,5},{5,4},{6,7},{7,6},{8,9},{9,8},{10,11... | collective-permute-start | bytes 1572872 | tf_op jit(solution)/shard_map/ppermute | solution.py:1178
  81.9 15.4 %collective-permute-start.8 = (bf16[2,512,256]{2,1,0:T(8,128)(2,1)S(1)}, bf16[2,512,256]{2,1,0:T(8,128)(2,1)S(1)}, u32[]{:S(2)}, u32[]{:S(2)}) collective-permute-start(bf16[2,512,256]{2,1,0:T(8,128)(2,1)S(1)} %get-tuple-element.81.refs_3_.refs_14_), channel_id=1, source_target_pairs={{0,1},{1,0},{2,3},{3,2},{4,5},{5,4},{6,7},{7,6},{8,9},{9,8},{10,11... | collective-permute-start | bytes 1572872 | tf_op jit(solution)/shard_map/ppermute | solution.py:1178
  82.5 14.9 %collective-permute-start.9 = (bf16[2,512,256]{2,1,0:T(8,128)(2,1)S(1)}, bf16[2,512,256]{2,1,0:T(8,128)(2,1)S(1)}, u32[]{:S(2)}, u32[]{:S(2)}) collective-permute-start(bf16[2,512,256]{2,1,0:T(8,128)(2,1)S(1)} %collective-permute-done.7.refs_4_.refs_15_), channel_id=1, source_target_pairs={{0,1},{1,0},{2,3},{3,2},{4,5},{5,4},{6,7},{7,6},{8,9},{9,8},{10,11... | collective-permute-start | bytes 1572872 | tf_op jit(solution)/shard_map/ppermute | solution.py:1178
  89.8 15.8 %collective-permute-start.19 = (bf16[2,256,768]{2,1,0:T(8,128)(2,1)S(1)}, bf16[2,256,768]{2,1,0:T(8,128)(2,1)S(1)}, u32[]{:S(2)}, u32[]{:S(2)}) collective-permute-start(bf16[2,256,768]{2,1,0:T(8,128)(2,1)S(1)} %get-tuple-element.92.refs_3_.refs_24_), channel_id=1, source_target_pairs={{0,1},{1,0},{2,3},{3,2},{4,5},{5,4},{6,7},{7,6},{8,9},{9,8},{10,11... | collective-permute-start | bytes 2359304 | tf_op jit(solution)/shard_map/ppermute | solution.py:1178
  90.3 15.4 %collective-permute-start.20 = (bf16[2,256,768]{2,1,0:T(8,128)(2,1)S(1)}, bf16[2,256,768]{2,1,0:T(8,128)(2,1)S(1)}, u32[]{:S(2)}, u32[]{:S(2)}) collective-permute-start(bf16[2,256,768]{2,1,0:T(8,128)(2,1)S(1)} %collective-permute-done.18.refs_4_.refs_25_), channel_id=1, source_target_pairs={{0,1},{1,0},{2,3},{3,2},{4,5},{5,4},{6,7},{7,6},{8,9},{9,8},{10,11... | collective-permute-start | bytes 2359304 | tf_op jit(solution)/shard_map/ppermute | solution.py:1178
  126.1 22.7 %collective-permute-start.21 = (bf16[2,256,768]{2,1,0:T(8,128)(2,1)}, bf16[2,256,768]{2,1,0:T(8,128)(2,1)}, u32[]{:S(2)}, u32[]{:S(2)}) collective-permute-start(bf16[2,256,768]{2,1,0:T(8,128)(2,1)} %get-tuple-element.94.refs_3_.refs_6_), channel_id=1, source_target_pairs={{0,4},{1,5},{2,6},{3,7},{4,0},{5,1},{6,2},{7,3},{8,12},{9,13},{10,... | collective-permute-start | bytes 2359304 | tf_op jit(solution)/shard_map/ppermute | solution.py:1178
  180.5 23.3 %collective-permute-start.24 = (bf16[256,768]{1,0:T(8,128)(2,1)S(1)}, bf16[256,768]{1,0:T(8,128)(2,1)S(1)}, u32[]{:S(2)}, u32[]{:S(2)}) collective-permute-start(bf16[256,768]{1,0:T(8,128)(2,1)S(1)} %get-tuple-element.157), channel_id=1, source_target_pairs={{0,8},{1,24},{2,10},{3,26},{4,12},{5,28},{6,14},{7,30},{8,0},{9,16... | collective-permute-start | bytes 1179656 | tf_op jit(solution)/shard_map/ppermute | solution.py:1178
  183.0 20.8 %collective-permute-start.25 = (bf16[256,768]{1,0:T(8,128)(2,1)S(1)}, bf16[256,768]{1,0:T(8,128)(2,1)S(1)}, u32[]{:S(2)}, u32[]{:S(2)}) collective-permute-start(bf16[256,768]{1,0:T(8,128)(2,1)S(1)} %get-tuple-element.158), channel_id=1, source_target_pairs={{0,0},{1,16},{2,2},{3,18},{4,4},{5,20},{6,6},{7,22},{8,8},{9,24},{... | collective-permute-start | bytes 1179656 | tf_op jit(solution)/shard_map/ppermute | solution.py:1178
  205.1 17.6 %collective-permute-start.29 = (bf16[2,256,384]{2,1,0:T(8,128)(2,1)S(1)}, bf16[2,256,384]{2,1,0:T(8,128)(2,1)S(1)}, u32[]{:S(2)}, u32[]{:S(2)}) collective-permute-start(bf16[2,256,384]{2,1,0:T(8,128)(2,1)S(1)} %slice.119), channel_id=1, source_target_pairs={{0,4},{1,5},{2,6},{3,7},{4,0},{5,1},{6,2},{7,3},{8,12},{9,13},{10,... | collective-permute-start | bytes 1179656 | tf_op jit(solution)/shard_map/ppermute | solution.py:1178
  445.8 13.9 %collective-permute-start.34 = (bf16[128,768]{1,0:T(8,128)(2,1)S(1)}, bf16[128,768]{1,0:T(8,128)(2,1)S(1)}, u32[]{:S(2)}, u32[]{:S(2)}) collective-permute-start(bf16[128,768]{1,0:T(8,128)(2,1)S(1)} %get-tuple-element.161), channel_id=1, source_target_pairs={{0,8},{1,24},{2,10},{3,26},{4,12},{5,28},{6,14},{7,30},{8,0},{9,16... | collective-permute-start | bytes 589832 | tf_op jit(solution)/shard_map/ppermute | solution.py:1178
  451.4 24.5 %collective-permute-start.33 = (bf16[256,768]{1,0:T(8,128)(2,1)S(1)}, bf16[256,768]{1,0:T(8,128)(2,1)S(1)}, u32[]{:S(2)}, u32[]{:S(2)}) collective-permute-start(bf16[256,768]{1,0:T(8,128)(2,1)S(1)} %copy-done.64), channel_id=1, source_target_pairs={{0,0},{1,16},{2,2},{3,18},{4,4},{5,20},{6,6},{7,22},{8,8},{9,24},{... | collective-permute-start | bytes 1179656 | tf_op jit(solution)/shard_map/ppermute | solution.py:1178
  (87 other events, 1576.6 us)

commit v3 on v2

--- a/solution.py
+++ b/solution.py
@@ -267,6 +267,18 @@
     return value * half, slope
 
 
+def fill_wide(wide, refs, rows, first):
+    at, there = 0, pl.ds(first, rows)
+    for ref in refs:
+        if len(ref.shape) == 3:
+            for pair in range(ref.shape[0]):
+                wide[there, at : at + LANES] = ref[pair]
+                at += LANES
+        else:
+            wide[there, at : at + ref.shape[1]] = ref[...]
+            at += ref.shape[1]
+
+
 def rest_kernel(steps, mixes, is_query, *refs):
     x_ref = refs[0]
     mixed_refs = refs[1 : 1 + mixes]
@@ -278,12 +290,8 @@
 
     @pl.when(step == 0)
     def _():
-        at = 0
         hidden = x_ref[...].astype(f32)
-        for mixed_ref in mixed_refs:
-            wide = mixed_ref.shape[1]
-            scratch[:, pl.ds(at, wide)] = mixed_ref[...]
-            at += wide
+        fill_wide(scratch, mixed_refs, scratch.shape[0], 0)
         hidden = hidden + dot(scratch[...], wo_ref[...])
         hidden_ref[...] = hidden
         second_ref[...] = norm(hidden, gain_ref[...])
@@ -303,7 +311,12 @@
         asked = norm(merged, next_gain_ref[...])
         asked_ref[...] = asked
         if is_query:
-            out_ref[...] = (dot(asked, next_refs[0][...]) * Q_SCALE).astype(bf16)
+            query = (dot(asked, next_refs[0][...]) * Q_SCALE).astype(bf16)
+            if len(out_ref.shape) == 3:
+                for pair in range(out_ref.shape[0]):
+                    out_ref[pair] = query[:, pair * LANES : (pair + 1) * LANES]
+            else:
+                out_ref[...] = query
         else:
             out_ref[0] = dot(asked, next_refs[0][...]).astype(bf16)
             out_ref[1] = dot(asked, next_refs[1][...]).astype(bf16)
@@ -319,6 +332,8 @@
     shape = lambda kind: jax.ShapeDtypeStruct((rows, width), kind)
     wide = jax.ShapeDtypeStruct((rows, up.shape[1]), bf16)
     last = (rows, width) if is_query else (2, rows, width)
+    if len(mixed[0].shape) == 3:
+        last = (width // LANES, rows, LANES)
     return pl.pallas_call(
         functools.partial(rest_kernel, steps, len(mixed), is_query),
         grid=(steps,),
@@ -346,17 +361,32 @@
     return pl.BlockSpec((rows, width), lambda i: (0, i))
 
 
-def back_kernel(steps, mixes, sizes, laid, *refs):
+def back_kernel(steps, mixes, sizes, laid, orders, *refs):
     gl_ref, gs_ref, al_ref, as_ref, sl_ref, ss_ref = refs[:6]
     cl_ref, cs_ref, hl_ref, hs_ref = refs[6:10]
     mixed_refs = refs[10 : 10 + mixes]
     mixed_s_ref, wo_ref, gain_ref, up_ref, down_ref = refs[10 + mixes : 15 + mixes]
-    outs = refs[15 + mixes :]
+    flows = len(orders)
+    locals_, outs = refs[15 + mixes : 15 + mixes + flows], refs[15 + mixes + flows :]
     (hgl_ref, hgs_ref, ml_ref, ms_ref, dup_ref, ddown_ref, dwo_ref, dgain_ref) = outs[:8]
-    branch, second, total, active, inner_grad, mixed = outs[8:]
+    sums, outs = outs[8 : 8 + flows], outs[8 + flows :]
+    branch, second, total, active, inner_grad, mixed = outs[:6]
     large, small = sizes
     top, bottom = pl.ds(0, large), pl.ds(large, small)
     step = pl.program_id(0)
+    if flows:
+        here = Here()
+        rest_refs = list(outs[6:])
+        running = [
+            Flow(here, order, local, rest_refs, True, False)
+            for order, local in zip(orders, locals_)
+        ]
+
+        @pl.when(step == 0)
+        def _():
+            here.greet(ALL_PARTNERS)
+            for flow in running:
+                flow.act(0)
 
     @pl.when(step == 0)
     def _():
@@ -402,23 +432,30 @@
         mixed_grad = dot(branch[...], wo_ref[...], NT).astype(bf16)
         ml_ref[...] = mixed_grad[:large]
         ms_ref[...] = mixed_grad[large:]
-        at = 0
-        for mixed_ref in mixed_refs:
-            wide = mixed_ref.shape[1]
-            mixed[top, pl.ds(at, wide)] = mixed_ref[...]
-            at += wide
-        mixed[bottom, :] = mixed_s_ref[...]
+        fill_wide(mixed, mixed_refs, large, 0)
+        fill_wide(mixed, [mixed_s_ref], small, large)
         value = dot(mixed[...], branch[...], TN).astype(bf16)
         if laid:
             rows, wide = dwo_ref.shape[1:]
-            for at, (core, y, tm) in enumerate(spots(BY_Y)):
+            for at, (core, y, tm) in enumerate(spots(BY_X)):
                 first = (tm * 2 + core) * rows
                 dwo_ref[at] = value[first : first + rows, y * wide : (y + 1) * wide]
         else:
             dwo_ref[...] = value
 
-
-def back(grad_l, grad_s, saved_l, saved_s, mixed_l, mixed_s, wo, gain, up, down, laid=False):
+    for flow in range(flows):
+        for stage, when in enumerate((0, 2, steps - 1)):
+
+            @pl.when(step == when)
+            def _(flow=flow, stage=stage):
+                running[flow].act(stage + 1)
+                if stage == 2:
+                    sums[flow][...] = running[flow].result()
+
+
+def back(
+    grad_l, grad_s, saved_l, saved_s, mixed_l, mixed_s, wo, gain, up, down, laid, flows=(), orders=()
+):
     (hidden_l, second_l, active_l, slope_l) = saved_l
     (hidden_s, second_s, active_s, slope_s) = saved_s
     large, width = grad_l.shape
@@ -432,6 +469,8 @@
     up_slab = slab_of(width, part)
     down_slab = pl.BlockSpec((part, width), lambda i: (i, 0))
     shape = jax.ShapeDtypeStruct
+    results = [flow_result(o, f.shape[1:], False) for o, f in zip(orders, flows)]
+    scratch = [s for o, f in zip(orders, flows) for s in flow_scratch(o, f.shape[1:], True, False)]
     out_up, out_down, out_square = up_slab, down_slab, square
     up_shape, down_shape, square_shape = up.shape, down.shape, (width, width)
     if laid:
@@ -441,14 +480,16 @@
         out_up = pl.BlockSpec((8,) + block, lambda i: (i, 0, 0))
         out_down, out_square = whole(down_shape), whole(square_shape)
     return pl.pallas_call(
-        functools.partial(back_kernel, steps, len(mixed_l), (large, small), laid),
+        functools.partial(back_kernel, steps, len(mixed_l), (large, small), laid, orders),
         grid=(steps,),
         in_specs=[fl, fs]
         + [slab_of(large, part), slab_of(small, part)] * 2
         + [fl, fs, fl, fs]
         + [whole(m.shape) for m in mixed_l]
-        + [fs, square, whole((1, width)), up_slab, down_slab],
-        out_specs=[fl, fs, fl, fs, out_up, out_down, out_square, whole((1, width))],
+        + [whole(mixed_s.shape), square, whole((1, width)), up_slab, down_slab]
+        + [pl.BlockSpec(memory_space=pl.ANY)] * len(flows),
+        out_specs=[fl, fs, fl, fs, out_up, out_down, out_square, whole((1, width))]
+        + [whole(result.shape) for result in results],
         out_shape=[
             shape((large, width), f32),
             shape((small, width), f32),
@@ -458,7 +499,8 @@
             shape(down_shape, bf16),
             shape(square_shape, bf16),
             shape((1, width), f32),
-        ],
+        ]
+        + results,
         scratch_shapes=[
             pltpu.VMEM((rows, width), bf16),
             pltpu.VMEM((rows, width), bf16),
@@ -466,8 +508,13 @@
             pltpu.VMEM((rows, part), bf16),
             pltpu.VMEM((rows, part), bf16),
             pltpu.VMEM((rows, width), bf16),
-        ],
-        compiler_params=pltpu.CompilerParams(vmem_limit_bytes=56 << 20),
+        ]
+        + scratch,
+        compiler_params=pltpu.CompilerParams(
+            vmem_limit_bytes=60 << 20,
+            has_side_effects=bool(flows),
+            collective_id=0 if flows else None,
+        ),
         cost_estimate=pl.CostEstimate(
             flops=2 * rows * width * (4 * hidden + 2 * width),
             bytes_accessed=width * width * 36 + rows * width * 40,
@@ -476,7 +523,7 @@
         name="back",
     )(
         grad_l, grad_s, active_l, active_s, slope_l, slope_s, second_l, second_s, hidden_l, hidden_s,
-        *mixed_l, mixed_s, wo, gain, up, down,
+        *mixed_l, mixed_s, wo, gain, up, down, *flows,
     )
 
 
@@ -530,31 +577,34 @@
 
 
 class Flow:
-    def __init__(self, here, order, refs):
-        self.here, self.order = here, order
-        self.local, self.keep = refs[0], refs[1]
-        self.got = refs[2:7]
-        self.out = refs[7]
-        self.send_sem, self.recv_sem = refs[8], refs[9]
+    def __init__(self, here, order, local, refs, keep, ends):
+        self.here, self.order, self.local = here, order, local
+        self.keep = refs.pop(0) if keep else None
+        self.got = [refs.pop(0) for _ in order]
+        self.out = refs.pop(0) if ends else None
+        self.sem = refs.pop(0)
+        self.last = len(order)
+        self.ends = ends
 
     def copy(self, step):
         name = self.order[step]
-        half = 16 >> step
+        half = 1 << (self.last - 1 - step)
         source = self.local if step == 0 else self.got[step - 1]
         at = (1 - self.here.bit[name]) * half
         return pltpu.make_async_remote_copy(
             src_ref=source.at[pl.ds(at, half)],
             dst_ref=self.got[step],
-            send_sem=self.send_sem.at[step],
-            recv_sem=self.recv_sem.at[step],
+            send_sem=self.sem.at[0, step],
+            recv_sem=self.sem.at[1, step],
             device_id=self.here.partner(name),
             device_id_type=MESH,
         )
 
     def keep_copy(self):
-        at = self.here.bit[self.order[0]] * 16
+        half = 1 << (self.last - 1)
+        at = self.here.bit[self.order[0]] * half
         return pltpu.make_async_copy(
-            self.local.at[pl.ds(at, 16)], self.keep, self.send_sem.at[8]
+            self.local.at[pl.ds(at, half)], self.keep, self.sem.at[0, self.last + 2]
         )
 
     def start(self, step):
@@ -563,7 +613,7 @@
             self.keep_copy().start()
 
     def finish(self, step):
-        half = 16 >> step
+        half = 1 << (self.last - 1 - step)
         self.copy(step).wait()
         got = self.got[step]
         at = self.here.bit[self.order[step]] * half
@@ -582,50 +632,56 @@
         else:
             lax.fori_loop(0, half, body, 0)
 
-    def spread_copies(self):
+    def spread_copy(self, which):
         here = self.here
-        slot = here.bit["core"] * 2 + here.bit["y"]
-        return [
-            pltpu.make_async_remote_copy(
-                src_ref=self.got[4].at[0],
-                dst_ref=self.out.at[slot],
-                send_sem=self.send_sem.at[5 + i],
-                recv_sem=self.recv_sem.at[5 + i],
-                device_id=here.partner(*names),
-                device_id_type=MESH,
-            )
-            for i, names in enumerate((("core",), ("y",), ("y", "core")))
-        ]
-
-    def spread(self):
-        for copy in self.spread_copies():
-            copy.start()
-        slot = self.here.bit["core"] * 2 + self.here.bit["y"]
-        self.out[slot] = self.got[4][0]
-
-    def gathered(self):
-        for copy in self.spread_copies():
-            copy.wait()
+        own = here.bit["core"] * 2
+        if which == 0:
+            source, there = self.got[-1].at[0], self.out.at[own + here.bit["y"]]
+        else:
+            source = there = self.out.at[pl.ds(own, 2)]
+        return pltpu.make_async_remote_copy(
+            src_ref=source,
+            dst_ref=there,
+            send_sem=self.sem.at[0, self.last + which],
+            recv_sem=self.sem.at[1, self.last + which],
+            device_id=here.partner(("y", "core")[which]),
+            device_id_type=MESH,
+        )
 
     def act(self, stage):
         if stage == 0:
             self.start(0)
-        elif stage < 5:
+        elif stage < self.last:
             self.finish(stage - 1)
             self.start(stage)
-        elif stage == 5:
-            self.finish(4)
-            self.spread()
-        else:
-            self.gathered()
-
-
-def flow_scratch(rows, wide, keep):
-    blocks = [pltpu.VMEM((16, rows, wide), bf16)] if keep else []
-    for half in (16, 8, 4, 2, 1):
-        blocks.append(pltpu.VMEM((half, rows, wide), bf16))
-    blocks.append(pltpu.VMEM((4, rows, wide), bf16))
-    return blocks + [pltpu.SemaphoreType.DMA((9,)), pltpu.SemaphoreType.DMA((8,))]
+        elif stage == self.last:
+            self.finish(stage - 1)
+            if self.ends:
+                self.spread_copy(0).start()
+                self.out[self.here.bit["core"] * 2 + self.here.bit["y"]] = self.got[-1][0]
+        elif stage == self.last + 1 and self.ends:
+            self.spread_copy(0).wait()
+            self.spread_copy(1).start()
+        elif stage == self.last + 2 and self.ends:
+            self.spread_copy(1).wait()
+
+    def result(self):
+        return self.out[...] if self.ends else self.got[-1][...]
+
+
+def flow_scratch(order, block, keep, ends):
+    steps = len(order)
+    blocks = [pltpu.VMEM((1 << (steps - 1),) + block, bf16)] if keep else []
+    for step in range(steps):
+        blocks.append(pltpu.VMEM((1 << (steps - 1 - step),) + block, bf16))
+    if ends:
+        blocks.append(pltpu.VMEM((4,) + block, bf16))
+    return blocks + [pltpu.SemaphoreType.DMA((2, steps + 3))]
+
+
+def flow_result(order, block, ends):
+    left = 4 if ends else 1
+    return jax.ShapeDtypeStruct((left,) + block, bf16)
 
 
 def pair_back(query, grad, out, logsum, mask, keys_at, values_at, mk_ref, block, store):
@@ -751,13 +807,18 @@
     ]
 
 
+def fill_keys(keys_at, values_at, kv_ref):
+    rows = kv_ref.shape[3]
+    for part in range(kv_ref.shape[0]):
+        there = pl.ds(part * rows, rows)
+        keys_at[there, :] = kv_ref[part, 0, 0]
+        values_at[there, :] = kv_ref[part, 0, 1]
+
+
 def selves_kernel(pairs, plan, blocks, *refs):
-    orders, shapes, stages = plan
-    large_refs, refs = refs[:6], refs[6:]
-    groups = 3
-    kv_large = [refs[4 * g : 4 * g + 4] for g in range(groups)]
-    refs = refs[4 * groups :]
-    small_refs, kv_small, refs = refs[:6], refs[6:10], refs[10:]
+    orders, ends, stages = plan
+    large_refs, kv_large, refs = refs[:6], refs[6], refs[7:]
+    small_refs, kv_small, refs = refs[:6], refs[6], refs[7:]
     flows = len(orders)
     locals_, refs = refs[:flows], refs[flows:]
     dq_l, dkv_l, dq_s, dkv_s = refs[:4]
@@ -767,10 +828,10 @@
     here = Here()
     rows_l, rows_s = keys_l.shape[0] // 4, keys_s.shape[0] // 4
     large, small = Exchange(here, rows_l, ex_l), Exchange(here, rows_s, ex_s)
-    running = []
-    for flow in range(flows):
-        running.append(Flow(here, orders[flow], [locals_[flow]] + list(refs[:9])))
-        refs = refs[9:]
+    refs = list(refs)
+    running = [
+        Flow(here, orders[flow], locals_[flow], refs, True, ends[flow]) for flow in range(flows)
+    ]
     step = pl.program_id(0)
 
     @pl.when(step == 0)
@@ -794,42 +855,28 @@
         def _():
             exchange.take(pair - 2, out_ref)
 
-    def attention(exchange, pair, refs, kv_of, keys_at, values_at, block, dq_ref):
+    def attention(exchange, pair, refs, kv_ref, keys_at, values_at, block, dq_ref):
         q_ref, do_ref, o_ref, l_ref, mq_ref, mk_ref = refs
-        for when, kv_refs in kv_of:
-
-            def fill(kv_refs=kv_refs):
-                at = 0
-                for kv_ref in kv_refs:
-                    there = pl.ds(at, kv_ref.shape[1])
-                    keys_at[there, :] = kv_ref[0]
-                    values_at[there, :] = kv_ref[1]
-                    at += kv_ref.shape[1]
-
-            if when is None:
-                fill()
-            else:
-                pl.when(when)(fill)
+        fill_keys(keys_at, values_at, kv_ref)
 
         @pl.when(pair >= 2)
         def _():
             exchange.free(pair - 2)
 
         dq_ref[...] = pair_back(
-            q_ref[...], do_ref[...], o_ref[...], l_ref[...], mq_ref[...],
+            q_ref[0], do_ref[...], o_ref[0], l_ref[0], mq_ref[...],
             keys_at, values_at, mk_ref, block, exchange.put(pair, keys_at.shape[0], block),
         )
 
     @pl.when(step < pairs)
     def _():
-        kv_of = [(step // 2 == g, kv_large[g]) for g in range(groups)]
-        attention(large, step, large_refs, kv_of, keys_l, values_l, blocks[0], dq_l)
+        attention(large, step, large_refs, kv_large, keys_l, values_l, blocks[0], dq_l)
         move(large, step, dkv_l)
 
     @pl.when(step >= pairs)
     def _():
         pair = step - pairs
-        attention(small, pair, small_refs, [(None, kv_small)], keys_s, values_s, blocks[1], dq_s)
+        attention(small, pair, small_refs, kv_small, keys_s, values_s, blocks[1], dq_s)
         move(small, pair, dkv_s)
 
     @pl.when(step == pairs)
@@ -850,10 +897,10 @@
 
     for at in range(2 * pairs):
         todo = []
-        for stage in range(1, 7):
-            for flow in range(flows):
-                if stages[flow][stage - 1] == at:
-                    todo.append((running[flow], stage))
+        for flow in range(flows):
+            for stage, when in enumerate(stages[flow]):
+                if when == at:
+                    todo.append((running[flow], stage + 1))
         if todo:
 
             @pl.when(step == at)
@@ -869,28 +916,27 @@
             small.free(pair)
             small.copy_x(pair).wait_send()
         for flow, sum_ref in zip(running, sums):
-            sum_ref[...] = flow.out[...]
-
-
-def selves_back(large, large_kv, small, small_kv, flows, orders, stages):
-    count, width = large[0].shape
-    few = small[0].shape[0]
+            sum_ref[...] = flow.result()
+
+
+def selves_back(large, large_kv, small, small_kv, flows, orders, ends, stages):
+    count, width = large[1].shape
+    few = small[1].shape[0]
     pairs = width // LANES
     total, less = large[5].shape[0], small[5].shape[0]
     shapes = [flow.shape[1:] for flow in flows]
+    results = [flow_result(*flow) for flow in zip(orders, shapes, ends)]
     blocks = (largest_block(total // 2, 512), largest_block(less // 2, 512))
     first = lambda i: jnp.minimum(i, pairs - 1)
     last = lambda i: jnp.maximum(i - pairs, 0)
-    in_specs = [pl.BlockSpec((count, LANES), lambda i: (0, first(i)))] * 4
-    in_specs += [whole((count, LANES)), whole((total, LANES))]
-    for group in range(3):
-        spec = pl.BlockSpec(
-            (2, count, LANES), lambda i, g=group: (0, 0, jnp.clip(i - 2 * g, 0, 1))
+    in_specs = []
+    for rows, keys, at in ((count, total, first), (few, less, last)):
+        major = pl.BlockSpec((1, rows, LANES), lambda i, at=at: (at(i), 0, 0))
+        minor = pl.BlockSpec((rows, LANES), lambda i, at=at: (0, at(i)))
+        in_specs += [major, minor, major, major, whole((rows, LANES)), whole((keys, LANES))]
+        in_specs.append(
+            pl.BlockSpec((4, 1, 2, rows, LANES), lambda i, at=at: (0, at(i), 0, 0, 0))
         )
-        in_specs += [spec] * 4
-    in_specs += [pl.BlockSpec((few, LANES), lambda i: (0, last(i)))] * 4
-    in_specs += [whole((few, LANES)), whole((less, LANES))]
-    in_specs += [pl.BlockSpec((2, few, LANES), lambda i: (0, 0, last(i)))] * 4
     in_specs += [pl.BlockSpec(memory_space=pl.ANY)] * len(flows)
     shape = jax.ShapeDtypeStruct
     out_shape = [
@@ -898,19 +944,19 @@
         shape((pairs, 2, count, LANES), bf16),
         shape((few, width), bf16),
         shape((pairs, 2, few, LANES), bf16),
-    ] + [shape((4,) + block, bf16) for block in shapes]
+    ] + results
     out_specs = [
         pl.BlockSpec((count, LANES), lambda i: (0, first(i))),
         whole((pairs, 2, count, LANES)),
         pl.BlockSpec((few, LANES), lambda i: (0, last(i))),
         whole((pairs, 2, few, LANES)),
-    ] + [whole((4,) + block) for block in shapes]
+    ] + [whole(result.shape) for result in results]
     scratch = [pltpu.VMEM((total, LANES), bf16)] * 2 + [pltpu.VMEM((less, LANES), bf16)] * 2
     scratch += exchange_scratch(pairs, count) + exchange_scratch(pairs, few)
-    for block in shapes:
-        scratch += flow_scratch(*block, True)
+    for flow in range(len(flows)):
+        scratch += flow_scratch(orders[flow], shapes[flow], True, ends[flow])
     result = pl.pallas_call(
-        functools.partial(selves_kernel, pairs, (orders, shapes, stages), blocks),
+        functools.partial(selves_kernel, pairs, (orders, ends, stages), blocks),
         grid=(2 * pairs,),
         in_specs=in_specs,
         out_specs=out_specs,
@@ -925,7 +971,7 @@
             transcendentals=count * total * width // HALF,
         ),
         name="selves_back",
-    )(*large, *[p for kv in large_kv for p in kv], *small, *small_kv, *flows)
+    )(*large, large_kv, *small, small_kv, *flows)
     return result[:4], result[4:]
 
 
@@ -977,22 +1023,26 @@
 
 LAST_ORDERS = (BY_YX, BY_X, BY_ZL)
 GAIN_ORDER = ("core", "y", "x", "zl", "zh")
-
-
-def last_kernel(pairs, sizes, *refs):
+LATE_ORDER = ("x", "zh")
+LATE_STAGES = {2: 1, 4: 2, 5: 3, 6: 4}
+
+
+def last_kernel(pairs, sizes, late, *refs):
     dql, dkvl, dqs, dkvs, nl, ns, gains = refs[:7]
-    sum_refs, gain_ref = refs[7:10], refs[10]
-    normed, grads, refs = refs[11], refs[12], refs[13:]
+    late_refs, refs = refs[7 : 7 + late], list(refs[7 + late :])
+    sum_refs = [refs.pop(0) for _ in range(3 + late)]
+    gain_ref, normed, grads = refs.pop(0), refs.pop(0), refs.pop(0)
     here = Here()
     flows = []
     for order in LAST_ORDERS:
-        local, refs = refs[0], refs[1:]
-        flows.append(Flow(here, order, [local, None] + list(refs[:8])))
-        refs = refs[8:]
+        flows.append(Flow(here, order, refs.pop(0), refs, False, True))
+    late_flows = [Flow(here, LATE_ORDER, ref, refs, False, True) for ref in late_refs]
     state, got, gain_sems = refs
     large, small = sizes
     top, bottom = pl.ds(0, large), pl.ds(large, small)
     here.greet(ALL_PARTNERS)
+    for flow in late_flows:
+        flow.act(0)
 
     def gain_copy(step):
         return pltpu.make_async_remote_copy(
@@ -1023,9 +1073,12 @@
             first = tm * 2 * rows + core * rows
             flow.local[at] = value[first : first + rows, y * wide : (y + 1) * wide]
         flow.act(0)
-    for stage in range(1, 7):
+    for stage in range(1, 8):
         for flow in flows:
             flow.act(stage)
+        if stage in LATE_STAGES:
+            for flow in late_flows:
+                flow.act(LATE_STAGES[stage])
         if stage <= 5:
             gain_copy(stage - 1).wait()
             total = state[stage - 1] + got[stage - 1]
@@ -1034,26 +1087,31 @@
                 gain_copy(stage).start()
             else:
                 gain_ref[...] = total
-    for flow, sum_ref in zip(flows, sum_refs):
-        sum_ref[...] = flow.out[...]
-
-
-def last_sums(selves, normed_l, normed_s, gains):
+    for flow, sum_ref in zip(flows + late_flows, sum_refs):
+        sum_ref[...] = flow.result()
+
+
+def last_sums(selves, normed_l, normed_s, gains, late):
     count, width = normed_l.shape
     few = normed_s.shape[0]
-    rows, wide = width // 16, width // 2
+    block = (width // 16, width // 2)
     shape = jax.ShapeDtypeStruct
     scratch = [pltpu.VMEM((count + few, width), bf16), pltpu.VMEM((count + few, width), bf16)]
-    for _ in LAST_ORDERS:
-        scratch += [pltpu.VMEM((32, rows, wide), bf16)] + flow_scratch(rows, wide, False)
+    for order in LAST_ORDERS:
+        scratch.append(pltpu.VMEM((32,) + block, bf16))
+        scratch += flow_scratch(order, block, False, True)
+    for local in late:
+        scratch += flow_scratch(LATE_ORDER, local.shape[1:], False, True)
     scratch += [
         pltpu.VMEM((5,) + gains.shape, f32),
         pltpu.VMEM((5,) + gains.shape, f32),
         pltpu.SemaphoreType.DMA((2, 5)),
     ]
     result = pl.pallas_call(
-        functools.partial(last_kernel, width // LANES, (count, few)),
-        out_shape=[shape((4, rows, wide), bf16)] * 3 + [shape(gains.shape, f32)],
+        functools.partial(last_kernel, width // LANES, (count, few), len(late)),
+        out_shape=[shape((4,) + block, bf16)] * 3
+        + [shape((4,) + local.shape[1:], bf16) for local in late]
+        + [shape(gains.shape, f32)],
         scratch_shapes=scratch,
         compiler_params=pltpu.CompilerParams(
             vmem_limit_bytes=48 << 20, collective_id=2, has_side_effects=True
@@ -1064,48 +1122,616 @@
             transcendentals=0,
         ),
         name="last_sums",
-    )(*selves, normed_l, normed_s, gains)
-    return result[:3], result[3]
+    )(*selves, normed_l, normed_s, gains, *late)
+    return result[:3], result[3:-1], result[-1]
+
+
+def cross_kernel(pairs, block, *refs):
+    (q_ref, do_ref, o_ref, l_ref, mq_ref, mk_ref), refs = refs[:6], refs[6:]
+    kv_ref, given, gains, refs = refs[0], refs[1:10], refs[10:12], refs[12:]
+    gl_ref, gs_ref, a_ref, b_ref, gain_l_ref, gain_s_ref = refs[:6]
+    keys_at, values_at, exchange_refs, refs = refs[6], refs[7], refs[8:14], refs[14:]
+    dkv, dq, dk, dv = refs[:4]
+    held, sems = refs[4:13], refs[13]
+    asked, context, united, grad_out, merged_l, merged_s, wq, wk, wv = held
+    here = Here()
+    exchange = Exchange(here, keys_at.shape[0] // 4, exchange_refs)
+    step = pl.program_id(0)
+    loads = [
+        pltpu.make_async_copy(source, there, sems.at[i])
+        for i, (source, there) in enumerate(zip(given, held))
+    ]
+
+    @pl.when(step == 0)
+    def _():
+        here.greet((("core",), ("x",)))
+        for load in loads:
+            load.start()
+
+    fill_keys(keys_at, values_at, kv_ref)
+
+    @pl.when(step >= 2)
+    def _():
+        exchange.free(step - 2)
+
+    dq[step] = pair_back(
+        q_ref[0], do_ref[...], o_ref[0], l_ref[0], mq_ref[...],
+        keys_at, values_at, mk_ref, block, exchange.put(step, keys_at.shape[0], block),
+    )
+    exchange.copy_core(step).start()
+
+    @pl.when((step >= 1) & (step < 3))
+    def _():
+        exchange.pass_on(step - 1, False)
+
+    @pl.when(step >= 3)
+    def _():
+        exchange.pass_on(step - 1, True)
+
+    @pl.when(step >= 2)
+    def _():
+        exchange.take(step - 2, dkv)
+
+    def lay(out_ref, which, value, order):
+        rows = out_ref.shape[1] // 4
+        for at, (core, y, tm) in enumerate(spots(order)):
+            if core == which:
+                first = (tm * 2 + y) * rows
+                out_ref[at // 4, at % 4 * rows : (at % 4 + 1) * rows, :] = value[
+                    first : first + rows
+                ]
+
+    @pl.when(step == pairs - 1)
+    def _():
+        exchange.pass_on(pairs - 1, True)
+        for load in loads:
+            load.wait()
+        grads = jnp.concatenate([united[i] for i in range(pairs)], axis=1)
+        lay(a_ref, 0, dot(grads, grad_out[...], TN).astype(bf16), BY_Y)
+        grads = jnp.concatenate([dq[i] for i in range(pairs)], axis=1)
+        lay(a_ref, 1, dot(asked[...], grads, TN).astype(bf16), BY_Y)
+        extra, gain_l_ref[...] = norm_back(dot(grads, wq[...], NT), merged_l[...], gains[0][...])
+        gl_ref[...] = grad_out[...].astype(f32) + extra
+        exchange.take(pairs - 2, dkv)
+        exchange.take(pairs - 1, dkv)
+        for pair in range(pairs):
+            lanes = pl.ds(pair * LANES, LANES)
+            dk[:, lanes] = dkv[pair, 0]
+            dv[:, lanes] = dkv[pair, 1]
+        lay(b_ref, 0, dot(context[...], dk[...], TN).astype(bf16), BY_ZL)
+        lay(b_ref, 1, dot(context[...], dv[...], TN).astype(bf16), BY_ZL)
+        grad = dot(dk[...], wk[...], NT) + dot(dv[...], wv[...], NT)
+        gs_ref[...], gain_s_ref[...] = norm_back(grad, merged_s[...], gains[1][...])
+        for pair in (pairs - 2, pairs - 1):
+            exchange.free(pair)
+            exchange.copy_x(pair).wait_send()
+
+
+def cross_back(attention, kv, given, gains):
+    count, width = attention[1].shape
+    few = kv.shape[3]
+    major = pl.BlockSpec((1, count, LANES), lambda i: (i, 0, 0))
+    pairs = width // LANES
+    total = attention[5].shape[0]
+    block = largest_block(total // 2, 512)
+    shape = jax.ShapeDtypeStruct
+    laid = (8, 4 * width // 16, width)
+    return pl.pallas_call(
+        functools.partial(cross_kernel, pairs, block),
+        grid=(pairs,),
+        in_specs=[major, columns(count, 0), major, major]
+        + [whole((count, LANES)), whole((total, LANES))]
+        + [pl.BlockSpec((4, 1, 2, few, LANES), lambda i: (0, i, 0, 0, 0))]
+        + [pl.BlockSpec(memory_space=pl.ANY)] * 9
+        + [whole((1, width))] * 2,
+        out_specs=[
+            whole((count, width)), whole((few, width)), whole(laid), whole(laid),
+            whole((1, width)), whole((1, width)),
+        ],
+        out_shape=[
+            shape((count, width), f32), shape((few, width), f32), shape(laid, bf16), shape(laid, bf16),
+            shape((1, width), f32), shape((1, width), f32),
+        ],
+        scratch_shapes=[pltpu.VMEM((total, LANES), bf16)] * 2
+        + exchange_scratch(pairs, few)
+        + [pltpu.VMEM((pairs, 2, few, LANES), bf16), pltpu.VMEM((pairs, count, LANES), bf16)]
+        + [pltpu.VMEM((few, width), bf16)] * 2
+        + [pltpu.VMEM(value.shape, value.dtype) for value in given]
+        + [pltpu.SemaphoreType.DMA((len(given),))],
+        compiler_params=pltpu.CompilerParams(
+            vmem_limit_bytes=56 << 20, collective_id=3, has_side_effects=True
+        ),
+        cost_estimate=pl.CostEstimate(
+            flops=20 * width * count * total,
+            bytes_accessed=64 * count * width,
+            transcendentals=count * total * width // HALF,
+        ),
+        name="cross_back",
+    )(*attention, kv, *given, *gains)
+
+
+def attend_pair(pair, q_ref, kv, mq_ref, mk_ref, spaces, o_ref, l_ref):
+    parts, rows = kv.shape[0], kv.shape[3]
+    total = parts * rows
+    ka0, ka1, va0, va1 = (space.at[pl.ds(0, total), :] for space in spaces)
+    low = lax.broadcasted_iota(jnp.int32, (rows, LANES), 1) < HALF
+    for part in range(parts):
+        here = pl.ds(part * rows, rows)
+        keys, values, mask = kv[part, pair, 0], kv[part, pair, 1], mk_ref[here, :]
+        one = jnp.ones_like(values)
+        ka0[here, :] = jnp.where(low, keys, mask)
+        ka1[here, :] = jnp.where(low, mask, keys)
+        va0[here, :] = jnp.where(low, values, one)
+        va1[here, :] = jnp.where(low, one, values)
+    count = q_ref.shape[1]
+    block = largest_block(count, 256)
+    low = lax.broadcasted_iota(jnp.int32, (block, LANES), 1) < HALF
+    for number in range(count // block):
+        here = pl.ds(number * block, block)
+        query, mask = q_ref[pair, here, :], mq_ref[here, :]
+        tops, sums = [], []
+        for head, keys, values in ((0, ka0, va0), (1, ka1, va1)):
+            mine = jnp.where(low, query, mask) if head == 0 else jnp.where(low, mask, query)
+            score = dot(mine, keys[...], NT)
+            top = jnp.max(score, axis=1, keepdims=True)
+            weight = jnp.exp2(score - top).astype(bf16)
+            sums.append(dot(weight, values[...]))
+            tops.append(jnp.broadcast_to(top, (block, LANES)))
+        total = jnp.where(low, sums[1], sums[0])
+        top = jnp.where(low, tops[1], tops[0])
+        out = jnp.where(low, sums[0], sums[1])
+        o_ref[pair, here, :] = (out / pltpu.roll(total, HALF, 1)).astype(bf16)
+        l_ref[pair, here, :] = top + jnp.log2(total)
+
+
+class Gather:
+    def __init__(self, here, kv, sems):
+        self.here, self.kv, self.sems = here, kv, sems
+
+    def copy(self, kind, at, size, sem):
+        source, there = ((0, 1), (0, 2), (1, 3))[kind]
+        pairs = pl.ds(at, size)
+        return pltpu.make_async_remote_copy(
+            src_ref=self.kv.at[source, pairs],
+            dst_ref=self.kv.at[there, pairs],
+            send_sem=self.sems.at[0, 3 * sem + kind],
+            recv_sem=self.sems.at[1, 3 * sem + kind],
+            device_id=self.here.partner(("x", "core", "core")[kind]),
+            device_id_type=MESH,
+        )
+
+
+def begin_kernel(pairs, *refs):
+    refs = list(refs)
+    take = lambda count: [refs.pop(0) for _ in range(count)]
+    large_ref, small_ref, cot_ref, clip_ref = take(4)
+    weight_refs = take(8)
+    first_gain, second_gain, context_gain = take(3)
+    xl_out, xs_out, cot_out, kvl_out, kvs_out, ckv_out = take(6)
+    nl_ref, ns_ref, ql_ref, qs_ref, ol_ref, ll_ref, os_ref, ls_ref = take(8)
+    merged_ref, hidden_ref, second_ref, active_ref, slope_ref, context_ref = take(6)
+    mql_ref, mkl_ref, mqs_ref, mks_ref = take(4)
+    xl, xs, cot, clip, kvl, kvs, ckv = take(7)
+    wq, wk, wv, wo, up, down, wck, wcv = weights = take(8)
+    spaces = take(4)
+    wide, total = take(2)
+    move_sems, gather_l, gather_s, gather_c, gather_clip, load_sems, out_sems = take(7)
+    here = Here()
+    z, core = here.tm // 2, here.bit["core"]
+    stay = core == z // 2
+
+    barrier = pltpu.get_barrier_semaphore()
+    for dz in range(4):
+        for dc in range(2):
+            if dz or dc:
+                place = (
+                    lax.rem(z + dz, 4) * 2 + here.bit["x"],
+                    here.bit["y"] * 2 + lax.rem(core + dc, 2),
+                )
+                pl.semaphore_signal(barrier, inc=1, device_id=place, device_id_type=MESH)
+    pl.semaphore_signal(barrier, inc=1, device_id=here.partner("x"), device_id_type=MESH)
+    pl.semaphore_wait(barrier, 8)
+
+    odd = lax.rem(z, 2)
+    from_seq = (odd, 1 - odd)
+
+    def far(which, turn, source, there):
+        rows = source.shape[1]
+        place = (
+            (2 * core + from_seq[turn]) * 2 + here.bit["x"],
+            here.bit["y"] * 2 + z // 2,
+        )
+        return pltpu.make_async_remote_copy(
+            src_ref=source.at[from_seq[turn]],
+            dst_ref=there.at[pl.ds(turn * rows, rows)],
+            send_sem=move_sems.at[0, 2 * which + turn],
+            recv_sem=move_sems.at[1, 2 * which + turn],
+            device_id=place,
+            device_id_type=MESH,
+        )
+
+    def near(which, source, there):
+        return pltpu.make_async_copy(
+            source.at[from_seq[0]],
+            there.at[pl.ds(0, source.shape[1])],
+            move_sems.at[1, 2 * which],
+        )
+
+    def move(which, source, there):
+        far(which, 1, source, there).start()
+
+        @pl.when(stay)
+        def _():
+            near(which, source, there).start()
+
+        @pl.when(jnp.logical_not(stay))
+        def _():
+            far(which, 0, source, there).start()
+
+    def moved_out(which, source, there):
+        far(which, 1, source, there).wait_send()
+
+        @pl.when(jnp.logical_not(stay))
+        def _():
+            far(which, 0, source, there).wait_send()
+
+    def moved_in(which, source, there):
+        far(which, 1, source, there).wait_recv()
+
+        @pl.when(stay)
+        def _():
+            near(which, source, there).wait()
+
+        @pl.when(jnp.logical_not(stay))
+        def _():
+            far(which, 0, source, there).wait_recv()
+
+    moves = ((0, clip_ref, clip.at[0, 0]), (1, small_ref, xs), (2, large_ref, xl), (3, cot_ref, cot))
+    move(*moves[0])
+    move(*moves[1])
+    loads = [
+        pltpu.make_async_copy(source, there, load_sems.at[i])
+        for i, (source, there) in enumerate(zip(weight_refs, weights))
+    ]
+    for load in loads:
+        load.start()
+    moved_out(*moves[0])
+    moved_out(*moves[1])
+    move(*moves[2])
+    outs = []
+
+    def keep(source, there):
+        copy = pltpu.make_async_copy(source, there, out_sems.at[len(outs)])
+        copy.start()
+        outs.append(copy)
+
+    def front_into(x, n_ref, q_ref, kv):
+        normed = norm(x[...].astype(f32), first_gain[...])
+        n_ref[...] = normed
+        keys = dot(normed, wk[...]).astype(bf16)
+        values = dot(normed, wv[...]).astype(bf16)
+        for pair in range(pairs):
+            lanes = slice(pair * LANES, (pair + 1) * LANES)
+            kv[0, pair, 0] = keys[:, lanes]
+            kv[0, pair, 1] = values[:, lanes]
+
+    def query_into(n_ref, q_ref):
+        query = (dot(n_ref[...], wq[...]) * Q_SCALE).astype(bf16)
+        for pair in range(pairs):
+            q_ref[pair] = query[:, pair * LANES : (pair + 1) * LANES]
+
+    large, small = Gather(here, kvl, gather_l), Gather(here, kvs, gather_s)
+    cross, clips = Gather(here, ckv, gather_c), Gather(here, clip, gather_clip)
+
+    moved_in(*moves[0])
+    for kind in (0, 1):
+        clips.copy(kind, 0, 1, 0).start()
+    moved_in(*moves[1])
+    keep(xs, xs_out)
+    for i in (0, 1, 2):
+        loads[i].wait()
+    front_into(xs, ns_ref, qs_ref, kvs)
+    for kind in (0, 1):
+        small.copy(kind, 0, pairs, 0).start()
+    query_into(ns_ref, qs_ref)
+    clips.copy(0, 0, 1, 0).wait_recv()
+    clips.copy(2, 0, 1, 0).start()
+    for kind in (1, 2):
+        clips.copy(kind, 0, 1, 0).wait_recv()
+
+    few = clip.shape[2]
+    spot = lax.broadcasted_iota(jnp.int32, (1, LANES), 1) % HALF
+    number = spot.astype(f32)
+    some = spot < 4
+    row = lax.broadcasted_iota(jnp.int32, (2 * few, few), 0) // 2
+    twice = jnp.where(row == lax.broadcasted_iota(jnp.int32, (2 * few, few), 1), 1.0, 0.0)
+    twice = twice.astype(bf16)
+    for part in range(4):
+        mine = clip[part, 0]
+        for value, mk_ref, mq_ref in (
+            (mine.astype(f32), mks_ref, mqs_ref),
+            (dot(twice, mine), mkl_ref, mql_ref),
+        ):
+            rows = value.shape[0]
+            mk_ref[pl.ds(part * rows, rows), :] = jnp.where(
+                some & (value != number), NEGATIVE, 0.0
+            ).astype(bf16)
+            if part == 0:
+                mq_ref[...] = jnp.where(some & (value == number), 1.0, 0.0).astype(bf16)
+
+    moved_in(*moves[2])
+    moved_out(*moves[2])
+    move(*moves[3])
+    keep(xl, xl_out)
+    front_into(xl, nl_ref, ql_ref, kvl)
+    third = pairs // 3
+    small.copy(0, 0, pairs, 0).wait_send()
+    large.copy(0, 0, third, 0).start()
+    for group in range(3):
+        large.copy(1, group * third, third, group).start()
+    query_into(nl_ref, ql_ref)
+
+    small.copy(0, 0, pairs, 0).wait_recv()
+    small.copy(2, 0, pairs, 0).start()
+    small.copy(1, 0, pairs, 0).wait_recv()
+    small.copy(2, 0, pairs, 0).wait_recv()
+    keep(kvs, kvs_out)
+
+    def small_pair(pair, carry):
+        attend_pair(pair, qs_ref, kvs, mqs_ref, mks_ref, spaces, os_ref, ls_ref)
+        return carry
+
+    lax.fori_loop(0, pairs, small_pair, 0)
+    loads[3].wait()
+    for pair in range(pairs):
+        wide[:, pair * LANES : (pair + 1) * LANES] = os_ref[pair]
+    hidden = xs[...].astype(f32) + dot(wide[...], wo[...])
+    hidden_ref[...] = hidden
+    second_ref[...] = norm(hidden, second_gain[...])
+    total[...] = hidden
+    loads[4].wait()
+    loads[5].wait()
+    width = wide.shape[1]
+    steps = up.shape[1] // width
+    for step in range(steps):
+        lanes = slice(step * width, (step + 1) * width)
+        active, slope = gelu_both(dot(second_ref[...], up[:, lanes]))
+        active = active.astype(bf16)
+        active_ref[:, lanes] = active
+        slope_ref[:, lanes] = slope.astype(bf16)
+        total[...] += dot(active, down[lanes, :])
+        if step == steps // 2:
+            large.copy(0, 0, third, 0).wait_send()
+            large.copy(0, third, third, 1).start()
+    merged = total[...]
+    merged_ref[...] = merged
+    context = norm(merged, context_gain[...])
+    context_ref[...] = context
+    loads[6].wait()
+    loads[7].wait()
+    keys = dot(context, wck[...]).astype(bf16)
+    values = dot(context, wcv[...]).astype(bf16)
+    for pair in range(pairs):
+        lanes = slice(pair * LANES, (pair + 1) * LANES)
+        ckv[0, pair, 0] = keys[:, lanes]
+        ckv[0, pair, 1] = values[:, lanes]
+    cross.copy(1, 0, pairs, 0).start()
+
+    def large_pair(pair, carry):
+        attend_pair(pair, ql_ref, kvl, mql_ref, mkl_ref, spaces, ol_ref, ll_ref)
+        return carry
+
+    for group in range(3):
+        at = group * third
+        large.copy(0, at, third, group).wait_recv()
+        large.copy(2, at, third, group).start()
+        if group == 0:
+            large.copy(0, third, third, 1).wait_send()
+            large.copy(0, 2 * third, third, 2).start()
+        if group == 2:
+            large.copy(0, 2 * third, third, 2).wait_send()
+            cross.copy(0, 0, pairs, 0).start()
+        large.copy(1, at, third, group).wait_recv()
+        large.copy(2, at, third, group).wait_recv()
+        if group == 2:
+            keep(kvl, kvl_out)
+        lax.fori_loop(at, at + third, large_pair, 0)
+    moved_in(*moves[3])
+    moved_out(*moves[3])
+    keep(cot, cot_out)
+    cross.copy(0, 0, pairs, 0).wait_recv()
+    cross.copy(2, 0, pairs, 0).start()
+    cross.copy(1, 0, pairs, 0).wait_recv()
+    cross.copy(2, 0, pairs, 0).wait_recv()
+    keep(ckv, ckv_out)
+    for copy in [small.copy(1, 0, pairs, 0), small.copy(2, 0, pairs, 0)]:
+        copy.wait_send()
+    for kind in (0, 1, 2):
+        clips.copy(kind, 0, 1, 0).wait_send()
+        cross.copy(kind, 0, pairs, 0).wait_send()
+        if kind:
+            for group in range(3):
+                large.copy(kind, group * third, third, group).wait_send()
+    for copy in outs:
+        copy.wait()
+
+
+def begin(large, small, cotangent, clip, weights, gains):
+    seqs, count, width = large.shape
+    few = small.shape[1]
+    count, few = 2 * count, 2 * few
+    pairs = width // LANES
+    hidden = weights[4].shape[1]
+    shape = jax.ShapeDtypeStruct
+    kv_l, kv_s = (4, pairs, 2, count, LANES), (4, pairs, 2, few, LANES)
+    anywhere = pl.BlockSpec(memory_space=pl.ANY)
+    vmem = pl.BlockSpec(memory_space=pltpu.VMEM)
+    out_shape = [
+        shape((count, width), bf16),
+        shape((few, width), bf16),
+        shape((count, width), bf16),
+        shape(kv_l, bf16),
+        shape(kv_s, bf16),
+        shape(kv_s, bf16),
+        shape((count, width), bf16),
+        shape((few, width), bf16),
+        shape((pairs, count, LANES), bf16),
+        shape((pairs, few, LANES), bf16),
+        shape((pairs, count, LANES), bf16),
+        shape((pairs, count, LANES), f32),
+        shape((pairs, few, LANES), bf16),
+        shape((pairs, few, LANES), f32),
+        shape((few, width), f32),
+        shape((few, width), f32),
+        shape((few, width), bf16),
+        shape((few, hidden), bf16),
+        shape((few, hidden), bf16),
+        shape((few, width), bf16),
+        shape((count, LANES), bf16),
+        shape((4 * count, LANES), bf16),
+        shape((few, LANES), bf16),
+        shape((4 * few, LANES), bf16),
+    ]
+    dma = pltpu.SemaphoreType.DMA
+    scratch = [
+        pltpu.VMEM((count, width), bf16),
+        pltpu.VMEM((few, width), bf16),
+        pltpu.VMEM((count, width), bf16),
+        pltpu.VMEM((4, 1, few, LANES), bf16),
+        pltpu.VMEM(kv_l, bf16),
+        pltpu.VMEM(kv_s, bf16),
+        pltpu.VMEM(kv_s, bf16),
+    ]
+    scratch += [pltpu.VMEM(weight.shape, bf16) for weight in weights]
+    scratch += [pltpu.VMEM((4 * count, LANES), bf16)] * 4
+    scratch += [pltpu.VMEM((few, width), bf16), pltpu.VMEM((few, width), f32)]
+    scratch += [dma((2, 8)), dma((2, 9)), dma((2, 3)), dma((2, 3)), dma((2, 3)), dma((8,)), dma((6,))]
+    return pl.pallas_call(
+        functools.partial(begin_kernel, pairs),
+        in_specs=[anywhere] * 12 + [vmem] * 3,
+        out_specs=[anywhere] * 6 + [vmem] * 18,
+        out_shape=out_shape,
+        scratch_shapes=scratch,
+        compiler_params=pltpu.CompilerParams(
+            vmem_limit_bytes=62 << 20, collective_id=4, has_side_effects=True
+        ),
+        cost_estimate=pl.CostEstimate(
+            flops=16 * count * 4 * count * width + 18 * few * width * hidden,
+            bytes_accessed=40 << 20,
+            transcendentals=count * count * 4 * width // HALF,
+        ),
+        name="begin",
+    )(large, small, cotangent, clip, *weights, *gains)
+
+
+def cross_attend_kernel(q_ref, kv_ref, mq_ref, mk_ref, o_ref, l_ref, *spaces):
+    attend_pair(0, q_ref, kv_ref, mq_ref, mk_ref, spaces, o_ref, l_ref)
+
+
+def cross_attend(query, kv, mask_q, mask_k):
+    pairs, count = query.shape[:2]
+    rows = kv.shape[3]
+    one = pl.BlockSpec((1, count, LANES), lambda i: (i, 0, 0))
+    return pl.pallas_call(
+        cross_attend_kernel,
+        grid=(pairs,),
+        in_specs=[
+            one,
+            pl.BlockSpec((4, 1, 2, rows, LANES), lambda i: (0, i, 0, 0, 0)),
+            whole((count, LANES)),
+            whole((4 * rows, LANES)),
+        ],
+        out_specs=[one, one],
+        out_shape=[
+            jax.ShapeDtypeStruct(query.shape, bf16),
+            jax.ShapeDtypeStruct(query.shape, f32),
+        ],
+        scratch_shapes=[pltpu.VMEM((4 * rows, LANES), bf16)] * 4,
+        compiler_params=pltpu.CompilerParams(vmem_limit_bytes=40 << 20),
+        cost_estimate=pl.CostEstimate(
+            flops=64 * count * rows * pairs * LANES,
+            bytes_accessed=32 * count * pairs * LANES,
+            transcendentals=8 * count * rows * pairs,
+        ),
+        name="cross_attend",
+    )(query, kv, mask_q, mask_k)
 
 
 def after(value, *needed):
     return lax.optimization_barrier((value, needed))[0]
 
 
-SELVES_ORDERS = (BY_Y, BY_ZL, BY_Y, BY_ZL)
+CROSS_ORDERS = (BY_Y[:3], BY_ZL[:3])
+SELVES_ORDERS = (BY_Y[:3], BY_ZL[:3], BY_X, LATE_ORDER, LATE_ORDER)
+SELVES_ENDS = (False, False, True, True, True)
 SELVES_STAGES = (
-    (0, 4, 6, 8, 9, 11),
-    (0, 4, 6, 8, 9, 11),
-    (0, 4, 6, 8, 10, 11),
-    (0, 6, 8, 9, 10, 11),
+    (0, 4, 11),
+    (0, 5, 11),
+    (0, 2, 4, 6, 8, 9, 10),
+    (2, 4, 6, 7),
+    (2, 4, 6, 7),
 )
 
 
-def paired_end(views, weights, large, large_kv, small, small_kv, grads, normed, gains, united_view, restore):
-    large_view, small_view, large_hidden, small_hidden, first_gain = views
-    up_grad, down_grad, output_grad, cross_parts = grads
+def paired_end(views, normed, large, small, cross, merged, weights, crosses, gains, united_view, restore):
+    large_view, small_view = views
+    large_normed, small_normed, asked, context = normed
+    large_q, large_mixed, large_logsum, large_mask_q, large_mask_k, large_kv = large
+    small_q, small_mixed, small_logsum, small_mask_q, small_mask_k, small_kv = small
+    cross_q, united, cross_logsum, cross_kv, united_grad, grad_out = cross
+    large_merged, large_saved, small_merged, small_saved = merged
+    query_weight, key_weight, value_weight, output_weight, up_weight, down_weight = weights
+    first_gain, second_gain, query_gain, context_gain = gains
     width = large_view.shape[1]
     rows = width // 8
-    names = ("core", "y", "zh", "zl", "x")
-    turn = [names.index(name) for name in SELVES_ORDERS[3]] + [5, 6]
-    cross = jnp.stack(cross_parts).reshape(2, 2, 2, 2, 2, rows, width)
-    cross = jnp.transpose(cross, turn).reshape(32, rows, width)
+    large_grad, small_grad, first, other, query_gain_grad, context_gain_grad = cross_back(
+        (cross_q, united_grad, united, cross_logsum, large_mask_q, small_mask_k),
+        cross_kv,
+        (asked, context, united, grad_out, large_merged, small_merged) + crosses,
+        (query_gain, context_gain),
+    )
+    (
+        large_hidden, small_hidden, large_mixed_grad, small_mixed_grad, up_grad, down_grad,
+        output_grad, second_gain_grad, first, other,
+    ) = back(
+        large_grad, small_grad, large_saved, small_saved, [large_mixed], small_mixed, output_weight,
+        second_gain, up_weight, down_weight, True, (first, other), CROSS_ORDERS,
+    )
+    eight = (8, 4 * rows, width)
+    four = (4, rows // 2, width)
     selves, sums = selves_back(
-        large, large_kv, small, small_kv, (up_grad, down_grad, output_grad, cross),
-        SELVES_ORDERS, SELVES_STAGES,
-    )
+        (large_q, large_mixed_grad, large_mixed, large_logsum, large_mask_q, large_mask_k),
+        large_kv,
+        (small_q, small_mixed_grad, small_mixed, small_logsum, small_mask_q, small_mask_k),
+        small_kv,
+        (
+            up_grad.reshape(eight), down_grad.reshape(eight), output_grad,
+            first.reshape(four), other.reshape(four),
+        ),
+        SELVES_ORDERS, SELVES_ENDS, SELVES_STAGES,
+    )
+    up, down, output, first, other = sums
     large_grad, small_grad, gain = view_grads(
-        selves, large_view, small_view, large_hidden, small_hidden, first_gain, weights
+        selves, large_view, small_view, large_hidden, small_hidden, first_gain,
+        (query_weight, key_weight, value_weight),
     )
     large_grad, small_grad = restore(large_grad), restore(small_grad)
-    gains = jnp.concatenate((gain,) + gains + (jnp.zeros((4, width), f32),), axis=0)
-    last, gains = last_sums(selves, *normed, gains)
+    gains = jnp.concatenate(
+        (gain, second_gain_grad, query_gain_grad, context_gain_grad, jnp.zeros((4, width), f32)),
+        axis=0,
+    )
+    last, late, gains = last_sums(
+        selves, large_normed, small_normed, gains,
+        (up.reshape(4, rows, width), down.reshape(4, rows, width)),
+    )
+    up, down = (total.astype(f32) for total in late)
 
     def square(total):
         total = total.astype(f32).reshape(2, 2, width // 16, width // 2)
         return jnp.transpose(total, (0, 2, 1, 3)).reshape(rows, width)
 
-    up, down, output, cross = (total.astype(f32) for total in sums)
+    first = first.astype(f32).reshape(2, rows, width)
+    other = other.astype(f32).reshape(2, rows, width)
     at = lax.axis_index("tm") * rows
     gains = [lax.dynamic_slice(gains, (i, at), (1, rows))[0] for i in range(4)]
     return (
@@ -1122,10 +1748,10 @@
         down.reshape(4 * rows, width),
         gains[2],
         gains[3],
-        cross[1],
-        cross[2],
-        cross[3],
-        cross[0],
+        first[1],
+        other[0],
+        other[1],
+        first[0],
     )
 
 
@@ -1221,6 +1847,42 @@
             total = total + by_x(sums[:, d * rows : (d + 1) * rows], -d).astype(f32)
         return total.astype(bf16)
 
+    if side == 2:
+        clip = jnp.broadcast_to(
+            clip_ids[:, ::2].astype(bf16)[:, :, None], (seqs, count // 2, LANES)
+        )
+        (
+            large, small, grad_out, large_kv, small_kv, cross_kv, large_normed, small_normed,
+            large_q, small_q, large_mixed, large_logsum, small_mixed, small_logsum, small_merged,
+            *small_saved, context, large_mask_q, large_mask_k, small_mask_q, small_mask_k,
+        ) = begin(
+            large_view, small_view, cotangent, clip,
+            (query_weight, key_weight, value_weight, output_weight, up_weight, down_weight,
+             cross_key, cross_value),
+            (first_gain, second_gain, context_gain),
+        )
+        united_grad = dot(grad_out, cross_output, NT).astype(bf16)
+        large_merged, *large_saved, asked, cross_q = rest(
+            large, [large_mixed], output_weight, second_gain, up_weight, down_weight,
+            query_gain, (cross_query,),
+        )
+        united, cross_logsum = cross_attend(cross_q, cross_kv, large_mask_q, small_mask_k)
+        flat = jnp.transpose(united, (1, 0, 2)).reshape(2 * count, width)
+        united_view = restore((large_merged + dot(flat, cross_output)).astype(bf16))
+        return paired_end(
+            (large, small),
+            (large_normed, small_normed, asked, context),
+            (large_q, large_mixed, large_logsum, large_mask_q, large_mask_k, large_kv),
+            (small_q, small_mixed, small_logsum, small_mask_q, small_mask_k, small_kv),
+            (cross_q, united, cross_logsum, cross_kv, united_grad, grad_out),
+            (large_merged, large_saved, small_merged, small_saved),
+            (query_weight, key_weight, value_weight, output_weight, up_weight, down_weight),
+            (cross_query, cross_key, cross_value),
+            (first_gain, second_gain, query_gain, context_gain),
+            united_view,
+            restore,
+        )
+
     groups = 3
     part = width // groups
     short_clips = gather(relocate(clip_ids[:, ::2].astype(f32)), 0)
@@ -1357,22 +2019,8 @@
         second_gain_grad,
     ) = back(
         large_merged_grad, small_merged_grad, large_saved, small_saved, [large_mixed], small_mixed,
-        output_weight, second_gain, up_weight, down_weight, side == 2,
-    )
-    if side == 2:
-        return paired_end(
-            (large, small, large_hidden_grad, small_hidden_grad, first_gain),
-            (query_weight, key_weight, value_weight),
-            (large_q, large_mixed_grad, large_mixed, large_logsum, large_mask_q, large_mask_k),
-            large_kv,
-            (small_q, small_mixed_grad, small_mixed, small_logsum, small_mask_q, small_mask_k),
-            small_kv,
-            (up_grad, down_grad, output_grad, cross_parts),
-            (large_normed, small_normed),
-            (second_gain_grad, query_gain_grad, context_gain_grad),
-            united_view,
-            restore,
-        )
+        output_weight, second_gain, up_weight, down_weight, False,
+    )
     cross_sum = Sum(jnp.concatenate(cross_parts, axis=1), by_y)
     up_sum = Sum(up_grad, by_y)
     down_sum = Sum(down_grad, by_zl)

time: 485 us -> 413 us (0.85)
  waiting for transfers between devices: 70 us -> 0.16 us
  Pallas kernels: 301 us -> 355 us
  starting transfers between devices: 46 us -> 13.1 us
  other arithmetic: 20.9 us -> 9.19 us
  local copies, waits for them, and re-layouts: 29.9 us -> 24.8 us
    ppermute x36 -> x6, waiting for transfers between devices: 70 us -> 0.16 us  [permute(): return lax.ppermute(value, ('tm', 'seq'), pairs)]
    pallas_call x10 -> x4, Pallas kernels: 207 us -> 244 us  [the longest x1 104 us: begin(): pl.pallas_call(functools.partial(begin_kernel, pairs), in_specs=[anywhere...]
    ppermute x36 -> x6, starting transfers between devices: 46 us -> 13.1 us  [permute(): return lax.ppermute(value, ('tm', 'seq'), pairs)]
    pallas_call x1, Pallas kernels: 31.2 us -> 49.1 us  [last_sums(): pl.pallas_call(functools.partial(last_kernel, width // LANES, (count, few...]
    pallas_call x2 -> x1, Pallas kernels: 26.4 us -> 15.2 us  [rest(): pl.pallas_call(functools.partial(rest_kernel, steps, len(mixed), is_query...]
    pallas_call x1, Pallas kernels: 28.7 us -> 39.5 us  [back(): pl.pallas_call(functools.partial(back_kernel, steps, len(mixed_l), (large...]
    unnamed x162 -> x76, local copies, waits for them, and re-layouts: 19.9 us -> 13.1 us
    select_n x5 -> x0, other arithmetic: 5.24 us -> none  [the longest x4 5.24 us: relocate(): far = jnp.where(odd, value[0], value[1])]
  transfers between devices with their start and end apart: 36 -> 6, of which waited for: 13 -> 1; matrix products, arithmetic and copies ran while one was open for 6% -> 4% of each run, Pallas kernels for 11% -> 54%
where the time goes in v3:
time: 413 us; the launch traced here: 408 us
  Pallas kernels  355 us (86%)
  local copies, waits for them, and re-layouts  24.8 us (6%)
  starting transfers between devices  13.1 us (3%)
  other arithmetic  9.19 us (2%)
    pallas_call x1, Pallas kernels, begin(): pl.pallas_call(functools.partial(begin_kernel, pairs), in_specs=[anywhere...  104 us
    pallas_call x1, Pallas kernels, selves_back(): pl.pallas_call(functools.partial(selves_kernel, pairs, (orders, ends, sta...  89.3 us
    pallas_call x1, Pallas kernels, last_sums(): pl.pallas_call(functools.partial(last_kernel, width // LANES, (count, few...  49.1 us
    pallas_call x1, Pallas kernels, back(): pl.pallas_call(functools.partial(back_kernel, steps, len(mixed_l), (large...  39.5 us
    pallas_call x1, Pallas kernels, cross_back(): pl.pallas_call(functools.partial(cross_kernel, pairs, block), grid=(pairs...  36.9 us
    pallas_call x1, Pallas kernels, rest(): pl.pallas_call(functools.partial(rest_kernel, steps, len(mixed), is_query...  15.2 us
    pallas_call x1, Pallas kernels, cross_attend(): pl.pallas_call(cross_attend_kernel, grid=(pairs,), in_specs=[one, pl.Bloc...  13.6 us
    unnamed x76, local copies, waits for them, and re-layouts  13.1 us
  transfers between devices with their start and end apart: 6, of which 1 were waited for; matrix products, arithmetic and copies ran while one was open for 4% of the time, Pallas kernels for 54%

profile of v3, /device:TPU:1, one launch (start us, length us, event | category | flops | bytes accessed | tf_op | source)
XLA Modules:
  0.0 407.8 jit_solution(14958058706943664257)
XLA Ops:
  1.7 1.3 reshape.170.refs_12_.refs_8_
  2.9 1.3 reshape.172.refs_13_.refs_3_
  4.2 1.3 reshape.174.refs_14_.refs_17_
  6.9 104.3 %begin.1 = (bf16[512,768]{1,0:T(8,128)(2,1)}, bf16[256,768]{1,0:T(8,128)(2,1)}, bf16[512,768]{1,0:T(8,128)(2,1)}, bf16[4,6,2,512,128]{4,3,2,1,0:T(8,128)(2,1)}, ...) custom-call(bf16[2,256,768]{2,1,0:T(8,128)(2,1)} %refs_0_.1, ...), custom_call_target="tpu_custom_call" | custom-call | flops 23756537856 | bytes 41943040 | tf_op jit(solution)/shard_map/begin/pallas_call | solution.py:1609
  112.3 1.3 copy-done.16
  113.6 1.1 copy-done.20
  114.7 15.2 %rest.1 = (f32[512,768]{1,0:T(8,128)}, f32[512,768]{1,0:T(8,128)}, bf16[512,768]{1,0:T(8,128)(2,1)S(1)}, bf16[512,3072]{1,0:T(8,128)(2,1)}, bf16[512,3072]{1,0:T...) custom-call(bf16[512,768]{1,0:T(8,128)(2,1)S(1)} %copy-done.2, ...), custom_call_target="tpu_custom_call" | custom-call | flops 6039797760 | bytes 25559040 | tf_op jit(solution)/shard_map/rest/pallas_call | solution.py:337
  130.0 13.6 %cross_attend.1 = (bf16[6,512,128]{2,1,0:T(8,128)(2,1)S(1)}, f32[6,512,128]{2,1,0:T(8,128)S(1)}) custom-call(bf16[6,512,128]{2,1,0:T(8,128)(2,1)S(1)} %get-tuple-element.87.q_ref.refs_0_, bf16[4,6,2,256,128]{4,3,2,1,0:T(8,128)(2,1)S(1)} %copy-done.19, bf16[512,128]{1,0:T(8,128)(2,1)S(1)} %copy-done.26, bf16[1024,128]{1,0:T(8,128)(2,1)S(1)} %copy-done.25), custom_call_target="tpu_custom_call" | custom-call | flops 6442450944 | bytes 12582912 | tf_op jit(solution)/shard_map/cross_attend/pallas_call | solution.py:1635
  145.1 2.2 add_convert_fusion
  148.3 1.9 collective-permute-start.1
  151.2 1.7 convolution_convert_fusion.refs_1_
  152.9 36.9 %cross_back.1 = (f32[512,768]{1,0:T(8,128)}, f32[256,768]{1,0:T(8,128)}, bf16[8,192,768]{2,1,0:T(8,128)(2,1)}, bf16[8,192,768]{2,1,0:T(8,128)(2,1)}, f32[1,768]{1,0:T(1,128)}, /*index=5*/f32[1,768]{1,0:T(1,128)}) custom-call(bf16[6,512,128]{2,1,0:T(8,128)(2,1)} %copy-done.23, bf16[512,768]{1,0:T(8,128)(2,1)} %convolution_convert_fusion.refs_1_, ...), custom_call_target="tpu_custom_call" | custom-call | flops 8053063680 | bytes 25165824 | tf_op jit(solution)/shard_map/cross_back/pallas_call | solution.py:1219
  189.8 39.5 %back.1 = (f32[512,768]{1,0:T(8,128)}, f32[256,768]{1,0:T(8,128)}, bf16[512,768]{1,0:T(8,128)(2,1)}, bf16[256,768]{1,0:T(8,128)(2,1)}, bf16[32,96,768]{2,1,0:T(8...) custom-call(f32[512,768]{1,0:T(8,128)} %get-tuple-element.98.refs_0_, ...), custom_call_target="tpu_custom_call" | custom-call | flops 16307453952 | bytes 44826624 | tf_op jit(solution)/shard_map/back/pallas_call | solution.py:482
  229.3 89.3 %selves_back.1 = (bf16[512,768]{1,0:T(8,128)(2,1)}, bf16[6,2,512,128]{3,2,1,0:T(8,128)(2,1)}, bf16[256,768]{1,0:T(8,128)(2,1)}, bf16[6,2,256,128]{3,2,1,0:T(8,12...) custom-call(bf16[6,512,128]{2,1,0:T(8,128)(2,1)} %get-tuple-element., ...), custom_call_target="tpu_custom_call" | custom-call | flops 20132659200 | bytes 25165824 | tf_op jit(solution)/shard_map/selves_back/pallas_call | solution.py:958
  319.9 1.1 copy-done.6
  322.0 7.3 %view_grads.1 = (bf16[512,768]{1,0:T(8,128)(2,1)S(1)}, bf16[256,768]{1,0:T(8,128)(2,1)S(1)}, f32[1,768]{1,0:T(1,128)S(1)}) custom-call(bf16[512,768]{1,0:T(8,128)(2,1)S(1)} %copy-done.4, bf16[6,2,512,128]{3,2,1,0:T(8,128)(2,1)} %get-tuple-element.126.refs_1_, bf16[256,768]{1,0:T(8,128)(2,1)S(1)} %copy-done.11, bf16[6,2,256,128]{3,2,1,0:T(8,128)(2,1)S(1)} %copy-done.6, ...), custom_call_target="tpu_custom_call" | custom-call | flops 2717908992 | bytes 15335424 | tf_op jit(solution)/shard_map/view_grads/pallas_call | solution.py:1006
  330.2 4.7 %collective-permute-start.3 = (bf16[256,768]{1,0:T(8,128)(2,1)}, bf16[256,768]{1,0:T(8,128)(2,1)}, u32[]{:S(2)}, u32[]{:S(2)}) collective-permute-start(bf16[256,768]{1,0:T(8,128)(2,1)} %get-tuple-element.152), channel_id=1, source_target_pairs={{0,0},{1,16},{2,2},{3,18},{4,4},{5,20},{6,6},{7,22},{8,8},{9,24},{... | collective-permute-start | bytes 1179656 | tf_op jit(solution)/shard_map/ppermute | solution.py:1804
  336.4 2.5 collective-permute-start.5
  341.1 49.1 %last_sums.1 = (bf16[4,48,384]{2,1,0:T(8,128)(2,1)S(1)}, bf16[4,48,384]{2,1,0:T(8,128)(2,1)S(1)}, bf16[4,48,384]{2,1,0:T(8,128)(2,1)S(1)}, bf16[4,96,768]{2,1,0:...) custom-call(bf16[512,768]{1,0:T(8,128)(2,1)S(1)} %copy-done.5, ...), custom_call_target="tpu_custom_call" | custom-call | flops 18119393280 | bytes 23592960 | tf_op jit(solution)/shard_map/last_sums/pallas_call | solution.py:1110
  392.6 2.3 collective-permute-start.4
  398.5 1.1 copy.45
  400.4 2.0 fusion.1
  402.4 2.5 maximum_select_fusion
  404.9 2.6 fusion
  (103 shorter events, 20.2 us)
Async XLA Ops:
  0.7 144.4 %copy-start = (bf16[768,768]{1,0:T(8,128)(2,1)S(1)}, bf16[768,768]{1,0:T(8,128)(2,1)}, u32[]{:S(2)}) copy-start(bf16[768,768]{1,0:T(8,128)(2,1)} %param.34) | copy-start | bytes 3538948
  6.2 105.0 %copy-start.15 = (f32[1,768]{1,0:T(1,128)}, f32[1,768]{1,0:T(1,128)S(1)}, u32[]{:S(2)}) copy-start(f32[1,768]{1,0:T(1,128)S(1)} %reshape.176.refs_6_.refs_16_) | copy-start | bytes 9220
  6.9 104.3 %copy-start.14 = (f32[1,768]{1,0:T(1,128)S(1)}, f32[1,768]{1,0:T(1,128)}, u32[]{:S(2)}) copy-start(f32[1,768]{1,0:T(1,128)} %reshape.172.refs_13_.refs_3_) | copy-start | bytes 9220
  114.7 15.2 %copy-start.19 = (bf16[4,6,2,256,128]{4,3,2,1,0:T(8,128)(2,1)S(1)}, bf16[4,6,2,256,128]{4,3,2,1,0:T(8,128)(2,1)}, u32[]{:S(2)}) copy-start(bf16[4,6,2,256,128]{4,3,2,1,0:T(8,128)(2,1)} %get-tuple-element.88.kv_ref.refs_6_) | copy-start | bytes 9437188
  114.7 15.2 %copy-start.25 = (bf16[1024,128]{1,0:T(8,128)(2,1)S(1)}, bf16[1024,128]{1,0:T(8,128)(2,1)}, u32[]{:S(2)}) copy-start(bf16[1024,128]{1,0:T(8,128)(2,1)} %get-tuple-element.90.mk_ref.refs_5_.refs_12_) | copy-start | bytes 786436
  114.7 15.2 %copy-start.26 = (bf16[512,128]{1,0:T(8,128)(2,1)S(1)}, bf16[512,128]{1,0:T(8,128)(2,1)}, u32[]{:S(2)}) copy-start(bf16[512,128]{1,0:T(8,128)(2,1)} %get-tuple-element.89.mq_ref.refs_4_) | copy-start | bytes 393220
  129.9 13.7 %copy-start.21 = (bf16[512,768]{1,0:T(8,128)(2,1)}, bf16[512,768]{1,0:T(8,128)(2,1)S(1)}, u32[]{:S(2)}) copy-start(bf16[512,768]{1,0:T(8,128)(2,1)S(1)} %get-tuple-element.104.refs_6_) | copy-start | bytes 2359300
  129.9 13.7 %copy-start.22 = (bf16[512,768]{1,0:T(8,128)(2,1)}, bf16[512,768]{1,0:T(8,128)(2,1)S(1)}, u32[]{:S(2)}) copy-start(bf16[512,768]{1,0:T(8,128)(2,1)S(1)} %get-tuple-element.95.refs_7_) | copy-start | bytes 2359300
  129.9 13.7 %copy-start.23 = (bf16[6,512,128]{2,1,0:T(8,128)(2,1)}, bf16[6,512,128]{2,1,0:T(8,128)(2,1)S(1)}, u32[]{:S(2)}) copy-start(bf16[6,512,128]{2,1,0:T(8,128)(2,1)S(1)} %get-tuple-element.87.q_ref.refs_0_) | copy-start | bytes 2359300
  148.3 254.0 %collective-permute-start.1 = (bf16[256,768]{1,0:T(8,128)(2,1)}, bf16[256,768]{1,0:T(8,128)(2,1)}, u32[]{:S(2)}, u32[]{:S(2)}) collective-permute-start(bf16[256,768]{1,0:T(8,128)(2,1)} %get-tuple-element.154), channel_id=1, source_target_pairs={{0,0},{1,16},{2,2},{3,18},{4,4},{5,20},{6,6},{7,22},{8,8},{9,24},{... | collective-permute-start | bytes 1179656 | tf_op jit(solution)/shard_map/ppermute | solution.py:1804
  150.2 252.1 %collective-permute-start = (bf16[256,768]{1,0:T(8,128)(2,1)}, bf16[256,768]{1,0:T(8,128)(2,1)}, u32[]{:S(2)}, u32[]{:S(2)}) collective-permute-start(bf16[256,768]{1,0:T(8,128)(2,1)} %get-tuple-element.153), channel_id=1, source_target_pairs={{0,8},{1,24},{2,10},{3,26},{4,12},{5,28},{6,14},{7,30},{8,0},{9,16... | collective-permute-start | bytes 1179656 | tf_op jit(solution)/shard_map/ppermute | solution.py:1804
  229.3 89.4 %copy-start.3 = (bf16[512,768]{1,0:T(8,128)(2,1)S(1)}, bf16[512,768]{1,0:T(8,128)(2,1)}, u32[]{:S(2)}) copy-start(bf16[512,768]{1,0:T(8,128)(2,1)} %get-tuple-element.84.refs_0_.refs_4_) | copy-start | bytes 2359300
  229.3 89.4 %copy-start.8 = (f32[256,768]{1,0:T(8,128)S(1)}, f32[256,768]{1,0:T(8,128)}, u32[]{:S(2)}) copy-start(f32[256,768]{1,0:T(8,128)} %get-tuple-element.131.refs_7_) | copy-start | bytes 2359300
  229.3 89.4 %copy-start.10 = (bf16[256,768]{1,0:T(8,128)(2,1)S(1)}, bf16[256,768]{1,0:T(8,128)(2,1)}, u32[]{:S(2)}) copy-start(bf16[256,768]{1,0:T(8,128)(2,1)} %get-tuple-element.129.refs_5_) | copy-start | bytes 1179652
  229.3 89.4 %copy-start.13 = (f32[1,768]{1,0:T(1,128)S(1)}, f32[1,768]{1,0:T(1,128)}, u32[]{:S(2)}) copy-start(f32[1,768]{1,0:T(1,128)} %reshape.170.refs_12_.refs_8_) | copy-start | bytes 9220
  322.0 17.0 %copy-start.17 = (bf16[1,384,768]{2,1,0:T(8,128)(2,1)S(1)}, bf16[1,384,768]{2,1,0:T(8,128)(2,1)}, u32[]{:S(2)}) copy-start(bf16[1,384,768]{2,1,0:T(8,128)(2,1)} %get-tuple-element.140) | copy-start | bytes 1769476
  322.0 17.0 %copy-start.18 = (bf16[1,384,768]{2,1,0:T(8,128)(2,1)S(1)}, bf16[1,384,768]{2,1,0:T(8,128)(2,1)}, u32[]{:S(2)}) copy-start(bf16[1,384,768]{2,1,0:T(8,128)(2,1)} %get-tuple-element.141) | copy-start | bytes 1769476
  329.3 9.7 %copy-start.5 = (bf16[512,768]{1,0:T(8,128)(2,1)S(1)}, bf16[512,768]{1,0:T(8,128)(2,1)}, u32[]{:S(2)}) copy-start(bf16[512,768]{1,0:T(8,128)(2,1)} %get-tuple-element.125.refs_0_) | copy-start | bytes 2359300
  329.3 9.7 %copy-start.7 = (bf16[6,2,256,128]{3,2,1,0:T(8,128)(2,1)S(1)}, bf16[6,2,256,128]{3,2,1,0:T(8,128)(2,1)}, u32[]{:S(2)}) copy-start(bf16[6,2,256,128]{3,2,1,0:T(8,128)(2,1)} %get-tuple-element.128.refs_3_) | copy-start | bytes 2359300
  329.3 9.7 %copy-start.12 = (bf16[256,768]{1,0:T(8,128)(2,1)S(1)}, bf16[256,768]{1,0:T(8,128)(2,1)}, u32[]{:S(2)}) copy-start(bf16[256,768]{1,0:T(8,128)(2,1)} %get-tuple-element.127.refs_2_) | copy-start | bytes 1179652
  330.2 74.6 %collective-permute-start.3 = (bf16[256,768]{1,0:T(8,128)(2,1)}, bf16[256,768]{1,0:T(8,128)(2,1)}, u32[]{:S(2)}, u32[]{:S(2)}) collective-permute-start(bf16[256,768]{1,0:T(8,128)(2,1)} %get-tuple-element.152), channel_id=1, source_target_pairs={{0,0},{1,16},{2,2},{3,18},{4,4},{5,20},{6,6},{7,22},{8,8},{9,24},{... | collective-permute-start | bytes 1179656 | tf_op jit(solution)/shard_map/ppermute | solution.py:1804
  335.0 69.9 %collective-permute-start.2 = (bf16[256,768]{1,0:T(8,128)(2,1)}, bf16[256,768]{1,0:T(8,128)(2,1)}, u32[]{:S(2)}, u32[]{:S(2)}) collective-permute-start(bf16[256,768]{1,0:T(8,128)(2,1)} %get-tuple-element.151), channel_id=1, source_target_pairs={{0,8},{1,24},{2,10},{3,26},{4,12},{5,28},{6,14},{7,30},{8,0},{9,16... | collective-permute-start | bytes 1179656 | tf_op jit(solution)/shard_map/ppermute | solution.py:1804
  336.4 56.2 %collective-permute-start.5 = (bf16[128,768]{1,0:T(8,128)(2,1)}, bf16[128,768]{1,0:T(8,128)(2,1)}, u32[]{:S(2)}, u32[]{:S(2)}) collective-permute-start(bf16[128,768]{1,0:T(8,128)(2,1)} %get-tuple-element.156), channel_id=1, source_target_pairs={{0,0},{1,16},{2,2},{3,18},{4,4},{5,20},{6,6},{7,22},{8,8},{9,24},{... | collective-permute-start | bytes 589832 | tf_op jit(solution)/shard_map/ppermute | solution.py:1804
  392.6 7.8 %collective-permute-start.4 = (bf16[128,768]{1,0:T(8,128)(2,1)S(1)}, bf16[128,768]{1,0:T(8,128)(2,1)S(1)}, u32[]{:S(2)}, u32[]{:S(2)}) collective-permute-start(bf16[128,768]{1,0:T(8,128)(2,1)S(1)} %get-tuple-element.155), channel_id=1, source_target_pairs={{0,8},{1,24},{2,10},{3,26},{4,12},{5,28},{6,14},{7,30},{8,0},{9,16... | collective-permute-start | bytes 589832 | tf_op jit(solution)/shard_map/ppermute | solution.py:1804
  (18 other events, 56.3 us)

commit v4 on v3

--- a/solution.py
+++ b/solution.py
@@ -437,19 +437,19 @@
         value = dot(mixed[...], branch[...], TN).astype(bf16)
         if laid:
             rows, wide = dwo_ref.shape[1:]
-            for at, (core, y, tm) in enumerate(spots(BY_X)):
+            for at, (core, y, tm) in enumerate(spots(BY_Y)):
                 first = (tm * 2 + core) * rows
                 dwo_ref[at] = value[first : first + rows, y * wide : (y + 1) * wide]
         else:
             dwo_ref[...] = value
 
     for flow in range(flows):
-        for stage, when in enumerate((0, 2, steps - 1)):
+        for stage, when in enumerate((0, steps - 1)):
 
             @pl.when(step == when)
             def _(flow=flow, stage=stage):
                 running[flow].act(stage + 1)
-                if stage == 2:
+                if stage == 1:
                     sums[flow][...] = running[flow].result()
 
 
@@ -573,7 +573,85 @@
         pl.semaphore_wait(barrier, len(partners))
 
 
-ALL_PARTNERS = (("core",), ("y",), ("zl",), ("x",), ("zh",), ("y", "core"))
+    def greet_line(self, *more):
+        barrier = pltpu.get_barrier_semaphore()
+        z, core = self.tm // 2, self.bit["core"]
+        places = [
+            (
+                lax.rem(z + dz, 4) * 2 + self.bit["x"],
+                self.bit["y"] * 2 + lax.rem(core + dc, 2),
+            )
+            for dz in range(4)
+            for dc in range(2)
+            if dz or dc
+        ] + [self.partner(name) for name in more]
+        for place in places:
+            pl.semaphore_signal(barrier, inc=1, device_id=place, device_id_type=MESH)
+        pl.semaphore_wait(barrier, len(places))
+
+
+ALL_PARTNERS = (("core",), ("y",), ("zl",), ("x",), ("zh",))
+
+
+class Restore:
+    def __init__(self, here, held, got, sems):
+        self.held, self.got, self.sems = held, got, sems
+        self.rows = got.shape[1]
+        z, core = here.tm // 2, here.bit["core"]
+        self.odd = lax.rem(z, 2)
+        self.stay = core == z // 2
+        turns = (self.odd, 1 - self.odd)
+        self.places = [
+            ((2 * core + turn) * 2 + here.bit["x"], here.bit["y"] * 2 + z // 2) for turn in turns
+        ]
+
+    def far(self, turn, arriving=False):
+        at = 1 - self.odd if arriving and turn else self.odd
+        return pltpu.make_async_remote_copy(
+            src_ref=self.held.at[pl.ds(turn * self.rows, self.rows)],
+            dst_ref=self.got.at[at],
+            send_sem=self.sems.at[0, turn],
+            recv_sem=self.sems.at[1, turn],
+            device_id=self.places[turn],
+            device_id_type=MESH,
+        )
+
+    def near(self):
+        return pltpu.make_async_copy(
+            self.held.at[pl.ds(0, self.rows)], self.got.at[self.odd], self.sems.at[1, 0]
+        )
+
+    def start(self):
+        self.far(1).start()
+
+        @pl.when(self.stay)
+        def _():
+            self.near().start()
+
+        @pl.when(jnp.logical_not(self.stay))
+        def _():
+            self.far(0).start()
+
+    def finish(self):
+        self.far(1).wait_send()
+        self.far(1, True).wait_recv()
+
+        @pl.when(self.stay)
+        def _():
+            self.near().wait()
+
+        @pl.when(jnp.logical_not(self.stay))
+        def _():
+            self.far(0).wait_send()
+            self.far(0).wait_recv()
+
+
+def restore_scratch(rows, width):
+    return [
+        pltpu.VMEM((2 * rows, width), bf16),
+        pltpu.VMEM((2, rows, width), bf16),
+        pltpu.SemaphoreType.DMA((2, 2)),
+    ]
 
 
 class Flow:
@@ -684,7 +762,7 @@
     return jax.ShapeDtypeStruct((left,) + block, bf16)
 
 
-def pair_back(query, grad, out, logsum, mask, keys_at, values_at, mk_ref, block, store):
+def pair_back(query, grad, out, logsum, mask, keys_at, values_at, mk_ref, block, exchange, pair):
     count = query.shape[0]
     total = keys_at.shape[0]
     lane = lax.broadcasted_iota(jnp.int32, (count, LANES), 1)
@@ -711,7 +789,7 @@
     spot_k = lane_k % HALF
     one = jnp.where((spot_k >= 4) & (spot_k < 7), 1.0, 0.0).astype(bf16)
     dq = jnp.zeros((count, LANES), f32)
-    for number in range(total // block):
+    for number in exchange.turns(total // block):
         here = pl.ds(number * block, block)
         keys, values = keys_at[here, :], values_at[here, :]
         side = mk_ref[here, :] + one
@@ -726,7 +804,7 @@
             dv += dot(prob.astype(bf16), grad_m[head], TN)
             dk += dot(score_grad, query_m[head], TN)
             dq += dot(score_grad, pick(keys, nought))
-        store(number, (dk * LN2).astype(bf16), dv.astype(bf16))
+        exchange.put(pair, number, block, (dk * LN2).astype(bf16), dv.astype(bf16))
     return (dq * HALF**-0.5).astype(bf16)
 
 
@@ -736,61 +814,75 @@
         self.sums, self.send, self.got_core, self.across, self.got_x = refs[:5]
         self.sems = refs[5]
 
-    def copy_core(self, pair):
+    def turns(self, blocks):
+        return (3, 1, 0, 2) if blocks == 4 else tuple(reversed(range(blocks)))
+
+    def copy_core(self, pair, far):
+        rows = pl.ds(far * self.rows, self.rows)
         return pltpu.make_async_remote_copy(
-            src_ref=self.send.at[pair % 2],
-            dst_ref=self.got_core.at[pair],
-            send_sem=self.sems.at[0, pair],
-            recv_sem=self.sems.at[1, pair],
+            src_ref=self.send.at[pair % 2, :, rows, :],
+            dst_ref=self.got_core.at[pair, :, rows, :],
+            send_sem=self.sems.at[2 * far, pair],
+            recv_sem=self.sems.at[2 * far + 1, pair],
             device_id=self.here.partner("core"),
             device_id_type=MESH,
         )
 
     def copy_x(self, pair):
         return pltpu.make_async_remote_copy(
-            src_ref=self.across.at[pair % 2],
+            src_ref=self.across.at[pair],
             dst_ref=self.got_x.at[pair],
-            send_sem=self.sems.at[2, pair],
-            recv_sem=self.sems.at[3, pair],
+            send_sem=self.sems.at[4, pair],
+            recv_sem=self.sems.at[5, pair],
             device_id=self.here.partner("x"),
             device_id_type=MESH,
         )
 
+    def end(self):
+        pairs = self.got_x.shape[0]
+        for pair in range(pairs):
+            if pair >= pairs - 2:
+                self.free(pair)
+            self.copy_x(pair).wait_send()
+
     def free(self, pair):
-        self.copy_core(pair).wait_send()
-
-    def put(self, pair, total, block):
-        half = total // 2
-
-        def store(number, dk, dv):
-            there = pl.ds(number * block % half, block)
-            if number * block < half:
-                self.sums[pair % 3, 0, there, :] = dk
-                self.sums[pair % 3, 1, there, :] = dv
-            else:
-                self.send[pair % 2, 0, there, :] = dk
-                self.send[pair % 2, 1, there, :] = dv
-
-        return store
-
-    def pass_on(self, pair, wait_before):
+        for far in (0, 1):
+            self.copy_core(pair, far).wait_send()
+
+    def put(self, pair, number, block, dk, dv):
+        half = 2 * self.rows
+        there = pl.ds(number * block % half, block)
+        ref, slot = (self.sums, pair) if number * block < half else (self.send, pair % 2)
+        ref[slot, 0, there, :] = dk
+        ref[slot, 1, there, :] = dv
+        if 2 * half == 4 * block:
+            if number == 3:
+                self.copy_core(pair, 1).start()
+            elif number == 2:
+                self.copy_core(pair, 0).start()
+            elif number == 0:
+                self.pass_on(pair)
+        elif number == 1:
+            for far in (1, 0):
+                self.copy_core(pair, far).start()
+        else:
+            self.pass_on(pair)
+
+    def pass_on(self, pair):
         rows = self.rows
-        self.copy_core(pair).wait_recv()
-        if wait_before:
-            self.copy_x(pair - 2).wait_send()
+        self.copy_core(pair, 1).wait_recv()
         far = pl.ds(rows, rows)
         for i in (0, 1):
-            self.across[pair % 2, i] = (
-                self.sums[pair % 3, i, far, :] + self.got_core[pair, i, far, :]
-            )
+            self.across[pair, i] = self.sums[pair, i, far, :] + self.got_core[pair, i, far, :]
         self.copy_x(pair).start()
 
     def take(self, pair, out_ref):
         near = pl.ds(0, self.rows)
+        self.copy_core(pair, 0).wait_recv()
         self.copy_x(pair).wait_recv()
         for i in (0, 1):
             out_ref[pair, i] = (
-                self.sums[pair % 3, i, near, :].astype(f32)
+                self.sums[pair, i, near, :].astype(f32)
                 + self.got_core[pair, i, near, :].astype(f32)
                 + self.got_x[pair, i].astype(f32)
             ).astype(bf16)
@@ -798,12 +890,12 @@
 
 def exchange_scratch(pairs, rows):
     return [
-        pltpu.VMEM((3, 2, 2 * rows, LANES), bf16),
+        pltpu.VMEM((pairs, 2, 2 * rows, LANES), bf16),
         pltpu.VMEM((2, 2, 2 * rows, LANES), bf16),
         pltpu.VMEM((pairs, 2, 2 * rows, LANES), bf16),
-        pltpu.VMEM((2, 2, rows, LANES), bf16),
         pltpu.VMEM((pairs, 2, rows, LANES), bf16),
-        pltpu.SemaphoreType.DMA((4, pairs)),
+        pltpu.VMEM((pairs, 2, rows, LANES), bf16),
+        pltpu.SemaphoreType.DMA((6, pairs)),
     ]
 
 
@@ -840,21 +932,6 @@
         for flow in running:
             flow.act(0)
 
-    def move(exchange, pair, out_ref):
-        exchange.copy_core(pair).start()
-
-        @pl.when((pair >= 1) & (pair < 3))
-        def _():
-            exchange.pass_on(pair - 1, False)
-
-        @pl.when(pair >= 3)
-        def _():
-            exchange.pass_on(pair - 1, True)
-
-        @pl.when(pair >= 2)
-        def _():
-            exchange.take(pair - 2, out_ref)
-
     def attention(exchange, pair, refs, kv_ref, keys_at, values_at, block, dq_ref):
         q_ref, do_ref, o_ref, l_ref, mq_ref, mk_ref = refs
         fill_keys(keys_at, values_at, kv_ref)
@@ -864,36 +941,30 @@
             exchange.free(pair - 2)
 
         dq_ref[...] = pair_back(
-            q_ref[0], do_ref[...], o_ref[0], l_ref[0], mq_ref[...],
-            keys_at, values_at, mk_ref, block, exchange.put(pair, keys_at.shape[0], block),
+            q_ref[0], do_ref[...], o_ref[0], l_ref[0], mq_ref[...], keys_at, values_at, mk_ref,
+            block, exchange, pair,
         )
 
-    @pl.when(step < pairs)
+    half = pairs // 2
+    late = step >= half + pairs
+
+    @pl.when((step >= half) & (step < half + pairs))
     def _():
-        attention(large, step, large_refs, kv_large, keys_l, values_l, blocks[0], dq_l)
-        move(large, step, dkv_l)
-
-    @pl.when(step >= pairs)
+        pair = step - half
+        attention(large, pair, large_refs, kv_large, keys_l, values_l, blocks[0], dq_l)
+
+    @pl.when((step < half) | late)
     def _():
-        pair = step - pairs
+        pair = jnp.where(late, step - pairs, step)
         attention(small, pair, small_refs, kv_small, keys_s, values_s, blocks[1], dq_s)
-        move(small, pair, dkv_s)
-
-    @pl.when(step == pairs)
-    def _():
-        large.pass_on(pairs - 1, True)
-        large.take(pairs - 2, dkv_l)
-
-    @pl.when(step == pairs + 1)
-    def _():
-        large.take(pairs - 1, dkv_l)
-        for pair in (pairs - 2, pairs - 1):
-            large.free(pair)
-            large.copy_x(pair).wait_send()
-
-    @pl.when(step == 2 * pairs - 1)
-    def _():
-        small.pass_on(pairs - 1, True)
+
+    takes = [(half + 1 + i, small, i, dkv_s) for i in range(half)]
+    takes += [(half + 3 + i, large, i, dkv_l) for i in range(pairs - 1)]
+    for when, exchange, pair, out_ref in takes:
+
+        @pl.when(step == when)
+        def _(exchange=exchange, pair=pair, out_ref=out_ref):
+            exchange.take(pair, out_ref)
 
     for at in range(2 * pairs):
         todo = []
@@ -910,11 +981,11 @@
 
     @pl.when(step == 2 * pairs - 1)
     def _():
-        small.take(pairs - 2, dkv_s)
-        small.take(pairs - 1, dkv_s)
-        for pair in (pairs - 2, pairs - 1):
-            small.free(pair)
-            small.copy_x(pair).wait_send()
+        large.take(pairs - 1, dkv_l)
+        for pair in range(half, pairs):
+            small.take(pair, dkv_s)
+        small.end()
+        large.end()
         for flow, sum_ref in zip(running, sums):
             sum_ref[...] = flow.result()
 
@@ -927,8 +998,9 @@
     shapes = [flow.shape[1:] for flow in flows]
     results = [flow_result(*flow) for flow in zip(orders, shapes, ends)]
     blocks = (largest_block(total // 2, 512), largest_block(less // 2, 512))
-    first = lambda i: jnp.minimum(i, pairs - 1)
-    last = lambda i: jnp.maximum(i - pairs, 0)
+    half = pairs // 2
+    first = lambda i: jnp.clip(i - half, 0, pairs - 1)
+    last = lambda i: jnp.where(i < half, i, jnp.maximum(i - pairs, half))
     in_specs = []
     for rows, keys, at in ((count, total, first), (few, less, last)):
         major = pl.BlockSpec((1, rows, LANES), lambda i, at=at: (at(i), 0, 0))
@@ -975,74 +1047,42 @@
     return result[:4], result[4:]
 
 
-def view_kernel(pairs, sizes, *refs):
-    (dql, dkvl, dqs, dkvs, xl, xs, hl, hs, gain, wq, wk, wv) = refs[:12]
-    gl_ref, gs_ref, gain_ref, grads = refs[12:]
-    large, small = sizes
-    top, bottom = pl.ds(0, large), pl.ds(large, small)
-    total = None
-    for which, weight in enumerate((wq, wk, wv)):
-        if which == 0:
-            grads[top, :] = dql[...]
-            grads[bottom, :] = dqs[...]
-        else:
-            for pair in range(pairs):
-                lanes = pl.ds(pair * LANES, LANES)
-                grads[top, lanes] = dkvl[pair, which - 1]
-                grads[bottom, lanes] = dkvs[pair, which - 1]
-        part = dot(grads[...], weight[...], NT)
-        total = part if total is None else total + part
-    extra, gain_l = norm_back(total[:large], xl[...].astype(f32), gain[...])
-    gl_ref[...] = (hl[...] + extra).astype(bf16)
-    extra, gain_s = norm_back(total[large:], xs[...].astype(f32), gain[...])
-    gs_ref[...] = (hs[...] + extra).astype(bf16)
-    gain_ref[...] = gain_l + gain_s
-
-
-def view_grads(selves, large, small, hidden_l, hidden_s, gain, weights):
-    count, width = large.shape
-    few = small.shape[0]
-    shape = jax.ShapeDtypeStruct
-    return pl.pallas_call(
-        functools.partial(view_kernel, width // LANES, (count, few)),
-        out_shape=[
-            shape((count, width), bf16),
-            shape((few, width), bf16),
-            shape((1, width), f32),
-        ],
-        scratch_shapes=[pltpu.VMEM((count + few, width), bf16)],
-        compiler_params=pltpu.CompilerParams(vmem_limit_bytes=48 << 20),
-        cost_estimate=pl.CostEstimate(
-            flops=6 * (count + few) * width * width,
-            bytes_accessed=6 * width * width + 20 * (count + few) * width,
-            transcendentals=0,
-        ),
-        name="view_grads",
-    )(*selves, large, small, hidden_l, hidden_s, gain, *weights)
-
-
-LAST_ORDERS = (BY_YX, BY_X, BY_ZL)
+LAST_ORDERS = (BY_YX, BY_X, BY_YX)
 GAIN_ORDER = ("core", "y", "x", "zl", "zh")
 LATE_ORDER = ("x", "zh")
-LATE_STAGES = {2: 1, 4: 2, 5: 3, 6: 4}
+LATE_STAGES = {1: 1, 4: 2, 5: 3, 6: 4}
 
 
 def last_kernel(pairs, sizes, late, *refs):
-    dql, dkvl, dqs, dkvs, nl, ns, gains = refs[:7]
-    late_refs, refs = refs[7 : 7 + late], list(refs[7 + late :])
-    sum_refs = [refs.pop(0) for _ in range(3 + late)]
-    gain_ref, normed, grads = refs.pop(0), refs.pop(0), refs.pop(0)
+    refs = list(refs)
+    take = lambda count: [refs.pop(0) for _ in range(count)]
+    given, late_refs = take(13), take(late)
+    gain, second_gain, query_gain, context_gain = take(4)
+    gl_ref, gs_ref = take(2)
+    sum_refs = take(3 + late)
+    (gain_ref,) = take(1)
+    held = take(13)
+    dql, dkvl, dqs, dkvs, wq, wk, wv, xl, xs, hl, hs, nl, ns = held
+    load_sems, normed, *grads = take(5)
+    large_back, small_back = take(3), take(3)
     here = Here()
     flows = []
     for order in LAST_ORDERS:
         flows.append(Flow(here, order, refs.pop(0), refs, False, True))
-    late_flows = [Flow(here, LATE_ORDER, ref, refs, False, True) for ref in late_refs]
+    late_flows = [Flow(here, LATE_ORDER, ref, refs, True, True) for ref in late_refs]
     state, got, gain_sems = refs
     large, small = sizes
     top, bottom = pl.ds(0, large), pl.ds(large, small)
-    here.greet(ALL_PARTNERS)
+    loads = [
+        pltpu.make_async_copy(source, there, load_sems.at[i])
+        for i, (source, there) in enumerate(zip(given, held))
+    ]
+    for load in loads:
+        load.start()
+    here.greet_line("x", "y")
     for flow in late_flows:
         flow.act(0)
+    homes = [Restore(here, *large_back), Restore(here, *small_back)]
 
     def gain_copy(step):
         return pltpu.make_async_remote_copy(
@@ -1054,20 +1094,39 @@
             device_id_type=MESH,
         )
 
-    state[0] = gains[...]
+    for load in loads[:4]:
+        load.wait()
+    total = None
+    for which, weight in enumerate((wq, wk, wv)):
+        if which == 0:
+            grads[0][top, :] = dql[...]
+            grads[0][bottom, :] = dqs[...]
+        else:
+            for pair in range(pairs):
+                lanes = pl.ds(pair * LANES, LANES)
+                grads[which][top, lanes] = dkvl[pair, which - 1]
+                grads[which][bottom, lanes] = dkvs[pair, which - 1]
+        loads[4 + which].wait()
+        part = dot(grads[which][...], weight[...], NT)
+        total = part if total is None else total + part
+    for load in loads[7:]:
+        load.wait()
+    extra, gain_l = norm_back(total[:large], xl[...].astype(f32), gain[...])
+    large_back[0][...] = (hl[...] + extra).astype(bf16)
+    homes[0].start()
+    extra, gain_s = norm_back(total[large:], xs[...].astype(f32), gain[...])
+    small_back[0][...] = (hs[...] + extra).astype(bf16)
+    homes[1].start()
+    state[0] = jnp.zeros(state.shape[1:], f32)
+    for row, value in enumerate(
+        (gain_l + gain_s, second_gain[...], query_gain[...], context_gain[...])
+    ):
+        state[0, row : row + 1, :] = value
     gain_copy(0).start()
     normed[top, :] = nl[...]
     normed[bottom, :] = ns[...]
     for which, flow in enumerate(flows):
-        if which == 0:
-            grads[top, :] = dql[...]
-            grads[bottom, :] = dqs[...]
-        else:
-            for pair in range(pairs):
-                lanes = pl.ds(pair * LANES, LANES)
-                grads[top, lanes] = dkvl[pair, which - 1]
-                grads[bottom, lanes] = dkvs[pair, which - 1]
-        value = dot(normed[...], grads[...], TN).astype(bf16)
+        value = dot(normed[...], grads[which][...], TN).astype(bf16)
         rows, wide = flow.local.shape[1:]
         for at, (core, y, tm) in enumerate(spots(flow.order)):
             first = tm * 2 * rows + core * rows
@@ -1089,51 +1148,66 @@
                 gain_ref[...] = total
     for flow, sum_ref in zip(flows + late_flows, sum_refs):
         sum_ref[...] = flow.result()
-
-
-def last_sums(selves, normed_l, normed_s, gains, late):
-    count, width = normed_l.shape
-    few = normed_s.shape[0]
+    homes[0].finish()
+    gl_ref[...] = large_back[1][...].astype(f32)
+    homes[1].finish()
+    gs_ref[...] = small_back[1][...].astype(f32)
+
+
+def last_sums(given, late, gains):
+    count, width = given[0].shape
+    few = given[2].shape[0]
     block = (width // 16, width // 2)
     shape = jax.ShapeDtypeStruct
-    scratch = [pltpu.VMEM((count + few, width), bf16), pltpu.VMEM((count + few, width), bf16)]
+    tokens = count + few
+    scratch = [pltpu.VMEM(value.shape, value.dtype) for value in given]
+    scratch += [pltpu.SemaphoreType.DMA((len(given),))]
+    scratch += [pltpu.VMEM((tokens, width), bf16)] * 4
+    scratch += restore_scratch(count // 2, width) + restore_scratch(few // 2, width)
     for order in LAST_ORDERS:
         scratch.append(pltpu.VMEM((32,) + block, bf16))
         scratch += flow_scratch(order, block, False, True)
     for local in late:
-        scratch += flow_scratch(LATE_ORDER, local.shape[1:], False, True)
+        scratch += flow_scratch(LATE_ORDER, local.shape[1:], True, True)
     scratch += [
-        pltpu.VMEM((5,) + gains.shape, f32),
-        pltpu.VMEM((5,) + gains.shape, f32),
+        pltpu.VMEM((5, 8, width), f32),
+        pltpu.VMEM((5, 8, width), f32),
         pltpu.SemaphoreType.DMA((2, 5)),
     ]
+    anywhere = pl.BlockSpec(memory_space=pl.ANY)
+    vmem = pl.BlockSpec(memory_space=pltpu.VMEM)
     result = pl.pallas_call(
         functools.partial(last_kernel, width // LANES, (count, few), len(late)),
-        out_shape=[shape((4,) + block, bf16)] * 3
+        in_specs=[anywhere] * (len(given) + len(late)) + [vmem] * 4,
+        out_shape=[
+            shape((2, count // 2, width), f32),
+            shape((2, few // 2, width), f32),
+        ]
+        + [shape((4,) + block, bf16)] * 3
         + [shape((4,) + local.shape[1:], bf16) for local in late]
-        + [shape(gains.shape, f32)],
+        + [shape((8, width), f32)],
         scratch_shapes=scratch,
         compiler_params=pltpu.CompilerParams(
-            vmem_limit_bytes=48 << 20, collective_id=2, has_side_effects=True
+            vmem_limit_bytes=60 << 20, collective_id=2, has_side_effects=True
         ),
         cost_estimate=pl.CostEstimate(
-            flops=40 * (count + few) * width * width,
-            bytes_accessed=40 * (count + few) * width,
+            flops=40 * tokens * width * width,
+            bytes_accessed=40 * tokens * width,
             transcendentals=0,
         ),
         name="last_sums",
-    )(*selves, normed_l, normed_s, gains, *late)
-    return result[:3], result[3:-1], result[-1]
+    )(*given, *late, *gains)
+    return result[:2], result[2:5], result[5:-1], result[-1]
 
 
 def cross_kernel(pairs, block, *refs):
     (q_ref, do_ref, o_ref, l_ref, mq_ref, mk_ref), refs = refs[:6], refs[6:]
-    kv_ref, given, gains, refs = refs[0], refs[1:10], refs[10:12], refs[12:]
-    gl_ref, gs_ref, a_ref, b_ref, gain_l_ref, gain_s_ref = refs[:6]
-    keys_at, values_at, exchange_refs, refs = refs[6], refs[7], refs[8:14], refs[14:]
+    kv_ref, given, gains, refs = refs[0], refs[1:11], refs[11:13], refs[13:]
+    view_ref, gl_ref, gs_ref, a_ref, b_ref, gain_l_ref, gain_s_ref = refs[:7]
+    keys_at, values_at, exchange_refs, refs = refs[7], refs[8], refs[9:15], refs[15:]
     dkv, dq, dk, dv = refs[:4]
-    held, sems = refs[4:13], refs[13]
-    asked, context, united, grad_out, merged_l, merged_s, wq, wk, wv = held
+    held, sems, home_refs = refs[4:14], refs[14], refs[15:18]
+    united, wo, merged_l, asked, context, grad_out, merged_s, wq, wk, wv = held
     here = Here()
     exchange = Exchange(here, keys_at.shape[0] // 4, exchange_refs)
     step = pl.program_id(0)
@@ -1144,9 +1218,19 @@
 
     @pl.when(step == 0)
     def _():
-        here.greet((("core",), ("x",)))
         for load in loads:
             load.start()
+        here.greet_line("x")
+
+    home = Restore(here, *home_refs)
+
+    @pl.when(step == 1)
+    def _():
+        for load in loads[:3]:
+            load.wait()
+        wide = jnp.concatenate([united[i] for i in range(pairs)], axis=1)
+        home_refs[0][...] = (merged_l[...] + dot(wide, wo[...])).astype(bf16)
+        home.start()
 
     fill_keys(keys_at, values_at, kv_ref)
 
@@ -1155,36 +1239,25 @@
         exchange.free(step - 2)
 
     dq[step] = pair_back(
-        q_ref[0], do_ref[...], o_ref[0], l_ref[0], mq_ref[...],
-        keys_at, values_at, mk_ref, block, exchange.put(step, keys_at.shape[0], block),
+        q_ref[0], do_ref[...], o_ref[0], l_ref[0], mq_ref[...], keys_at, values_at, mk_ref,
+        block, exchange, step,
     )
-    exchange.copy_core(step).start()
-
-    @pl.when((step >= 1) & (step < 3))
-    def _():
-        exchange.pass_on(step - 1, False)
 
     @pl.when(step >= 3)
     def _():
-        exchange.pass_on(step - 1, True)
-
-    @pl.when(step >= 2)
-    def _():
-        exchange.take(step - 2, dkv)
+        exchange.take(step - 3, dkv)
 
     def lay(out_ref, which, value, order):
-        rows = out_ref.shape[1] // 4
+        left = 32 // out_ref.shape[0]
+        rows = out_ref.shape[1] // left
         for at, (core, y, tm) in enumerate(spots(order)):
             if core == which:
-                first = (tm * 2 + y) * rows
-                out_ref[at // 4, at % 4 * rows : (at % 4 + 1) * rows, :] = value[
-                    first : first + rows
-                ]
+                first, there = (tm * 2 + y) * rows, at % left * rows
+                out_ref[at // left, there : there + rows, :] = value[first : first + rows]
 
     @pl.when(step == pairs - 1)
     def _():
-        exchange.pass_on(pairs - 1, True)
-        for load in loads:
+        for load in loads[3:]:
             load.wait()
         grads = jnp.concatenate([united[i] for i in range(pairs)], axis=1)
         lay(a_ref, 0, dot(grads, grad_out[...], TN).astype(bf16), BY_Y)
@@ -1192,8 +1265,8 @@
         lay(a_ref, 1, dot(asked[...], grads, TN).astype(bf16), BY_Y)
         extra, gain_l_ref[...] = norm_back(dot(grads, wq[...], NT), merged_l[...], gains[0][...])
         gl_ref[...] = grad_out[...].astype(f32) + extra
-        exchange.take(pairs - 2, dkv)
-        exchange.take(pairs - 1, dkv)
+        for pair in range(pairs - 3, pairs):
+            exchange.take(pair, dkv)
         for pair in range(pairs):
             lanes = pl.ds(pair * LANES, LANES)
             dk[:, lanes] = dkv[pair, 0]
@@ -1202,9 +1275,9 @@
         lay(b_ref, 1, dot(context[...], dv[...], TN).astype(bf16), BY_ZL)
         grad = dot(dk[...], wk[...], NT) + dot(dv[...], wv[...], NT)
         gs_ref[...], gain_s_ref[...] = norm_back(grad, merged_s[...], gains[1][...])
-        for pair in (pairs - 2, pairs - 1):
-            exchange.free(pair)
-            exchange.copy_x(pair).wait_send()
+        exchange.end()
+        home.finish()
+        view_ref[...] = home_refs[1][...]
 
 
 def cross_back(attention, kv, given, gains):
@@ -1215,20 +1288,21 @@
     total = attention[5].shape[0]
     block = largest_block(total // 2, 512)
     shape = jax.ShapeDtypeStruct
-    laid = (8, 4 * width // 16, width)
+    laid = (4, 8 * width // 16, width)
     return pl.pallas_call(
         functools.partial(cross_kernel, pairs, block),
         grid=(pairs,),
         in_specs=[major, columns(count, 0), major, major]
         + [whole((count, LANES)), whole((total, LANES))]
         + [pl.BlockSpec((4, 1, 2, few, LANES), lambda i: (0, i, 0, 0, 0))]
-        + [pl.BlockSpec(memory_space=pl.ANY)] * 9
+        + [pl.BlockSpec(memory_space=pl.ANY)] * len(given)
         + [whole((1, width))] * 2,
         out_specs=[
-            whole((count, width)), whole((few, width)), whole(laid), whole(laid),
+            whole((2, count // 2, width)), whole((count, width)), whole((few, width)), whole(laid), whole(laid),
             whole((1, width)), whole((1, width)),
         ],
         out_shape=[
+            shape((2, count // 2, width), bf16),
             shape((count, width), f32), shape((few, width), f32), shape(laid, bf16), shape(laid, bf16),
             shape((1, width), f32), shape((1, width), f32),
         ],
@@ -1237,9 +1311,10 @@
         + [pltpu.VMEM((pairs, 2, few, LANES), bf16), pltpu.VMEM((pairs, count, LANES), bf16)]
         + [pltpu.VMEM((few, width), bf16)] * 2
         + [pltpu.VMEM(value.shape, value.dtype) for value in given]
-        + [pltpu.SemaphoreType.DMA((len(given),))],
+        + [pltpu.SemaphoreType.DMA((len(given),))]
+        + restore_scratch(count // 2, width),
         compiler_params=pltpu.CompilerParams(
-            vmem_limit_bytes=56 << 20, collective_id=3, has_side_effects=True
+            vmem_limit_bytes=60 << 20, collective_id=3, has_side_effects=True
         ),
         cost_estimate=pl.CostEstimate(
             flops=20 * width * count * total,
@@ -1320,17 +1395,7 @@
     z, core = here.tm // 2, here.bit["core"]
     stay = core == z // 2
 
-    barrier = pltpu.get_barrier_semaphore()
-    for dz in range(4):
-        for dc in range(2):
-            if dz or dc:
-                place = (
-                    lax.rem(z + dz, 4) * 2 + here.bit["x"],
-                    here.bit["y"] * 2 + lax.rem(core + dc, 2),
-                )
-                pl.semaphore_signal(barrier, inc=1, device_id=place, device_id_type=MESH)
-    pl.semaphore_signal(barrier, inc=1, device_id=here.partner("x"), device_id_type=MESH)
-    pl.semaphore_wait(barrier, 8)
+    here.greet_line("x")
 
     odd = lax.rem(z, 2)
     from_seq = (odd, 1 - odd)
@@ -1661,19 +1726,19 @@
     return lax.optimization_barrier((value, needed))[0]
 
 
-CROSS_ORDERS = (BY_Y[:3], BY_ZL[:3])
-SELVES_ORDERS = (BY_Y[:3], BY_ZL[:3], BY_X, LATE_ORDER, LATE_ORDER)
-SELVES_ENDS = (False, False, True, True, True)
+CROSS_ORDERS = (BY_Y[:2], BY_ZL[:2])
+SELVES_ORDERS = (BY_Y[:3], BY_ZL[:3], BY_Y[:3], BY_Y[2:], BY_ZL[2:])
+SELVES_ENDS = (False, False, False, True, True)
 SELVES_STAGES = (
-    (0, 4, 11),
-    (0, 5, 11),
-    (0, 2, 4, 6, 8, 9, 10),
-    (2, 4, 6, 7),
-    (2, 4, 6, 7),
+    (1, 6, 11),
+    (1, 7, 11),
+    (1, 7, 11),
+    (4, 6, 8, 9, 10),
+    (4, 6, 8, 9, 10),
 )
 
 
-def paired_end(views, normed, large, small, cross, merged, weights, crosses, gains, united_view, restore):
+def paired_end(views, normed, large, small, cross, merged, weights, crosses, gains):
     large_view, small_view = views
     large_normed, small_normed, asked, context = normed
     large_q, large_mixed, large_logsum, large_mask_q, large_mask_k, large_kv = large
@@ -1684,10 +1749,12 @@
     first_gain, second_gain, query_gain, context_gain = gains
     width = large_view.shape[1]
     rows = width // 8
-    large_grad, small_grad, first, other, query_gain_grad, context_gain_grad = cross_back(
+    (
+        united_view, large_grad, small_grad, first, other, query_gain_grad, context_gain_grad,
+    ) = cross_back(
         (cross_q, united_grad, united, cross_logsum, large_mask_q, small_mask_k),
         cross_kv,
-        (asked, context, united, grad_out, large_merged, small_merged) + crosses,
+        (united, crosses[3], large_merged, asked, context, grad_out, small_merged) + crosses[:3],
         (query_gain, context_gain),
     )
     (
@@ -1698,33 +1765,30 @@
         second_gain, up_weight, down_weight, True, (first, other), CROSS_ORDERS,
     )
     eight = (8, 4 * rows, width)
-    four = (4, rows // 2, width)
+    still = (8, rows // 2, width)
     selves, sums = selves_back(
         (large_q, large_mixed_grad, large_mixed, large_logsum, large_mask_q, large_mask_k),
         large_kv,
         (small_q, small_mixed_grad, small_mixed, small_logsum, small_mask_q, small_mask_k),
         small_kv,
         (
-            up_grad.reshape(eight), down_grad.reshape(eight), output_grad,
-            first.reshape(four), other.reshape(four),
+            up_grad.reshape(eight), down_grad.reshape(eight),
+            output_grad.reshape(8, 2 * rows, width // 2),
+            first.reshape(still), other.reshape(still),
         ),
         SELVES_ORDERS, SELVES_ENDS, SELVES_STAGES,
     )
     up, down, output, first, other = sums
-    large_grad, small_grad, gain = view_grads(
-        selves, large_view, small_view, large_hidden, small_hidden, first_gain,
-        (query_weight, key_weight, value_weight),
+    (large_grad, small_grad), last, late, gains = last_sums(
+        tuple(selves) + (query_weight, key_weight, value_weight, large_view, small_view)
+        + (large_hidden, small_hidden, large_normed, small_normed),
+        (
+            up.reshape(4, rows, width), down.reshape(4, rows, width),
+            output.reshape(4, rows // 2, width // 2),
+        ),
+        (first_gain, second_gain_grad, query_gain_grad, context_gain_grad),
     )
-    large_grad, small_grad = restore(large_grad), restore(small_grad)
-    gains = jnp.concatenate(
-        (gain, second_gain_grad, query_gain_grad, context_gain_grad, jnp.zeros((4, width), f32)),
-        axis=0,
-    )
-    last, late, gains = last_sums(
-        selves, large_normed, small_normed, gains,
-        (up.reshape(4, rows, width), down.reshape(4, rows, width)),
-    )
-    up, down = (total.astype(f32) for total in late)
+    up, down, output = (total.astype(f32) for total in late)
 
     def square(total):
         total = total.astype(f32).reshape(2, 2, width // 16, width // 2)
@@ -1736,8 +1800,8 @@
     gains = [lax.dynamic_slice(gains, (i, at), (1, rows))[0] for i in range(4)]
     return (
         united_view,
-        large_grad.astype(f32),
-        small_grad.astype(f32),
+        large_grad,
+        small_grad,
         gains[0],
         square(last[0]),
         square(last[1]),
@@ -1778,11 +1842,8 @@
     ) = args
     seqs, count, width = large_view.shape
     side = tm // 4
-    gains = [
-        g.astype(f32).reshape(1, width)
-        for g in (first_gain, second_gain, query_gain, context_gain)
-    ]
-    first_gain, second_gain, query_gain, context_gain = gains
+    gains = jnp.stack((first_gain, second_gain, query_gain, context_gain)).astype(f32)
+    first_gain, second_gain, query_gain, context_gain = (gains[i : i + 1] for i in range(4))
 
     tm_at = lax.axis_index("tm")
     seq_at = lax.axis_index("seq")
@@ -1867,8 +1928,6 @@
             query_gain, (cross_query,),
         )
         united, cross_logsum = cross_attend(cross_q, cross_kv, large_mask_q, small_mask_k)
-        flat = jnp.transpose(united, (1, 0, 2)).reshape(2 * count, width)
-        united_view = restore((large_merged + dot(flat, cross_output)).astype(bf16))
         return paired_end(
             (large, small),
             (large_normed, small_normed, asked, context),
@@ -1877,10 +1936,8 @@
             (cross_q, united, cross_logsum, cross_kv, united_grad, grad_out),
             (large_merged, large_saved, small_merged, small_saved),
             (query_weight, key_weight, value_weight, output_weight, up_weight, down_weight),
-            (cross_query, cross_key, cross_value),
+            (cross_query, cross_key, cross_value, cross_output),
             (first_gain, second_gain, query_gain, context_gain),
-            united_view,
-            restore,
         )
 
     groups = 3

time: 413 us -> 376 us (0.910)
  starting transfers between devices: 13.1 us -> 0 us
  Pallas kernels: 355 us -> 347 us
  local copies, waits for them, and re-layouts: 24.8 us -> 18.4 us
  other arithmetic: 9.19 us -> 3.08 us
    pallas_call x1, Pallas kernels: 49.1 us -> 64.7 us  [last_sums(): pl.pallas_call(functools.partial(last_kernel, width // LANES, (count, few...]
    ppermute x6 -> x0, starting transfers between devices: 13.1 us -> none  [permute(): return lax.ppermute(value, ('tm', 'seq'), pairs)]
    pallas_call x1, Pallas kernels: 89.3 us -> 82 us  [selves_back(): pl.pallas_call(functools.partial(selves_kernel, pairs, (orders, ends, sta...]
    pallas_call x1 -> x0, Pallas kernels: 7.26 us -> none  [view_grads(): pl.pallas_call(functools.partial(view_kernel, width // LANES, (count, few...]
    pallas_call x1, Pallas kernels: 39.5 us -> 33.6 us  [back(): pl.pallas_call(functools.partial(back_kernel, steps, len(mixed_l), (large...]
    convert_element_type x2 -> x1, other arithmetic: 4.61 us -> 0.02 us  [per_device(): jnp.stack((first_gain, second_gain, query_gain, context_gain)).astype(f32)]
    reshape x4 -> x0, local copies, waits for them, and re-layouts: 4.47 us -> none  [per_device(): g.astype(f32).reshape(1, width)]
    unnamed x76 -> x53, local copies, waits for them, and re-layouts: 13.1 us -> 8.71 us
  transfers between devices with their start and end apart: 6 -> 0, of which waited for: 1 -> 0; matrix products, arithmetic and copies ran while one was open for 4% -> 0% of each run, Pallas kernels for 54% -> 0%
where the time goes in v4:
time: 376 us; the launch traced here: 372 us
  Pallas kernels  347 us (92%)
  local copies, waits for them, and re-layouts  18.4 us (5%)
    pallas_call x1, Pallas kernels, begin(): pl.pallas_call(functools.partial(begin_kernel, pairs), in_specs=[anywhere...  104 us
    pallas_call x1, Pallas kernels, selves_back(): pl.pallas_call(functools.partial(selves_kernel, pairs, (orders, ends, sta...  82 us
    pallas_call x1, Pallas kernels, last_sums(): pl.pallas_call(functools.partial(last_kernel, width // LANES, (count, few...  64.7 us
    pallas_call x1, Pallas kernels, cross_back(): pl.pallas_call(functools.partial(cross_kernel, pairs, block), grid=(pairs...  33.8 us
    pallas_call x1, Pallas kernels, back(): pl.pallas_call(functools.partial(back_kernel, steps, len(mixed_l), (large...  33.6 us
    pallas_call x1, Pallas kernels, rest(): pl.pallas_call(functools.partial(rest_kernel, steps, len(mixed), is_query...  15.2 us
    pallas_call x1, Pallas kernels, cross_attend(): pl.pallas_call(cross_attend_kernel, grid=(pairs,), in_specs=[one, pl.Bloc...  13.6 us
    unnamed x53, local copies, waits for them, and re-layouts  8.71 us

profile of v4, /device:TPU:1, one launch (start us, length us, event | category | flops | bytes accessed | tf_op | source)
XLA Modules:
  0.0 371.7 jit_solution(1757275202012548112)
XLA Ops:
  4.0 0.7 convert.18
  4.9 0.7 broadcast_in_dim.2.refs_3_
  5.7 104.4 %begin.1 = (bf16[512,768]{1,0:T(8,128)(2,1)}, bf16[256,768]{1,0:T(8,128)(2,1)}, bf16[512,768]{1,0:T(8,128)(2,1)}, bf16[4,6,2,512,128]{4,3,2,1,0:T(8,128)(2,1)}, ...) custom-call(bf16[2,256,768]{2,1,0:T(8,128)(2,1)} %refs_0_.1, ...), custom_call_target="tpu_custom_call" | custom-call | flops 23756537856 | bytes 41943040 | tf_op jit(solution)/shard_map/begin/pallas_call | solution.py:1674
  110.1 1.1 copy-done.5
  111.3 1.1 copy-done.6
  112.4 15.2 %rest.1 = (f32[512,768]{1,0:T(8,128)}, f32[512,768]{1,0:T(8,128)}, bf16[512,768]{1,0:T(8,128)(2,1)S(1)}, bf16[512,3072]{1,0:T(8,128)(2,1)}, bf16[512,3072]{1,0:T...) custom-call(bf16[512,768]{1,0:T(8,128)(2,1)S(1)} %copy-done.5, ...), custom_call_target="tpu_custom_call" | custom-call | flops 6039797760 | bytes 25559040 | tf_op jit(solution)/shard_map/rest/pallas_call | solution.py:337
  127.6 13.6 %cross_attend.1 = (bf16[6,512,128]{2,1,0:T(8,128)(2,1)S(1)}, f32[6,512,128]{2,1,0:T(8,128)S(1)}) custom-call(bf16[6,512,128]{2,1,0:T(8,128)(2,1)S(1)} %get-tuple-element.87.q_ref.refs_0_, bf16[4,6,2,256,128]{4,3,2,1,0:T(8,128)(2,1)S(1)} %copy-done.3, bf16[512,128]{1,0:T(8,128)(2,1)S(1)} %copy-done.12, bf16[1024,128]{1,0:T(8,128)(2,1)S(1)} %copy-done.11), custom_call_target="tpu_custom_call" | custom-call | flops 6442450944 | bytes 12582912 | tf_op jit(solution)/shard_map/cross_attend/pallas_call | solution.py:1700
  141.3 1.7 convolution_convert_fusion.refs_1_
  143.0 33.8 %cross_back.1 = (bf16[2,256,768]{2,1,0:T(8,128)(2,1)}, f32[512,768]{1,0:T(8,128)}, f32[256,768]{1,0:T(8,128)}, bf16[4,384,768]{2,1,0:T(8,128)(2,1)}, bf16[4,384,...) custom-call(bf16[6,512,128]{2,1,0:T(8,128)(2,1)} %copy-done.9, ...), custom_call_target="tpu_custom_call" | custom-call | flops 8053063680 | bytes 25165824 | tf_op jit(solution)/shard_map/cross_back/pallas_call | solution.py:1292
  176.9 33.6 %back.1 = (f32[512,768]{1,0:T(8,128)}, f32[256,768]{1,0:T(8,128)}, bf16[512,768]{1,0:T(8,128)(2,1)}, bf16[256,768]{1,0:T(8,128)(2,1)}, bf16[32,96,768]{2,1,0:T(8...) custom-call(f32[512,768]{1,0:T(8,128)} %get-tuple-element.100.refs_0, ...), custom_call_target="tpu_custom_call" | custom-call | flops 16307453952 | bytes 44826624 | tf_op jit(solution)/shard_map/back/pallas_call | solution.py:482
  210.5 82.0 %selves_back.1 = (bf16[512,768]{1,0:T(8,128)(2,1)}, bf16[6,2,512,128]{3,2,1,0:T(8,128)(2,1)}, bf16[256,768]{1,0:T(8,128)(2,1)}, bf16[6,2,256,128]{3,2,1,0:T(8,12...) custom-call(bf16[6,512,128]{2,1,0:T(8,128)(2,1)} %get-tuple-element., ...), custom_call_target="tpu_custom_call" | custom-call | flops 20132659200 | bytes 25165824 | tf_op jit(solution)/shard_map/selves_back/pallas_call | solution.py:1030
  292.5 2.2 fusion
  294.6 64.7 %last_sums.1 = (f32[2,256,768]{2,1,0:T(8,128)}, f32[2,128,768]{2,1,0:T(8,128)}, bf16[4,48,384]{2,1,0:T(8,128)(2,1)}, bf16[4,48,384]{2,1,0:T(8,128)(2,1)}, bf16[4...) custom-call(bf16[512,768]{1,0:T(8,128)(2,1)} %get-tuple-element.127., ...), custom_call_target="tpu_custom_call" | custom-call | flops 18119393280 | bytes 23592960 | tf_op jit(solution)/shard_map/last_sums/pallas_call | solution.py:1179
  359.4 1.2 convert_bitcast_fusion
  360.6 1.1 copy.44
  361.7 1.1 bitcast_convert_fusion
  363.0 0.7 copy.45
  363.9 0.7 copy.46
  364.9 0.7 copy.47
  365.8 0.7 copy.48
  366.5 1.4 dynamic-slice_bitcast_fusion
  368.0 0.9 copy.52
  368.9 1.1 copy.53
  370.5 0.9 copy.54
  (59 shorter events, 4.9 us)
Async XLA Ops:
  4.0 106.1 %copy-start.1 = (f32[1,768]{1,0:T(1,128)}, f32[1,768]{1,0:T(1,128)S(1)}, u32[]{:S(2)}) copy-start(f32[1,768]{1,0:T(1,128)S(1)} %get-tuple-element.161.refs_6_.refs_17_) | copy-start | bytes 9220
  5.7 104.4 %copy-start = (f32[1,768]{1,0:T(1,128)S(1)}, f32[1,768]{1,0:T(1,128)}, u32[]{:S(2)}) copy-start(f32[1,768]{1,0:T(1,128)} %get-tuple-element.163.refs_13_.refs_3_) | copy-start | bytes 9220
  5.7 104.4 %copy-start.2 = (bf16[768,768]{1,0:T(8,128)(2,1)S(1)}, bf16[768,768]{1,0:T(8,128)(2,1)}, u32[]{:S(2)}) copy-start(bf16[768,768]{1,0:T(8,128)(2,1)} %refs_12_.1) | copy-start | bytes 3538948
  110.1 1.1 copy-start.5
  111.2 1.1 copy-start.6
  112.4 15.2 %copy-start.3 = (bf16[4,6,2,256,128]{4,3,2,1,0:T(8,128)(2,1)S(1)}, bf16[4,6,2,256,128]{4,3,2,1,0:T(8,128)(2,1)}, u32[]{:S(2)}) copy-start(bf16[4,6,2,256,128]{4,3,2,1,0:T(8,128)(2,1)} %get-tuple-element.89.kv_ref.refs_6_) | copy-start | bytes 9437188
  112.4 15.2 %copy-start.11 = (bf16[1024,128]{1,0:T(8,128)(2,1)S(1)}, bf16[1024,128]{1,0:T(8,128)(2,1)}, u32[]{:S(2)}) copy-start(bf16[1024,128]{1,0:T(8,128)(2,1)} %get-tuple-element.91.mk_ref.refs_5_.refs_12_) | copy-start | bytes 786436
  112.4 15.2 %copy-start.12 = (bf16[512,128]{1,0:T(8,128)(2,1)S(1)}, bf16[512,128]{1,0:T(8,128)(2,1)}, u32[]{:S(2)}) copy-start(bf16[512,128]{1,0:T(8,128)(2,1)} %get-tuple-element.90.mq_ref.refs_4_) | copy-start | bytes 393220
  127.6 13.7 %copy-start.7 = (bf16[512,768]{1,0:T(8,128)(2,1)}, bf16[512,768]{1,0:T(8,128)(2,1)S(1)}, u32[]{:S(2)}) copy-start(bf16[512,768]{1,0:T(8,128)(2,1)S(1)} %get-tuple-element.106.refs_6_) | copy-start | bytes 2359300
  127.6 13.7 %copy-start.8 = (bf16[512,768]{1,0:T(8,128)(2,1)}, bf16[512,768]{1,0:T(8,128)(2,1)S(1)}, u32[]{:S(2)}) copy-start(bf16[512,768]{1,0:T(8,128)(2,1)S(1)} %get-tuple-element.95.refs_10_) | copy-start | bytes 2359300
  127.6 13.7 %copy-start.9 = (bf16[6,512,128]{2,1,0:T(8,128)(2,1)}, bf16[6,512,128]{2,1,0:T(8,128)(2,1)S(1)}, u32[]{:S(2)}) copy-start(bf16[6,512,128]{2,1,0:T(8,128)(2,1)S(1)} %get-tuple-element.87.q_ref.refs_0_) | copy-start | bytes 2359300
  127.6 13.7 %copy-start.21 = (bf16[768,768]{1,0:T(8,128)(2,1)S(1)}, bf16[768,768]{1,0:T(8,128)(2,1)}, u32[]{:S(2)}) copy-start(bf16[768,768]{1,0:T(8,128)(2,1)} %refs_8_.3) | copy-start | bytes 3538948
  127.6 13.7 %copy-start.22 = (bf16[512,768]{1,0:T(8,128)(2,1)S(1)}, bf16[512,768]{1,0:T(8,128)(2,1)}, u32[]{:S(2)}) copy-start(bf16[512,768]{1,0:T(8,128)(2,1)} %get-tuple-element.88.refs_12_) | copy-start | bytes 2359300
  141.3 1.7 copy-start.4
  141.3 1.7 copy-start.10
  360.5 1.2 copy-start.16
  360.6 2.3 copy-start.20
  361.7 2.1 copy-start.19
  362.8 1.8 copy-start.18
  363.8 1.8 copy-start.17
  364.7 3.3 copy-start.14
  365.6 3.2 copy-start.13
  368.9 1.7 copy-start.15

commit v5 on v4

--- a/solution.py
+++ b/solution.py
@@ -406,7 +406,7 @@
     if laid:
         rows = dup_ref.shape[1]
         for at in range(8):
-            zl, x, zh = at // 4, at // 2 % 2, at % 2
+            zl, zh, x = at // 4, at // 2 % 2, at % 2
             first = ((zh * 2 + zl) * 2 + x) * rows
             dup_ref[at] = upper[first : first + rows]
         for x, core, y in ((a, b, c) for a in (0, 1) for b in (0, 1) for c in (0, 1)):
@@ -437,7 +437,7 @@
         value = dot(mixed[...], branch[...], TN).astype(bf16)
         if laid:
             rows, wide = dwo_ref.shape[1:]
-            for at, (core, y, tm) in enumerate(spots(BY_Y)):
+            for at, (core, y, tm) in enumerate(spots(BY_Y_LATE)):
                 first = (tm * 2 + core) * rows
                 dwo_ref[at] = value[first : first + rows, y * wide : (y + 1) * wide]
         else:
@@ -529,6 +529,7 @@
 
 MESH = pl.DeviceIdType.MESH
 BY_Y = ("core", "y", "zl", "x", "zh")
+BY_Y_LATE = ("core", "y", "zl", "zh", "x")
 BY_ZL = ("core", "zl", "y", "x", "zh")
 BY_X = ("core", "x", "zl", "y", "zh")
 BY_YX = ("core", "y", "x", "zl", "zh")
@@ -1047,10 +1048,14 @@
     return result[:4], result[4:]
 
 
-LAST_ORDERS = (BY_YX, BY_X, BY_YX)
+LAST_ORDERS = (BY_YX, BY_X, BY_ZL)
 GAIN_ORDER = ("core", "y", "x", "zl", "zh")
-LATE_ORDER = ("x", "zh")
-LATE_STAGES = {1: 1, 4: 2, 5: 3, 6: 4}
+LATE_ORDERS = (("x",), ("x", "zh"), ("x",))
+LATE_STAGES = (
+    {2: 2, 4: 3},
+    {2: 2, 3: 3, 4: 4},
+    {2: 2, 4: 3},
+)
 
 
 def last_kernel(pairs, sizes, late, *refs):
@@ -1062,14 +1067,16 @@
     sum_refs = take(3 + late)
     (gain_ref,) = take(1)
     held = take(13)
-    dql, dkvl, dqs, dkvs, wq, wk, wv, xl, xs, hl, hs, nl, ns = held
+    dql, dkvl, dqs, dkvs, nl, ns, wq, wk, wv, xl, xs, hl, hs = held
     load_sems, normed, *grads = take(5)
     large_back, small_back = take(3), take(3)
     here = Here()
     flows = []
     for order in LAST_ORDERS:
         flows.append(Flow(here, order, refs.pop(0), refs, False, True))
-    late_flows = [Flow(here, LATE_ORDER, ref, refs, True, True) for ref in late_refs]
+    late_flows = [
+        Flow(here, order, ref, refs, True, True) for order, ref in zip(LATE_ORDERS, late_refs)
+    ]
     state, got, gain_sems = refs
     large, small = sizes
     top, bottom = pl.ds(0, large), pl.ds(large, small)
@@ -1094,10 +1101,11 @@
             device_id_type=MESH,
         )
 
-    for load in loads[:4]:
+    for load in loads[:6]:
         load.wait()
-    total = None
-    for which, weight in enumerate((wq, wk, wv)):
+    normed[top, :] = nl[...]
+    normed[bottom, :] = ns[...]
+    for which, flow in enumerate(flows):
         if which == 0:
             grads[0][top, :] = dql[...]
             grads[0][bottom, :] = dqs[...]
@@ -1106,14 +1114,26 @@
                 lanes = pl.ds(pair * LANES, LANES)
                 grads[which][top, lanes] = dkvl[pair, which - 1]
                 grads[which][bottom, lanes] = dkvs[pair, which - 1]
-        loads[4 + which].wait()
+        value = dot(normed[...], grads[which][...], TN).astype(bf16)
+        rows, wide = flow.local.shape[1:]
+        for at, (core, y, tm) in enumerate(spots(flow.order)):
+            first = tm * 2 * rows + core * rows
+            flow.local[at] = value[first : first + rows, y * wide : (y + 1) * wide]
+        flow.act(0)
+    total = None
+    for which, weight in enumerate((wq, wk, wv)):
+        loads[6 + which].wait()
         part = dot(grads[which][...], weight[...], NT)
         total = part if total is None else total + part
-    for load in loads[7:]:
+    for load in loads[9:]:
         load.wait()
+    for flow in late_flows:
+        flow.act(1)
     extra, gain_l = norm_back(total[:large], xl[...].astype(f32), gain[...])
     large_back[0][...] = (hl[...] + extra).astype(bf16)
     homes[0].start()
+    for flow in flows:
+        flow.act(1)
     extra, gain_s = norm_back(total[large:], xs[...].astype(f32), gain[...])
     small_back[0][...] = (hs[...] + extra).astype(bf16)
     homes[1].start()
@@ -1123,21 +1143,13 @@
     ):
         state[0, row : row + 1, :] = value
     gain_copy(0).start()
-    normed[top, :] = nl[...]
-    normed[bottom, :] = ns[...]
-    for which, flow in enumerate(flows):
-        value = dot(normed[...], grads[which][...], TN).astype(bf16)
-        rows, wide = flow.local.shape[1:]
-        for at, (core, y, tm) in enumerate(spots(flow.order)):
-            first = tm * 2 * rows + core * rows
-            flow.local[at] = value[first : first + rows, y * wide : (y + 1) * wide]
-        flow.act(0)
     for stage in range(1, 8):
-        for flow in flows:
-            flow.act(stage)
-        if stage in LATE_STAGES:
-            for flow in late_flows:
-                flow.act(LATE_STAGES[stage])
+        if stage > 1:
+            for flow in flows:
+                flow.act(stage)
+        for flow, stages in zip(late_flows, LATE_STAGES):
+            if stage in stages:
+                flow.act(stages[stage])
         if stage <= 5:
             gain_copy(stage - 1).wait()
             total = state[stage - 1] + got[stage - 1]
@@ -1145,13 +1157,15 @@
                 state[stage] = total
                 gain_copy(stage).start()
             else:
-                gain_ref[...] = total
+                wide = total.shape[1]
+                turned = pltpu.roll(total, lax.rem(wide - here.tm * (wide // 8), wide), 1)
+                gain_ref[...] = turned[:, : gain_ref.shape[1]]
     for flow, sum_ref in zip(flows + late_flows, sum_refs):
         sum_ref[...] = flow.result()
     homes[0].finish()
-    gl_ref[...] = large_back[1][...].astype(f32)
+    gl_ref[...] = large_back[1][...]
     homes[1].finish()
-    gs_ref[...] = small_back[1][...].astype(f32)
+    gs_ref[...] = small_back[1][...]
 
 
 def last_sums(given, late, gains):
@@ -1167,8 +1181,8 @@
     for order in LAST_ORDERS:
         scratch.append(pltpu.VMEM((32,) + block, bf16))
         scratch += flow_scratch(order, block, False, True)
-    for local in late:
-        scratch += flow_scratch(LATE_ORDER, local.shape[1:], True, True)
+    for order, local in zip(LATE_ORDERS, late):
+        scratch += flow_scratch(order, local.shape[1:], True, True)
     scratch += [
         pltpu.VMEM((5, 8, width), f32),
         pltpu.VMEM((5, 8, width), f32),
@@ -1180,12 +1194,12 @@
         functools.partial(last_kernel, width // LANES, (count, few), len(late)),
         in_specs=[anywhere] * (len(given) + len(late)) + [vmem] * 4,
         out_shape=[
-            shape((2, count // 2, width), f32),
-            shape((2, few // 2, width), f32),
+            shape((2, count // 2, width), bf16),
+            shape((2, few // 2, width), bf16),
         ]
         + [shape((4,) + block, bf16)] * 3
         + [shape((4,) + local.shape[1:], bf16) for local in late]
-        + [shape((8, width), f32)],
+        + [shape((8, LANES), f32)],
         scratch_shapes=scratch,
         compiler_params=pltpu.CompilerParams(
             vmem_limit_bytes=60 << 20, collective_id=2, has_side_effects=True
@@ -1198,6 +1212,59 @@
         name="last_sums",
     )(*given, *late, *gains)
     return result[:2], result[2:5], result[5:-1], result[-1]
+
+
+def results_kernel(*refs):
+    outs, given, sems = refs[12:29], refs[29:41], refs[41]
+    loads = [
+        pltpu.make_async_copy(source, there, sems.at[i])
+        for i, (source, there) in enumerate(zip(refs, given))
+    ]
+    for load in loads:
+        load.start()
+    for load in loads:
+        load.wait()
+    united, large, small, q, k, v, up, down, output, first, other, gains = given
+    for source, there in zip((united, large, small), outs[:3]):
+        there[...] = source[...].astype(there.dtype)
+    for source, there in zip((q, k, v, output), (outs[4], outs[5], outs[6], outs[7])):
+        rows, wide = source.shape[1:]
+        for at in range(4):
+            core, y = at // 2, at % 2
+            there[core * rows : (core + 1) * rows, y * wide : (y + 1) * wide] = source[at].astype(f32)
+    rows, wide = up.shape[1:]
+    for at in range(4):
+        outs[9][:, at * wide : (at + 1) * wide] = up[at].astype(f32)
+        outs[10][at * rows : (at + 1) * rows, :] = down[at].astype(f32)
+        half = rows // 2
+        there = slice(at % 2 * half, (at % 2 + 1) * half)
+        (outs[16] if at < 2 else outs[13])[there, :] = first[at].astype(f32)
+        (outs[14] if at < 2 else outs[15])[there, :] = other[at].astype(f32)
+    for row, at in enumerate((3, 8, 11, 12)):
+        outs[at][...] = gains[row : row + 1, : outs[at].shape[1]]
+
+
+def results(united, large, small, last, late, first, other, gains):
+    shape = jax.ShapeDtypeStruct
+    rows, width = late[0].shape[1:]
+    square, vector = shape((rows, width), f32), shape((1, rows), f32)
+    given = (united, large, small, *last, *late, first, other, gains)
+    out = pl.pallas_call(
+        results_kernel,
+        in_specs=[pl.BlockSpec(memory_space=pl.ANY)] * len(given),
+        scratch_shapes=[pltpu.VMEM(value.shape, value.dtype) for value in given]
+        + [pltpu.SemaphoreType.DMA((len(given),))],
+        out_shape=[
+            shape(united.shape, bf16), shape(large.shape, f32), shape(small.shape, f32), vector,
+            square, square, square, square, vector,
+            shape((rows, 4 * width), f32), shape((4 * rows, width), f32), vector, vector,
+            square, square, square, square,
+        ],
+        compiler_params=pltpu.CompilerParams(vmem_limit_bytes=60 << 20),
+        cost_estimate=pl.CostEstimate(flops=0, bytes_accessed=14 << 20, transcendentals=0),
+        name="results",
+    )(*given)
+    return tuple(value.reshape(rows) if value.shape == (1, rows) else value for value in out)
 
 
 def cross_kernel(pairs, block, *refs):
@@ -1380,17 +1447,24 @@
     refs = list(refs)
     take = lambda count: [refs.pop(0) for _ in range(count)]
     large_ref, small_ref, cot_ref, clip_ref = take(4)
-    weight_refs = take(8)
-    first_gain, second_gain, context_gain = take(3)
+    weight_refs = take(9)
+    (gains,) = take(1)
+    first_gain, second_gain, query_gain, context_gain = (
+        gains.at[i : i + 1, :] for i in range(4)
+    )
     xl_out, xs_out, cot_out, kvl_out, kvs_out, ckv_out = take(6)
     nl_ref, ns_ref, ql_ref, qs_ref, ol_ref, ll_ref, os_ref, ls_ref = take(8)
     merged_ref, hidden_ref, second_ref, active_ref, slope_ref, context_ref = take(6)
     mql_ref, mkl_ref, mqs_ref, mks_ref = take(4)
+    for gain, gain_out in zip((first_gain, second_gain, query_gain, context_gain), take(4)):
+        gain_out[...] = gain[...]
+    (grad_ref,) = take(1)
     xl, xs, cot, clip, kvl, kvs, ckv = take(7)
-    wq, wk, wv, wo, up, down, wck, wcv = weights = take(8)
+    wq, wk, wv, wo, up, down, wck, wcv, wco = weights = take(9)
     spaces = take(4)
     wide, total = take(2)
     move_sems, gather_l, gather_s, gather_c, gather_clip, load_sems, out_sems = take(7)
+    near_l, near_s, near_c, x_sems = take(4)
     here = Here()
     z, core = here.tm // 2, here.bit["core"]
     stay = core == z // 2
@@ -1470,15 +1544,27 @@
         copy.start()
         outs.append(copy)
 
-    def front_into(x, n_ref, q_ref, kv):
-        normed = norm(x[...].astype(f32), first_gain[...])
-        n_ref[...] = normed
-        keys = dot(normed, wk[...]).astype(bf16)
-        values = dot(normed, wv[...]).astype(bf16)
+    def split(kv, part, value, key_weight, value_weight):
+        keys = dot(value, key_weight[...]).astype(bf16)
+        values = dot(value, value_weight[...]).astype(bf16)
         for pair in range(pairs):
             lanes = slice(pair * LANES, (pair + 1) * LANES)
-            kv[0, pair, 0] = keys[:, lanes]
-            kv[0, pair, 1] = values[:, lanes]
+            kv[part, pair, 0] = keys[:, lanes]
+            kv[part, pair, 1] = values[:, lanes]
+
+    def to_x(which, source, there):
+        return pltpu.make_async_remote_copy(
+            src_ref=source,
+            dst_ref=there,
+            send_sem=x_sems.at[0, which],
+            recv_sem=x_sems.at[1, which],
+            device_id=here.partner("x"),
+            device_id_type=MESH,
+        )
+
+    x_small, x_large, x_cross = (
+        to_x(0, ns_ref, near_s), to_x(1, nl_ref, near_l), to_x(2, context_ref, near_c)
+    )
 
     def query_into(n_ref, q_ref):
         query = (dot(n_ref[...], wq[...]) * Q_SCALE).astype(bf16)
@@ -1493,11 +1579,12 @@
         clips.copy(kind, 0, 1, 0).start()
     moved_in(*moves[1])
     keep(xs, xs_out)
+    ns_ref[...] = norm(xs[...].astype(f32), first_gain[...])
+    x_small.start()
     for i in (0, 1, 2):
         loads[i].wait()
-    front_into(xs, ns_ref, qs_ref, kvs)
-    for kind in (0, 1):
-        small.copy(kind, 0, pairs, 0).start()
+    split(kvs, 0, ns_ref[...], wk, wv)
+    small.copy(1, 0, pairs, 0).start()
     query_into(ns_ref, qs_ref)
     clips.copy(0, 0, 1, 0).wait_recv()
     clips.copy(2, 0, 1, 0).start()
@@ -1524,20 +1611,19 @@
             if part == 0:
                 mq_ref[...] = jnp.where(some & (value == number), 1.0, 0.0).astype(bf16)
 
+    x_small.wait_recv()
+    split(kvs, 1, near_s[...], wk, wv)
+    small.copy(2, 0, pairs, 0).start()
     moved_in(*moves[2])
     moved_out(*moves[2])
     move(*moves[3])
     keep(xl, xl_out)
-    front_into(xl, nl_ref, ql_ref, kvl)
-    third = pairs // 3
-    small.copy(0, 0, pairs, 0).wait_send()
-    large.copy(0, 0, third, 0).start()
-    for group in range(3):
-        large.copy(1, group * third, third, group).start()
+    nl_ref[...] = norm(xl[...].astype(f32), first_gain[...])
+    x_large.start()
+    split(kvl, 0, nl_ref[...], wk, wv)
+    large.copy(1, 0, pairs, 0).start()
     query_into(nl_ref, ql_ref)
 
-    small.copy(0, 0, pairs, 0).wait_recv()
-    small.copy(2, 0, pairs, 0).start()
     small.copy(1, 0, pairs, 0).wait_recv()
     small.copy(2, 0, pairs, 0).wait_recv()
     keep(kvs, kvs_out)
@@ -1565,58 +1651,46 @@
         active_ref[:, lanes] = active
         slope_ref[:, lanes] = slope.astype(bf16)
         total[...] += dot(active, down[lanes, :])
-        if step == steps // 2:
-            large.copy(0, 0, third, 0).wait_send()
-            large.copy(0, third, third, 1).start()
     merged = total[...]
     merged_ref[...] = merged
     context = norm(merged, context_gain[...])
     context_ref[...] = context
+    x_cross.start()
+    x_large.wait_recv()
+    split(kvl, 1, near_l[...], wk, wv)
+    large.copy(2, 0, pairs, 0).start()
     loads[6].wait()
     loads[7].wait()
-    keys = dot(context, wck[...]).astype(bf16)
-    values = dot(context, wcv[...]).astype(bf16)
-    for pair in range(pairs):
-        lanes = slice(pair * LANES, (pair + 1) * LANES)
-        ckv[0, pair, 0] = keys[:, lanes]
-        ckv[0, pair, 1] = values[:, lanes]
+    split(ckv, 0, context, wck, wcv)
     cross.copy(1, 0, pairs, 0).start()
 
     def large_pair(pair, carry):
         attend_pair(pair, ql_ref, kvl, mql_ref, mkl_ref, spaces, ol_ref, ll_ref)
         return carry
 
-    for group in range(3):
-        at = group * third
-        large.copy(0, at, third, group).wait_recv()
-        large.copy(2, at, third, group).start()
-        if group == 0:
-            large.copy(0, third, third, 1).wait_send()
-            large.copy(0, 2 * third, third, 2).start()
-        if group == 2:
-            large.copy(0, 2 * third, third, 2).wait_send()
-            cross.copy(0, 0, pairs, 0).start()
-        large.copy(1, at, third, group).wait_recv()
-        large.copy(2, at, third, group).wait_recv()
-        if group == 2:
-            keep(kvl, kvl_out)
-        lax.fori_loop(at, at + third, large_pair, 0)
+    large.copy(1, 0, pairs, 0).wait_recv()
+    large.copy(2, 0, pairs, 0).wait_recv()
+    keep(kvl, kvl_out)
+    lax.fori_loop(0, pairs // 2, large_pair, 0)
+    x_cross.wait_recv()
+    split(ckv, 1, near_c[...], wck, wcv)
+    cross.copy(2, 0, pairs, 0).start()
     moved_in(*moves[3])
     moved_out(*moves[3])
     keep(cot, cot_out)
-    cross.copy(0, 0, pairs, 0).wait_recv()
-    cross.copy(2, 0, pairs, 0).start()
+    loads[8].wait()
+    grad_ref[...] = dot(cot[...], wco[...], NT).astype(bf16)
+    lax.fori_loop(pairs // 2, pairs, large_pair, 0)
     cross.copy(1, 0, pairs, 0).wait_recv()
     cross.copy(2, 0, pairs, 0).wait_recv()
     keep(ckv, ckv_out)
-    for copy in [small.copy(1, 0, pairs, 0), small.copy(2, 0, pairs, 0)]:
-        copy.wait_send()
     for kind in (0, 1, 2):
         clips.copy(kind, 0, 1, 0).wait_send()
-        cross.copy(kind, 0, pairs, 0).wait_send()
         if kind:
-            for group in range(3):
-                large.copy(kind, group * third, third, group).wait_send()
+            for gathered in (small, large, cross):
+                gathered.copy(kind, 0, pairs, 0).wait_send()
+    for copy in (x_small, x_large, x_cross):
+        copy.wait_send()
     for copy in outs:
         copy.wait()
 
@@ -1656,6 +1730,8 @@
         shape((4 * count, LANES), bf16),
         shape((few, LANES), bf16),
         shape((4 * few, LANES), bf16),
+        *[shape((1, width), f32)] * 4,
+        shape((count, width), bf16),
     ]
     dma = pltpu.SemaphoreType.DMA
     scratch = [
@@ -1670,11 +1746,17 @@
     scratch += [pltpu.VMEM(weight.shape, bf16) for weight in weights]
     scratch += [pltpu.VMEM((4 * count, LANES), bf16)] * 4
     scratch += [pltpu.VMEM((few, width), bf16), pltpu.VMEM((few, width), f32)]
-    scratch += [dma((2, 8)), dma((2, 9)), dma((2, 3)), dma((2, 3)), dma((2, 3)), dma((8,)), dma((6,))]
+    scratch += [dma((2, 8))] + [dma((2, 3))] * 4 + [dma((9,)), dma((6,))]
+    scratch += [
+        pltpu.VMEM((count, width), bf16),
+        pltpu.VMEM((few, width), bf16),
+        pltpu.VMEM((few, width), bf16),
+        dma((2, 3)),
+    ]
     return pl.pallas_call(
         functools.partial(begin_kernel, pairs),
-        in_specs=[anywhere] * 12 + [vmem] * 3,
-        out_specs=[anywhere] * 6 + [vmem] * 18,
+        in_specs=[anywhere] * 13 + [vmem],
+        out_specs=[anywhere] * 6 + [vmem] * 23,
         out_shape=out_shape,
         scratch_shapes=scratch,
         compiler_params=pltpu.CompilerParams(
@@ -1686,7 +1768,7 @@
             transcendentals=count * count * 4 * width // HALF,
         ),
         name="begin",
-    )(large, small, cotangent, clip, *weights, *gains)
+    )(large, small, cotangent, clip, *weights, gains)
 
 
 def cross_attend_kernel(q_ref, kv_ref, mq_ref, mk_ref, o_ref, l_ref, *spaces):
@@ -1727,14 +1809,14 @@
 
 
 CROSS_ORDERS = (BY_Y[:2], BY_ZL[:2])
-SELVES_ORDERS = (BY_Y[:3], BY_ZL[:3], BY_Y[:3], BY_Y[2:], BY_ZL[2:])
+SELVES_ORDERS = (BY_Y_LATE[:4], BY_ZL[:3], BY_Y_LATE[:4], BY_Y[2:], BY_ZL[2:])
 SELVES_ENDS = (False, False, False, True, True)
 SELVES_STAGES = (
+    (1, 6, 8, 11),
     (1, 6, 11),
-    (1, 7, 11),
-    (1, 7, 11),
-    (4, 6, 8, 9, 10),
-    (4, 6, 8, 9, 10),
+    (1, 6, 8, 11),
+    (3, 5, 7, 8, 9),
+    (3, 5, 7, 8, 9),
 )
 
 
@@ -1764,7 +1846,6 @@
         large_grad, small_grad, large_saved, small_saved, [large_mixed], small_mixed, output_weight,
         second_gain, up_weight, down_weight, True, (first, other), CROSS_ORDERS,
     )
-    eight = (8, 4 * rows, width)
     still = (8, rows // 2, width)
     selves, sums = selves_back(
         (large_q, large_mixed_grad, large_mixed, large_logsum, large_mask_q, large_mask_k),
@@ -1772,51 +1853,23 @@
         (small_q, small_mixed_grad, small_mixed, small_logsum, small_mask_q, small_mask_k),
         small_kv,
         (
-            up_grad.reshape(eight), down_grad.reshape(eight),
-            output_grad.reshape(8, 2 * rows, width // 2),
+            up_grad.reshape(16, 2 * rows, width), down_grad.reshape(8, 4 * rows, width),
+            output_grad.reshape(16, rows, width // 2),
             first.reshape(still), other.reshape(still),
         ),
         SELVES_ORDERS, SELVES_ENDS, SELVES_STAGES,
     )
     up, down, output, first, other = sums
     (large_grad, small_grad), last, late, gains = last_sums(
-        tuple(selves) + (query_weight, key_weight, value_weight, large_view, small_view)
-        + (large_hidden, small_hidden, large_normed, small_normed),
+        tuple(selves) + (large_normed, small_normed, query_weight, key_weight, value_weight)
+        + (large_view, small_view, large_hidden, small_hidden),
         (
-            up.reshape(4, rows, width), down.reshape(4, rows, width),
-            output.reshape(4, rows // 2, width // 2),
+            up.reshape(2, rows, width), down.reshape(4, rows, width),
+            output.reshape(2, rows // 2, width // 2),
         ),
         (first_gain, second_gain_grad, query_gain_grad, context_gain_grad),
     )
-    up, down, output = (total.astype(f32) for total in late)
-
-    def square(total):
-        total = total.astype(f32).reshape(2, 2, width // 16, width // 2)
-        return jnp.transpose(total, (0, 2, 1, 3)).reshape(rows, width)
-
-    first = first.astype(f32).reshape(2, rows, width)
-    other = other.astype(f32).reshape(2, rows, width)
-    at = lax.axis_index("tm") * rows
-    gains = [lax.dynamic_slice(gains, (i, at), (1, rows))[0] for i in range(4)]
-    return (
-        united_view,
-        large_grad,
-        small_grad,
-        gains[0],
-        square(last[0]),
-        square(last[1]),
-        square(last[2]),
-        square(output),
-        gains[1],
-        jnp.transpose(up, (1, 0, 2)).reshape(rows, 4 * width),
-        down.reshape(4 * rows, width),
-        gains[2],
-        gains[3],
-        first[1],
-        other[0],
-        other[1],
-        first[0],
-    )
+    return results(united_view, large_grad, small_grad, last, late, first, other, gains)
 
 
 def per_device(tm, seq_size, *args):
@@ -1842,7 +1895,8 @@
     ) = args
     seqs, count, width = large_view.shape
     side = tm // 4
-    gains = jnp.stack((first_gain, second_gain, query_gain, context_gain)).astype(f32)
+    gains = jnp.concatenate((first_gain, second_gain, query_gain, context_gain))
+    gains = gains.astype(f32).reshape(4, width)
     first_gain, second_gain, query_gain, context_gain = (gains[i : i + 1] for i in range(4))
 
     tm_at = lax.axis_index("tm")
@@ -1916,13 +1970,13 @@
             large, small, grad_out, large_kv, small_kv, cross_kv, large_normed, small_normed,
             large_q, small_q, large_mixed, large_logsum, small_mixed, small_logsum, small_merged,
             *small_saved, context, large_mask_q, large_mask_k, small_mask_q, small_mask_k,
+            first_gain, second_gain, query_gain, context_gain, united_grad,
         ) = begin(
             large_view, small_view, cotangent, clip,
             (query_weight, key_weight, value_weight, output_weight, up_weight, down_weight,
-             cross_key, cross_value),
-            (first_gain, second_gain, context_gain),
+             cross_key, cross_value, cross_output),
+            gains,
         )
-        united_grad = dot(grad_out, cross_output, NT).astype(bf16)
         large_merged, *large_saved, asked, cross_q = rest(
             large, [large_mixed], output_weight, second_gain, up_weight, down_weight,
             query_gain, (cross_query,),

time: 376 us -> 345 us (0.918)
  Pallas kernels: 347 us -> 331 us
  local copies, waits for them, and re-layouts: 18.4 us -> 7.22 us
    pallas_call x1, Pallas kernels: 104 us -> 80.9 us  [begin(): pl.pallas_call(functools.partial(begin_kernel, pairs), in_specs=[anywhere...]
    pallas_call x0 -> x1, Pallas kernels: none -> 5.58 us  [results(): pl.pallas_call(results_kernel, in_specs=[pl.BlockSpec(memory_space=pl.ANY...]
    unnamed x53 -> x26, local copies, waits for them, and re-layouts: 8.71 us -> 5.66 us
where the time goes in v5:
time: 345 us; the launch traced here: 340 us
  Pallas kernels  331 us (96%)
  local copies, waits for them, and re-layouts  7.22 us (2%)
    pallas_call x1, Pallas kernels, selves_back(): pl.pallas_call(functools.partial(selves_kernel, pairs, (orders, ends, sta...  81.2 us
    pallas_call x1, Pallas kernels, begin(): pl.pallas_call(functools.partial(begin_kernel, pairs), in_specs=[anywhere...  80.9 us
    pallas_call x1, Pallas kernels, last_sums(): pl.pallas_call(functools.partial(last_kernel, width // LANES, (count, few...  64.7 us
    pallas_call x1, Pallas kernels, cross_back(): pl.pallas_call(functools.partial(cross_kernel, pairs, block), grid=(pairs...  37.2 us
    pallas_call x1, Pallas kernels, back(): pl.pallas_call(functools.partial(back_kernel, steps, len(mixed_l), (large...  32.9 us
    pallas_call x1, Pallas kernels, rest(): pl.pallas_call(functools.partial(rest_kernel, steps, len(mixed), is_query...  15.2 us
    pallas_call x1, Pallas kernels, cross_attend(): pl.pallas_call(cross_attend_kernel, grid=(pairs,), in_specs=[one, pl.Bloc...  13.2 us

profile of v5, /device:TPU:1, one launch (start us, length us, event | category | flops | bytes accessed | tf_op | source)
XLA Modules:
  0.0 340.4 jit_solution(1907982732830835135)
XLA Ops:
  0.7 0.7 convert.4
  1.3 0.2 slice.4
  1.6 0.7 maximum_convert_fusion
  2.3 0.6 reshape.87.refs_13_
  2.9 0.7 broadcast_in_dim.2.refs_3_
  3.7 80.9 %begin.1 = (bf16[512,768]{1,0:T(8,128)(2,1)}, bf16[256,768]{1,0:T(8,128)(2,1)}, bf16[512,768]{1,0:T(8,128)(2,1)}, bf16[4,6,2,512,128]{4,3,2,1,0:T(8,128)(2,1)}, ...) custom-call(bf16[2,256,768]{2,1,0:T(8,128)(2,1)} %refs_0_.1, ...), custom_call_target="tpu_custom_call" | custom-call | flops 23756537856 | bytes 41943040 | tf_op jit(solution)/shard_map/begin/pallas_call | solution.py:1756
  84.5 0.0 copy-done
  84.6 1.1 copy-done.3
  85.7 1.1 copy-done.4
  86.8 0.7 copy-done.11
  87.5 0.7 copy-done.12
  88.2 15.2 %rest.1 = (f32[512,768]{1,0:T(8,128)}, f32[512,768]{1,0:T(8,128)}, bf16[512,768]{1,0:T(8,128)(2,1)S(1)}, bf16[512,3072]{1,0:T(8,128)(2,1)}, bf16[512,3072]{1,0:T...) custom-call(bf16[512,768]{1,0:T(8,128)(2,1)S(1)} %copy-done.3, ...), custom_call_target="tpu_custom_call" | custom-call | flops 6039797760 | bytes 25559040 | tf_op jit(solution)/shard_map/rest/pallas_call | solution.py:337
  103.4 0.0 copy-start.7
  103.4 0.0 copy-done.1
  103.4 0.0 copy-done.9
  103.4 0.0 copy-done.10
  103.4 13.2 %cross_attend.1 = (bf16[6,512,128]{2,1,0:T(8,128)(2,1)S(1)}, f32[6,512,128]{2,1,0:T(8,128)S(1)}) custom-call(bf16[6,512,128]{2,1,0:T(8,128)(2,1)S(1)} %get-tuple-element.111.q_ref.refs_0_, bf16[4,6,2,256,128]{4,3,2,1,0:T(8,128)(2,1)S(1)} %copy-done.1, bf16[512,128]{1,0:T(8,128)(2,1)S(1)} %copy-done.10, bf16[1024,128]{1,0:T(8,128)(2,1)S(1)} %copy-done.9), custom_call_target="tpu_custom_call" | custom-call | flops 6442450944 | bytes 12582912 | tf_op jit(solution)/shard_map/cross_attend/pallas_call | solution.py:1782
  116.7 1.1 copy-done.2
  117.8 0.9 copy-done.8
  118.7 37.2 %cross_back.1 = (bf16[2,256,768]{2,1,0:T(8,128)(2,1)}, f32[512,768]{1,0:T(8,128)}, f32[256,768]{1,0:T(8,128)}, bf16[4,384,768]{2,1,0:T(8,128)(2,1)}, bf16[4,384,...) custom-call(bf16[6,512,128]{2,1,0:T(8,128)(2,1)} %copy-done.7, ...), custom_call_target="tpu_custom_call" | custom-call | flops 8053063680 | bytes 25165824 | tf_op jit(solution)/shard_map/cross_back/pallas_call | solution.py:1359
  155.9 32.9 %back.1 = (f32[512,768]{1,0:T(8,128)}, f32[256,768]{1,0:T(8,128)}, bf16[512,768]{1,0:T(8,128)(2,1)}, bf16[256,768]{1,0:T(8,128)(2,1)}, bf16[32,96,768]{2,1,0:T(8...) custom-call(f32[512,768]{1,0:T(8,128)} %get-tuple-element.126.refs_0, ...), custom_call_target="tpu_custom_call" | custom-call | flops 16307453952 | bytes 44826624 | tf_op jit(solution)/shard_map/back/pallas_call | solution.py:482
  188.8 81.2 %selves_back.1 = (bf16[512,768]{1,0:T(8,128)(2,1)}, bf16[6,2,512,128]{3,2,1,0:T(8,128)(2,1)}, bf16[256,768]{1,0:T(8,128)(2,1)}, bf16[6,2,256,128]{3,2,1,0:T(8,12...) custom-call(bf16[6,512,128]{2,1,0:T(8,128)(2,1)} %get-tuple-element., ...), custom_call_target="tpu_custom_call" | custom-call | flops 20132659200 | bytes 25165824 | tf_op jit(solution)/shard_map/selves_back/pallas_call | solution.py:1031
  269.9 64.7 %last_sums.1 = (bf16[2,256,768]{2,1,0:T(8,128)(2,1)}, bf16[2,128,768]{2,1,0:T(8,128)(2,1)}, bf16[4,48,384]{2,1,0:T(8,128)(2,1)}, bf16[4,48,384]{2,1,0:T(8,128)(2...) custom-call(bf16[512,768]{1,0:T(8,128)(2,1)} %get-tuple-element.153., ...), custom_call_target="tpu_custom_call" | custom-call | flops 18119393280 | bytes 23592960 | tf_op jit(solution)/shard_map/last_sums/pallas_call | solution.py:1193
  334.6 5.6 %results.1 = (bf16[2,256,768]{2,1,0:T(8,128)(2,1)}, f32[2,256,768]{2,1,0:T(8,128)}, f32[2,128,768]{2,1,0:T(8,128)}, f32[1,96]{1,0:T(1,128)}, f32[96,768]{1,0:T(8...) custom-call(bf16[2,256,768]{2,1,0:T(8,128)(2,1)} %get-tuple-element., ...), custom_call_target="tpu_custom_call" | custom-call | bytes 14680064 | tf_op jit(solution)/shard_map/results/pallas_call | solution.py:1252
  (15 shorter events, 0.0 us)
Async XLA Ops:
  3.7 80.9 %copy-start = (bf16[768,768]{1,0:T(8,128)(2,1)S(1)}, bf16[768,768]{1,0:T(8,128)(2,1)}, u32[]{:S(2)}) copy-start(bf16[768,768]{1,0:T(8,128)(2,1)} %refs_12_.3) | copy-start | bytes 3538948
  84.6 1.1 copy-start.3
  85.7 1.1 copy-start.4
  86.8 0.7 copy-start.11
  87.5 0.7 copy-start.12
  88.2 15.2 %copy-start.1 = (bf16[4,6,2,256,128]{4,3,2,1,0:T(8,128)(2,1)S(1)}, bf16[4,6,2,256,128]{4,3,2,1,0:T(8,128)(2,1)}, u32[]{:S(2)}) copy-start(bf16[4,6,2,256,128]{4,3,2,1,0:T(8,128)(2,1)} %get-tuple-element.113.kv_ref.refs_6_) | copy-start | bytes 9437188
  88.2 15.2 %copy-start.9 = (bf16[1024,128]{1,0:T(8,128)(2,1)S(1)}, bf16[1024,128]{1,0:T(8,128)(2,1)}, u32[]{:S(2)}) copy-start(bf16[1024,128]{1,0:T(8,128)(2,1)} %get-tuple-element.115.mk_ref.refs_5_.refs_12_) | copy-start | bytes 786436
  88.2 15.2 %copy-start.10 = (bf16[512,128]{1,0:T(8,128)(2,1)S(1)}, bf16[512,128]{1,0:T(8,128)(2,1)}, u32[]{:S(2)}) copy-start(bf16[512,128]{1,0:T(8,128)(2,1)} %get-tuple-element.114.mq_ref.refs_4_) | copy-start | bytes 393220
  103.4 13.3 %copy-start.5 = (bf16[512,768]{1,0:T(8,128)(2,1)}, bf16[512,768]{1,0:T(8,128)(2,1)S(1)}, u32[]{:S(2)}) copy-start(bf16[512,768]{1,0:T(8,128)(2,1)S(1)} %get-tuple-element.132.refs_6_) | copy-start | bytes 2359300
  103.4 13.3 %copy-start.6 = (bf16[512,768]{1,0:T(8,128)(2,1)}, bf16[512,768]{1,0:T(8,128)(2,1)S(1)}, u32[]{:S(2)}) copy-start(bf16[512,768]{1,0:T(8,128)(2,1)S(1)} %get-tuple-element.119.refs_10_) | copy-start | bytes 2359300
  103.4 13.3 %copy-start.7 = (bf16[6,512,128]{2,1,0:T(8,128)(2,1)}, bf16[6,512,128]{2,1,0:T(8,128)(2,1)S(1)}, u32[]{:S(2)}) copy-start(bf16[6,512,128]{2,1,0:T(8,128)(2,1)S(1)} %get-tuple-element.111.q_ref.refs_0_) | copy-start | bytes 2359300
  116.7 1.1 copy-start.2
  117.8 0.9 copy-start.8

commit v6 on v5

--- a/solution.py
+++ b/solution.py
@@ -297,12 +297,15 @@
         second_ref[...] = norm(hidden, gain_ref[...])
         total[...] = hidden
 
-    inner = dot(second_ref[...], up_ref[...])
-    active, slope = gelu_both(inner)
-    active = active.astype(bf16)
-    active_ref[...] = active
-    slope_ref[...] = slope.astype(bf16)
-    total[...] += dot(active, down_ref[...])
+    rows = total.shape[0] // 2
+    halves = [pl.ds(at * rows, rows) for at in (0, 1)]
+    inners = [dot(second_ref[half, :], up_ref[...]) for half in halves]
+    for half, inner in zip(halves, inners):
+        active, slope = gelu_both(inner)
+        active = active.astype(bf16)
+        active_ref[half, :] = active
+        slope_ref[half, :] = slope.astype(bf16)
+        total[half, :] += dot(active, down_ref[...])
 
     @pl.when(step == steps - 1)
     def _():
@@ -347,7 +350,7 @@
         out_shape=[shape(f32), shape(f32), shape(bf16), wide, wide, shape(bf16)]
         + [jax.ShapeDtypeStruct(last, bf16)],
         scratch_shapes=[pltpu.VMEM((rows, width), f32), pltpu.VMEM((rows, width), bf16)],
-        compiler_params=pltpu.CompilerParams(vmem_limit_bytes=48 << 20),
+        compiler_params=pltpu.CompilerParams(vmem_limit_bytes=62 << 20),
         cost_estimate=pl.CostEstimate(
             flops=2 * rows * width * (4 * up.shape[1] // 2 + 2 * width),
             bytes_accessed=width * width * 22 + rows * width * 32,
@@ -384,7 +387,8 @@
 
         @pl.when(step == 0)
         def _():
-            here.greet(ALL_PARTNERS)
+            here.hail(*ALL_PARTNERS)
+            here.heard(len(ALL_PARTNERS))
             for flow in running:
                 flow.act(0)
 
@@ -406,7 +410,7 @@
     if laid:
         rows = dup_ref.shape[1]
         for at in range(8):
-            zl, zh, x = at // 4, at // 2 % 2, at % 2
+            zl, x, zh = at // 4, at // 2 % 2, at % 2
             first = ((zh * 2 + zl) * 2 + x) * rows
             dup_ref[at] = upper[first : first + rows]
         for x, core, y in ((a, b, c) for a in (0, 1) for b in (0, 1) for c in (0, 1)):
@@ -437,7 +441,7 @@
         value = dot(mixed[...], branch[...], TN).astype(bf16)
         if laid:
             rows, wide = dwo_ref.shape[1:]
-            for at, (core, y, tm) in enumerate(spots(BY_Y_LATE)):
+            for at, (core, y, tm) in enumerate(spots(BY_Y)):
                 first = (tm * 2 + core) * rows
                 dwo_ref[at] = value[first : first + rows, y * wide : (y + 1) * wide]
         else:
@@ -529,7 +533,6 @@
 
 MESH = pl.DeviceIdType.MESH
 BY_Y = ("core", "y", "zl", "x", "zh")
-BY_Y_LATE = ("core", "y", "zl", "zh", "x")
 BY_ZL = ("core", "zl", "y", "x", "zh")
 BY_X = ("core", "x", "zl", "y", "zh")
 BY_YX = ("core", "y", "x", "zl", "zh")
@@ -565,30 +568,31 @@
                 tm = tm + one * {"zh": 4, "zl": 2, "x": 1}[name]
         return (tm, seq)
 
-    def greet(self, partners):
+    def hail(self, *partners):
+        self.hail_all([self.partner(*names) for names in partners])
+
+    def hail_line(self, *more):
+        z, core = self.tm // 2, self.bit["core"]
+        self.hail_all(
+            [
+                (
+                    lax.rem(z + dz, 4) * 2 + self.bit["x"],
+                    self.bit["y"] * 2 + lax.rem(core + dc, 2),
+                )
+                for dz in range(4)
+                for dc in range(2)
+                if dz or dc
+            ]
+            + [self.partner(name) for name in more]
+        )
+
+    def hail_all(self, places):
         barrier = pltpu.get_barrier_semaphore()
-        for names in partners:
-            pl.semaphore_signal(
-                barrier, inc=1, device_id=self.partner(*names), device_id_type=MESH
-            )
-        pl.semaphore_wait(barrier, len(partners))
-
-
-    def greet_line(self, *more):
-        barrier = pltpu.get_barrier_semaphore()
-        z, core = self.tm // 2, self.bit["core"]
-        places = [
-            (
-                lax.rem(z + dz, 4) * 2 + self.bit["x"],
-                self.bit["y"] * 2 + lax.rem(core + dc, 2),
-            )
-            for dz in range(4)
-            for dc in range(2)
-            if dz or dc
-        ] + [self.partner(name) for name in more]
         for place in places:
             pl.semaphore_signal(barrier, inc=1, device_id=place, device_id_type=MESH)
-        pl.semaphore_wait(barrier, len(places))
+
+    def heard(self, count):
+        pl.semaphore_wait(pltpu.get_barrier_semaphore(), count)
 
 
 ALL_PARTNERS = (("core",), ("y",), ("zl",), ("x",), ("zh",))
@@ -814,6 +818,7 @@
         self.here, self.rows = here, rows
         self.sums, self.send, self.got_core, self.across, self.got_x = refs[:5]
         self.sems = refs[5]
+        self.before = None
 
     def turns(self, blocks):
         return (3, 1, 0, 2) if blocks == 4 else tuple(reversed(range(blocks)))
@@ -858,12 +863,16 @@
         ref[slot, 1, there, :] = dv
         if 2 * half == 4 * block:
             if number == 3:
+                if self.before is not None:
+                    self.before()
                 self.copy_core(pair, 1).start()
             elif number == 2:
                 self.copy_core(pair, 0).start()
             elif number == 0:
                 self.pass_on(pair)
         elif number == 1:
+            if self.before is not None:
+                self.before()
             for far in (1, 0):
                 self.copy_core(pair, far).start()
         else:
@@ -914,8 +923,10 @@
     small_refs, kv_small, refs = refs[:6], refs[6], refs[7:]
     flows = len(orders)
     locals_, refs = refs[:flows], refs[flows:]
-    dq_l, dkv_l, dq_s, dkv_s = refs[:4]
-    sums, refs = refs[4 : 4 + flows], refs[4 + flows :]
+    given, gain, refs = refs[:5], refs[5], refs[6:]
+    dq_l, dkv_l, dq_s, dkv_s, view_ref, gain_ref = refs[:6]
+    sums, refs = refs[6 : 6 + flows], refs[6 + flows :]
+    held, load_sems, dq_all, grads, home_refs, refs = refs[:5], refs[5], refs[6], refs[7], refs[8:11], refs[11:]
     keys_l, values_l, keys_s, values_s = refs[:4]
     ex_l, ex_s, refs = refs[4:10], refs[10:16], refs[16:]
     here = Here()
@@ -926,12 +937,26 @@
         Flow(here, orders[flow], locals_[flow], refs, True, ends[flow]) for flow in range(flows)
     ]
     step = pl.program_id(0)
+    home = Restore(here, *home_refs)
+    loads = [
+        pltpu.make_async_copy(source, there, load_sems.at[i])
+        for i, (source, there) in enumerate(zip(given, held))
+    ]
 
     @pl.when(step == 0)
     def _():
-        here.greet(ALL_PARTNERS)
-        for flow in running:
-            flow.act(0)
+        here.hail_line("x", "y")
+        for load in loads:
+            load.start()
+
+    def before():
+        @pl.when(step == 0)
+        def _():
+            here.heard(9)
+            for flow in running:
+                flow.act(0)
+
+    large.before = before
 
     def attention(exchange, pair, refs, kv_ref, keys_at, values_at, block, dq_ref):
         q_ref, do_ref, o_ref, l_ref, mq_ref, mk_ref = refs
@@ -946,26 +971,36 @@
             block, exchange, pair,
         )
 
-    half = pairs // 2
-    late = step >= half + pairs
-
-    @pl.when((step >= half) & (step < half + pairs))
+    @pl.when(step < pairs)
     def _():
-        pair = step - half
-        attention(large, pair, large_refs, kv_large, keys_l, values_l, blocks[0], dq_l)
-
-    @pl.when((step < half) | late)
+        attention(large, step, large_refs, kv_large, keys_l, values_l, blocks[0], dq_l)
+        dq_all[step] = dq_l[...]
+
+    @pl.when(step >= pairs)
     def _():
-        pair = jnp.where(late, step - pairs, step)
-        attention(small, pair, small_refs, kv_small, keys_s, values_s, blocks[1], dq_s)
-
-    takes = [(half + 1 + i, small, i, dkv_s) for i in range(half)]
-    takes += [(half + 3 + i, large, i, dkv_l) for i in range(pairs - 1)]
-    for when, exchange, pair, out_ref in takes:
-
-        @pl.when(step == when)
-        def _(exchange=exchange, pair=pair, out_ref=out_ref):
-            exchange.take(pair, out_ref)
+        attention(small, step - pairs, small_refs, kv_small, keys_s, values_s, blocks[1], dq_s)
+
+    for pair in range(pairs):
+
+        @pl.when(step == pair + 2 + pair // (pairs - 1))
+        def _(pair=pair):
+            large.take(pair, dkv_l)
+
+    @pl.when(step == pairs + 2)
+    def _():
+        *weights, hidden_grad, view = held
+        for load in loads:
+            load.wait()
+        total = None
+        for which, weight in enumerate(weights):
+            for pair in range(pairs):
+                lanes = slice(pair * LANES, (pair + 1) * LANES)
+                grads[:, lanes] = dkv_l[pair, which - 1] if which else dq_all[pair]
+            product = dot(grads[...], weight[...], NT)
+            total = product if total is None else total + product
+        extra, gain_ref[...] = norm_back(total, view[...].astype(f32), gain[...])
+        home_refs[0][...] = (hidden_grad[...] + extra).astype(bf16)
+        home.start()
 
     for at in range(2 * pairs):
         todo = []
@@ -982,16 +1017,17 @@
 
     @pl.when(step == 2 * pairs - 1)
     def _():
-        large.take(pairs - 1, dkv_l)
-        for pair in range(half, pairs):
+        for pair in range(pairs):
             small.take(pair, dkv_s)
         small.end()
         large.end()
         for flow, sum_ref in zip(running, sums):
             sum_ref[...] = flow.result()
-
-
-def selves_back(large, large_kv, small, small_kv, flows, orders, ends, stages):
+        home.finish()
+        view_ref[...] = home_refs[1][...]
+
+
+def selves_back(large, large_kv, small, small_kv, flows, view, gain, orders, ends, stages):
     count, width = large[1].shape
     few = small[1].shape[0]
     pairs = width // LANES
@@ -999,9 +1035,8 @@
     shapes = [flow.shape[1:] for flow in flows]
     results = [flow_result(*flow) for flow in zip(orders, shapes, ends)]
     blocks = (largest_block(total // 2, 512), largest_block(less // 2, 512))
-    half = pairs // 2
-    first = lambda i: jnp.clip(i - half, 0, pairs - 1)
-    last = lambda i: jnp.where(i < half, i, jnp.maximum(i - pairs, half))
+    first = lambda i: jnp.minimum(i, pairs - 1)
+    last = lambda i: jnp.maximum(i - pairs, 0)
     in_specs = []
     for rows, keys, at in ((count, total, first), (few, less, last)):
         major = pl.BlockSpec((1, rows, LANES), lambda i, at=at: (at(i), 0, 0))
@@ -1010,21 +1045,29 @@
         in_specs.append(
             pl.BlockSpec((4, 1, 2, rows, LANES), lambda i, at=at: (0, at(i), 0, 0, 0))
         )
-    in_specs += [pl.BlockSpec(memory_space=pl.ANY)] * len(flows)
+    in_specs += [pl.BlockSpec(memory_space=pl.ANY)] * (len(flows) + len(view))
+    in_specs.append(whole((1, width)))
     shape = jax.ShapeDtypeStruct
     out_shape = [
         shape((count, width), bf16),
         shape((pairs, 2, count, LANES), bf16),
         shape((few, width), bf16),
         shape((pairs, 2, few, LANES), bf16),
+        shape((2, count // 2, width), bf16),
+        shape((1, width), f32),
     ] + results
     out_specs = [
         pl.BlockSpec((count, LANES), lambda i: (0, first(i))),
         whole((pairs, 2, count, LANES)),
         pl.BlockSpec((few, LANES), lambda i: (0, last(i))),
         whole((pairs, 2, few, LANES)),
+        whole((2, count // 2, width)),
+        whole((1, width)),
     ] + [whole(result.shape) for result in results]
-    scratch = [pltpu.VMEM((total, LANES), bf16)] * 2 + [pltpu.VMEM((less, LANES), bf16)] * 2
+    scratch = [pltpu.VMEM(value.shape, value.dtype) for value in view]
+    scratch += [pltpu.SemaphoreType.DMA((len(view),)), pltpu.VMEM((pairs, count, LANES), bf16)]
+    scratch += [pltpu.VMEM((count, width), bf16)] + restore_scratch(count // 2, width)
+    scratch += [pltpu.VMEM((total, LANES), bf16)] * 2 + [pltpu.VMEM((less, LANES), bf16)] * 2
     scratch += exchange_scratch(pairs, count) + exchange_scratch(pairs, few)
     for flow in range(len(flows)):
         scratch += flow_scratch(orders[flow], shapes[flow], True, ends[flow])
@@ -1044,32 +1087,29 @@
             transcendentals=count * total * width // HALF,
         ),
         name="selves_back",
-    )(*large, large_kv, *small, small_kv, *flows)
-    return result[:4], result[4:]
-
-
-LAST_ORDERS = (BY_YX, BY_X, BY_ZL)
+    )(*large, large_kv, *small, small_kv, *flows, *view, gain)
+    return result[:4], result[4:6], result[6:]
+
+
+LAST_ORDERS = (BY_YX, BY_X, BY_YX)
 GAIN_ORDER = ("core", "y", "x", "zl", "zh")
-LATE_ORDERS = (("x",), ("x", "zh"), ("x",))
-LATE_STAGES = (
-    {2: 2, 4: 3},
-    {2: 2, 3: 3, 4: 4},
-    {2: 2, 4: 3},
-)
+LATE_ORDER = ("x", "zh")
+LATE_ORDERS = (LATE_ORDER,) * 3
+LATE_STAGES = {3: 2, 5: 3, 6: 4}
 
 
 def last_kernel(pairs, sizes, late, *refs):
     refs = list(refs)
     take = lambda count: [refs.pop(0) for _ in range(count)]
-    given, late_refs = take(13), take(late)
-    gain, second_gain, query_gain, context_gain = take(4)
-    gl_ref, gs_ref = take(2)
+    given, late_refs = take(11), take(late)
+    gain, gain_l, second_gain, query_gain, context_gain = take(5)
+    (gs_ref,) = take(1)
     sum_refs = take(3 + late)
     (gain_ref,) = take(1)
-    held = take(13)
-    dql, dkvl, dqs, dkvs, nl, ns, wq, wk, wv, xl, xs, hl, hs = held
+    held = take(11)
+    dql, dkvl, dqs, dkvs, nl, ns, wq, wk, wv, xs, hs = held
     load_sems, normed, *grads = take(5)
-    large_back, small_back = take(3), take(3)
+    small_back = take(3)
     here = Here()
     flows = []
     for order in LAST_ORDERS:
@@ -1084,12 +1124,10 @@
         pltpu.make_async_copy(source, there, load_sems.at[i])
         for i, (source, there) in enumerate(zip(given, held))
     ]
+    here.hail_line("x", "y")
     for load in loads:
         load.start()
-    here.greet_line("x", "y")
-    for flow in late_flows:
-        flow.act(0)
-    homes = [Restore(here, *large_back), Restore(here, *small_back)]
+    home = Restore(here, *small_back)
 
     def gain_copy(step):
         return pltpu.make_async_remote_copy(
@@ -1115,6 +1153,10 @@
                 grads[which][top, lanes] = dkvl[pair, which - 1]
                 grads[which][bottom, lanes] = dkvs[pair, which - 1]
         value = dot(normed[...], grads[which][...], TN).astype(bf16)
+        if which == 0:
+            here.heard(9)
+            for late_flow in late_flows:
+                late_flow.act(0)
         rows, wide = flow.local.shape[1:]
         for at, (core, y, tm) in enumerate(spots(flow.order)):
             first = tm * 2 * rows + core * rows
@@ -1123,23 +1165,20 @@
     total = None
     for which, weight in enumerate((wq, wk, wv)):
         loads[6 + which].wait()
-        part = dot(grads[which][...], weight[...], NT)
+        part = dot(grads[which][bottom, :], weight[...], NT)
         total = part if total is None else total + part
     for load in loads[9:]:
         load.wait()
     for flow in late_flows:
         flow.act(1)
-    extra, gain_l = norm_back(total[:large], xl[...].astype(f32), gain[...])
-    large_back[0][...] = (hl[...] + extra).astype(bf16)
-    homes[0].start()
+    extra, gain_s = norm_back(total, xs[...].astype(f32), gain[...])
+    small_back[0][...] = (hs[...] + extra).astype(bf16)
+    home.start()
     for flow in flows:
         flow.act(1)
-    extra, gain_s = norm_back(total[large:], xs[...].astype(f32), gain[...])
-    small_back[0][...] = (hs[...] + extra).astype(bf16)
-    homes[1].start()
     state[0] = jnp.zeros(state.shape[1:], f32)
     for row, value in enumerate(
-        (gain_l + gain_s, second_gain[...], query_gain[...], context_gain[...])
+        (gain_l[...] + gain_s, second_gain[...], query_gain[...], context_gain[...])
     ):
         state[0, row : row + 1, :] = value
     gain_copy(0).start()
@@ -1147,9 +1186,9 @@
         if stage > 1:
             for flow in flows:
                 flow.act(stage)
-        for flow, stages in zip(late_flows, LATE_STAGES):
-            if stage in stages:
-                flow.act(stages[stage])
+        if stage in LATE_STAGES:
+            for flow in late_flows:
+                flow.act(LATE_STAGES[stage])
         if stage <= 5:
             gain_copy(stage - 1).wait()
             total = state[stage - 1] + got[stage - 1]
@@ -1162,9 +1201,7 @@
                 gain_ref[...] = turned[:, : gain_ref.shape[1]]
     for flow, sum_ref in zip(flows + late_flows, sum_refs):
         sum_ref[...] = flow.result()
-    homes[0].finish()
-    gl_ref[...] = large_back[1][...]
-    homes[1].finish()
+    home.finish()
     gs_ref[...] = small_back[1][...]
 
 
@@ -1177,7 +1214,7 @@
     scratch = [pltpu.VMEM(value.shape, value.dtype) for value in given]
     scratch += [pltpu.SemaphoreType.DMA((len(given),))]
     scratch += [pltpu.VMEM((tokens, width), bf16)] * 4
-    scratch += restore_scratch(count // 2, width) + restore_scratch(few // 2, width)
+    scratch += restore_scratch(few // 2, width)
     for order in LAST_ORDERS:
         scratch.append(pltpu.VMEM((32,) + block, bf16))
         scratch += flow_scratch(order, block, False, True)
@@ -1192,9 +1229,8 @@
     vmem = pl.BlockSpec(memory_space=pltpu.VMEM)
     result = pl.pallas_call(
         functools.partial(last_kernel, width // LANES, (count, few), len(late)),
-        in_specs=[anywhere] * (len(given) + len(late)) + [vmem] * 4,
+        in_specs=[anywhere] * (len(given) + len(late)) + [vmem] * 5,
         out_shape=[
-            shape((2, count // 2, width), bf16),
             shape((2, few // 2, width), bf16),
         ]
         + [shape((4,) + block, bf16)] * 3
@@ -1211,7 +1247,7 @@
         ),
         name="last_sums",
     )(*given, *late, *gains)
-    return result[:2], result[2:5], result[5:-1], result[-1]
+    return result[0], result[1:4], result[4:-1], result[-1]
 
 
 def results_kernel(*refs):
@@ -1285,11 +1321,28 @@
 
     @pl.when(step == 0)
     def _():
+        here.hail_line("x")
         for load in loads:
             load.start()
-        here.greet_line("x")
-
+
+    def before():
+        @pl.when(step == 0)
+        def _():
+            here.heard(8)
+
+    exchange.before = before
     home = Restore(here, *home_refs)
+
+    fill_keys(keys_at, values_at, kv_ref)
+
+    @pl.when(step >= 2)
+    def _():
+        exchange.free(step - 2)
+
+    dq[step] = pair_back(
+        q_ref[0], do_ref[...], o_ref[0], l_ref[0], mq_ref[...], keys_at, values_at, mk_ref,
+        block, exchange, step,
+    )
 
     @pl.when(step == 1)
     def _():
@@ -1298,17 +1351,6 @@
         wide = jnp.concatenate([united[i] for i in range(pairs)], axis=1)
         home_refs[0][...] = (merged_l[...] + dot(wide, wo[...])).astype(bf16)
         home.start()
-
-    fill_keys(keys_at, values_at, kv_ref)
-
-    @pl.when(step >= 2)
-    def _():
-        exchange.free(step - 2)
-
-    dq[step] = pair_back(
-        q_ref[0], do_ref[...], o_ref[0], l_ref[0], mq_ref[...], keys_at, values_at, mk_ref,
-        block, exchange, step,
-    )
 
     @pl.when(step >= 3)
     def _():
@@ -1469,7 +1511,7 @@
     z, core = here.tm // 2, here.bit["core"]
     stay = core == z // 2
 
-    here.greet_line("x")
+    here.hail_line("x")
 
     odd = lax.rem(z, 2)
     from_seq = (odd, 1 - odd)
@@ -1526,6 +1568,7 @@
             far(which, 0, source, there).wait_recv()
 
     moves = ((0, clip_ref, clip.at[0, 0]), (1, small_ref, xs), (2, large_ref, xl), (3, cot_ref, cot))
+    here.heard(8)
     move(*moves[0])
     move(*moves[1])
     loads = [
@@ -1794,7 +1837,7 @@
             jax.ShapeDtypeStruct(query.shape, f32),
         ],
         scratch_shapes=[pltpu.VMEM((4 * rows, LANES), bf16)] * 4,
-        compiler_params=pltpu.CompilerParams(vmem_limit_bytes=40 << 20),
+        compiler_params=pltpu.CompilerParams(vmem_limit_bytes=62 << 20),
         cost_estimate=pl.CostEstimate(
             flops=64 * count * rows * pairs * LANES,
             bytes_accessed=32 * count * pairs * LANES,
@@ -1809,14 +1852,14 @@
 
 
 CROSS_ORDERS = (BY_Y[:2], BY_ZL[:2])
-SELVES_ORDERS = (BY_Y_LATE[:4], BY_ZL[:3], BY_Y_LATE[:4], BY_Y[2:], BY_ZL[2:])
+SELVES_ORDERS = (BY_Y[:3], BY_ZL[:3], BY_Y[:3], BY_Y[2:], BY_ZL[2:])
 SELVES_ENDS = (False, False, False, True, True)
 SELVES_STAGES = (
-    (1, 6, 8, 11),
-    (1, 6, 11),
-    (1, 6, 8, 11),
-    (3, 5, 7, 8, 9),
-    (3, 5, 7, 8, 9),
+    (0, 4, 11),
+    (0, 4, 11),
+    (0, 5, 11),
+    (1, 3, 5, 7, 9),
+    (1, 3, 5, 7, 9),
 )
 
 
@@ -1847,27 +1890,28 @@
         second_gain, up_weight, down_weight, True, (first, other), CROSS_ORDERS,
     )
     still = (8, rows // 2, width)
-    selves, sums = selves_back(
+    selves, (large_grad, large_gain), sums = selves_back(
         (large_q, large_mixed_grad, large_mixed, large_logsum, large_mask_q, large_mask_k),
         large_kv,
         (small_q, small_mixed_grad, small_mixed, small_logsum, small_mask_q, small_mask_k),
         small_kv,
         (
-            up_grad.reshape(16, 2 * rows, width), down_grad.reshape(8, 4 * rows, width),
-            output_grad.reshape(16, rows, width // 2),
+            up_grad.reshape(8, 4 * rows, width), down_grad.reshape(8, 4 * rows, width),
+            output_grad.reshape(8, 2 * rows, width // 2),
             first.reshape(still), other.reshape(still),
         ),
+        (query_weight, key_weight, value_weight, large_hidden, large_view), first_gain,
         SELVES_ORDERS, SELVES_ENDS, SELVES_STAGES,
     )
     up, down, output, first, other = sums
-    (large_grad, small_grad), last, late, gains = last_sums(
+    small_grad, last, late, gains = last_sums(
         tuple(selves) + (large_normed, small_normed, query_weight, key_weight, value_weight)
-        + (large_view, small_view, large_hidden, small_hidden),
+        + (small_view, small_hidden),
         (
-            up.reshape(2, rows, width), down.reshape(4, rows, width),
-            output.reshape(2, rows // 2, width // 2),
+            up.reshape(4, rows, width), down.reshape(4, rows, width),
+            output.reshape(4, rows // 2, width // 2),
         ),
-        (first_gain, second_gain_grad, query_gain_grad, context_gain_grad),
+        (first_gain, large_gain, second_gain_grad, query_gain_grad, context_gain_grad),
     )
     return results(united_view, large_grad, small_grad, last, late, first, other, gains)
 

time: 345 us -> 340 us (0.986)
  local copies, waits for them, and re-layouts: 7.22 us -> 1.56 us
    pallas_call x1, Pallas kernels: 64.7 us -> 54.6 us  [last_sums(): pl.pallas_call(functools.partial(last_kernel, width // LANES, (count, few...]
    pallas_call x1, Pallas kernels: 81.2 us -> 89.5 us  [selves_back(): pl.pallas_call(functools.partial(selves_kernel, pairs, (orders, ends, sta...]
    unnamed x26 -> x0, local copies, waits for them, and re-layouts: 5.66 us -> none
where the time goes in v6:
time: 340 us; the launch traced here: 335 us
  Pallas kernels  331 us (97%)
    pallas_call x1, Pallas kernels, selves_back(): pl.pallas_call(functools.partial(selves_kernel, pairs, (orders, ends, sta...  89.5 us
    pallas_call x1, Pallas kernels, begin(): pl.pallas_call(functools.partial(begin_kernel, pairs), in_specs=[anywhere...  80.9 us
    pallas_call x1, Pallas kernels, last_sums(): pl.pallas_call(functools.partial(last_kernel, width // LANES, (count, few...  54.6 us
    pallas_call x1, Pallas kernels, cross_back(): pl.pallas_call(functools.partial(cross_kernel, pairs, block), grid=(pairs...  36.5 us
    pallas_call x1, Pallas kernels, back(): pl.pallas_call(functools.partial(back_kernel, steps, len(mixed_l), (large...  32.8 us
    pallas_call x1, Pallas kernels, rest(): pl.pallas_call(functools.partial(rest_kernel, steps, len(mixed), is_query...  16.1 us
    pallas_call x1, Pallas kernels, cross_attend(): pl.pallas_call(cross_attend_kernel, grid=(pairs,), in_specs=[one, pl.Bloc...  15.1 us

profile of v6, /device:TPU:1, one launch (start us, length us, event | category | flops | bytes accessed | tf_op | source)
XLA Modules:
  0.0 335.3 jit_solution(5925632556572418816)
XLA Ops:
  0.7 0.7 convert.4
  1.3 0.2 slice.4
  1.6 0.7 maximum_convert_fusion
  2.3 0.6 reshape.87.refs_13_
  2.9 0.7 broadcast_in_dim.2.refs_3_
  3.7 80.9 %begin.1 = (bf16[512,768]{1,0:T(8,128)(2,1)}, bf16[256,768]{1,0:T(8,128)(2,1)}, bf16[512,768]{1,0:T(8,128)(2,1)}, bf16[4,6,2,512,128]{4,3,2,1,0:T(8,128)(2,1)}, ...) custom-call(bf16[2,256,768]{2,1,0:T(8,128)(2,1)} %refs_0_.1, ...), custom_call_target="tpu_custom_call" | custom-call | flops 23756537856 | bytes 41943040 | tf_op jit(solution)/shard_map/begin/pallas_call | solution.py:1799
  84.6 16.1 %rest.1 = (f32[512,768]{1,0:T(8,128)}, f32[512,768]{1,0:T(8,128)}, bf16[512,768]{1,0:T(8,128)(2,1)}, bf16[512,3072]{1,0:T(8,128)(2,1)}, bf16[512,3072]{1,0:T(8,1...) custom-call(bf16[512,768]{1,0:T(8,128)(2,1)} %get-tuple-element.108.refs_0_.refs_23_, ...), custom_call_target="tpu_custom_call" | custom-call | flops 6039797760 | bytes 25559040 | tf_op jit(solution)/shard_map/rest/pallas_call | solution.py:340
  100.7 15.1 %cross_attend.1 = (bf16[6,512,128]{2,1,0:T(8,128)(2,1)}, f32[6,512,128]{2,1,0:T(8,128)}) custom-call(bf16[6,512,128]{2,1,0:T(8,128)(2,1)} %get-tuple-element.112.q_ref.refs_0_, bf16[4,6,2,256,128]{4,3,2,1,0:T(8,128)(2,1)} %get-tuple-element.114.kv_ref.refs_6_, bf16[512,128]{1,0:T(8,128)(2,1)} %get-tuple-element.115.mq_ref.refs_4_, ...), custom_call_target="tpu_custom_call" | custom-call | flops 6442450944 | bytes 12582912 | tf_op jit(solution)/shard_map/cross_attend/pallas_call | solution.py:1825
  115.8 36.5 %cross_back.1 = (bf16[2,256,768]{2,1,0:T(8,128)(2,1)}, f32[512,768]{1,0:T(8,128)}, f32[256,768]{1,0:T(8,128)}, bf16[4,384,768]{2,1,0:T(8,128)(2,1)}, bf16[4,384,...) custom-call(bf16[6,512,128]{2,1,0:T(8,128)(2,1)} %get-tuple-element.112.q_ref.refs_0_, ...), custom_call_target="tpu_custom_call" | custom-call | flops 8053063680 | bytes 25165824 | tf_op jit(solution)/shard_map/cross_back/pallas_call | solution.py:1401
  152.2 32.8 %back.1 = (f32[512,768]{1,0:T(8,128)}, f32[256,768]{1,0:T(8,128)}, bf16[512,768]{1,0:T(8,128)(2,1)}, bf16[256,768]{1,0:T(8,128)(2,1)}, bf16[32,96,768]{2,1,0:T(8...) custom-call(f32[512,768]{1,0:T(8,128)} %get-tuple-element.127.refs_0, ...), custom_call_target="tpu_custom_call" | custom-call | flops 16307453952 | bytes 44826624 | tf_op jit(solution)/shard_map/back/pallas_call | solution.py:486
  185.1 89.5 %selves_back.1 = (bf16[512,768]{1,0:T(8,128)(2,1)}, bf16[6,2,512,128]{3,2,1,0:T(8,128)(2,1)}, bf16[256,768]{1,0:T(8,128)(2,1)}, bf16[6,2,256,128]{3,2,1,0:T(8,12...) custom-call(bf16[6,512,128]{2,1,0:T(8,128)(2,1)} %get-tuple-element., ...), custom_call_target="tpu_custom_call" | custom-call | flops 20132659200 | bytes 25165824 | tf_op jit(solution)/shard_map/selves_back/pallas_call | solution.py:1074
  274.6 54.6 %last_sums.1 = (bf16[2,128,768]{2,1,0:T(8,128)(2,1)}, bf16[4,48,384]{2,1,0:T(8,128)(2,1)}, bf16[4,48,384]{2,1,0:T(8,128)(2,1)}, bf16[4,48,384]{2,1,0:T(8,128)(2,...) custom-call(bf16[512,768]{1,0:T(8,128)(2,1)} %get-tuple-element.157., ...), custom_call_target="tpu_custom_call" | custom-call | flops 18119393280 | bytes 23592960 | tf_op jit(solution)/shard_map/last_sums/pallas_call | solution.py:1230
  329.2 5.6 %results.1 = (bf16[2,256,768]{2,1,0:T(8,128)(2,1)}, f32[2,256,768]{2,1,0:T(8,128)}, f32[2,128,768]{2,1,0:T(8,128)}, f32[1,96]{1,0:T(1,128)}, f32[96,768]{1,0:T(8...) custom-call(bf16[2,256,768]{2,1,0:T(8,128)(2,1)} %get-tuple-element., ...), custom_call_target="tpu_custom_call" | custom-call | bytes 14680064 | tf_op jit(solution)/shard_map/results/pallas_call | solution.py:1288

commit v7 on v6

--- a/solution.py
+++ b/solution.py
@@ -1169,13 +1169,13 @@
         total = part if total is None else total + part
     for load in loads[9:]:
         load.wait()
+    for flow in flows:
+        flow.act(1)
     for flow in late_flows:
         flow.act(1)
     extra, gain_s = norm_back(total, xs[...].astype(f32), gain[...])
     small_back[0][...] = (hs[...] + extra).astype(bf16)
     home.start()
-    for flow in flows:
-        flow.act(1)
     state[0] = jnp.zeros(state.shape[1:], f32)
     for row, value in enumerate(
         (gain_l[...] + gain_s, second_gain[...], query_gain[...], context_gain[...])
@@ -1857,9 +1857,9 @@
 SELVES_STAGES = (
     (0, 4, 11),
     (0, 4, 11),
-    (0, 5, 11),
-    (1, 3, 5, 7, 9),
-    (1, 3, 5, 7, 9),
+    (0, 6, 11),
+    (1, 3, 6, 8, 10),
+    (1, 3, 6, 8, 10),
 )
 
 

time: 340 us -> 329 us (0.968)
  Pallas kernels: 331 us -> 320 us
    pallas_call x1, Pallas kernels: 89.5 us -> 83.7 us  [selves_back(): pl.pallas_call(functools.partial(selves_kernel, pairs, (orders, ends, sta...]
    pallas_call x1, Pallas kernels: 54.6 us -> 49.6 us  [last_sums(): pl.pallas_call(functools.partial(last_kernel, width // LANES, (count, few...]
where the time goes in v7:
time: 329 us; the launch traced here: 324 us
  Pallas kernels  320 us (97%)
    pallas_call x1, Pallas kernels, selves_back(): pl.pallas_call(functools.partial(selves_kernel, pairs, (orders, ends, sta...  83.7 us
    pallas_call x1, Pallas kernels, begin(): pl.pallas_call(functools.partial(begin_kernel, pairs), in_specs=[anywhere...  80.9 us
    pallas_call x1, Pallas kernels, last_sums(): pl.pallas_call(functools.partial(last_kernel, width // LANES, (count, few...  49.6 us
    pallas_call x1, Pallas kernels, cross_back(): pl.pallas_call(functools.partial(cross_kernel, pairs, block), grid=(pairs...  36.5 us
    pallas_call x1, Pallas kernels, back(): pl.pallas_call(functools.partial(back_kernel, steps, len(mixed_l), (large...  32.8 us
    pallas_call x1, Pallas kernels, rest(): pl.pallas_call(functools.partial(rest_kernel, steps, len(mixed), is_query...  16.1 us
    pallas_call x1, Pallas kernels, cross_attend(): pl.pallas_call(cross_attend_kernel, grid=(pairs,), in_specs=[one, pl.Bloc...  15.1 us

profile of v7, /device:TPU:1, one launch (start us, length us, event | category | flops | bytes accessed | tf_op | source)
XLA Modules:
  0.0 324.5 jit_solution(16947409604968763086)
XLA Ops:
  0.7 0.7 convert.4
  1.3 0.2 slice.4
  1.6 0.7 maximum_convert_fusion
  2.3 0.6 reshape.87.refs_13_
  2.9 0.7 broadcast_in_dim.2.refs_3_
  3.7 80.9 %begin.1 = (bf16[512,768]{1,0:T(8,128)(2,1)}, bf16[256,768]{1,0:T(8,128)(2,1)}, bf16[512,768]{1,0:T(8,128)(2,1)}, bf16[4,6,2,512,128]{4,3,2,1,0:T(8,128)(2,1)}, ...) custom-call(bf16[2,256,768]{2,1,0:T(8,128)(2,1)} %refs_0_.1, ...), custom_call_target="tpu_custom_call" | custom-call | flops 23756537856 | bytes 41943040 | tf_op jit(solution)/shard_map/begin/pallas_call | solution.py:1799
  84.6 16.1 %rest.1 = (f32[512,768]{1,0:T(8,128)}, f32[512,768]{1,0:T(8,128)}, bf16[512,768]{1,0:T(8,128)(2,1)}, bf16[512,3072]{1,0:T(8,128)(2,1)}, bf16[512,3072]{1,0:T(8,1...) custom-call(bf16[512,768]{1,0:T(8,128)(2,1)} %get-tuple-element.108.refs_0_.refs_23_, ...), custom_call_target="tpu_custom_call" | custom-call | flops 6039797760 | bytes 25559040 | tf_op jit(solution)/shard_map/rest/pallas_call | solution.py:340
  100.7 15.1 %cross_attend.1 = (bf16[6,512,128]{2,1,0:T(8,128)(2,1)}, f32[6,512,128]{2,1,0:T(8,128)}) custom-call(bf16[6,512,128]{2,1,0:T(8,128)(2,1)} %get-tuple-element.112.q_ref.refs_0_, bf16[4,6,2,256,128]{4,3,2,1,0:T(8,128)(2,1)} %get-tuple-element.114.kv_ref.refs_6_, bf16[512,128]{1,0:T(8,128)(2,1)} %get-tuple-element.115.mq_ref.refs_4_, ...), custom_call_target="tpu_custom_call" | custom-call | flops 6442450944 | bytes 12582912 | tf_op jit(solution)/shard_map/cross_attend/pallas_call | solution.py:1825
  115.8 36.5 %cross_back.1 = (bf16[2,256,768]{2,1,0:T(8,128)(2,1)}, f32[512,768]{1,0:T(8,128)}, f32[256,768]{1,0:T(8,128)}, bf16[4,384,768]{2,1,0:T(8,128)(2,1)}, bf16[4,384,...) custom-call(bf16[6,512,128]{2,1,0:T(8,128)(2,1)} %get-tuple-element.112.q_ref.refs_0_, ...), custom_call_target="tpu_custom_call" | custom-call | flops 8053063680 | bytes 25165824 | tf_op jit(solution)/shard_map/cross_back/pallas_call | solution.py:1401
  152.2 32.8 %back.1 = (f32[512,768]{1,0:T(8,128)}, f32[256,768]{1,0:T(8,128)}, bf16[512,768]{1,0:T(8,128)(2,1)}, bf16[256,768]{1,0:T(8,128)(2,1)}, bf16[32,96,768]{2,1,0:T(8...) custom-call(f32[512,768]{1,0:T(8,128)} %get-tuple-element.127.refs_0, ...), custom_call_target="tpu_custom_call" | custom-call | flops 16307453952 | bytes 44826624 | tf_op jit(solution)/shard_map/back/pallas_call | solution.py:486
  185.1 83.7 %selves_back.1 = (bf16[512,768]{1,0:T(8,128)(2,1)}, bf16[6,2,512,128]{3,2,1,0:T(8,128)(2,1)}, bf16[256,768]{1,0:T(8,128)(2,1)}, bf16[6,2,256,128]{3,2,1,0:T(8,12...) custom-call(bf16[6,512,128]{2,1,0:T(8,128)(2,1)} %get-tuple-element., ...), custom_call_target="tpu_custom_call" | custom-call | flops 20132659200 | bytes 25165824 | tf_op jit(solution)/shard_map/selves_back/pallas_call | solution.py:1074
  268.8 49.6 %last_sums.1 = (bf16[2,128,768]{2,1,0:T(8,128)(2,1)}, bf16[4,48,384]{2,1,0:T(8,128)(2,1)}, bf16[4,48,384]{2,1,0:T(8,128)(2,1)}, bf16[4,48,384]{2,1,0:T(8,128)(2,...) custom-call(bf16[512,768]{1,0:T(8,128)(2,1)} %get-tuple-element.157., ...), custom_call_target="tpu_custom_call" | custom-call | flops 18119393280 | bytes 23592960 | tf_op jit(solution)/shard_map/last_sums/pallas_call | solution.py:1230
  318.4 5.6 %results.1 = (bf16[2,256,768]{2,1,0:T(8,128)(2,1)}, f32[2,256,768]{2,1,0:T(8,128)}, f32[2,128,768]{2,1,0:T(8,128)}, f32[1,96]{1,0:T(1,128)}, f32[96,768]{1,0:T(8...) custom-call(bf16[2,256,768]{2,1,0:T(8,128)(2,1)} %get-tuple-element., ...), custom_call_target="tpu_custom_call" | custom-call | bytes 14680064 | tf_op jit(solution)/shard_map/results/pallas_call | solution.py:1288

commit v8 on v7

--- a/solution.py
+++ b/solution.py
@@ -1448,7 +1448,7 @@
         va0[here, :] = jnp.where(low, values, one)
         va1[here, :] = jnp.where(low, one, values)
     count = q_ref.shape[1]
-    block = largest_block(count, 256)
+    block = largest_block(count, 256 if total > 1024 else 512)
     low = lax.broadcasted_iota(jnp.int32, (block, LANES), 1) < HALF
     for number in range(count // block):
         here = pl.ds(number * block, block)

time: 329 us -> 329 us (level)
  no operation moved by 1% of the time
where the time goes in v8:
time: 329 us; the launch traced here: 324 us
  Pallas kernels  320 us (97%)
    pallas_call x1, Pallas kernels, selves_back(): pl.pallas_call(functools.partial(selves_kernel, pairs, (orders, ends, sta...  83.7 us
    pallas_call x1, Pallas kernels, begin(): pl.pallas_call(functools.partial(begin_kernel, pairs), in_specs=[anywhere...  80.9 us
    pallas_call x1, Pallas kernels, last_sums(): pl.pallas_call(functools.partial(last_kernel, width // LANES, (count, few...  49.6 us
    pallas_call x1, Pallas kernels, cross_back(): pl.pallas_call(functools.partial(cross_kernel, pairs, block), grid=(pairs...  36.5 us
    pallas_call x1, Pallas kernels, back(): pl.pallas_call(functools.partial(back_kernel, steps, len(mixed_l), (large...  32.8 us
    pallas_call x1, Pallas kernels, rest(): pl.pallas_call(functools.partial(rest_kernel, steps, len(mixed), is_query...  16.1 us
    pallas_call x1, Pallas kernels, cross_attend(): pl.pallas_call(cross_attend_kernel, grid=(pairs,), in_specs=[one, pl.Bloc...  14.5 us

profile of v8, /device:TPU:1, one launch (start us, length us, event | category | flops | bytes accessed | tf_op | source)
XLA Modules:
  0.0 324.0 jit_solution(17399098742377030813)
XLA Ops:
  0.7 0.7 convert.4
  1.3 0.2 slice.4
  1.6 0.7 maximum_convert_fusion
  2.3 0.6 reshape.87.refs_13_
  2.9 0.7 broadcast_in_dim.2.refs_3_
  3.7 80.9 %begin.1 = (bf16[512,768]{1,0:T(8,128)(2,1)}, bf16[256,768]{1,0:T(8,128)(2,1)}, bf16[512,768]{1,0:T(8,128)(2,1)}, bf16[4,6,2,512,128]{4,3,2,1,0:T(8,128)(2,1)}, ...) custom-call(bf16[2,256,768]{2,1,0:T(8,128)(2,1)} %refs_0_.1, ...), custom_call_target="tpu_custom_call" | custom-call | flops 23756537856 | bytes 41943040 | tf_op jit(solution)/shard_map/begin/pallas_call | solution.py:1799
  84.6 16.1 %rest.1 = (f32[512,768]{1,0:T(8,128)}, f32[512,768]{1,0:T(8,128)}, bf16[512,768]{1,0:T(8,128)(2,1)}, bf16[512,3072]{1,0:T(8,128)(2,1)}, bf16[512,3072]{1,0:T(8,1...) custom-call(bf16[512,768]{1,0:T(8,128)(2,1)} %get-tuple-element.108.refs_0_.refs_23_, ...), custom_call_target="tpu_custom_call" | custom-call | flops 6039797760 | bytes 25559040 | tf_op jit(solution)/shard_map/rest/pallas_call | solution.py:340
  100.7 14.5 %cross_attend.1 = (bf16[6,512,128]{2,1,0:T(8,128)(2,1)}, f32[6,512,128]{2,1,0:T(8,128)}) custom-call(bf16[6,512,128]{2,1,0:T(8,128)(2,1)} %get-tuple-element.112.q_ref.refs_0_, bf16[4,6,2,256,128]{4,3,2,1,0:T(8,128)(2,1)} %get-tuple-element.114.kv_ref.refs_6_, bf16[512,128]{1,0:T(8,128)(2,1)} %get-tuple-element.115.mq_ref.refs_4_, ...), custom_call_target="tpu_custom_call" | custom-call | flops 6442450944 | bytes 12582912 | tf_op jit(solution)/shard_map/cross_attend/pallas_call | solution.py:1825
  115.2 36.5 %cross_back.1 = (bf16[2,256,768]{2,1,0:T(8,128)(2,1)}, f32[512,768]{1,0:T(8,128)}, f32[256,768]{1,0:T(8,128)}, bf16[4,384,768]{2,1,0:T(8,128)(2,1)}, bf16[4,384,...) custom-call(bf16[6,512,128]{2,1,0:T(8,128)(2,1)} %get-tuple-element.112.q_ref.refs_0_, ...), custom_call_target="tpu_custom_call" | custom-call | flops 8053063680 | bytes 25165824 | tf_op jit(solution)/shard_map/cross_back/pallas_call | solution.py:1401
  151.7 32.8 %back.1 = (f32[512,768]{1,0:T(8,128)}, f32[256,768]{1,0:T(8,128)}, bf16[512,768]{1,0:T(8,128)(2,1)}, bf16[256,768]{1,0:T(8,128)(2,1)}, bf16[32,96,768]{2,1,0:T(8...) custom-call(f32[512,768]{1,0:T(8,128)} %get-tuple-element.127.refs_0, ...), custom_call_target="tpu_custom_call" | custom-call | flops 16307453952 | bytes 44826624 | tf_op jit(solution)/shard_map/back/pallas_call | solution.py:486
  184.6 83.7 %selves_back.1 = (bf16[512,768]{1,0:T(8,128)(2,1)}, bf16[6,2,512,128]{3,2,1,0:T(8,128)(2,1)}, bf16[256,768]{1,0:T(8,128)(2,1)}, bf16[6,2,256,128]{3,2,1,0:T(8,12...) custom-call(bf16[6,512,128]{2,1,0:T(8,128)(2,1)} %get-tuple-element., ...), custom_call_target="tpu_custom_call" | custom-call | flops 20132659200 | bytes 25165824 | tf_op jit(solution)/shard_map/selves_back/pallas_call | solution.py:1074
  268.3 49.6 %last_sums.1 = (bf16[2,128,768]{2,1,0:T(8,128)(2,1)}, bf16[4,48,384]{2,1,0:T(8,128)(2,1)}, bf16[4,48,384]{2,1,0:T(8,128)(2,1)}, bf16[4,48,384]{2,1,0:T(8,128)(2,...) custom-call(bf16[512,768]{1,0:T(8,128)(2,1)} %get-tuple-element.157., ...), custom_call_target="tpu_custom_call" | custom-call | flops 18119393280 | bytes 23592960 | tf_op jit(solution)/shard_map/last_sums/pallas_call | solution.py:1230
  317.9 5.6 %results.1 = (bf16[2,256,768]{2,1,0:T(8,128)(2,1)}, f32[2,256,768]{2,1,0:T(8,128)}, f32[2,128,768]{2,1,0:T(8,128)}, f32[1,96]{1,0:T(1,128)}, f32[96,768]{1,0:T(8...) custom-call(bf16[2,256,768]{2,1,0:T(8,128)(2,1)} %get-tuple-element., ...), custom_call_target="tpu_custom_call" | custom-call | bytes 14680064 | tf_op jit(solution)/shard_map/results/pallas_call | solution.py:1288
